TPU v7x, 32 devices: a whole 2x2x4 slice. The times are simulated.
32 devices in a mesh: cuts: 8 (over z, x), stem: 4 (over y, core).
Axes of the slice: x: 2, y: 2, z: 4, core: 2. Of those that a mesh axis runs over, the one named last changes fastest.
Arguments:
- stem_tensor: bfloat16 [8, 64, 1024], P('stem'), may hold values from -6 to 6
- mid_tensors: bfloat16 [512, 512, 128], P(('cuts', 'stem')), may hold values from -0.1875 to 0.1875
- right_tensors: bfloat16 [8, 512, 64, 128], P(None, ('cuts', 'stem')), may hold values from -0.0078125 to 0.0078125
Outputs:
- amplitudes: float32 [8192], P('cuts')
All inputs are finite; a program needn't handle non-finite values.
Results may differ from a plain program's by a relative error of at most 0.0029.
Values may be sent and summed in bfloat16 or wider, within the bound.
No kernel may reach another device: no remote copies, remote signals or barrier semaphores. Data moves between devices by JAX's collectives and lax.ppermute only.
A program may use at most 64 MiB of HBM per device.

v0:
```python
import jax
import jax.numpy as jnp
from jax import lax
from jax.sharding import PartitionSpec as P


def widen(tensor):
    half_width = tensor.shape[-1] // 2
    real_part = tensor[..., :half_width]
    imag_part = tensor[..., half_width:]
    upper_rows = jnp.concatenate([real_part, imag_part], axis=-1)
    lower_rows = jnp.concatenate([-imag_part, real_part], axis=-1)
    return jnp.concatenate([upper_rows, lower_rows], axis=-2)


def on_device(stem_tensor, mid_tensors, right_tensors):
    local_blocks, rows_a, width = stem_tensor.shape
    cols_b = right_tensors.shape[-1]
    widened = jnp.moveaxis(widen(mid_tensors), 0, 1).reshape(width, -1)
    fragment = lax.all_gather(stem_tensor, "stem", axis=0, tiled=True)
    flattened = fragment.reshape(-1, width)
    product = jnp.dot(flattened, widened, preferred_element_type=jnp.float32)
    first_step = product.astype(jnp.bfloat16).reshape(fragment.shape[0], rows_a, -1)
    right_wide = widen(right_tensors).reshape(first_step.shape[0], -1, cols_b)
    partial_sum = jnp.einsum(
        "iaq,iqb->ab", first_step, right_wide, preferred_element_type=jnp.float32
    ).reshape(-1)
    summed = lax.psum(partial_sum, ("cuts", "stem"))
    portion = partial_sum.shape[0] // lax.axis_size("cuts")
    return lax.dynamic_slice_in_dim(summed, lax.axis_index("cuts") * portion, portion)


def solution(mesh):
    return jax.shard_map(
        on_device,
        mesh=mesh,
        in_specs=(
            P("stem", None, None),
            P(("cuts", "stem"), None, None),
            P(None, ("cuts", "stem"), None, None),
        ),
        out_specs=P("cuts"),
        check_vma=False,
    )
```

profile of v0, /device:TPU:0, one launch (start us, length us, event | category | flops | bytes accessed | tf_op | source)
XLA Modules:
  0.0 81.2 jit_solution(12711142892477624268)
XLA Ops:
  6.5 0.0 all-gather.2.cloned.1.call-start
  6.5 0.7 all-gather.2.cloned.1.call-update
  7.3 2.9 %copy.9 = bf16[16,512,128]{1,2,0:T(8,128)(2,1)S(1)} copy(bf16[16,512,128]{2,1,0:T(8,128)(2,1)} %param.4) | data formatting | bytes 4194304 | tf_op args[1]
  10.1 0.1 slice_negate_fusion.1
  10.3 0.0 copy-start.1
  10.3 2.2 %maximum_maximum_fusion = bf16[16,1024,128]{1,2,0:T(8,128)(2,1)} fusion(bf16[16,512,64]{1,2,0:T(8,128)(2,1)S(1)} %get-tuple-element.8, bf16[16,512,64]{1,2,0:T(8,128)(2,1)S(1)} %get-tuple-element.7, bf16[16,512,128]{1,2,0:T(8,128)(2,1)S(1)} %copy.9), kind=kLoop, calls=%fused_computation | loop fusion | flops 12582912 | bytes 8388608 | tf_op jit(solution)/shard_map/concatenate | solution.py:13
  12.5 0.1 copy-done.1
  12.6 0.9 %slice_negate_fusion = (bf16[8,16,64,64]{3,2,1,0:T(8,128)(2,1)S(1)}, bf16[8,16,64,64]{3,2,1,0:T(8,128)(2,1)S(1)}) fusion(bf16[8,16,64,128]{3,2,1,0:T(8,128)(2,1)S(1)} %copy-done.1), kind=kLoop, calls=%fused_computation.3 | loop fusion | flops 524288 | bytes 4194304 | tf_op jit(solution)/shard_map/neg | solution.py:12
  13.5 3.5 %maximum_maximum_fusion.1 = bf16[8,16,128,128]{3,2,1,0:T(8,128)(2,1)} fusion(bf16[8,16,64,64]{3,2,1,0:T(8,128)(2,1)S(1)} %get-tuple-element.6, bf16[8,16,64,64]{3,2,1,0:T(8,128)(2,1)S(1)} %get-tuple-element.5, bf16[8,16,64,128]{3,2,1,0:T(8,128)(2,1)S(1)} %copy-done.1), kind=kLoop, calls=%fused_computation.1 | loop fusion | flops 12582912 | bytes 8388608 | tf_op jit(solution)/shard_map/concatenate | solution.py:13
  17.0 11.4 %all-gather.2.cloned.1.call-done = bf16[8,64,1024]{2,1,0:T(8,128)(2,1)} async-done(((bf16[2,64,1024]{2,1,0:T(8,128)(2,1)}), bf16[8,64,1024]{2,1,0:T(8,128)(2,1)}) %all-gather.2.cloned.1.call-update) | async-done | bytes 1048592 | tf_op jit(solution)/shard_map/all_gather | solution.py:20
  28.4 0.0 copy-start
  28.4 5.0 %convolution_convert_fusion = bf16[2048,512]{0,1:T(8,128)(2,1)S(1)} fusion(bf16[1024,2048]{0,1:T(8,128)(2,1)} %bitcast.18, bf16[512,1024]{1,0:T(8,128)(2,1)} %bitcast.19), kind=kOutput, calls=%fused_computation.2 | convolution fusion | flops 2148532224 | bytes 7340032 | tf_op jit(solution)/shard_map/dot_general | solution.py:22
  33.4 0.0 copy-done
  33.4 0.9 %convolution_bitcast_fusion = f32[8192]{0:T(1024)S(1)} fusion(bf16[8,64,2048]{2,1,0:T(8,128)(2,1)S(1)} %bitcast.17, bf16[8,2048,128]{2,1,0:T(8,128)(2,1)S(1)} %bitcast.16), kind=kOutput, calls=%fused_computation.4 | convolution fusion | flops 268435456 | bytes 6324224 | tf_op jit(solution)/shard_map/iaq,iqb->ab/dot_general | solution.py:25
  34.3 39.5 %psum.7 = f32[8192]{0:T(1024)S(1)} all-reduce(f32[8192]{0:T(1024)S(1)} %convolution_bitcast_fusion), channel_id=1, replica_groups=mesh['cuts'=8,'stem'=4] {'cuts','stem'}, use_global_device_ids=true, to_apply=%region_0.0 | all-reduce | flops 8192 | bytes 65536 | tf_op jit(solution)/shard_map/psum | solution.py:28
  73.8 0.6 dynamic_slice.3
Async XLA Ops:
  6.5 21.8 %all-gather.2.cloned.1.call-start = ((), (), s32[]{:S(2)}) async-start(), calls=%async_computation | async-start | bytes 1310720 | tf_op jit(solution)/shard_map/all_gather | solution.py:20
  10.3 2.3 %copy-start.1 = (bf16[8,16,64,128]{3,2,1,0:T(8,128)(2,1)S(1)}, bf16[8,16,64,128]{3,2,1,0:T(8,128)(2,1)}, u32[]{:S(2)}) copy-start(bf16[8,16,64,128]{3,2,1,0:T(8,128)(2,1)} %param.5) | copy-start | bytes 6291460
  28.4 5.0 %copy-start = (bf16[8,16,128,128]{3,2,1,0:T(8,128)(2,1)S(1)}, bf16[8,16,128,128]{3,2,1,0:T(8,128)(2,1)}, u32[]{:S(2)}) copy-start(bf16[8,16,128,128]{3,2,1,0:T(8,128)(2,1)} %maximum_maximum_fusion.1) | copy-start | bytes 12582916
Sparse Core Ops, SparseCore 0:
  8.9 19.4 all-gather.1
where the time goes:
time: 81.5 us; the launch traced here: 81.2 us
  blocking collectives  39.5 us (48%)
  between operations  13.5 us (17%)
  waiting for transfers between devices  12.1 us (15%)
  other arithmetic  6.78 us (8%)
  matrix products  5.86 us (7%)
  local copies, waits for them, and re-layouts  3.54 us (4%)
    psum x1, blocking collectives, on_device(): summed = lax.psum(partial_sum, ('cuts', 'stem'))  39.5 us
    all_gather x1, waiting for transfers between devices, on_device(): fragment = lax.all_gather(stem_tensor, 'stem', axis=0, tiled=True)  11.4 us
    concatenate x2, other arithmetic, widen(): return jnp.concatenate([upper_rows, lower_rows], axis=-2)  5.77 us
    dot_general x1, matrix products, on_device(): product = jnp.dot(flattened, widened, preferred_element_type=jnp.float32)  5 us
    unnamed x5, local copies, waits for them, and re-layouts  2.94 us
  transfers between devices with their start and end apart: 1, of which 1 were waited for; matrix products, arithmetic and copies ran while one was open for 12% of the time, Pallas kernels for 0%

commit v1 on v0

v1 whole, which is shorter than its diff:
```python
import functools

import jax
import jax.numpy as jnp
from jax import lax
from jax.experimental import pallas as pl
from jax.experimental.pallas import tpu as pltpu
from jax.sharding import PartitionSpec as P


def turn(x):
    half = x.shape[-1] // 2
    lane = lax.broadcasted_iota(jnp.int32, x.shape, x.ndim - 1)
    rolled = pltpu.roll(x, half, x.ndim - 1)
    return jnp.where(lane < half, -rolled, rolled)


def branch_kernel(place_ref, mid_ref, right_ref, out_ref):
    pairs, _, width = mid_ref.shape
    blocks = right_ref.shape[0]
    left = jnp.concatenate([mid_ref[j] for j in range(pairs)], axis=1)
    columns = []
    for i in range(blocks):
        rows = []
        for j in range(pairs):
            w = right_ref[i, j]
            rows += [w, turn(w.astype(jnp.float32)).astype(w.dtype)]
        columns.append(jnp.concatenate(rows, axis=0))
    wide = jnp.concatenate(columns, axis=1)
    full = jnp.dot(left, wide, preferred_element_type=jnp.float32)
    high = full.astype(jnp.bfloat16)
    low = (full - high.astype(jnp.float32)).astype(jnp.bfloat16)
    for i in range(blocks):
        cols = slice(i * width, (i + 1) * width)
        out_ref[i] = jnp.concatenate([high[:, cols], low[:, cols]], axis=1)


def branch_sums(place, mid, right, stems):
    pairs, depth, width = mid.shape
    blocks = right.shape[0] // stems
    flops = 2 * depth * pairs * width * right.shape[0] * width
    return pl.pallas_call(
        branch_kernel,
        grid_spec=pltpu.PrefetchScalarGridSpec(
            num_scalar_prefetch=1,
            grid=(stems,),
            in_specs=[
                pl.BlockSpec(mid.shape, lambda p, place: (0, 0, 0)),
                pl.BlockSpec((blocks,) + right.shape[1:], lambda p, place: (place[0] ^ p, 0, 0, 0)),
            ],
            out_specs=pl.BlockSpec((blocks, depth, 2 * width), lambda p, place: (p, 0, 0)),
        ),
        out_shape=jax.ShapeDtypeStruct((right.shape[0], depth, 2 * width), jnp.bfloat16),
        compiler_params=pltpu.CompilerParams(vmem_limit_bytes=40 * 1024 * 1024),
        cost_estimate=pl.CostEstimate(flops=flops, bytes_accessed=6 << 20, transcendentals=0),
        name="branch_sums",
    )(place, mid, right)


def close_kernel(*refs):
    *stem_refs, sums_ref, out_ref = refs
    total = None
    at = 0
    for ref in stem_refs:
        for i in range(ref.shape[0]):
            block = ref[i]
            half = block.shape[-1] // 2
            rows = jnp.concatenate([block[:, :half], block[:, half:]], axis=0)
            term = jnp.dot(rows, sums_ref[at], preferred_element_type=jnp.float32)
            total = term if total is None else total + term
            at += 1
    width = total.shape[-1] // 2
    total = total[:, :width] + total[:, width:]
    half = total.shape[0] // 2
    out_ref[...] = total[:half] + turn(total[half:])


def close(stem_pieces, sums):
    rows = stem_pieces[0].shape[1]
    width = sums.shape[-1] // 2
    return pl.pallas_call(
        close_kernel,
        out_shape=jax.ShapeDtypeStruct((rows, width), jnp.float32),
        compiler_params=pltpu.CompilerParams(vmem_limit_bytes=40 * 1024 * 1024),
        cost_estimate=pl.CostEstimate(flops=4 * rows * sums.size, bytes_accessed=3 << 20, transcendentals=0),
        name="close",
    )(*stem_pieces, sums)


def on_device(stem_tensor, mid_tensors, right_tensors):
    stems = lax.axis_size("stem")
    cuts = lax.axis_size("cuts")

    def swap(x, p):
        return lax.ppermute(x, "stem", [(s, s ^ p) for s in range(stems)])

    pieces = [stem_tensor]
    step = stems // 2
    pieces = {0: stem_tensor}
    while step:
        for p in list(pieces):
            pieces[p ^ step] = swap(pieces[p], step)
        step //= 2
    place = lax.axis_index("stem").astype(jnp.int32).reshape(1)
    sums = branch_sums(place, mid_tensors, right_tensors, stems)
    partial_sum = close([pieces[p] for p in range(stems)], sums)
    blocks = partial_sum.reshape(cuts, 1, -1)
    spread = jnp.broadcast_to(blocks, (cuts, stems, blocks.shape[-1])).reshape(cuts * stems, -1)
    got = lax.all_to_all(spread, ("cuts", "stem"), 0, 0, tiled=True)
    return jnp.sum(got, axis=0)


def solution(mesh):
    return jax.shard_map(
        on_device,
        mesh=mesh,
        in_specs=(
            P("stem", None, None),
            P(("cuts", "stem"), None, None),
            P(None, ("cuts", "stem"), None, None),
        ),
        out_specs=P("cuts"),
        check_vma=False,
    )
```

time: 81.5 us -> 31.8 us (0.39)
  blocking collectives: 39.5 us -> 14.2 us
  between operations: 13.5 us -> 0.07 us
  other arithmetic: 6.78 us -> 0.69 us
  matrix products: 5.86 us -> 0 us
  waiting for transfers between devices: 12.1 us -> 6.51 us
  Pallas kernels: 0 us -> 3.73 us
  starting transfers between devices: 0.01 us -> 2.97 us
    psum x1 -> x0, blocking collectives: 39.5 us -> none  [on_device(): summed = lax.psum(partial_sum, ('cuts', 'stem'))]
    all_to_all x0 -> x1, blocking collectives: none -> 14.2 us  [on_device(): got = lax.all_to_all(spread, ('cuts', 'stem'), 0, 0, tiled=True)]
    all_gather x1 -> x0, waiting for transfers between devices: 11.4 us -> none  [on_device(): fragment = lax.all_gather(stem_tensor, 'stem', axis=0, tiled=True)]
    ppermute x0 -> x3, waiting for transfers between devices: none -> 6.51 us  [swap(): return lax.ppermute(x, 'stem', [(s, s ^ p) for s in range(stems)])]
    dot_general x2 -> x0, matrix products: 5.86 us -> none  [the longest x1 5 us: on_device(): product = jnp.dot(flattened, widened, preferred_element_type=jnp.float32)]
    concatenate x2 -> x0, other arithmetic: 5.77 us -> none  [widen(): return jnp.concatenate([upper_rows, lower_rows], axis=-2)]
    pallas_call x0 -> x2, Pallas kernels: none -> 3.73 us  [the longest x1 3.2 us: branch_sums(): pl.pallas_call(branch_kernel, grid_spec=pltpu.PrefetchScalarGridSpec(num_...]
    ppermute x0 -> x3, starting transfers between devices: none -> 2.97 us  [swap(): return lax.ppermute(x, 'stem', [(s, s ^ p) for s in range(stems)])]
  transfers between devices with their start and end apart: 1 -> 3, of which waited for: 1 -> 1; matrix products, arithmetic and copies ran while one was open for 12% -> 0% of each run, Pallas kernels for 0% -> 10%
where the time goes in v1:
time: 31.8 us; the launch traced here: 31.6 us
  blocking collectives  14.2 us (45%)
  waiting for transfers between devices  6.51 us (20%)
  Pallas kernels  3.73 us (12%)
  local copies, waits for them, and re-layouts  3.39 us (11%)
  starting transfers between devices  2.97 us (9%)
  other arithmetic  0.69 us (2%)
    all_to_all x1, blocking collectives, on_device(): got = lax.all_to_all(spread, ('cuts', 'stem'), 0, 0, tiled=True)  14.2 us
    ppermute x3, waiting for transfers between devices, swap(): return lax.ppermute(x, 'stem', [(s, s ^ p) for s in range(stems)])  6.51 us
    pallas_call x1, Pallas kernels, branch_sums(): pl.pallas_call(branch_kernel, grid_spec=pltpu.PrefetchScalarGridSpec(num_...  3.2 us
    unnamed x6, local copies, waits for them, and re-layouts  3.19 us
    ppermute x3, starting transfers between devices, swap(): return lax.ppermute(x, 'stem', [(s, s ^ p) for s in range(stems)])  2.97 us
    reduce_sum x1, other arithmetic, on_device(): return jnp.sum(got, axis=0)  0.69 us
  transfers between devices with their start and end apart: 3, of which 1 were waited for; matrix products, arithmetic and copies ran while one was open for 0% of the time, Pallas kernels for 10%

profile of v1, /device:TPU:0, one launch (start us, length us, event | category | flops | bytes accessed | tf_op | source)
XLA Modules:
  0.0 31.6 jit_solution(2773232854240000100)
XLA Ops:
  0.0 3.0 %collective-permute-start.1 = (bf16[2,64,1024]{2,1,0:T(8,128)(2,1)}, bf16[2,64,1024]{2,1,0:T(8,128)(2,1)S(1)}, u32[]{:S(2)}, u32[]{:S(2)}) collective-permute-start(bf16[2,64,1024]{2,1,0:T(8,128)(2,1)} %refs_0_.1), channel_id=1, source_target_pairs={{0,2},{1,3},{2,0},{3,1},{4,6},{5,7},{6,4},{7,5},{8,10},{9,11},{10,... | collective-permute-start | bytes 786440 | tf_op jit(solution)/shard_map/ppermute | solution.py:95
  3.0 0.0 collective-permute-start
  3.0 6.5 %collective-permute-done.1.refs_2_ = bf16[2,64,1024]{2,1,0:T(8,128)(2,1)S(1)} collective-permute-done((bf16[2,64,1024]{2,1,0:T(8,128)(2,1)}, bf16[2,64,1024]{2,1,0:T(8,128)(2,1)S(1)}, u32[]{:S(2)}, u32[]{:S(2)}) %collective-permute-start.1) | collective-permute-done | bytes 262176 | tf_op jit(solution)/shard_map/ppermute | solution.py:95
  9.5 0.0 collective-permute-start.2
  9.5 0.0 copy-start.1
  9.5 1.6 %copy-done.1 = bf16[16,512,128]{2,1,0:T(8,128)(2,1)S(1)} copy-done((bf16[16,512,128]{2,1,0:T(8,128)(2,1)S(1)}, bf16[16,512,128]{2,1,0:T(8,128)(2,1)}, u32[]{:S(2)}) %copy-start.1) | copy-done | bytes 2097176
  11.1 0.0 copy-start.2
  11.1 1.6 %copy-done.2 = bf16[8,16,64,128]{3,2,1,0:T(8,128)(2,1)S(1)} copy-done((bf16[8,16,64,128]{3,2,1,0:T(8,128)(2,1)S(1)}, bf16[8,16,64,128]{3,2,1,0:T(8,128)(2,1)}, u32[]{:S(2)}) %copy-start.2) | copy-done | bytes 2097176
  12.7 0.0 copy-start
  12.7 3.2 %branch_sums.1.refs_4_ = bf16[8,512,256]{2,1,0:T(8,128)(2,1)S(1)} custom-call(s32[1]{0:T(128)} %bitcast.place_ref, bf16[16,512,128]{2,1,0:T(8,128)(2,1)S(1)} %copy-done.1, bf16[8,16,64,128]{3,2,1,0:T(8,128)(2,1)S(1)} %copy-done.2), custom_call_target="tpu_custom_call" | custom-call | flops 2147483648 | bytes 6291456 | tf_op jit(solution)/shard_map/branch_sums/pallas_call | solution.py:42
  15.9 0.0 collective-permute-done.refs_1_
  15.9 0.0 collective-permute-done.2.refs_3_
  15.9 0.0 copy-done
  15.9 0.5 %close.1 = f32[64,128]{1,0:T(8,128)S(1)} custom-call(bf16[2,64,1024]{2,1,0:T(8,128)(2,1)S(1)} %copy-done, bf16[2,64,1024]{2,1,0:T(8,128)(2,1)S(1)} %collective-permute-done.refs_1_, bf16[2,64,1024]{2,1,0:T(8,128)(2,1)S(1)} %collective-permute-done.1.refs_2_, bf16[2,64,1024]{2,1,0:T(8,128)(2,1)S(1)} %collective-permute-done.2.refs_3_, ...), custom_call_target="tpu_custom_call" | custom-call | flops 268435456 | bytes 3145728 | tf_op jit(solution)/shard_map/close/pallas_call | solution.py:81
  16.5 0.2 all_to_all.6
  16.7 14.2 %all_to_all.9 = f32[32,1,1024]{2,1,0:T(1,128)S(1)} all-to-all(f32[32,1,1024]{2,1,0:T(1,128)S(1)} %all_to_all.6), channel_id=1, replica_groups=mesh['cuts'=8,'stem'=4] {'cuts','stem'}, dimensions={0} | all-to-all | bytes 262144 | tf_op jit(solution)/shard_map/all_to_all | solution.py:109
  30.9 0.7 %reduce_sum.9 = f32[1024]{0:T(1024)} reduce(f32[32,1,1024]{2,1,0:T(1,128)S(1)} %all_to_all.9, f32[]{:T(128)} %constant.1.clone.1), dimensions={0,1}, to_apply=%region_0.0 | reduce | flops 31744 | bytes 135172 | tf_op jit(solution)/shard_map/reduce_sum | solution.py:110
  (2 shorter events, 0.0 us)
Async XLA Ops:
  0.0 9.5 %collective-permute-start.1 = (bf16[2,64,1024]{2,1,0:T(8,128)(2,1)}, bf16[2,64,1024]{2,1,0:T(8,128)(2,1)S(1)}, u32[]{:S(2)}, u32[]{:S(2)}) collective-permute-start(bf16[2,64,1024]{2,1,0:T(8,128)(2,1)} %refs_0_.1), channel_id=1, source_target_pairs={{0,2},{1,3},{2,0},{3,1},{4,6},{5,7},{6,4},{7,5},{8,10},{9,11},{10,... | collective-permute-start | bytes 786440 | tf_op jit(solution)/shard_map/ppermute | solution.py:95
  3.0 12.9 %collective-permute-start = (bf16[2,64,1024]{2,1,0:T(8,128)(2,1)}, bf16[2,64,1024]{2,1,0:T(8,128)(2,1)S(1)}, u32[]{:S(2)}, u32[]{:S(2)}) collective-permute-start(bf16[2,64,1024]{2,1,0:T(8,128)(2,1)} %refs_0_.1), channel_id=1, source_target_pairs={{0,1},{1,0},{2,3},{3,2},{4,5},{5,4},{6,7},{7,6},{8,9},{9,8},{10,11... | collective-permute-start | bytes 786440 | tf_op jit(solution)/shard_map/ppermute | solution.py:95
  9.5 6.4 %collective-permute-start.2 = (bf16[2,64,1024]{2,1,0:T(8,128)(2,1)S(1)}, bf16[2,64,1024]{2,1,0:T(8,128)(2,1)S(1)}, u32[]{:S(2)}, u32[]{:S(2)}) collective-permute-start(bf16[2,64,1024]{2,1,0:T(8,128)(2,1)S(1)} %collective-permute-done.1.refs_2_), channel_id=1, source_target_pairs={{0,1},{1,0},{2,3},{3,2},{4,5},{5,4},{6,7},{7,6},{8,9},{9,8},{10,11... | collective-permute-start | bytes 786440 | tf_op jit(solution)/shard_map/ppermute | solution.py:95
  9.5 1.6 %copy-start.1 = (bf16[16,512,128]{2,1,0:T(8,128)(2,1)S(1)}, bf16[16,512,128]{2,1,0:T(8,128)(2,1)}, u32[]{:S(2)}) copy-start(bf16[16,512,128]{2,1,0:T(8,128)(2,1)} %mid_ref.1) | copy-start | bytes 6291460
  11.1 1.6 %copy-start.2 = (bf16[8,16,64,128]{3,2,1,0:T(8,128)(2,1)S(1)}, bf16[8,16,64,128]{3,2,1,0:T(8,128)(2,1)}, u32[]{:S(2)}) copy-start(bf16[8,16,64,128]{3,2,1,0:T(8,128)(2,1)} %right_ref.1) | copy-start | bytes 6291460
  12.7 3.2 %copy-start = (bf16[2,64,1024]{2,1,0:T(8,128)(2,1)S(1)}, bf16[2,64,1024]{2,1,0:T(8,128)(2,1)}, u32[]{:S(2)}) copy-start(bf16[2,64,1024]{2,1,0:T(8,128)(2,1)} %refs_0_.1) | copy-start | bytes 786436

commit v2 on v0

v2 whole, which is shorter than its diff:
```python
import jax
import jax.numpy as jnp
from jax import lax
from jax.experimental import pallas as pl
from jax.experimental.pallas import tpu as pltpu
from jax.sharding import PartitionSpec as P

VMEM_LIMIT = 52 * 1024 * 1024


def turn(x):
    half = x.shape[-1] // 2
    lane = lax.broadcasted_iota(jnp.int32, x.shape, x.ndim - 1)
    rolled = pltpu.roll(x, half, x.ndim - 1)
    return jnp.where(lane < half, -rolled, rolled)


def two_parts(full):
    high = full.astype(jnp.bfloat16)
    low = (full - high.astype(jnp.float32)).astype(jnp.bfloat16)
    return jnp.concatenate([high, low], axis=1)


def apply_stem(block, sums):
    half = block.shape[-1] // 2
    rows = jnp.concatenate([block[:, :half], block[:, half:]], axis=0)
    both = jnp.dot(rows, two_parts(sums), preferred_element_type=jnp.float32)
    width = both.shape[-1] // 2
    return both[:, :width] + both[:, width:]


def branch_kernel(mid_hbm, right_hbm, own_ref, near_ref, kept_ref, sent_ref, part_ref,
                  mid_ref, right_ref, mid_sem, right_sem):
    pairs, depth, width = mid_ref.shape
    blocks = own_ref.shape[0]
    groups = right_ref.shape[0] // blocks
    me = lax.axis_index("stem")
    mid_copies = [
        pltpu.make_async_copy(mid_hbm.at[pl.ds(j, 4)], mid_ref.at[pl.ds(j, 4)], mid_sem.at[j // 4])
        for j in range(0, pairs, 4)
    ]
    right_copies = [
        pltpu.make_async_copy(
            right_hbm.at[pl.ds((me ^ p) * blocks, blocks)], right_ref.at[pl.ds(p * blocks, blocks)], right_sem.at[p]
        )
        for p in range(groups)
    ]
    order = list(range(groups - 1, -1, -1))
    right_copies[order[0]].start()
    for copy in mid_copies:
        copy.start()
    for p in order[1:]:
        right_copies[p].start()
    for copy in mid_copies:
        copy.wait()
    part = None
    for p in order:
        right_copies[p].wait()
        left = jnp.concatenate([mid_ref[j] for j in range(pairs)], axis=1)
        columns = []
        for b in range(blocks):
            rows = []
            for j in range(pairs):
                w = right_ref[p * blocks + b, j]
                rows += [w, turn(w.astype(jnp.float32)).astype(w.dtype)]
            columns.append(jnp.concatenate(rows, axis=0))
        sums = jnp.dot(left, jnp.concatenate(columns, axis=1), preferred_element_type=jnp.float32)
        for b in range(blocks):
            one = sums[:, b * width:(b + 1) * width]
            if p < 2:
                term = apply_stem((own_ref, near_ref)[p][b], one)
                part = term if part is None else part + term
            elif p % 2:
                sent_ref[(p // 2 - 1) * blocks + b] = one.astype(jnp.bfloat16)
            else:
                kept_ref[(p // 2 - 1) * blocks + b] = one
    part_ref[...] = part


def branch_sums(mid, right, own, near):
    pairs, depth, width = mid.shape
    total = right.shape[0]
    blocks, rows, _ = own.shape
    groups = total // blocks
    far = (groups // 2 - 1) * blocks
    vmem = pl.BlockSpec(memory_space=pltpu.VMEM)
    hbm = pl.BlockSpec(memory_space=pltpu.HBM)
    return pl.pallas_call(
        branch_kernel,
        in_specs=[hbm, hbm, vmem, vmem],
        out_specs=[vmem, vmem, vmem],
        out_shape=[
            jax.ShapeDtypeStruct((far, depth, width), jnp.float32),
            jax.ShapeDtypeStruct((far, depth, width), jnp.bfloat16),
            jax.ShapeDtypeStruct((2 * rows, width), jnp.float32),
        ],
        scratch_shapes=[
            pltpu.VMEM(mid.shape, mid.dtype),
            pltpu.VMEM(right.shape, right.dtype),
            pltpu.SemaphoreType.DMA((pairs // 4,)),
            pltpu.SemaphoreType.DMA((groups,)),
        ],
        compiler_params=pltpu.CompilerParams(vmem_limit_bytes=VMEM_LIMIT),
        cost_estimate=pl.CostEstimate(
            flops=2 * depth * pairs * width * total * width, bytes_accessed=6 << 20, transcendentals=0
        ),
        name="branch_sums",
    )(mid, right, own, near)


def close_kernel(*refs):
    *far_refs, kept_ref, got_ref, part_ref, out_ref = refs
    part = part_ref[...]
    at = 0
    for ref in far_refs:
        for b in range(ref.shape[0]):
            part += apply_stem(ref[b], kept_ref[at] + got_ref[at].astype(jnp.float32))
            at += 1
    half = part.shape[0] // 2
    out_ref[...] = part[:half] + turn(part[half:])


def close(far, kept, got, part):
    rows, width = part.shape[0] // 2, part.shape[1]
    return pl.pallas_call(
        close_kernel,
        out_shape=jax.ShapeDtypeStruct((rows, width), jnp.float32),
        compiler_params=pltpu.CompilerParams(vmem_limit_bytes=VMEM_LIMIT // 2),
        cost_estimate=pl.CostEstimate(flops=8 * rows * kept.size, bytes_accessed=1 << 20, transcendentals=0),
        name="close",
    )(*far, kept, got, part)


def on_device(stem_tensor, mid_tensors, right_tensors):
    stems = lax.axis_size("stem")
    cuts = lax.axis_size("cuts")

    def swap(x, p):
        return lax.ppermute(x, "stem", [(s, s ^ p) for s in range(stems)])

    far = [swap(stem_tensor, p) for p in range(2, stems, 2)]
    near = swap(stem_tensor, 1)
    kept, sent, part = branch_sums(mid_tensors, right_tensors, stem_tensor, near)
    got = swap(sent, 1)
    partial_sum = close(far, kept, got, part)
    spread = lax.all_to_all(partial_sum.reshape(cuts, -1), "cuts", 0, 0, tiled=True)
    amplitudes = jnp.sum(spread, axis=0)
    step = 1
    while step < stems:
        amplitudes = amplitudes + swap(amplitudes, step)
        step *= 2
    return amplitudes


def solution(mesh):
    return jax.shard_map(
        on_device,
        mesh=mesh,
        in_specs=(
            P("stem", None, None),
            P(("cuts", "stem"), None, None),
            P(None, ("cuts", "stem"), None, None),
        ),
        out_specs=P("cuts"),
        check_vma=False,
    )
```

time: 81.5 us -> 31.7 us (0.39)
  blocking collectives: 39.5 us -> 12.5 us
  between operations: 13.5 us -> 0.03 us
  Pallas kernels: 0 us -> 8.02 us
  waiting for transfers between devices: 12.1 us -> 4.55 us
  other arithmetic: 6.78 us -> 0.63 us
  matrix products: 5.86 us -> 0 us
  starting transfers between devices: 0.01 us -> 4.85 us
  local copies, waits for them, and re-layouts: 3.54 us -> 0.98 us
    psum x1 -> x0, blocking collectives: 39.5 us -> none  [on_device(): summed = lax.psum(partial_sum, ('cuts', 'stem'))]
    all_to_all x0 -> x1, blocking collectives: none -> 12.5 us  [on_device(): lax.all_to_all(partial_sum.reshape(cuts, -1), 'cuts', 0, 0, tiled=True)]
    all_gather x1 -> x0, waiting for transfers between devices: 11.4 us -> none  [on_device(): fragment = lax.all_gather(stem_tensor, 'stem', axis=0, tiled=True)]
    pallas_call x0 -> x2, Pallas kernels: none -> 8.02 us  [the longest x1 7.7 us: branch_sums(): pl.pallas_call(branch_kernel, in_specs=[hbm, hbm, vmem, vmem], out_specs=...]
    dot_general x2 -> x0, matrix products: 5.86 us -> none  [the longest x1 5 us: on_device(): product = jnp.dot(flattened, widened, preferred_element_type=jnp.float32)]
    concatenate x2 -> x0, other arithmetic: 5.77 us -> none  [widen(): return jnp.concatenate([upper_rows, lower_rows], axis=-2)]
    ppermute x0 -> x5, starting transfers between devices: none -> 4.85 us  [swap(): return lax.ppermute(x, 'stem', [(s, s ^ p) for s in range(stems)])]
    ppermute x0 -> x5, waiting for transfers between devices: none -> 4.55 us  [swap(): return lax.ppermute(x, 'stem', [(s, s ^ p) for s in range(stems)])]
  transfers between devices with their start and end apart: 1 -> 5, of which waited for: 1 -> 3; matrix products, arithmetic and copies ran while one was open for 12% -> 0% of each run, Pallas kernels for 0% -> 24%
where the time goes in v2:
time: 31.7 us; the launch traced here: 31.6 us
  blocking collectives  12.5 us (39%)
  Pallas kernels  8.02 us (25%)
  starting transfers between devices  4.85 us (15%)
  waiting for transfers between devices  4.55 us (14%)
  local copies, waits for them, and re-layouts  0.98 us (3%)
  other arithmetic  0.63 us (2%)
    all_to_all x1, blocking collectives, on_device(): lax.all_to_all(partial_sum.reshape(cuts, -1), 'cuts', 0, 0, tiled=True)  12.5 us
    pallas_call x1, Pallas kernels, branch_sums(): pl.pallas_call(branch_kernel, in_specs=[hbm, hbm, vmem, vmem], out_specs=...  7.7 us
    ppermute x5, starting transfers between devices, swap(): return lax.ppermute(x, 'stem', [(s, s ^ p) for s in range(stems)])  4.85 us
    ppermute x5, waiting for transfers between devices, swap(): return lax.ppermute(x, 'stem', [(s, s ^ p) for s in range(stems)])  4.55 us
    unnamed x2, local copies, waits for them, and re-layouts  0.98 us
  transfers between devices with their start and end apart: 5, of which 3 were waited for; matrix products, arithmetic and copies ran while one was open for 0% of the time, Pallas kernels for 24%

profile of v2, /device:TPU:0, one launch (start us, length us, event | category | flops | bytes accessed | tf_op | source)
XLA Modules:
  0.0 31.6 jit_solution(3386503414994083271)
XLA Ops:
  0.0 0.5 %collective-permute-start.1 = (bf16[2,64,1024]{2,1,0:T(8,128)(2,1)}, bf16[2,64,1024]{2,1,0:T(8,128)(2,1)S(1)}, u32[]{:S(2)}, u32[]{:S(2)}) collective-permute-start(bf16[2,64,1024]{2,1,0:T(8,128)(2,1)} %own_ref.1), channel_id=1, source_target_pairs={{0,1},{1,0},{2,3},{3,2},{4,5},{5,4},{6,7},{7,6},{8,9},{9,8},{10,11... | collective-permute-start | bytes 786440 | tf_op jit(solution)/shard_map/ppermute | solution.py:139
  0.5 2.5 %collective-permute-start = (bf16[2,64,1024]{2,1,0:T(8,128)(2,1)}, bf16[2,64,1024]{2,1,0:T(8,128)(2,1)S(1)}, u32[]{:S(2)}, u32[]{:S(2)}) collective-permute-start(bf16[2,64,1024]{2,1,0:T(8,128)(2,1)} %own_ref.1), channel_id=1, source_target_pairs={{0,2},{1,3},{2,0},{3,1},{4,6},{5,7},{6,4},{7,5},{8,10},{9,11},{10,... | collective-permute-start | bytes 786440 | tf_op jit(solution)/shard_map/ppermute | solution.py:139
  3.0 0.0 collective-permute-done.1.near_ref
  3.0 0.0 copy-start
  3.0 1.0 %copy-done = bf16[2,64,1024]{2,1,0:T(8,128)(2,1)S(1)} copy-done((bf16[2,64,1024]{2,1,0:T(8,128)(2,1)S(1)}, bf16[2,64,1024]{2,1,0:T(8,128)(2,1)}, u32[]{:S(2)}) %copy-start) | copy-done | bytes 262168
  4.0 7.7 %branch_sums.1 = (f32[2,512,128]{2,1,0:T(8,128)S(1)}, bf16[2,512,128]{2,1,0:T(8,128)(2,1)S(1)}, f32[128,128]{1,0:T(8,128)S(1)}) custom-call(bf16[16,512,128]{2,1,0:T(8,128)(2,1)} %mid_hbm.1, bf16[8,16,64,128]{3,2,1,0:T(8,128)(2,1)} %right_hbm.1, bf16[2,64,1024]{2,1,0:T(8,128)(2,1)S(1)} %copy-done, bf16[2,64,1024]{2,1,0:T(8,128)(2,1)S(1)} %collective-permute-done.1.near_ref), custom_call_target="tpu_custom_call" | custom-call | flops 2147483648 | bytes 6291456 | tf_op jit(solution)/shard_map/branch_sums/pallas_call | solution.py:88
  11.7 0.3 collective-permute-start.2
  12.0 0.0 collective-permute-done.refs_0_
  12.0 1.3 %collective-permute-done.2.refs_2_ = bf16[2,512,128]{2,1,0:T(8,128)(2,1)S(1)} collective-permute-done((bf16[2,512,128]{2,1,0:T(8,128)(2,1)S(1)}, bf16[2,512,128]{2,1,0:T(8,128)(2,1)S(1)}, u32[]{:S(2)}, u32[]{:S(2)}) %collective-permute-start.2) | collective-permute-done | bytes 262176 | tf_op jit(solution)/shard_map/ppermute | solution.py:139
  13.3 0.3 %close.1 = f32[64,128]{1,0:T(8,128)S(1)} custom-call(bf16[2,64,1024]{2,1,0:T(8,128)(2,1)S(1)} %collective-permute-done.refs_0_, f32[2,512,128]{2,1,0:T(8,128)S(1)} %get-tuple-element.8.refs_1_, bf16[2,512,128]{2,1,0:T(8,128)(2,1)S(1)} %collective-permute-done.2.refs_2_, f32[128,128]{1,0:T(8,128)S(1)} %get-tuple-element.10.refs_3_), custom_call_target="tpu_custom_call" | custom-call | flops 67108864 | bytes 1048576 | tf_op jit(solution)/shard_map/close/pallas_call | solution.py:125
  13.6 12.5 %all_to_all.9 = f32[8,1,1024]{2,1,0:T(1,128)S(1)} all-to-all(f32[8,1,1024]{2,1,0:T(1,128)S(1)} %bitcast.1), channel_id=1, replica_groups=mesh['cuts'=8,'stem'=4] {'cuts'}, dimensions={0} | all-to-all | bytes 65536 | tf_op jit(solution)/shard_map/all_to_all | solution.py:146
  26.1 0.1 collective-permute-start.3
  26.2 1.2 %collective-permute-done.3 = f32[1024]{0:T(1024)S(1)} collective-permute-done((f32[1024]{0:T(1024)S(1)}, f32[1024]{0:T(1024)S(1)}, u32[]{:S(2)}, u32[]{:S(2)}) %collective-permute-start.3) | collective-permute-done | bytes 4128 | tf_op jit(solution)/shard_map/ppermute | solution.py:139
  27.3 1.5 %collective-permute-start.4 = (f32[1024]{0:T(1024)S(1)}, f32[1024]{0:T(1024)S(1)}, u32[]{:S(2)}, u32[]{:S(2)}) collective-permute-start(f32[1024]{0:T(1024)S(1)} %add.6), channel_id=1, source_target_pairs={{0,2},{1,3},{2,0},{3,1},{4,6},{5,7},{6,4},{7,5},{8,10},{9,11},{10,... | collective-permute-start | bytes 12296 | tf_op jit(solution)/shard_map/ppermute | solution.py:139
  28.9 2.1 %collective-permute-done.4 = f32[1024]{0:T(1024)S(1)} collective-permute-done((f32[1024]{0:T(1024)S(1)}, f32[1024]{0:T(1024)S(1)}, u32[]{:S(2)}, u32[]{:S(2)}) %collective-permute-start.4) | collective-permute-done | bytes 4128 | tf_op jit(solution)/shard_map/ppermute | solution.py:139
  31.0 0.6 %add.7 = f32[1024]{0:T(1024)} add(f32[1024]{0:T(1024)S(1)} %add.6, f32[1024]{0:T(1024)S(1)} %collective-permute-done.4) | non-fusion elementwise | flops 1024 | bytes 12288 | tf_op jit(solution)/shard_map/add | solution.py:150
  (2 shorter events, 0.0 us)
Async XLA Ops:
  0.0 3.0 %collective-permute-start.1 = (bf16[2,64,1024]{2,1,0:T(8,128)(2,1)}, bf16[2,64,1024]{2,1,0:T(8,128)(2,1)S(1)}, u32[]{:S(2)}, u32[]{:S(2)}) collective-permute-start(bf16[2,64,1024]{2,1,0:T(8,128)(2,1)} %own_ref.1), channel_id=1, source_target_pairs={{0,1},{1,0},{2,3},{3,2},{4,5},{5,4},{6,7},{7,6},{8,9},{9,8},{10,11... | collective-permute-start | bytes 786440 | tf_op jit(solution)/shard_map/ppermute | solution.py:139
  0.5 11.5 %collective-permute-start = (bf16[2,64,1024]{2,1,0:T(8,128)(2,1)}, bf16[2,64,1024]{2,1,0:T(8,128)(2,1)S(1)}, u32[]{:S(2)}, u32[]{:S(2)}) collective-permute-start(bf16[2,64,1024]{2,1,0:T(8,128)(2,1)} %own_ref.1), channel_id=1, source_target_pairs={{0,2},{1,3},{2,0},{3,1},{4,6},{5,7},{6,4},{7,5},{8,10},{9,11},{10,... | collective-permute-start | bytes 786440 | tf_op jit(solution)/shard_map/ppermute | solution.py:139
  3.0 1.0 %copy-start = (bf16[2,64,1024]{2,1,0:T(8,128)(2,1)S(1)}, bf16[2,64,1024]{2,1,0:T(8,128)(2,1)}, u32[]{:S(2)}) copy-start(bf16[2,64,1024]{2,1,0:T(8,128)(2,1)} %own_ref.1) | copy-start | bytes 786436
  11.7 1.6 %collective-permute-start.2 = (bf16[2,512,128]{2,1,0:T(8,128)(2,1)S(1)}, bf16[2,512,128]{2,1,0:T(8,128)(2,1)S(1)}, u32[]{:S(2)}, u32[]{:S(2)}) collective-permute-start(bf16[2,512,128]{2,1,0:T(8,128)(2,1)S(1)} %get-tuple-element.9), channel_id=1, source_target_pairs={{0,1},{1,0},{2,3},{3,2},{4,5},{5,4},{6,7},{7,6},{8,9},{9,8},{10,11... | collective-permute-start | bytes 786440 | tf_op jit(solution)/shard_map/ppermute | solution.py:139
  26.1 1.2 %collective-permute-start.3 = (f32[1024]{0:T(1024)S(1)}, f32[1024]{0:T(1024)S(1)}, u32[]{:S(2)}, u32[]{:S(2)}) collective-permute-start(f32[1024]{0:T(1024)S(1)} %reduce_sum.9), channel_id=1, source_target_pairs={{0,1},{1,0},{2,3},{3,2},{4,5},{5,4},{6,7},{7,6},{8,9},{9,8},{10,11... | collective-permute-start | bytes 12296 | tf_op jit(solution)/shard_map/ppermute | solution.py:139
  27.3 3.6 %collective-permute-start.4 = (f32[1024]{0:T(1024)S(1)}, f32[1024]{0:T(1024)S(1)}, u32[]{:S(2)}, u32[]{:S(2)}) collective-permute-start(f32[1024]{0:T(1024)S(1)} %add.6), channel_id=1, source_target_pairs={{0,2},{1,3},{2,0},{3,1},{4,6},{5,7},{6,4},{7,5},{8,10},{9,11},{10,... | collective-permute-start | bytes 12296 | tf_op jit(solution)/shard_map/ppermute | solution.py:139

commit v3 on v0

v3 whole, which is shorter than its diff:
```python
import jax
import jax.numpy as jnp
from jax import lax
from jax.experimental import pallas as pl
from jax.experimental.pallas import tpu as pltpu
from jax.sharding import PartitionSpec as P

MIB = 1024 * 1024


def turn(x):
    half = x.shape[-1] // 2
    lane = lax.broadcasted_iota(jnp.int32, x.shape, x.ndim - 1)
    rolled = pltpu.roll(x, half, x.ndim - 1)
    return jnp.where(lane < half, -rolled, rolled)


def branch_kernel(mid_hbm, right_hbm, kept_ref, *refs):
    *sent_refs, mid_ref, right_ref, mid_sem, right_sem = refs
    pairs, depth, width = mid_ref.shape
    groups = right_sem.shape[0]
    half = groups // 2
    blocks = right_ref.shape[0] // groups
    me = lax.axis_index("stem")
    chunk = pairs // mid_sem.shape[0]

    def mid_copy(n):
        at = pl.ds(n * chunk, chunk)
        return pltpu.make_async_copy(mid_hbm.at[at], mid_ref.at[at], mid_sem.at[n])

    def right_copy(q):
        p = jnp.where(q < half, 2 * q + 1, 2 * q - groups)
        source = right_hbm.at[pl.ds((me ^ p) * blocks, blocks)]
        return pltpu.make_async_copy(source, right_ref.at[pl.ds(q * blocks, blocks)], right_sem.at[q])

    for n in range(mid_sem.shape[0]):
        mid_copy(n).start()
    for q in range(groups):
        right_copy(q).start()
    for n in range(mid_sem.shape[0]):
        mid_copy(n).wait()

    def group(q, carry):
        right_copy(q).wait()
        left = jnp.concatenate([mid_ref[j] for j in range(pairs)], axis=1)
        columns = []
        for b in range(blocks):
            rows = []
            for j in range(pairs):
                w = right_ref[q * blocks + b, j]
                rows += [w, turn(w.astype(jnp.float32)).astype(w.dtype)]
            columns.append(jnp.concatenate(rows, axis=0))
        sums = jnp.dot(left, jnp.concatenate(columns, axis=1), preferred_element_type=jnp.float32)

        for at in range(half):
            @pl.when(q == at)
            def _():
                for b in range(blocks):
                    part = sums[:, b * width:(b + 1) * width]
                    sent_refs[at * blocks + b][...] = part.astype(jnp.bfloat16)

        @pl.when(q >= half)
        def _():
            for b in range(blocks):
                kept_ref[(q - half) * blocks + b] = sums[:, b * width:(b + 1) * width]

        return carry

    lax.fori_loop(0, groups, group, 0)


def branch_sums(mid, right, groups):
    pairs, depth, width = mid.shape
    total = right.shape[0]
    vmem = pl.BlockSpec(memory_space=pltpu.VMEM)
    hbm = pl.BlockSpec(memory_space=pltpu.HBM)
    return pl.pallas_call(
        branch_kernel,
        in_specs=[hbm, hbm],
        out_specs=[vmem] * (1 + total // 2),
        out_shape=[
            jax.ShapeDtypeStruct((total // 2, depth, width), jnp.float32),
        ] + [jax.ShapeDtypeStruct((depth, width), jnp.bfloat16)] * (total // 2),
        scratch_shapes=[
            pltpu.VMEM(mid.shape, mid.dtype),
            pltpu.VMEM(right.shape, right.dtype),
            pltpu.SemaphoreType.DMA((4,)),
            pltpu.SemaphoreType.DMA((groups,)),
        ],
        compiler_params=pltpu.CompilerParams(vmem_limit_bytes=52 * MIB),
        cost_estimate=pl.CostEstimate(
            flops=2 * depth * pairs * width * total * width, bytes_accessed=6 * MIB, transcendentals=0
        ),
        name="branch_sums",
    )(mid, right)


def close_kernel(*refs):
    *more, kept_ref, out_ref = refs
    stem_refs, got_refs = more[:-kept_ref.shape[0]], more[-kept_ref.shape[0]:]
    part = None
    at = 0
    for ref in stem_refs:
        for b in range(ref.shape[0]):
            block = ref[b]
            half = block.shape[-1] // 2
            rows = jnp.concatenate([block[:, :half], block[:, half:]], axis=0)
            sums = kept_ref[at] + got_refs[at][...].astype(jnp.float32)
            high = sums.astype(jnp.bfloat16)
            low = (sums - high.astype(jnp.float32)).astype(jnp.bfloat16)
            term = jnp.dot(rows, jnp.concatenate([high, low], axis=1), preferred_element_type=jnp.float32)
            part = term if part is None else part + term
            at += 1
    width = part.shape[1] // 2
    part = part[:, :width] + part[:, width:]
    half = part.shape[0] // 2
    total = part[:half] + turn(part[half:])
    if len(out_ref.shape) == 2:
        out_ref[...] = total
    else:
        cuts, copies, rows, _ = out_ref.shape
        for c in range(cuts):
            for s in range(copies):
                out_ref[c, s] = total[c * rows:(c + 1) * rows]


def close(stems, kept, got, cuts, copies):
    rows, width = stems[0].shape[1], kept.shape[2]
    whole_tiles = rows % (8 * cuts) == 0
    shape = (cuts, copies, rows // cuts, width) if whole_tiles else (rows, width)
    out = pl.pallas_call(
        close_kernel,
        out_shape=jax.ShapeDtypeStruct(shape, jnp.float32),
        compiler_params=pltpu.CompilerParams(vmem_limit_bytes=24 * MIB),
        cost_estimate=pl.CostEstimate(flops=8 * rows * kept.size, bytes_accessed=MIB, transcendentals=0),
        name="close",
    )(*stems, *got, kept)
    if whole_tiles:
        return out.reshape(cuts * copies, rows // cuts, width)
    out = out.reshape(cuts, 1, -1)
    return jnp.broadcast_to(out, (cuts, copies, out.shape[-1])).reshape(cuts * copies, -1)


def on_device(stem_tensor, mid_tensors, right_tensors):
    stems = lax.axis_size("stem")
    cuts = lax.axis_size("cuts")

    def swap(x, p):
        return lax.ppermute(x, "stem", [(s, s ^ p) for s in range(stems)])

    pieces = [stem_tensor] + [swap(stem_tensor, p) for p in range(2, stems, 2)]
    kept, *sent = branch_sums(mid_tensors, right_tensors, stems)
    got = [swap(x, 1) for x in sent]
    spread = close(pieces, kept, got, cuts, stems)
    parts = lax.all_to_all(spread, ("cuts", "stem"), 0, 0, tiled=True)
    return jnp.sum(parts, axis=0).reshape(-1)


def solution(mesh):
    return jax.shard_map(
        on_device,
        mesh=mesh,
        in_specs=(
            P("stem", None, None),
            P(("cuts", "stem"), None, None),
            P(None, ("cuts", "stem"), None, None),
        ),
        out_specs=P("cuts"),
        check_vma=False,
    )
```

time: 81.5 us -> 24.8 us (0.30)
  blocking collectives: 39.5 us -> 13.2 us
  between operations: 13.5 us -> 0.03 us
  waiting for transfers between devices: 12.1 us -> 1.03 us
  other arithmetic: 6.78 us -> 0.63 us
  matrix products: 5.86 us -> 0 us
  Pallas kernels: 0 us -> 5.77 us
  starting transfers between devices: 0.01 us -> 4.04 us
  local copies, waits for them, and re-layouts: 3.54 us -> 0.01 us
    psum x1 -> x0, blocking collectives: 39.5 us -> none  [on_device(): summed = lax.psum(partial_sum, ('cuts', 'stem'))]
    all_to_all x0 -> x1, blocking collectives: none -> 13.2 us  [on_device(): parts = lax.all_to_all(spread, ('cuts', 'stem'), 0, 0, tiled=True)]
    all_gather x1 -> x0, waiting for transfers between devices: 11.4 us -> none  [on_device(): fragment = lax.all_gather(stem_tensor, 'stem', axis=0, tiled=True)]
    dot_general x2 -> x0, matrix products: 5.86 us -> none  [the longest x1 5 us: on_device(): product = jnp.dot(flattened, widened, preferred_element_type=jnp.float32)]
    pallas_call x0 -> x2, Pallas kernels: none -> 5.77 us  [the longest x1 5.34 us: branch_sums(): pl.pallas_call(branch_kernel, in_specs=[hbm, hbm], out_specs=[vmem] * (1...]
    concatenate x2 -> x0, other arithmetic: 5.77 us -> none  [widen(): return jnp.concatenate([upper_rows, lower_rows], axis=-2)]
    ppermute x0 -> x5, starting transfers between devices: none -> 4.04 us  [swap(): return lax.ppermute(x, 'stem', [(s, s ^ p) for s in range(stems)])]
    unnamed x5 -> x2, local copies, waits for them, and re-layouts: 2.94 us -> 0.01 us
  transfers between devices with their start and end apart: 1 -> 5, of which waited for: 1 -> 4; matrix products, arithmetic and copies ran while one was open for 12% -> 0% of each run, Pallas kernels for 0% -> 22%
where the time goes in v3:
time: 24.8 us; the launch traced here: 24.7 us
  blocking collectives  13.2 us (53%)
  Pallas kernels  5.77 us (23%)
  starting transfers between devices  4.04 us (16%)
  waiting for transfers between devices  1.03 us (4%)
  other arithmetic  0.63 us (3%)
    all_to_all x1, blocking collectives, on_device(): parts = lax.all_to_all(spread, ('cuts', 'stem'), 0, 0, tiled=True)  13.2 us
    pallas_call x1, Pallas kernels, branch_sums(): pl.pallas_call(branch_kernel, in_specs=[hbm, hbm], out_specs=[vmem] * (1...  5.34 us
    ppermute x5, starting transfers between devices, swap(): return lax.ppermute(x, 'stem', [(s, s ^ p) for s in range(stems)])  4.04 us
    ppermute x5, waiting for transfers between devices, swap(): return lax.ppermute(x, 'stem', [(s, s ^ p) for s in range(stems)])  1.03 us
    reduce_sum x1, other arithmetic, on_device(): return jnp.sum(parts, axis=0).reshape(-1)  0.63 us
  transfers between devices with their start and end apart: 5, of which 4 were waited for; matrix products, arithmetic and copies ran while one was open for 0% of the time, Pallas kernels for 22%

profile of v3, /device:TPU:0, one launch (start us, length us, event | category | flops | bytes accessed | tf_op | source)
XLA Modules:
  0.0 24.7 jit_solution(12286788178638379774)
XLA Ops:
  0.0 0.0 copy-start
  0.0 3.0 %collective-permute-start = (bf16[2,64,1024]{2,1,0:T(8,128)(2,1)}, bf16[2,64,1024]{2,1,0:T(8,128)(2,1)S(1)}, u32[]{:S(2)}, u32[]{:S(2)}) collective-permute-start(bf16[2,64,1024]{2,1,0:T(8,128)(2,1)} %refs_0_.1), channel_id=1, source_target_pairs={{0,2},{1,3},{2,0},{3,1},{4,6},{5,7},{6,4},{7,5},{8,10},{9,11},{10,... | collective-permute-start | bytes 786440 | tf_op jit(solution)/shard_map/ppermute | solution.py:149
  3.0 5.3 %branch_sums.1 = (f32[4,512,128]{2,1,0:T(8,128)S(1)}, bf16[512,128]{1,0:T(8,128)(2,1)S(1)}, bf16[512,128]{1,0:T(8,128)(2,1)S(1)}, bf16[512,128]{1,0:T(8,128)(2,1)S(1)}, bf16[512,128]{1,0:T(8,128)(2,1)S(1)}) custom-call(bf16[16,512,128]{2,1,0:T(8,128)(2,1)} %mid_hbm.1, bf16[8,16,64,128]{3,2,1,0:T(8,128)(2,1)} %right_hbm.1), custom_call_target="tpu_custom_call" | custom-call | flops 2147483648 | bytes 6291456 | tf_op jit(solution)/shard_map/branch_sums/pallas_call | solution.py:77
  8.3 0.1 collective-permute-start.1
  8.4 0.5 %collective-permute-start.2 = (bf16[512,128]{1,0:T(8,128)(2,1)S(1)}, bf16[512,128]{1,0:T(8,128)(2,1)S(1)}, u32[]{:S(2)}, u32[]{:S(2)}) collective-permute-start(bf16[512,128]{1,0:T(8,128)(2,1)S(1)} %get-tuple-element.11), channel_id=1, source_target_pairs={{0,1},{1,0},{2,3},{3,2},{4,5},{5,4},{6,7},{7,6},{8,9},{9,8},{10,11... | collective-permute-start | bytes 393224 | tf_op jit(solution)/shard_map/ppermute | solution.py:149
  8.9 0.1 collective-permute-start.3
  9.0 0.4 %collective-permute-start.4 = (bf16[512,128]{1,0:T(8,128)(2,1)S(1)}, bf16[512,128]{1,0:T(8,128)(2,1)S(1)}, u32[]{:S(2)}, u32[]{:S(2)}) collective-permute-start(bf16[512,128]{1,0:T(8,128)(2,1)S(1)} %get-tuple-element.13), channel_id=1, source_target_pairs={{0,1},{1,0},{2,3},{3,2},{4,5},{5,4},{6,7},{7,6},{8,9},{9,8},{10,11... | collective-permute-start | bytes 393224 | tf_op jit(solution)/shard_map/ppermute | solution.py:149
  9.4 0.3 %collective-permute-done.1.refs_2_ = bf16[512,128]{1,0:T(8,128)(2,1)S(1)} collective-permute-done((bf16[512,128]{1,0:T(8,128)(2,1)S(1)}, bf16[512,128]{1,0:T(8,128)(2,1)S(1)}, u32[]{:S(2)}, u32[]{:S(2)}) %collective-permute-start.1) | collective-permute-done | bytes 131104 | tf_op jit(solution)/shard_map/ppermute | solution.py:149
  9.7 0.2 collective-permute-done.2.refs_3_
  9.9 0.3 %collective-permute-done.3.refs_4_ = bf16[512,128]{1,0:T(8,128)(2,1)S(1)} collective-permute-done((bf16[512,128]{1,0:T(8,128)(2,1)S(1)}, bf16[512,128]{1,0:T(8,128)(2,1)S(1)}, u32[]{:S(2)}, u32[]{:S(2)}) %collective-permute-start.3) | collective-permute-done | bytes 131104 | tf_op jit(solution)/shard_map/ppermute | solution.py:149
  10.2 0.2 collective-permute-done.4.refs_5_
  10.4 0.0 collective-permute-done.refs_1_
  10.4 0.0 copy-done
  10.4 0.4 %close.1 = f32[8,4,8,128]{3,2,1,0:T(8,128)S(1)} custom-call(bf16[2,64,1024]{2,1,0:T(8,128)(2,1)S(1)} %copy-done, bf16[2,64,1024]{2,1,0:T(8,128)(2,1)S(1)} %collective-permute-done.refs_1_, bf16[512,128]{1,0:T(8,128)(2,1)S(1)} %collective-permute-done.1.refs_2_, bf16[512,128]{1,0:T(8,128)(2,1)S(1)} %collective-permute-done.2.refs_3_, ...), custom_call_target="tpu_custom_call" | custom-call | flops 134217728 | bytes 1048576 | tf_op jit(solution)/shard_map/close/pallas_call | solution.py:131
  10.9 13.2 %all_to_all.5 = f32[32,8,128]{2,1,0:T(8,128)S(1)} all-to-all(f32[32,8,128]{2,1,0:T(8,128)S(1)} %bitcast.2), channel_id=1, replica_groups=mesh['cuts'=8,'stem'=4] {'cuts','stem'}, dimensions={0} | all-to-all | bytes 262144 | tf_op jit(solution)/shard_map/all_to_all | solution.py:155
  24.0 0.6 %reduce_sum.9 = f32[8,128]{1,0:T(8,128)} reduce(f32[32,8,128]{2,1,0:T(8,128)S(1)} %all_to_all.5, f32[]{:T(128)} %constant.0.clone.1), dimensions={0}, to_apply=%region_0.0 | reduce | flops 31744 | bytes 135172 | tf_op jit(solution)/shard_map/reduce_sum | solution.py:156
Async XLA Ops:
  0.0 10.4 %copy-start = (bf16[2,64,1024]{2,1,0:T(8,128)(2,1)S(1)}, bf16[2,64,1024]{2,1,0:T(8,128)(2,1)}, u32[]{:S(2)}) copy-start(bf16[2,64,1024]{2,1,0:T(8,128)(2,1)} %refs_0_.1) | copy-start | bytes 786436
  0.0 10.4 %collective-permute-start = (bf16[2,64,1024]{2,1,0:T(8,128)(2,1)}, bf16[2,64,1024]{2,1,0:T(8,128)(2,1)S(1)}, u32[]{:S(2)}, u32[]{:S(2)}) collective-permute-start(bf16[2,64,1024]{2,1,0:T(8,128)(2,1)} %refs_0_.1), channel_id=1, source_target_pairs={{0,2},{1,3},{2,0},{3,1},{4,6},{5,7},{6,4},{7,5},{8,10},{9,11},{10,... | collective-permute-start | bytes 786440 | tf_op jit(solution)/shard_map/ppermute | solution.py:149
  8.3 1.4 %collective-permute-start.1 = (bf16[512,128]{1,0:T(8,128)(2,1)S(1)}, bf16[512,128]{1,0:T(8,128)(2,1)S(1)}, u32[]{:S(2)}, u32[]{:S(2)}) collective-permute-start(bf16[512,128]{1,0:T(8,128)(2,1)S(1)} %get-tuple-element.10), channel_id=1, source_target_pairs={{0,1},{1,0},{2,3},{3,2},{4,5},{5,4},{6,7},{7,6},{8,9},{9,8},{10,11... | collective-permute-start | bytes 393224 | tf_op jit(solution)/shard_map/ppermute | solution.py:149
  8.4 1.5 %collective-permute-start.2 = (bf16[512,128]{1,0:T(8,128)(2,1)S(1)}, bf16[512,128]{1,0:T(8,128)(2,1)S(1)}, u32[]{:S(2)}, u32[]{:S(2)}) collective-permute-start(bf16[512,128]{1,0:T(8,128)(2,1)S(1)} %get-tuple-element.11), channel_id=1, source_target_pairs={{0,1},{1,0},{2,3},{3,2},{4,5},{5,4},{6,7},{7,6},{8,9},{9,8},{10,11... | collective-permute-start | bytes 393224 | tf_op jit(solution)/shard_map/ppermute | solution.py:149
  8.9 1.3 %collective-permute-start.3 = (bf16[512,128]{1,0:T(8,128)(2,1)S(1)}, bf16[512,128]{1,0:T(8,128)(2,1)S(1)}, u32[]{:S(2)}, u32[]{:S(2)}) collective-permute-start(bf16[512,128]{1,0:T(8,128)(2,1)S(1)} %get-tuple-element.12), channel_id=1, source_target_pairs={{0,1},{1,0},{2,3},{3,2},{4,5},{5,4},{6,7},{7,6},{8,9},{9,8},{10,11... | collective-permute-start | bytes 393224 | tf_op jit(solution)/shard_map/ppermute | solution.py:149
  9.0 1.5 %collective-permute-start.4 = (bf16[512,128]{1,0:T(8,128)(2,1)S(1)}, bf16[512,128]{1,0:T(8,128)(2,1)S(1)}, u32[]{:S(2)}, u32[]{:S(2)}) collective-permute-start(bf16[512,128]{1,0:T(8,128)(2,1)S(1)} %get-tuple-element.13), channel_id=1, source_target_pairs={{0,1},{1,0},{2,3},{3,2},{4,5},{5,4},{6,7},{7,6},{8,9},{9,8},{10,11... | collective-permute-start | bytes 393224 | tf_op jit(solution)/shard_map/ppermute | solution.py:149

commit v4 on v3

--- a/solution.py
+++ b/solution.py
@@ -121,7 +121,7 @@
         cuts, copies, rows, _ = out_ref.shape
         for c in range(cuts):
             for s in range(copies):
-                out_ref[c, s] = total[c * rows:(c + 1) * rows]
+                out_ref[c, s] = total[c * rows:(c + 1) * rows].astype(out_ref.dtype)
 
 
 def close(stems, kept, got, cuts, copies):
@@ -130,7 +130,7 @@
     shape = (cuts, copies, rows // cuts, width) if whole_tiles else (rows, width)
     out = pl.pallas_call(
         close_kernel,
-        out_shape=jax.ShapeDtypeStruct(shape, jnp.float32),
+        out_shape=jax.ShapeDtypeStruct(shape, jnp.bfloat16 if whole_tiles else jnp.float32),
         compiler_params=pltpu.CompilerParams(vmem_limit_bytes=24 * MIB),
         cost_estimate=pl.CostEstimate(flops=8 * rows * kept.size, bytes_accessed=MIB, transcendentals=0),
         name="close",
@@ -153,7 +153,7 @@
     got = [swap(x, 1) for x in sent]
     spread = close(pieces, kept, got, cuts, stems)
     parts = lax.all_to_all(spread, ("cuts", "stem"), 0, 0, tiled=True)
-    return jnp.sum(parts, axis=0).reshape(-1)
+    return jnp.sum(parts.astype(jnp.float32), axis=0).reshape(-1)
 
 
 def solution(mesh):

time: 24.8 us -> 24 us (0.968)
  blocking collectives: 13.2 us -> 12.3 us
    all_to_all x1, blocking collectives: 13.2 us -> 12.3 us  [on_device(): parts = lax.all_to_all(spread, ('cuts', 'stem'), 0, 0, tiled=True)]
where the time goes in v4:
time: 24 us; the launch traced here: 23.8 us
  blocking collectives  12.3 us (51%)
  Pallas kernels  5.77 us (24%)
  starting transfers between devices  4.04 us (17%)
  waiting for transfers between devices  1.03 us (4%)
  other arithmetic  0.63 us (3%)
    all_to_all x1, blocking collectives, on_device(): parts = lax.all_to_all(spread, ('cuts', 'stem'), 0, 0, tiled=True)  12.3 us
    pallas_call x1, Pallas kernels, branch_sums(): pl.pallas_call(branch_kernel, in_specs=[hbm, hbm], out_specs=[vmem] * (1...  5.34 us
    ppermute x5, starting transfers between devices, swap(): return lax.ppermute(x, 'stem', [(s, s ^ p) for s in range(stems)])  4.04 us
    ppermute x5, waiting for transfers between devices, swap(): return lax.ppermute(x, 'stem', [(s, s ^ p) for s in range(stems)])  1.03 us
    reduce_sum x1, other arithmetic, on_device(): return jnp.sum(parts.astype(jnp.float32), axis=0).reshape(-1)  0.63 us
  transfers between devices with their start and end apart: 5, of which 4 were waited for; matrix products, arithmetic and copies ran while one was open for 0% of the time, Pallas kernels for 22%

profile of v4, /device:TPU:0, one launch (start us, length us, event | category | flops | bytes accessed | tf_op | source)
XLA Modules:
  0.0 23.8 jit_solution(2958126259673091954)
XLA Ops:
  0.0 0.0 copy-start
  0.0 3.0 %collective-permute-start = (bf16[2,64,1024]{2,1,0:T(8,128)(2,1)}, bf16[2,64,1024]{2,1,0:T(8,128)(2,1)S(1)}, u32[]{:S(2)}, u32[]{:S(2)}) collective-permute-start(bf16[2,64,1024]{2,1,0:T(8,128)(2,1)} %refs_0_.1), channel_id=1, source_target_pairs={{0,2},{1,3},{2,0},{3,1},{4,6},{5,7},{6,4},{7,5},{8,10},{9,11},{10,... | collective-permute-start | bytes 786440 | tf_op jit(solution)/shard_map/ppermute | solution.py:149
  3.0 5.3 %branch_sums.1 = (f32[4,512,128]{2,1,0:T(8,128)S(1)}, bf16[512,128]{1,0:T(8,128)(2,1)S(1)}, bf16[512,128]{1,0:T(8,128)(2,1)S(1)}, bf16[512,128]{1,0:T(8,128)(2,1)S(1)}, bf16[512,128]{1,0:T(8,128)(2,1)S(1)}) custom-call(bf16[16,512,128]{2,1,0:T(8,128)(2,1)} %mid_hbm.1, bf16[8,16,64,128]{3,2,1,0:T(8,128)(2,1)} %right_hbm.1), custom_call_target="tpu_custom_call" | custom-call | flops 2147483648 | bytes 6291456 | tf_op jit(solution)/shard_map/branch_sums/pallas_call | solution.py:77
  8.3 0.1 collective-permute-start.1
  8.4 0.5 %collective-permute-start.2 = (bf16[512,128]{1,0:T(8,128)(2,1)S(1)}, bf16[512,128]{1,0:T(8,128)(2,1)S(1)}, u32[]{:S(2)}, u32[]{:S(2)}) collective-permute-start(bf16[512,128]{1,0:T(8,128)(2,1)S(1)} %get-tuple-element.11), channel_id=1, source_target_pairs={{0,1},{1,0},{2,3},{3,2},{4,5},{5,4},{6,7},{7,6},{8,9},{9,8},{10,11... | collective-permute-start | bytes 393224 | tf_op jit(solution)/shard_map/ppermute | solution.py:149
  8.9 0.1 collective-permute-start.3
  9.0 0.4 %collective-permute-start.4 = (bf16[512,128]{1,0:T(8,128)(2,1)S(1)}, bf16[512,128]{1,0:T(8,128)(2,1)S(1)}, u32[]{:S(2)}, u32[]{:S(2)}) collective-permute-start(bf16[512,128]{1,0:T(8,128)(2,1)S(1)} %get-tuple-element.13), channel_id=1, source_target_pairs={{0,1},{1,0},{2,3},{3,2},{4,5},{5,4},{6,7},{7,6},{8,9},{9,8},{10,11... | collective-permute-start | bytes 393224 | tf_op jit(solution)/shard_map/ppermute | solution.py:149
  9.4 0.3 %collective-permute-done.1.refs_2_ = bf16[512,128]{1,0:T(8,128)(2,1)S(1)} collective-permute-done((bf16[512,128]{1,0:T(8,128)(2,1)S(1)}, bf16[512,128]{1,0:T(8,128)(2,1)S(1)}, u32[]{:S(2)}, u32[]{:S(2)}) %collective-permute-start.1) | collective-permute-done | bytes 131104 | tf_op jit(solution)/shard_map/ppermute | solution.py:149
  9.7 0.2 collective-permute-done.2.refs_3_
  9.9 0.3 %collective-permute-done.3.refs_4_ = bf16[512,128]{1,0:T(8,128)(2,1)S(1)} collective-permute-done((bf16[512,128]{1,0:T(8,128)(2,1)S(1)}, bf16[512,128]{1,0:T(8,128)(2,1)S(1)}, u32[]{:S(2)}, u32[]{:S(2)}) %collective-permute-start.3) | collective-permute-done | bytes 131104 | tf_op jit(solution)/shard_map/ppermute | solution.py:149
  10.2 0.2 collective-permute-done.4.refs_5_
  10.4 0.0 collective-permute-done.refs_1_
  10.4 0.0 copy-done
  10.4 0.4 %close.1 = bf16[8,4,8,128]{3,2,1,0:T(8,128)(2,1)S(1)} custom-call(bf16[2,64,1024]{2,1,0:T(8,128)(2,1)S(1)} %copy-done, bf16[2,64,1024]{2,1,0:T(8,128)(2,1)S(1)} %collective-permute-done.refs_1_, bf16[512,128]{1,0:T(8,128)(2,1)S(1)} %collective-permute-done.1.refs_2_, bf16[512,128]{1,0:T(8,128)(2,1)S(1)} %collective-permute-done.2.refs_3_, ...), custom_call_target="tpu_custom_call" | custom-call | flops 134217728 | bytes 1048576 | tf_op jit(solution)/shard_map/close/pallas_call | solution.py:131
  10.9 12.3 %all_to_all.5 = bf16[32,8,128]{2,1,0:T(8,128)(2,1)S(1)} all-to-all(bf16[32,8,128]{2,1,0:T(8,128)(2,1)S(1)} %bitcast.2), channel_id=1, replica_groups=mesh['cuts'=8,'stem'=4] {'cuts','stem'}, dimensions={0} | all-to-all | bytes 131072 | tf_op jit(solution)/shard_map/all_to_all | solution.py:155
  23.2 0.6 %convert_reduce_fusion = f32[8,128]{1,0:T(8,128)} fusion(bf16[32,8,128]{2,1,0:T(8,128)(2,1)S(1)} %all_to_all.5), kind=kLoop, calls=%fused_computation | loop fusion | flops 64512 | bytes 69632 | tf_op jit(solution)/shard_map/reduce_sum | solution.py:156
Async XLA Ops:
  0.0 10.4 %copy-start = (bf16[2,64,1024]{2,1,0:T(8,128)(2,1)S(1)}, bf16[2,64,1024]{2,1,0:T(8,128)(2,1)}, u32[]{:S(2)}) copy-start(bf16[2,64,1024]{2,1,0:T(8,128)(2,1)} %refs_0_.1) | copy-start | bytes 786436
  0.0 10.4 %collective-permute-start = (bf16[2,64,1024]{2,1,0:T(8,128)(2,1)}, bf16[2,64,1024]{2,1,0:T(8,128)(2,1)S(1)}, u32[]{:S(2)}, u32[]{:S(2)}) collective-permute-start(bf16[2,64,1024]{2,1,0:T(8,128)(2,1)} %refs_0_.1), channel_id=1, source_target_pairs={{0,2},{1,3},{2,0},{3,1},{4,6},{5,7},{6,4},{7,5},{8,10},{9,11},{10,... | collective-permute-start | bytes 786440 | tf_op jit(solution)/shard_map/ppermute | solution.py:149
  8.3 1.4 %collective-permute-start.1 = (bf16[512,128]{1,0:T(8,128)(2,1)S(1)}, bf16[512,128]{1,0:T(8,128)(2,1)S(1)}, u32[]{:S(2)}, u32[]{:S(2)}) collective-permute-start(bf16[512,128]{1,0:T(8,128)(2,1)S(1)} %get-tuple-element.10), channel_id=1, source_target_pairs={{0,1},{1,0},{2,3},{3,2},{4,5},{5,4},{6,7},{7,6},{8,9},{9,8},{10,11... | collective-permute-start | bytes 393224 | tf_op jit(solution)/shard_map/ppermute | solution.py:149
  8.4 1.5 %collective-permute-start.2 = (bf16[512,128]{1,0:T(8,128)(2,1)S(1)}, bf16[512,128]{1,0:T(8,128)(2,1)S(1)}, u32[]{:S(2)}, u32[]{:S(2)}) collective-permute-start(bf16[512,128]{1,0:T(8,128)(2,1)S(1)} %get-tuple-element.11), channel_id=1, source_target_pairs={{0,1},{1,0},{2,3},{3,2},{4,5},{5,4},{6,7},{7,6},{8,9},{9,8},{10,11... | collective-permute-start | bytes 393224 | tf_op jit(solution)/shard_map/ppermute | solution.py:149
  8.9 1.3 %collective-permute-start.3 = (bf16[512,128]{1,0:T(8,128)(2,1)S(1)}, bf16[512,128]{1,0:T(8,128)(2,1)S(1)}, u32[]{:S(2)}, u32[]{:S(2)}) collective-permute-start(bf16[512,128]{1,0:T(8,128)(2,1)S(1)} %get-tuple-element.12), channel_id=1, source_target_pairs={{0,1},{1,0},{2,3},{3,2},{4,5},{5,4},{6,7},{7,6},{8,9},{9,8},{10,11... | collective-permute-start | bytes 393224 | tf_op jit(solution)/shard_map/ppermute | solution.py:149
  9.0 1.5 %collective-permute-start.4 = (bf16[512,128]{1,0:T(8,128)(2,1)S(1)}, bf16[512,128]{1,0:T(8,128)(2,1)S(1)}, u32[]{:S(2)}, u32[]{:S(2)}) collective-permute-start(bf16[512,128]{1,0:T(8,128)(2,1)S(1)} %get-tuple-element.13), channel_id=1, source_target_pairs={{0,1},{1,0},{2,3},{3,2},{4,5},{5,4},{6,7},{7,6},{8,9},{9,8},{10,11... | collective-permute-start | bytes 393224 | tf_op jit(solution)/shard_map/ppermute | solution.py:149

commit v5 on v4

--- a/solution.py
+++ b/solution.py
@@ -114,31 +114,39 @@
     width = part.shape[1] // 2
     part = part[:, :width] + part[:, width:]
     half = part.shape[0] // 2
-    total = part[:half] + turn(part[half:])
-    if len(out_ref.shape) == 2:
-        out_ref[...] = total
-    else:
-        cuts, copies, rows, _ = out_ref.shape
-        for c in range(cuts):
-            for s in range(copies):
-                out_ref[c, s] = total[c * rows:(c + 1) * rows].astype(out_ref.dtype)
+    out_ref[...] = part[:half] + turn(part[half:])
 
 
-def close(stems, kept, got, cuts, copies):
+def close(stems, kept, got):
     rows, width = stems[0].shape[1], kept.shape[2]
-    whole_tiles = rows % (8 * cuts) == 0
-    shape = (cuts, copies, rows // cuts, width) if whole_tiles else (rows, width)
-    out = pl.pallas_call(
+    return pl.pallas_call(
         close_kernel,
-        out_shape=jax.ShapeDtypeStruct(shape, jnp.bfloat16 if whole_tiles else jnp.float32),
+        out_shape=jax.ShapeDtypeStruct((rows, width), jnp.float32),
         compiler_params=pltpu.CompilerParams(vmem_limit_bytes=24 * MIB),
         cost_estimate=pl.CostEstimate(flops=8 * rows * kept.size, bytes_accessed=MIB, transcendentals=0),
         name="close",
     )(*stems, *got, kept)
-    if whole_tiles:
-        return out.reshape(cuts * copies, rows // cuts, width)
-    out = out.reshape(cuts, 1, -1)
-    return jnp.broadcast_to(out, (cuts, copies, out.shape[-1])).reshape(cuts * copies, -1)
+
+
+def deal(terms, sections, place):
+    rows, width = terms[0].shape
+    size = rows // sections
+
+    def kernel(*refs):
+        for m, out_ref in enumerate(refs[len(terms):]):
+            at = pl.ds(pl.multiple_of((place() ^ m) * size, size), size)
+            total = refs[0][at]
+            for ref in refs[1:len(terms)]:
+                total += ref[at]
+            out_ref[...] = total
+
+    return pl.pallas_call(
+        kernel,
+        out_shape=[jax.ShapeDtypeStruct((size, width), jnp.float32)] * sections,
+        compiler_params=pltpu.CompilerParams(vmem_limit_bytes=24 * MIB),
+        cost_estimate=pl.CostEstimate(flops=4 * rows * width, bytes_accessed=8 * rows * width, transcendentals=0),
+        name="deal",
+    )(*terms)
 
 
 def on_device(stem_tensor, mid_tensors, right_tensors):
@@ -151,9 +159,27 @@
     pieces = [stem_tensor] + [swap(stem_tensor, p) for p in range(2, stems, 2)]
     kept, *sent = branch_sums(mid_tensors, right_tensors, stems)
     got = [swap(x, 1) for x in sent]
-    spread = close(pieces, kept, got, cuts, stems)
-    parts = lax.all_to_all(spread, ("cuts", "stem"), 0, 0, tiled=True)
-    return jnp.sum(parts.astype(jnp.float32), axis=0).reshape(-1)
+    partial_sum = close(pieces, kept, got)
+    if partial_sum.shape[0] % (8 * cuts) or cuts % 2:
+        parts = partial_sum.reshape(cuts, 1, -1)
+        parts = jnp.broadcast_to(parts, (cuts, stems, parts.shape[-1])).reshape(cuts * stems, -1)
+        return jnp.sum(lax.all_to_all(parts, ("cuts", "stem"), 0, 0, tiled=True), axis=0)
+
+    def send(x, c, s):
+        pairs = [(i * stems + j, (i ^ c) * stems + (j ^ s)) for i in range(cuts) for j in range(stems)]
+        return lax.ppermute(x, ("cuts", "stem"), pairs)
+
+    high, low = cuts // 2, 2
+    chip = [partial_sum, send(partial_sum, 0, 1)]
+    own, *away = deal(chip, high, lambda: lax.axis_index("cuts") // low)
+    line = [own] + [send(x, low * m, 0) for m, x in enumerate(away, 1)]
+    own, away = deal(line, low, lambda: lax.axis_index("cuts") % low)
+    total = own
+    for s in range(0, stems, 2):
+        total = total + send(away, 1, s)
+        if s:
+            total = total + send(own, 0, s)
+    return total.reshape(-1)
 
 
 def solution(mesh):

time: 24 us -> 29.1 us (1.21)
  blocking collectives: 12.3 us -> 0 us
  waiting for transfers between devices: 1.03 us -> 10.2 us
  starting transfers between devices: 4.04 us -> 12.3 us
    all_to_all x1 -> x0, blocking collectives: 12.3 us -> none  [on_device(): parts = lax.all_to_all(spread, ('cuts', 'stem'), 0, 0, tiled=True)]
    ppermute x0 -> x7, waiting for transfers between devices: none -> 9.18 us  [send(): return lax.ppermute(x, ('cuts', 'stem'), pairs)]
    ppermute x0 -> x7, starting transfers between devices: none -> 8.27 us  [send(): return lax.ppermute(x, ('cuts', 'stem'), pairs)]
    reduce_sum x1 -> x0, other arithmetic: 0.63 us -> none  [on_device(): return jnp.sum(parts.astype(jnp.float32), axis=0).reshape(-1)]
    reshape x0 -> x1, other arithmetic: none -> 0.6 us  [on_device(): return total.reshape(-1)]
  transfers between devices with their start and end apart: 5 -> 12, of which waited for: 4 -> 10; matrix products, arithmetic and copies ran while one was open for 0% -> 0% of each run, Pallas kernels for 22% -> 18%
where the time goes in v5:
time: 29.1 us; the launch traced here: 28.9 us
  starting transfers between devices  12.3 us (42%)
  waiting for transfers between devices  10.2 us (35%)
  Pallas kernels  5.78 us (20%)
  other arithmetic  0.6 us (2%)
    ppermute x7, waiting for transfers between devices, send(): return lax.ppermute(x, ('cuts', 'stem'), pairs)  9.18 us
    ppermute x7, starting transfers between devices, send(): return lax.ppermute(x, ('cuts', 'stem'), pairs)  8.27 us
    pallas_call x1, Pallas kernels, branch_sums(): pl.pallas_call(branch_kernel, in_specs=[hbm, hbm], out_specs=[vmem] * (1...  5.34 us
    ppermute x5, starting transfers between devices, swap(): return lax.ppermute(x, 'stem', [(s, s ^ p) for s in range(stems)])  4.04 us
    ppermute x5, waiting for transfers between devices, swap(): return lax.ppermute(x, 'stem', [(s, s ^ p) for s in range(stems)])  1.03 us
    reshape x1, other arithmetic, on_device(): return total.reshape(-1)  0.6 us
  transfers between devices with their start and end apart: 12, of which 10 were waited for; matrix products, arithmetic and copies ran while one was open for 0% of the time, Pallas kernels for 18%

profile of v5, /device:TPU:0, one launch (start us, length us, event | category | flops | bytes accessed | tf_op | source)
XLA Modules:
  0.0 28.9 jit_solution(6223823882722206108)
XLA Ops:
  0.0 0.0 copy-start
  0.0 3.0 %collective-permute-start = (bf16[2,64,1024]{2,1,0:T(8,128)(2,1)}, bf16[2,64,1024]{2,1,0:T(8,128)(2,1)S(1)}, u32[]{:S(2)}, u32[]{:S(2)}) collective-permute-start(bf16[2,64,1024]{2,1,0:T(8,128)(2,1)} %refs_0_.1), channel_id=1, source_target_pairs={{0,2},{1,3},{2,0},{3,1},{4,6},{5,7},{6,4},{7,5},{8,10},{9,11},{10,... | collective-permute-start | bytes 786440 | tf_op jit(solution)/shard_map/ppermute | solution.py:157
  3.0 5.3 %branch_sums.1 = (f32[4,512,128]{2,1,0:T(8,128)S(1)}, bf16[512,128]{1,0:T(8,128)(2,1)S(1)}, bf16[512,128]{1,0:T(8,128)(2,1)S(1)}, bf16[512,128]{1,0:T(8,128)(2,1)S(1)}, bf16[512,128]{1,0:T(8,128)(2,1)S(1)}) custom-call(bf16[16,512,128]{2,1,0:T(8,128)(2,1)} %mid_hbm.1, bf16[8,16,64,128]{3,2,1,0:T(8,128)(2,1)} %right_hbm.1), custom_call_target="tpu_custom_call" | custom-call | flops 2147483648 | bytes 6291456 | tf_op jit(solution)/shard_map/branch_sums/pallas_call | solution.py:77
  8.3 0.1 collective-permute-start.1
  8.4 0.5 %collective-permute-start.2 = (bf16[512,128]{1,0:T(8,128)(2,1)S(1)}, bf16[512,128]{1,0:T(8,128)(2,1)S(1)}, u32[]{:S(2)}, u32[]{:S(2)}) collective-permute-start(bf16[512,128]{1,0:T(8,128)(2,1)S(1)} %get-tuple-element.17), channel_id=1, source_target_pairs={{0,1},{1,0},{2,3},{3,2},{4,5},{5,4},{6,7},{7,6},{8,9},{9,8},{10,11... | collective-permute-start | bytes 393224 | tf_op jit(solution)/shard_map/ppermute | solution.py:157
  8.9 0.1 collective-permute-start.3
  9.0 0.4 %collective-permute-start.4 = (bf16[512,128]{1,0:T(8,128)(2,1)S(1)}, bf16[512,128]{1,0:T(8,128)(2,1)S(1)}, u32[]{:S(2)}, u32[]{:S(2)}) collective-permute-start(bf16[512,128]{1,0:T(8,128)(2,1)S(1)} %get-tuple-element.19), channel_id=1, source_target_pairs={{0,1},{1,0},{2,3},{3,2},{4,5},{5,4},{6,7},{7,6},{8,9},{9,8},{10,11... | collective-permute-start | bytes 393224 | tf_op jit(solution)/shard_map/ppermute | solution.py:157
  9.4 0.3 %collective-permute-done.1.refs_2_ = bf16[512,128]{1,0:T(8,128)(2,1)S(1)} collective-permute-done((bf16[512,128]{1,0:T(8,128)(2,1)S(1)}, bf16[512,128]{1,0:T(8,128)(2,1)S(1)}, u32[]{:S(2)}, u32[]{:S(2)}) %collective-permute-start.1) | collective-permute-done | bytes 131104 | tf_op jit(solution)/shard_map/ppermute | solution.py:157
  9.7 0.2 collective-permute-done.2.refs_3_
  9.9 0.3 %collective-permute-done.3.refs_4_ = bf16[512,128]{1,0:T(8,128)(2,1)S(1)} collective-permute-done((bf16[512,128]{1,0:T(8,128)(2,1)S(1)}, bf16[512,128]{1,0:T(8,128)(2,1)S(1)}, u32[]{:S(2)}, u32[]{:S(2)}) %collective-permute-start.3) | collective-permute-done | bytes 131104 | tf_op jit(solution)/shard_map/ppermute | solution.py:157
  10.2 0.2 collective-permute-done.4.refs_5_
  10.4 0.0 collective-permute-done.refs_1_
  10.4 0.0 copy-done
  10.4 0.4 %close.1.refs_0_ = f32[64,128]{1,0:T(8,128)S(1)} custom-call(bf16[2,64,1024]{2,1,0:T(8,128)(2,1)S(1)} %copy-done, bf16[2,64,1024]{2,1,0:T(8,128)(2,1)S(1)} %collective-permute-done.refs_1_, bf16[512,128]{1,0:T(8,128)(2,1)S(1)} %collective-permute-done.1.refs_2_, bf16[512,128]{1,0:T(8,128)(2,1)S(1)} %collective-permute-done.2.refs_3_, ...), custom_call_target="tpu_custom_call" | custom-call | flops 134217728 | bytes 1048576 | tf_op jit(solution)/shard_map/close/pallas_call | solution.py:122
  10.9 0.4 %collective-permute-start.5 = (f32[64,128]{1,0:T(8,128)S(1)}, f32[64,128]{1,0:T(8,128)S(1)}, u32[]{:S(2)}, u32[]{:S(2)}) collective-permute-start(f32[64,128]{1,0:T(8,128)S(1)} %close.1.refs_0_), channel_id=1, source_target_pairs={{0,1},{1,0},{2,3},{3,2},{4,5},{5,4},{6,7},{7,6},{8,9},{9,8},{10,11... | collective-permute-start | bytes 98312 | tf_op jit(solution)/shard_map/ppermute | solution.py:170
  11.3 0.9 %collective-permute-done.5.refs_1_ = f32[64,128]{1,0:T(8,128)S(1)} collective-permute-done((f32[64,128]{1,0:T(8,128)S(1)}, f32[64,128]{1,0:T(8,128)S(1)}, u32[]{:S(2)}, u32[]{:S(2)}) %collective-permute-start.5) | collective-permute-done | bytes 32800 | tf_op jit(solution)/shard_map/ppermute | solution.py:170
  12.2 1.6 %collective-permute-start.6 = (f32[16,128]{1,0:T(8,128)S(1)}, f32[16,128]{1,0:T(8,128)S(1)}, u32[]{:S(2)}, u32[]{:S(2)}) collective-permute-start(f32[16,128]{1,0:T(8,128)S(1)} %get-tuple-element.22), channel_id=1, source_target_pairs={{0,8},{1,9},{2,10},{3,11},{4,12},{5,13},{6,14},{7,15},{8,0},{9,1},... | collective-permute-start | bytes 24584 | tf_op jit(solution)/shard_map/ppermute | solution.py:170
  13.7 2.6 %collective-permute-start.7 = (f32[16,128]{1,0:T(8,128)S(1)}, f32[16,128]{1,0:T(8,128)S(1)}, u32[]{:S(2)}, u32[]{:S(2)}) collective-permute-start(f32[16,128]{1,0:T(8,128)S(1)} %get-tuple-element.23), channel_id=1, source_target_pairs={{0,16},{1,17},{2,18},{3,19},{4,20},{5,21},{6,22},{7,23},{8,24},{9,... | collective-permute-start | bytes 24584 | tf_op jit(solution)/shard_map/ppermute | solution.py:170
  16.3 0.2 collective-permute-start.8
  16.5 0.0 collective-permute-done.6.refs_1_
  16.5 1.7 %collective-permute-done.7.refs_2_ = f32[16,128]{1,0:T(8,128)S(1)} collective-permute-done((f32[16,128]{1,0:T(8,128)S(1)}, f32[16,128]{1,0:T(8,128)S(1)}, u32[]{:S(2)}, u32[]{:S(2)}) %collective-permute-start.7) | collective-permute-done | bytes 8224 | tf_op jit(solution)/shard_map/ppermute | solution.py:170
  18.3 3.5 %collective-permute-done.8.refs_3_ = f32[16,128]{1,0:T(8,128)S(1)} collective-permute-done((f32[16,128]{1,0:T(8,128)S(1)}, f32[16,128]{1,0:T(8,128)S(1)}, u32[]{:S(2)}, u32[]{:S(2)}) %collective-permute-start.8) | collective-permute-done | bytes 8224 | tf_op jit(solution)/shard_map/ppermute | solution.py:170
  21.8 1.7 %collective-permute-start.10 = (f32[8,128]{1,0:T(8,128)S(1)}, f32[8,128]{1,0:T(8,128)S(1)}, u32[]{:S(2)}, u32[]{:S(2)}) collective-permute-start(f32[8,128]{1,0:T(8,128)S(1)} %get-tuple-element.26), channel_id=1, source_target_pairs={{0,6},{1,7},{2,4},{3,5},{4,2},{5,3},{6,0},{7,1},{8,14},{9,15},{10,... | collective-permute-start | bytes 12296 | tf_op jit(solution)/shard_map/ppermute | solution.py:170
  23.5 1.2 %collective-permute-start.11 = (f32[8,128]{1,0:T(8,128)S(1)}, f32[8,128]{1,0:T(8,128)S(1)}, u32[]{:S(2)}, u32[]{:S(2)}) collective-permute-start(f32[8,128]{1,0:T(8,128)S(1)} %get-tuple-element.25), channel_id=1, source_target_pairs={{0,2},{1,3},{2,0},{3,1},{4,6},{5,7},{6,4},{7,5},{8,10},{9,11},{10,... | collective-permute-start | bytes 12296 | tf_op jit(solution)/shard_map/ppermute | solution.py:170
  24.7 0.5 %collective-permute-start.9 = (f32[8,128]{1,0:T(8,128)S(1)}, f32[8,128]{1,0:T(8,128)S(1)}, u32[]{:S(2)}, u32[]{:S(2)}) collective-permute-start(f32[8,128]{1,0:T(8,128)S(1)} %get-tuple-element.26), channel_id=1, source_target_pairs={{0,4},{1,5},{2,6},{3,7},{4,0},{5,1},{6,2},{7,3},{8,12},{9,13},{10,... | collective-permute-start | bytes 12296 | tf_op jit(solution)/shard_map/ppermute | solution.py:170
  25.3 1.0 %collective-permute-done.10 = f32[8,128]{1,0:T(8,128)S(1)} collective-permute-done((f32[8,128]{1,0:T(8,128)S(1)}, f32[8,128]{1,0:T(8,128)S(1)}, u32[]{:S(2)}, u32[]{:S(2)}) %collective-permute-start.10) | collective-permute-done | bytes 4128 | tf_op jit(solution)/shard_map/ppermute | solution.py:170
  26.3 0.8 %collective-permute-done.11 = f32[8,128]{1,0:T(8,128)S(1)} collective-permute-done((f32[8,128]{1,0:T(8,128)S(1)}, f32[8,128]{1,0:T(8,128)S(1)}, u32[]{:S(2)}, u32[]{:S(2)}) %collective-permute-start.11) | collective-permute-done | bytes 4128 | tf_op jit(solution)/shard_map/ppermute | solution.py:170
  27.1 1.2 %collective-permute-done.9 = f32[8,128]{1,0:T(8,128)S(1)} collective-permute-done((f32[8,128]{1,0:T(8,128)S(1)}, f32[8,128]{1,0:T(8,128)S(1)}, u32[]{:S(2)}, u32[]{:S(2)}) %collective-permute-start.9) | collective-permute-done | bytes 4128 | tf_op jit(solution)/shard_map/ppermute | solution.py:170
  28.3 0.6 %add_bitcast_fusion = f32[1024]{0:T(1024)} fusion(f32[8,128]{1,0:T(8,128)S(1)} %collective-permute-done.11, f32[8,128]{1,0:T(8,128)S(1)} %collective-permute-done.10, f32[8,128]{1,0:T(8,128)S(1)} %get-tuple-element.25, f32[8,128]{1,0:T(8,128)S(1)} %collective-permute-done.9), kind=kLoop, calls=%fused_computation | loop fusion | flops 3072 | bytes 20480 | tf_op jit(solution)/shard_map/reshape | solution.py:182
  (2 shorter events, 0.0 us)
Async XLA Ops:
  0.0 10.4 %copy-start = (bf16[2,64,1024]{2,1,0:T(8,128)(2,1)S(1)}, bf16[2,64,1024]{2,1,0:T(8,128)(2,1)}, u32[]{:S(2)}) copy-start(bf16[2,64,1024]{2,1,0:T(8,128)(2,1)} %refs_0_.1) | copy-start | bytes 786436
  0.0 10.4 %collective-permute-start = (bf16[2,64,1024]{2,1,0:T(8,128)(2,1)}, bf16[2,64,1024]{2,1,0:T(8,128)(2,1)S(1)}, u32[]{:S(2)}, u32[]{:S(2)}) collective-permute-start(bf16[2,64,1024]{2,1,0:T(8,128)(2,1)} %refs_0_.1), channel_id=1, source_target_pairs={{0,2},{1,3},{2,0},{3,1},{4,6},{5,7},{6,4},{7,5},{8,10},{9,11},{10,... | collective-permute-start | bytes 786440 | tf_op jit(solution)/shard_map/ppermute | solution.py:157
  8.3 1.4 %collective-permute-start.1 = (bf16[512,128]{1,0:T(8,128)(2,1)S(1)}, bf16[512,128]{1,0:T(8,128)(2,1)S(1)}, u32[]{:S(2)}, u32[]{:S(2)}) collective-permute-start(bf16[512,128]{1,0:T(8,128)(2,1)S(1)} %get-tuple-element.16), channel_id=1, source_target_pairs={{0,1},{1,0},{2,3},{3,2},{4,5},{5,4},{6,7},{7,6},{8,9},{9,8},{10,11... | collective-permute-start | bytes 393224 | tf_op jit(solution)/shard_map/ppermute | solution.py:157
  8.4 1.5 %collective-permute-start.2 = (bf16[512,128]{1,0:T(8,128)(2,1)S(1)}, bf16[512,128]{1,0:T(8,128)(2,1)S(1)}, u32[]{:S(2)}, u32[]{:S(2)}) collective-permute-start(bf16[512,128]{1,0:T(8,128)(2,1)S(1)} %get-tuple-element.17), channel_id=1, source_target_pairs={{0,1},{1,0},{2,3},{3,2},{4,5},{5,4},{6,7},{7,6},{8,9},{9,8},{10,11... | collective-permute-start | bytes 393224 | tf_op jit(solution)/shard_map/ppermute | solution.py:157
  8.9 1.3 %collective-permute-start.3 = (bf16[512,128]{1,0:T(8,128)(2,1)S(1)}, bf16[512,128]{1,0:T(8,128)(2,1)S(1)}, u32[]{:S(2)}, u32[]{:S(2)}) collective-permute-start(bf16[512,128]{1,0:T(8,128)(2,1)S(1)} %get-tuple-element.18), channel_id=1, source_target_pairs={{0,1},{1,0},{2,3},{3,2},{4,5},{5,4},{6,7},{7,6},{8,9},{9,8},{10,11... | collective-permute-start | bytes 393224 | tf_op jit(solution)/shard_map/ppermute | solution.py:157
  9.0 1.5 %collective-permute-start.4 = (bf16[512,128]{1,0:T(8,128)(2,1)S(1)}, bf16[512,128]{1,0:T(8,128)(2,1)S(1)}, u32[]{:S(2)}, u32[]{:S(2)}) collective-permute-start(bf16[512,128]{1,0:T(8,128)(2,1)S(1)} %get-tuple-element.19), channel_id=1, source_target_pairs={{0,1},{1,0},{2,3},{3,2},{4,5},{5,4},{6,7},{7,6},{8,9},{9,8},{10,11... | collective-permute-start | bytes 393224 | tf_op jit(solution)/shard_map/ppermute | solution.py:157
  10.9 1.3 %collective-permute-start.5 = (f32[64,128]{1,0:T(8,128)S(1)}, f32[64,128]{1,0:T(8,128)S(1)}, u32[]{:S(2)}, u32[]{:S(2)}) collective-permute-start(f32[64,128]{1,0:T(8,128)S(1)} %close.1.refs_0_), channel_id=1, source_target_pairs={{0,1},{1,0},{2,3},{3,2},{4,5},{5,4},{6,7},{7,6},{8,9},{9,8},{10,11... | collective-permute-start | bytes 98312 | tf_op jit(solution)/shard_map/ppermute | solution.py:170
  12.2 4.4 %collective-permute-start.6 = (f32[16,128]{1,0:T(8,128)S(1)}, f32[16,128]{1,0:T(8,128)S(1)}, u32[]{:S(2)}, u32[]{:S(2)}) collective-permute-start(f32[16,128]{1,0:T(8,128)S(1)} %get-tuple-element.22), channel_id=1, source_target_pairs={{0,8},{1,9},{2,10},{3,11},{4,12},{5,13},{6,14},{7,15},{8,0},{9,1},... | collective-permute-start | bytes 24584 | tf_op jit(solution)/shard_map/ppermute | solution.py:170
  13.7 4.5 %collective-permute-start.7 = (f32[16,128]{1,0:T(8,128)S(1)}, f32[16,128]{1,0:T(8,128)S(1)}, u32[]{:S(2)}, u32[]{:S(2)}) collective-permute-start(f32[16,128]{1,0:T(8,128)S(1)} %get-tuple-element.23), channel_id=1, source_target_pairs={{0,16},{1,17},{2,18},{3,19},{4,20},{5,21},{6,22},{7,23},{8,24},{9,... | collective-permute-start | bytes 24584 | tf_op jit(solution)/shard_map/ppermute | solution.py:170
  16.3 5.4 %collective-permute-start.8 = (f32[16,128]{1,0:T(8,128)S(1)}, f32[16,128]{1,0:T(8,128)S(1)}, u32[]{:S(2)}, u32[]{:S(2)}) collective-permute-start(f32[16,128]{1,0:T(8,128)S(1)} %get-tuple-element.24), channel_id=1, source_target_pairs={{0,24},{1,25},{2,26},{3,27},{4,28},{5,29},{6,30},{7,31},{8,16},{9,... | collective-permute-start | bytes 24584 | tf_op jit(solution)/shard_map/ppermute | solution.py:170
  21.8 4.5 %collective-permute-start.10 = (f32[8,128]{1,0:T(8,128)S(1)}, f32[8,128]{1,0:T(8,128)S(1)}, u32[]{:S(2)}, u32[]{:S(2)}) collective-permute-start(f32[8,128]{1,0:T(8,128)S(1)} %get-tuple-element.26), channel_id=1, source_target_pairs={{0,6},{1,7},{2,4},{3,5},{4,2},{5,3},{6,0},{7,1},{8,14},{9,15},{10,... | collective-permute-start | bytes 12296 | tf_op jit(solution)/shard_map/ppermute | solution.py:170
  23.5 3.6 %collective-permute-start.11 = (f32[8,128]{1,0:T(8,128)S(1)}, f32[8,128]{1,0:T(8,128)S(1)}, u32[]{:S(2)}, u32[]{:S(2)}) collective-permute-start(f32[8,128]{1,0:T(8,128)S(1)} %get-tuple-element.25), channel_id=1, source_target_pairs={{0,2},{1,3},{2,0},{3,1},{4,6},{5,7},{6,4},{7,5},{8,10},{9,11},{10,... | collective-permute-start | bytes 12296 | tf_op jit(solution)/shard_map/ppermute | solution.py:170
  24.7 3.6 %collective-permute-start.9 = (f32[8,128]{1,0:T(8,128)S(1)}, f32[8,128]{1,0:T(8,128)S(1)}, u32[]{:S(2)}, u32[]{:S(2)}) collective-permute-start(f32[8,128]{1,0:T(8,128)S(1)} %get-tuple-element.26), channel_id=1, source_target_pairs={{0,4},{1,5},{2,6},{3,7},{4,0},{5,1},{6,2},{7,3},{8,12},{9,13},{10,... | collective-permute-start | bytes 12296 | tf_op jit(solution)/shard_map/ppermute | solution.py:170

commit v6 on v5

--- a/solution.py
+++ b/solution.py
@@ -165,21 +165,24 @@
         parts = jnp.broadcast_to(parts, (cuts, stems, parts.shape[-1])).reshape(cuts * stems, -1)
         return jnp.sum(lax.all_to_all(parts, ("cuts", "stem"), 0, 0, tiled=True), axis=0)
 
-    def send(x, c, s):
-        pairs = [(i * stems + j, (i ^ c) * stems + (j ^ s)) for i in range(cuts) for j in range(stems)]
+    def send(x, c, s, cores=(1,)):
+        pairs = [
+            (i * stems + j, (i ^ c) * stems + (j ^ s)) for i in range(cuts) for j in range(stems) if j % 2 in cores
+        ]
         return lax.ppermute(x, ("cuts", "stem"), pairs)
 
     high, low = cuts // 2, 2
-    chip = [partial_sum, send(partial_sum, 0, 1)]
+    chip = [partial_sum, send(partial_sum, 0, 1, (0,))]
     own, *away = deal(chip, high, lambda: lax.axis_index("cuts") // low)
-    line = [own] + [send(x, low * m, 0) for m, x in enumerate(away, 1)]
+    line = [own] + [send(x, low * m, 0) for m, x in reversed(list(enumerate(away, 1)))]
     own, away = deal(line, low, lambda: lax.axis_index("cuts") % low)
     total = own
     for s in range(0, stems, 2):
         total = total + send(away, 1, s)
         if s:
             total = total + send(own, 0, s)
-    return total.reshape(-1)
+    shared = send(total, 0, 1)
+    return jnp.where(lax.axis_index("stem") % 2 == 1, total, shared).reshape(-1)
 
 
 def solution(mesh):

time: 29.1 us -> 39.2 us (1.35)
  waiting for transfers between devices: 10.2 us -> 20.9 us
  starting transfers between devices: 12.3 us -> 11.5 us
    ppermute x7 -> x8, waiting for transfers between devices: 9.18 us -> 19.8 us  [send(): return lax.ppermute(x, ('cuts', 'stem'), pairs)]
    ppermute x7 -> x8, starting transfers between devices: 8.27 us -> 7.49 us  [send(): return lax.ppermute(x, ('cuts', 'stem'), pairs)]
  transfers between devices with their start and end apart: 12 -> 13, of which waited for: 10 -> 6; matrix products, arithmetic and copies ran while one was open for 0% -> 0% of each run, Pallas kernels for 18% -> 14%
where the time goes in v6:
time: 39.2 us; the launch traced here: 39 us
  waiting for transfers between devices  20.9 us (53%)
  starting transfers between devices  11.5 us (29%)
  Pallas kernels  5.8 us (15%)
  other arithmetic  0.6 us (2%)
    ppermute x8, waiting for transfers between devices, send(): return lax.ppermute(x, ('cuts', 'stem'), pairs)  19.8 us
    ppermute x8, starting transfers between devices, send(): return lax.ppermute(x, ('cuts', 'stem'), pairs)  7.49 us
    pallas_call x1, Pallas kernels, branch_sums(): pl.pallas_call(branch_kernel, in_specs=[hbm, hbm], out_specs=[vmem] * (1...  5.34 us
    ppermute x5, starting transfers between devices, swap(): return lax.ppermute(x, 'stem', [(s, s ^ p) for s in range(stems)])  4.04 us
    ppermute x5, waiting for transfers between devices, swap(): return lax.ppermute(x, 'stem', [(s, s ^ p) for s in range(stems)])  1.03 us
  transfers between devices with their start and end apart: 13, of which 6 were waited for; matrix products, arithmetic and copies ran while one was open for 0% of the time, Pallas kernels for 14%

profile of v6, /device:TPU:0, one launch (start us, length us, event | category | flops | bytes accessed | tf_op | source)
XLA Modules:
  0.0 39.0 jit_solution(11251281139326885006)
XLA Ops:
  0.0 0.0 copy-start
  0.0 3.0 %collective-permute-start = (bf16[2,64,1024]{2,1,0:T(8,128)(2,1)}, bf16[2,64,1024]{2,1,0:T(8,128)(2,1)S(1)}, u32[]{:S(2)}, u32[]{:S(2)}) collective-permute-start(bf16[2,64,1024]{2,1,0:T(8,128)(2,1)} %refs_0_.1), channel_id=1, source_target_pairs={{0,2},{1,3},{2,0},{3,1},{4,6},{5,7},{6,4},{7,5},{8,10},{9,11},{10,... | collective-permute-start | bytes 786440 | tf_op jit(solution)/shard_map/ppermute | solution.py:157
  3.0 5.3 %branch_sums.1 = (f32[4,512,128]{2,1,0:T(8,128)S(1)}, bf16[512,128]{1,0:T(8,128)(2,1)S(1)}, bf16[512,128]{1,0:T(8,128)(2,1)S(1)}, bf16[512,128]{1,0:T(8,128)(2,1)S(1)}, bf16[512,128]{1,0:T(8,128)(2,1)S(1)}) custom-call(bf16[16,512,128]{2,1,0:T(8,128)(2,1)} %mid_hbm.1, bf16[8,16,64,128]{3,2,1,0:T(8,128)(2,1)} %right_hbm.1), custom_call_target="tpu_custom_call" | custom-call | flops 2147483648 | bytes 6291456 | tf_op jit(solution)/shard_map/branch_sums/pallas_call | solution.py:77
  8.3 0.1 collective-permute-start.1
  8.4 0.5 %collective-permute-start.2 = (bf16[512,128]{1,0:T(8,128)(2,1)S(1)}, bf16[512,128]{1,0:T(8,128)(2,1)S(1)}, u32[]{:S(2)}, u32[]{:S(2)}) collective-permute-start(bf16[512,128]{1,0:T(8,128)(2,1)S(1)} %get-tuple-element.17), channel_id=1, source_target_pairs={{0,1},{1,0},{2,3},{3,2},{4,5},{5,4},{6,7},{7,6},{8,9},{9,8},{10,11... | collective-permute-start | bytes 393224 | tf_op jit(solution)/shard_map/ppermute | solution.py:157
  8.9 0.1 collective-permute-start.3
  9.0 0.4 %collective-permute-start.4 = (bf16[512,128]{1,0:T(8,128)(2,1)S(1)}, bf16[512,128]{1,0:T(8,128)(2,1)S(1)}, u32[]{:S(2)}, u32[]{:S(2)}) collective-permute-start(bf16[512,128]{1,0:T(8,128)(2,1)S(1)} %get-tuple-element.19), channel_id=1, source_target_pairs={{0,1},{1,0},{2,3},{3,2},{4,5},{5,4},{6,7},{7,6},{8,9},{9,8},{10,11... | collective-permute-start | bytes 393224 | tf_op jit(solution)/shard_map/ppermute | solution.py:157
  9.4 0.3 collective-permute-done.1.refs_2_
  9.7 0.2 collective-permute-done.2.refs_3_
  9.9 0.3 collective-permute-done.3.refs_4_
  10.2 0.2 collective-permute-done.4.refs_5_
  10.4 0.0 collective-permute-done.refs_1_
  10.4 0.0 copy-done
  10.4 0.4 %close.1.refs_0_ = f32[64,128]{1,0:T(8,128)S(1)} custom-call(bf16[2,64,1024]{2,1,0:T(8,128)(2,1)S(1)} %copy-done, bf16[2,64,1024]{2,1,0:T(8,128)(2,1)S(1)} %collective-permute-done.refs_1_, bf16[512,128]{1,0:T(8,128)(2,1)S(1)} %collective-permute-done.1.refs_2_, bf16[512,128]{1,0:T(8,128)(2,1)S(1)} %collective-permute-done.2.refs_3_, ...), custom_call_target="tpu_custom_call" | custom-call | flops 134217728 | bytes 1048576 | tf_op jit(solution)/shard_map/close/pallas_call | solution.py:122
  10.9 2.2 %collective-permute-start.5 = (f32[64,128]{1,0:T(8,128)S(1)}, f32[64,128]{1,0:T(8,128)S(1)}, u32[]{:S(2)}, u32[]{:S(2)}) collective-permute-start(f32[64,128]{1,0:T(8,128)S(1)} %close.1.refs_0_), channel_id=1, source_target_pairs={{0,1},{2,3},{4,5},{6,7},{8,9},{10,11},{12,13},{14,15},{16,17},{18,... | collective-permute-start | bytes 98312 | tf_op jit(solution)/shard_map/ppermute | solution.py:172
  13.1 0.8 %collective-permute-done.5.refs_1_ = f32[64,128]{1,0:T(8,128)S(1)} collective-permute-done((f32[64,128]{1,0:T(8,128)S(1)}, f32[64,128]{1,0:T(8,128)S(1)}, u32[]{:S(2)}, u32[]{:S(2)}) %collective-permute-start.5) | collective-permute-done | bytes 32800 | tf_op jit(solution)/shard_map/ppermute | solution.py:172
  14.0 0.6 %collective-permute-start.6 = (f32[16,128]{1,0:T(8,128)S(1)}, f32[16,128]{1,0:T(8,128)S(1)}, u32[]{:S(2)}, u32[]{:S(2)}) collective-permute-start(f32[16,128]{1,0:T(8,128)S(1)} %get-tuple-element.22), channel_id=1, source_target_pairs={{1,25},{3,27},{5,29},{7,31},{9,17},{11,19},{13,21},{15,23},{17,9},... | collective-permute-start | bytes 24584 | tf_op jit(solution)/shard_map/ppermute | solution.py:172
  14.6 0.7 %collective-permute-start.7 = (f32[16,128]{1,0:T(8,128)S(1)}, f32[16,128]{1,0:T(8,128)S(1)}, u32[]{:S(2)}, u32[]{:S(2)}) collective-permute-start(f32[16,128]{1,0:T(8,128)S(1)} %get-tuple-element.23), channel_id=1, source_target_pairs={{1,17},{3,19},{5,21},{7,23},{9,25},{11,27},{13,29},{15,31},{17,1},... | collective-permute-start | bytes 24584 | tf_op jit(solution)/shard_map/ppermute | solution.py:172
  15.3 0.7 %collective-permute-start.8 = (f32[16,128]{1,0:T(8,128)S(1)}, f32[16,128]{1,0:T(8,128)S(1)}, u32[]{:S(2)}, u32[]{:S(2)}) collective-permute-start(f32[16,128]{1,0:T(8,128)S(1)} %get-tuple-element.24), channel_id=1, source_target_pairs={{1,9},{3,11},{5,13},{7,15},{9,1},{11,3},{13,5},{15,7},{17,25},{19,... | collective-permute-start | bytes 24584 | tf_op jit(solution)/shard_map/ppermute | solution.py:172
  16.0 0.0 collective-permute-done.6.refs_1_
  16.0 0.0 collective-permute-done.7.refs_2_
  16.0 0.0 collective-permute-done.8.refs_3_
  16.0 0.7 %collective-permute-start.10 = (f32[8,128]{1,0:T(8,128)S(1)}, f32[8,128]{1,0:T(8,128)S(1)}, u32[]{:S(2)}, u32[]{:S(2)}) collective-permute-start(f32[8,128]{1,0:T(8,128)S(1)} %get-tuple-element.26), channel_id=1, source_target_pairs={{1,7},{3,5},{5,3},{7,1},{9,15},{11,13},{13,11},{15,9},{17,23},{19,... | collective-permute-start | bytes 12296 | tf_op jit(solution)/shard_map/ppermute | solution.py:172
  16.7 0.7 %collective-permute-start.11 = (f32[8,128]{1,0:T(8,128)S(1)}, f32[8,128]{1,0:T(8,128)S(1)}, u32[]{:S(2)}, u32[]{:S(2)}) collective-permute-start(f32[8,128]{1,0:T(8,128)S(1)} %get-tuple-element.25), channel_id=1, source_target_pairs={{1,3},{3,1},{5,7},{7,5},{9,11},{11,9},{13,15},{15,13},{17,19},{19,... | collective-permute-start | bytes 12296 | tf_op jit(solution)/shard_map/ppermute | solution.py:172
  17.4 0.7 %collective-permute-start.9 = (f32[8,128]{1,0:T(8,128)S(1)}, f32[8,128]{1,0:T(8,128)S(1)}, u32[]{:S(2)}, u32[]{:S(2)}) collective-permute-start(f32[8,128]{1,0:T(8,128)S(1)} %get-tuple-element.26), channel_id=1, source_target_pairs={{1,5},{3,7},{5,1},{7,3},{9,13},{11,15},{13,9},{15,11},{17,21},{19,... | collective-permute-start | bytes 12296 | tf_op jit(solution)/shard_map/ppermute | solution.py:172
  18.0 0.0 collective-permute-done.10
  18.0 0.0 collective-permute-done.11
  18.1 0.0 collective-permute-done.9
  18.1 1.3 %collective-permute-start.12 = (f32[8,128]{1,0:T(8,128)S(1)}, f32[8,128]{1,0:T(8,128)S(1)}, u32[]{:S(2)}, u32[]{:S(2)}) collective-permute-start(f32[8,128]{1,0:T(8,128)S(1)} %add_add_fusion), channel_id=1, source_target_pairs={{1,0},{3,2},{5,4},{7,6},{9,8},{11,10},{13,12},{15,14},{17,16},{19,... | collective-permute-start | bytes 12296 | tf_op jit(solution)/shard_map/ppermute | solution.py:172
  19.4 19.0 %collective-permute-done.12 = f32[8,128]{1,0:T(8,128)S(1)} collective-permute-done((f32[8,128]{1,0:T(8,128)S(1)}, f32[8,128]{1,0:T(8,128)S(1)}, u32[]{:S(2)}, u32[]{:S(2)}) %collective-permute-start.12) | collective-permute-done | bytes 4128 | tf_op jit(solution)/shard_map/ppermute | solution.py:172
  38.4 0.6 %select_bitcast_fusion = f32[1024]{0:T(1024)} fusion(f32[8,128]{1,0:T(8,128)S(1)} %add_add_fusion, f32[8,128]{1,0:T(8,128)S(1)} %collective-permute-done.12, pred[]{:T(512)S(6)} %eq.5), kind=kLoop, calls=%fused_computation | loop fusion | flops 1024 | bytes 12289 | tf_op jit(solution)/shard_map/reshape | solution.py:185
  (3 shorter events, 0.0 us)
Async XLA Ops:
  0.0 10.4 %copy-start = (bf16[2,64,1024]{2,1,0:T(8,128)(2,1)S(1)}, bf16[2,64,1024]{2,1,0:T(8,128)(2,1)}, u32[]{:S(2)}) copy-start(bf16[2,64,1024]{2,1,0:T(8,128)(2,1)} %refs_0_.1) | copy-start | bytes 786436
  0.0 10.4 %collective-permute-start = (bf16[2,64,1024]{2,1,0:T(8,128)(2,1)}, bf16[2,64,1024]{2,1,0:T(8,128)(2,1)S(1)}, u32[]{:S(2)}, u32[]{:S(2)}) collective-permute-start(bf16[2,64,1024]{2,1,0:T(8,128)(2,1)} %refs_0_.1), channel_id=1, source_target_pairs={{0,2},{1,3},{2,0},{3,1},{4,6},{5,7},{6,4},{7,5},{8,10},{9,11},{10,... | collective-permute-start | bytes 786440 | tf_op jit(solution)/shard_map/ppermute | solution.py:157
  8.3 1.4 %collective-permute-start.1 = (bf16[512,128]{1,0:T(8,128)(2,1)S(1)}, bf16[512,128]{1,0:T(8,128)(2,1)S(1)}, u32[]{:S(2)}, u32[]{:S(2)}) collective-permute-start(bf16[512,128]{1,0:T(8,128)(2,1)S(1)} %get-tuple-element.16), channel_id=1, source_target_pairs={{0,1},{1,0},{2,3},{3,2},{4,5},{5,4},{6,7},{7,6},{8,9},{9,8},{10,11... | collective-permute-start | bytes 393224 | tf_op jit(solution)/shard_map/ppermute | solution.py:157
  8.4 1.5 %collective-permute-start.2 = (bf16[512,128]{1,0:T(8,128)(2,1)S(1)}, bf16[512,128]{1,0:T(8,128)(2,1)S(1)}, u32[]{:S(2)}, u32[]{:S(2)}) collective-permute-start(bf16[512,128]{1,0:T(8,128)(2,1)S(1)} %get-tuple-element.17), channel_id=1, source_target_pairs={{0,1},{1,0},{2,3},{3,2},{4,5},{5,4},{6,7},{7,6},{8,9},{9,8},{10,11... | collective-permute-start | bytes 393224 | tf_op jit(solution)/shard_map/ppermute | solution.py:157
  8.9 1.3 %collective-permute-start.3 = (bf16[512,128]{1,0:T(8,128)(2,1)S(1)}, bf16[512,128]{1,0:T(8,128)(2,1)S(1)}, u32[]{:S(2)}, u32[]{:S(2)}) collective-permute-start(bf16[512,128]{1,0:T(8,128)(2,1)S(1)} %get-tuple-element.18), channel_id=1, source_target_pairs={{0,1},{1,0},{2,3},{3,2},{4,5},{5,4},{6,7},{7,6},{8,9},{9,8},{10,11... | collective-permute-start | bytes 393224 | tf_op jit(solution)/shard_map/ppermute | solution.py:157
  9.0 1.5 %collective-permute-start.4 = (bf16[512,128]{1,0:T(8,128)(2,1)S(1)}, bf16[512,128]{1,0:T(8,128)(2,1)S(1)}, u32[]{:S(2)}, u32[]{:S(2)}) collective-permute-start(bf16[512,128]{1,0:T(8,128)(2,1)S(1)} %get-tuple-element.19), channel_id=1, source_target_pairs={{0,1},{1,0},{2,3},{3,2},{4,5},{5,4},{6,7},{7,6},{8,9},{9,8},{10,11... | collective-permute-start | bytes 393224 | tf_op jit(solution)/shard_map/ppermute | solution.py:157
  10.9 3.1 %collective-permute-start.5 = (f32[64,128]{1,0:T(8,128)S(1)}, f32[64,128]{1,0:T(8,128)S(1)}, u32[]{:S(2)}, u32[]{:S(2)}) collective-permute-start(f32[64,128]{1,0:T(8,128)S(1)} %close.1.refs_0_), channel_id=1, source_target_pairs={{0,1},{2,3},{4,5},{6,7},{8,9},{10,11},{12,13},{14,15},{16,17},{18,... | collective-permute-start | bytes 98312 | tf_op jit(solution)/shard_map/ppermute | solution.py:172
  14.0 2.0 %collective-permute-start.6 = (f32[16,128]{1,0:T(8,128)S(1)}, f32[16,128]{1,0:T(8,128)S(1)}, u32[]{:S(2)}, u32[]{:S(2)}) collective-permute-start(f32[16,128]{1,0:T(8,128)S(1)} %get-tuple-element.22), channel_id=1, source_target_pairs={{1,25},{3,27},{5,29},{7,31},{9,17},{11,19},{13,21},{15,23},{17,9},... | collective-permute-start | bytes 24584 | tf_op jit(solution)/shard_map/ppermute | solution.py:172
  14.6 1.4 %collective-permute-start.7 = (f32[16,128]{1,0:T(8,128)S(1)}, f32[16,128]{1,0:T(8,128)S(1)}, u32[]{:S(2)}, u32[]{:S(2)}) collective-permute-start(f32[16,128]{1,0:T(8,128)S(1)} %get-tuple-element.23), channel_id=1, source_target_pairs={{1,17},{3,19},{5,21},{7,23},{9,25},{11,27},{13,29},{15,31},{17,1},... | collective-permute-start | bytes 24584 | tf_op jit(solution)/shard_map/ppermute | solution.py:172
  15.3 0.7 %collective-permute-start.8 = (f32[16,128]{1,0:T(8,128)S(1)}, f32[16,128]{1,0:T(8,128)S(1)}, u32[]{:S(2)}, u32[]{:S(2)}) collective-permute-start(f32[16,128]{1,0:T(8,128)S(1)} %get-tuple-element.24), channel_id=1, source_target_pairs={{1,9},{3,11},{5,13},{7,15},{9,1},{11,3},{13,5},{15,7},{17,25},{19,... | collective-permute-start | bytes 24584 | tf_op jit(solution)/shard_map/ppermute | solution.py:172
  16.0 2.0 %collective-permute-start.10 = (f32[8,128]{1,0:T(8,128)S(1)}, f32[8,128]{1,0:T(8,128)S(1)}, u32[]{:S(2)}, u32[]{:S(2)}) collective-permute-start(f32[8,128]{1,0:T(8,128)S(1)} %get-tuple-element.26), channel_id=1, source_target_pairs={{1,7},{3,5},{5,3},{7,1},{9,15},{11,13},{13,11},{15,9},{17,23},{19,... | collective-permute-start | bytes 12296 | tf_op jit(solution)/shard_map/ppermute | solution.py:172
  16.7 1.4 %collective-permute-start.11 = (f32[8,128]{1,0:T(8,128)S(1)}, f32[8,128]{1,0:T(8,128)S(1)}, u32[]{:S(2)}, u32[]{:S(2)}) collective-permute-start(f32[8,128]{1,0:T(8,128)S(1)} %get-tuple-element.25), channel_id=1, source_target_pairs={{1,3},{3,1},{5,7},{7,5},{9,11},{11,9},{13,15},{15,13},{17,19},{19,... | collective-permute-start | bytes 12296 | tf_op jit(solution)/shard_map/ppermute | solution.py:172
  17.4 0.7 %collective-permute-start.9 = (f32[8,128]{1,0:T(8,128)S(1)}, f32[8,128]{1,0:T(8,128)S(1)}, u32[]{:S(2)}, u32[]{:S(2)}) collective-permute-start(f32[8,128]{1,0:T(8,128)S(1)} %get-tuple-element.26), channel_id=1, source_target_pairs={{1,5},{3,7},{5,1},{7,3},{9,13},{11,15},{13,9},{15,11},{17,21},{19,... | collective-permute-start | bytes 12296 | tf_op jit(solution)/shard_map/ppermute | solution.py:172
  18.1 20.3 %collective-permute-start.12 = (f32[8,128]{1,0:T(8,128)S(1)}, f32[8,128]{1,0:T(8,128)S(1)}, u32[]{:S(2)}, u32[]{:S(2)}) collective-permute-start(f32[8,128]{1,0:T(8,128)S(1)} %add_add_fusion), channel_id=1, source_target_pairs={{1,0},{3,2},{5,4},{7,6},{9,8},{11,10},{13,12},{15,14},{17,16},{19,... | collective-permute-start | bytes 12296 | tf_op jit(solution)/shard_map/ppermute | solution.py:172

commit v7 on v6

--- a/solution.py
+++ b/solution.py
@@ -165,14 +165,15 @@
         parts = jnp.broadcast_to(parts, (cuts, stems, parts.shape[-1])).reshape(cuts * stems, -1)
         return jnp.sum(lax.all_to_all(parts, ("cuts", "stem"), 0, 0, tiled=True), axis=0)
 
-    def send(x, c, s, cores=(1,)):
+    def send(x, c, s):
         pairs = [
-            (i * stems + j, (i ^ c) * stems + (j ^ s)) for i in range(cuts) for j in range(stems) if j % 2 in cores
+            (i * stems + j, (i ^ c) * stems + (j ^ s) if s % 2 or j % 2 else i * stems + j)
+            for i in range(cuts) for j in range(stems)
         ]
         return lax.ppermute(x, ("cuts", "stem"), pairs)
 
     high, low = cuts // 2, 2
-    chip = [partial_sum, send(partial_sum, 0, 1, (0,))]
+    chip = [partial_sum, send(partial_sum, 0, 1)]
     own, *away = deal(chip, high, lambda: lax.axis_index("cuts") // low)
     line = [own] + [send(x, low * m, 0) for m, x in reversed(list(enumerate(away, 1)))]
     own, away = deal(line, low, lambda: lax.axis_index("cuts") % low)

time: 39.2 us -> 36.3 us (0.926)
  waiting for transfers between devices: 20.9 us -> 2.74 us
  starting transfers between devices: 11.5 us -> 26.7 us
    ppermute x8, waiting for transfers between devices: 19.8 us -> 1.72 us  [send(): return lax.ppermute(x, ('cuts', 'stem'), pairs)]
    ppermute x8, starting transfers between devices: 7.49 us -> 22.7 us  [send(): return lax.ppermute(x, ('cuts', 'stem'), pairs)]
  transfers between devices with their start and end apart: 13 -> 13, of which waited for: 6 -> 6; matrix products, arithmetic and copies ran while one was open for 0% -> 0% of each run, Pallas kernels for 14% -> 15%
where the time goes in v7:
time: 36.3 us; the launch traced here: 36 us
  starting transfers between devices  26.7 us (74%)
  Pallas kernels  5.8 us (16%)
  waiting for transfers between devices  2.74 us (8%)
  other arithmetic  0.6 us (2%)
    ppermute x8, starting transfers between devices, send(): return lax.ppermute(x, ('cuts', 'stem'), pairs)  22.7 us
    pallas_call x1, Pallas kernels, branch_sums(): pl.pallas_call(branch_kernel, in_specs=[hbm, hbm], out_specs=[vmem] * (1...  5.34 us
    ppermute x5, starting transfers between devices, swap(): return lax.ppermute(x, 'stem', [(s, s ^ p) for s in range(stems)])  4.04 us
    ppermute x8, waiting for transfers between devices, send(): return lax.ppermute(x, ('cuts', 'stem'), pairs)  1.72 us
    ppermute x5, waiting for transfers between devices, swap(): return lax.ppermute(x, 'stem', [(s, s ^ p) for s in range(stems)])  1.03 us
  transfers between devices with their start and end apart: 13, of which 6 were waited for; matrix products, arithmetic and copies ran while one was open for 0% of the time, Pallas kernels for 15%

profile of v7, /device:TPU:0, one launch (start us, length us, event | category | flops | bytes accessed | tf_op | source)
XLA Modules:
  0.0 36.0 jit_solution(5377582438727596225)
XLA Ops:
  0.0 0.0 copy-start
  0.0 3.0 %collective-permute-start = (bf16[2,64,1024]{2,1,0:T(8,128)(2,1)}, bf16[2,64,1024]{2,1,0:T(8,128)(2,1)S(1)}, u32[]{:S(2)}, u32[]{:S(2)}) collective-permute-start(bf16[2,64,1024]{2,1,0:T(8,128)(2,1)} %refs_0_.1), channel_id=1, source_target_pairs={{0,2},{1,3},{2,0},{3,1},{4,6},{5,7},{6,4},{7,5},{8,10},{9,11},{10,... | collective-permute-start | bytes 786440 | tf_op jit(solution)/shard_map/ppermute | solution.py:157
  3.0 5.3 %branch_sums.1 = (f32[4,512,128]{2,1,0:T(8,128)S(1)}, bf16[512,128]{1,0:T(8,128)(2,1)S(1)}, bf16[512,128]{1,0:T(8,128)(2,1)S(1)}, bf16[512,128]{1,0:T(8,128)(2,1)S(1)}, bf16[512,128]{1,0:T(8,128)(2,1)S(1)}) custom-call(bf16[16,512,128]{2,1,0:T(8,128)(2,1)} %mid_hbm.1, bf16[8,16,64,128]{3,2,1,0:T(8,128)(2,1)} %right_hbm.1), custom_call_target="tpu_custom_call" | custom-call | flops 2147483648 | bytes 6291456 | tf_op jit(solution)/shard_map/branch_sums/pallas_call | solution.py:77
  8.3 0.1 collective-permute-start.1
  8.4 0.5 %collective-permute-start.2 = (bf16[512,128]{1,0:T(8,128)(2,1)S(1)}, bf16[512,128]{1,0:T(8,128)(2,1)S(1)}, u32[]{:S(2)}, u32[]{:S(2)}) collective-permute-start(bf16[512,128]{1,0:T(8,128)(2,1)S(1)} %get-tuple-element.17), channel_id=1, source_target_pairs={{0,1},{1,0},{2,3},{3,2},{4,5},{5,4},{6,7},{7,6},{8,9},{9,8},{10,11... | collective-permute-start | bytes 393224 | tf_op jit(solution)/shard_map/ppermute | solution.py:157
  8.9 0.1 collective-permute-start.3
  9.0 0.4 %collective-permute-start.4 = (bf16[512,128]{1,0:T(8,128)(2,1)S(1)}, bf16[512,128]{1,0:T(8,128)(2,1)S(1)}, u32[]{:S(2)}, u32[]{:S(2)}) collective-permute-start(bf16[512,128]{1,0:T(8,128)(2,1)S(1)} %get-tuple-element.19), channel_id=1, source_target_pairs={{0,1},{1,0},{2,3},{3,2},{4,5},{5,4},{6,7},{7,6},{8,9},{9,8},{10,11... | collective-permute-start | bytes 393224 | tf_op jit(solution)/shard_map/ppermute | solution.py:157
  9.4 0.3 collective-permute-done.1.refs_2_
  9.7 0.2 collective-permute-done.2.refs_3_
  9.9 0.3 collective-permute-done.3.refs_4_
  10.2 0.2 collective-permute-done.4.refs_5_
  10.4 0.0 collective-permute-done.refs_1_
  10.4 0.0 copy-done
  10.4 0.4 %close.1.refs_0_ = f32[64,128]{1,0:T(8,128)S(1)} custom-call(bf16[2,64,1024]{2,1,0:T(8,128)(2,1)S(1)} %copy-done, bf16[2,64,1024]{2,1,0:T(8,128)(2,1)S(1)} %collective-permute-done.refs_1_, bf16[512,128]{1,0:T(8,128)(2,1)S(1)} %collective-permute-done.1.refs_2_, bf16[512,128]{1,0:T(8,128)(2,1)S(1)} %collective-permute-done.2.refs_3_, ...), custom_call_target="tpu_custom_call" | custom-call | flops 134217728 | bytes 1048576 | tf_op jit(solution)/shard_map/close/pallas_call | solution.py:122
  10.9 0.4 %collective-permute-start.5 = (f32[64,128]{1,0:T(8,128)S(1)}, f32[64,128]{1,0:T(8,128)S(1)}, u32[]{:S(2)}, u32[]{:S(2)}) collective-permute-start(f32[64,128]{1,0:T(8,128)S(1)} %close.1.refs_0_), channel_id=1, source_target_pairs={{0,1},{1,0},{2,3},{3,2},{4,5},{5,4},{6,7},{7,6},{8,9},{9,8},{10,11... | collective-permute-start | bytes 98312 | tf_op jit(solution)/shard_map/ppermute | solution.py:173
  11.3 0.9 %collective-permute-done.5.refs_1_ = f32[64,128]{1,0:T(8,128)S(1)} collective-permute-done((f32[64,128]{1,0:T(8,128)S(1)}, f32[64,128]{1,0:T(8,128)S(1)}, u32[]{:S(2)}, u32[]{:S(2)}) %collective-permute-start.5) | collective-permute-done | bytes 32800 | tf_op jit(solution)/shard_map/ppermute | solution.py:173
  12.2 0.7 %collective-permute-start.6 = (f32[16,128]{1,0:T(8,128)S(1)}, f32[16,128]{1,0:T(8,128)S(1)}, u32[]{:S(2)}, u32[]{:S(2)}) collective-permute-start(f32[16,128]{1,0:T(8,128)S(1)} %get-tuple-element.22), channel_id=1, source_target_pairs={{0,0},{1,25},{2,2},{3,27},{4,4},{5,29},{6,6},{7,31},{8,8},{9,17},{... | collective-permute-start | bytes 24584 | tf_op jit(solution)/shard_map/ppermute | solution.py:173
  12.8 0.7 %collective-permute-start.7 = (f32[16,128]{1,0:T(8,128)S(1)}, f32[16,128]{1,0:T(8,128)S(1)}, u32[]{:S(2)}, u32[]{:S(2)}) collective-permute-start(f32[16,128]{1,0:T(8,128)S(1)} %get-tuple-element.23), channel_id=1, source_target_pairs={{0,0},{1,17},{2,2},{3,19},{4,4},{5,21},{6,6},{7,23},{8,8},{9,25},{... | collective-permute-start | bytes 24584 | tf_op jit(solution)/shard_map/ppermute | solution.py:173
  13.5 0.7 %collective-permute-start.8 = (f32[16,128]{1,0:T(8,128)S(1)}, f32[16,128]{1,0:T(8,128)S(1)}, u32[]{:S(2)}, u32[]{:S(2)}) collective-permute-start(f32[16,128]{1,0:T(8,128)S(1)} %get-tuple-element.24), channel_id=1, source_target_pairs={{0,0},{1,9},{2,2},{3,11},{4,4},{5,13},{6,6},{7,15},{8,8},{9,1},{10... | collective-permute-start | bytes 24584 | tf_op jit(solution)/shard_map/ppermute | solution.py:173
  14.1 0.0 collective-permute-done.6.refs_1_
  14.2 0.0 collective-permute-done.7.refs_2_
  14.2 0.0 collective-permute-done.8.refs_3_
  14.2 0.7 %collective-permute-start.10 = (f32[8,128]{1,0:T(8,128)S(1)}, f32[8,128]{1,0:T(8,128)S(1)}, u32[]{:S(2)}, u32[]{:S(2)}) collective-permute-start(f32[8,128]{1,0:T(8,128)S(1)} %get-tuple-element.26), channel_id=1, source_target_pairs={{0,0},{1,7},{2,2},{3,5},{4,4},{5,3},{6,6},{7,1},{8,8},{9,15},{10,1... | collective-permute-start | bytes 12296 | tf_op jit(solution)/shard_map/ppermute | solution.py:173
  14.9 0.7 %collective-permute-start.11 = (f32[8,128]{1,0:T(8,128)S(1)}, f32[8,128]{1,0:T(8,128)S(1)}, u32[]{:S(2)}, u32[]{:S(2)}) collective-permute-start(f32[8,128]{1,0:T(8,128)S(1)} %get-tuple-element.25), channel_id=1, source_target_pairs={{0,0},{1,3},{2,2},{3,1},{4,4},{5,7},{6,6},{7,5},{8,8},{9,11},{10,1... | collective-permute-start | bytes 12296 | tf_op jit(solution)/shard_map/ppermute | solution.py:173
  15.6 0.7 %collective-permute-start.9 = (f32[8,128]{1,0:T(8,128)S(1)}, f32[8,128]{1,0:T(8,128)S(1)}, u32[]{:S(2)}, u32[]{:S(2)}) collective-permute-start(f32[8,128]{1,0:T(8,128)S(1)} %get-tuple-element.26), channel_id=1, source_target_pairs={{0,0},{1,5},{2,2},{3,7},{4,4},{5,1},{6,6},{7,3},{8,8},{9,13},{10,1... | collective-permute-start | bytes 12296 | tf_op jit(solution)/shard_map/ppermute | solution.py:173
  16.2 0.0 collective-permute-done.10
  16.2 0.0 collective-permute-done.11
  16.2 0.0 collective-permute-done.9
  16.3 18.3 %collective-permute-start.12 = (f32[8,128]{1,0:T(8,128)S(1)}, f32[8,128]{1,0:T(8,128)S(1)}, u32[]{:S(2)}, u32[]{:S(2)}) collective-permute-start(f32[8,128]{1,0:T(8,128)S(1)} %add_add_fusion), channel_id=1, source_target_pairs={{0,1},{1,0},{2,3},{3,2},{4,5},{5,4},{6,7},{7,6},{8,9},{9,8},{10,11... | collective-permute-start | bytes 12296 | tf_op jit(solution)/shard_map/ppermute | solution.py:173
  34.6 0.8 %collective-permute-done.12 = f32[8,128]{1,0:T(8,128)S(1)} collective-permute-done((f32[8,128]{1,0:T(8,128)S(1)}, f32[8,128]{1,0:T(8,128)S(1)}, u32[]{:S(2)}, u32[]{:S(2)}) %collective-permute-start.12) | collective-permute-done | bytes 4128 | tf_op jit(solution)/shard_map/ppermute | solution.py:173
  35.4 0.6 %select_bitcast_fusion = f32[1024]{0:T(1024)} fusion(f32[8,128]{1,0:T(8,128)S(1)} %add_add_fusion, f32[8,128]{1,0:T(8,128)S(1)} %collective-permute-done.12, pred[]{:T(512)S(6)} %eq.5), kind=kLoop, calls=%fused_computation | loop fusion | flops 1024 | bytes 12289 | tf_op jit(solution)/shard_map/reshape | solution.py:186
  (3 shorter events, 0.0 us)
Async XLA Ops:
  0.0 10.4 %copy-start = (bf16[2,64,1024]{2,1,0:T(8,128)(2,1)S(1)}, bf16[2,64,1024]{2,1,0:T(8,128)(2,1)}, u32[]{:S(2)}) copy-start(bf16[2,64,1024]{2,1,0:T(8,128)(2,1)} %refs_0_.1) | copy-start | bytes 786436
  0.0 10.4 %collective-permute-start = (bf16[2,64,1024]{2,1,0:T(8,128)(2,1)}, bf16[2,64,1024]{2,1,0:T(8,128)(2,1)S(1)}, u32[]{:S(2)}, u32[]{:S(2)}) collective-permute-start(bf16[2,64,1024]{2,1,0:T(8,128)(2,1)} %refs_0_.1), channel_id=1, source_target_pairs={{0,2},{1,3},{2,0},{3,1},{4,6},{5,7},{6,4},{7,5},{8,10},{9,11},{10,... | collective-permute-start | bytes 786440 | tf_op jit(solution)/shard_map/ppermute | solution.py:157
  8.3 1.4 %collective-permute-start.1 = (bf16[512,128]{1,0:T(8,128)(2,1)S(1)}, bf16[512,128]{1,0:T(8,128)(2,1)S(1)}, u32[]{:S(2)}, u32[]{:S(2)}) collective-permute-start(bf16[512,128]{1,0:T(8,128)(2,1)S(1)} %get-tuple-element.16), channel_id=1, source_target_pairs={{0,1},{1,0},{2,3},{3,2},{4,5},{5,4},{6,7},{7,6},{8,9},{9,8},{10,11... | collective-permute-start | bytes 393224 | tf_op jit(solution)/shard_map/ppermute | solution.py:157
  8.4 1.5 %collective-permute-start.2 = (bf16[512,128]{1,0:T(8,128)(2,1)S(1)}, bf16[512,128]{1,0:T(8,128)(2,1)S(1)}, u32[]{:S(2)}, u32[]{:S(2)}) collective-permute-start(bf16[512,128]{1,0:T(8,128)(2,1)S(1)} %get-tuple-element.17), channel_id=1, source_target_pairs={{0,1},{1,0},{2,3},{3,2},{4,5},{5,4},{6,7},{7,6},{8,9},{9,8},{10,11... | collective-permute-start | bytes 393224 | tf_op jit(solution)/shard_map/ppermute | solution.py:157
  8.9 1.3 %collective-permute-start.3 = (bf16[512,128]{1,0:T(8,128)(2,1)S(1)}, bf16[512,128]{1,0:T(8,128)(2,1)S(1)}, u32[]{:S(2)}, u32[]{:S(2)}) collective-permute-start(bf16[512,128]{1,0:T(8,128)(2,1)S(1)} %get-tuple-element.18), channel_id=1, source_target_pairs={{0,1},{1,0},{2,3},{3,2},{4,5},{5,4},{6,7},{7,6},{8,9},{9,8},{10,11... | collective-permute-start | bytes 393224 | tf_op jit(solution)/shard_map/ppermute | solution.py:157
  9.0 1.5 %collective-permute-start.4 = (bf16[512,128]{1,0:T(8,128)(2,1)S(1)}, bf16[512,128]{1,0:T(8,128)(2,1)S(1)}, u32[]{:S(2)}, u32[]{:S(2)}) collective-permute-start(bf16[512,128]{1,0:T(8,128)(2,1)S(1)} %get-tuple-element.19), channel_id=1, source_target_pairs={{0,1},{1,0},{2,3},{3,2},{4,5},{5,4},{6,7},{7,6},{8,9},{9,8},{10,11... | collective-permute-start | bytes 393224 | tf_op jit(solution)/shard_map/ppermute | solution.py:157
  10.9 1.3 %collective-permute-start.5 = (f32[64,128]{1,0:T(8,128)S(1)}, f32[64,128]{1,0:T(8,128)S(1)}, u32[]{:S(2)}, u32[]{:S(2)}) collective-permute-start(f32[64,128]{1,0:T(8,128)S(1)} %close.1.refs_0_), channel_id=1, source_target_pairs={{0,1},{1,0},{2,3},{3,2},{4,5},{5,4},{6,7},{7,6},{8,9},{9,8},{10,11... | collective-permute-start | bytes 98312 | tf_op jit(solution)/shard_map/ppermute | solution.py:173
  12.2 2.0 %collective-permute-start.6 = (f32[16,128]{1,0:T(8,128)S(1)}, f32[16,128]{1,0:T(8,128)S(1)}, u32[]{:S(2)}, u32[]{:S(2)}) collective-permute-start(f32[16,128]{1,0:T(8,128)S(1)} %get-tuple-element.22), channel_id=1, source_target_pairs={{0,0},{1,25},{2,2},{3,27},{4,4},{5,29},{6,6},{7,31},{8,8},{9,17},{... | collective-permute-start | bytes 24584 | tf_op jit(solution)/shard_map/ppermute | solution.py:173
  12.8 1.4 %collective-permute-start.7 = (f32[16,128]{1,0:T(8,128)S(1)}, f32[16,128]{1,0:T(8,128)S(1)}, u32[]{:S(2)}, u32[]{:S(2)}) collective-permute-start(f32[16,128]{1,0:T(8,128)S(1)} %get-tuple-element.23), channel_id=1, source_target_pairs={{0,0},{1,17},{2,2},{3,19},{4,4},{5,21},{6,6},{7,23},{8,8},{9,25},{... | collective-permute-start | bytes 24584 | tf_op jit(solution)/shard_map/ppermute | solution.py:173
  13.5 0.7 %collective-permute-start.8 = (f32[16,128]{1,0:T(8,128)S(1)}, f32[16,128]{1,0:T(8,128)S(1)}, u32[]{:S(2)}, u32[]{:S(2)}) collective-permute-start(f32[16,128]{1,0:T(8,128)S(1)} %get-tuple-element.24), channel_id=1, source_target_pairs={{0,0},{1,9},{2,2},{3,11},{4,4},{5,13},{6,6},{7,15},{8,8},{9,1},{10... | collective-permute-start | bytes 24584 | tf_op jit(solution)/shard_map/ppermute | solution.py:173
  14.2 2.0 %collective-permute-start.10 = (f32[8,128]{1,0:T(8,128)S(1)}, f32[8,128]{1,0:T(8,128)S(1)}, u32[]{:S(2)}, u32[]{:S(2)}) collective-permute-start(f32[8,128]{1,0:T(8,128)S(1)} %get-tuple-element.26), channel_id=1, source_target_pairs={{0,0},{1,7},{2,2},{3,5},{4,4},{5,3},{6,6},{7,1},{8,8},{9,15},{10,1... | collective-permute-start | bytes 12296 | tf_op jit(solution)/shard_map/ppermute | solution.py:173
  14.9 1.4 %collective-permute-start.11 = (f32[8,128]{1,0:T(8,128)S(1)}, f32[8,128]{1,0:T(8,128)S(1)}, u32[]{:S(2)}, u32[]{:S(2)}) collective-permute-start(f32[8,128]{1,0:T(8,128)S(1)} %get-tuple-element.25), channel_id=1, source_target_pairs={{0,0},{1,3},{2,2},{3,1},{4,4},{5,7},{6,6},{7,5},{8,8},{9,11},{10,1... | collective-permute-start | bytes 12296 | tf_op jit(solution)/shard_map/ppermute | solution.py:173
  15.6 0.7 %collective-permute-start.9 = (f32[8,128]{1,0:T(8,128)S(1)}, f32[8,128]{1,0:T(8,128)S(1)}, u32[]{:S(2)}, u32[]{:S(2)}) collective-permute-start(f32[8,128]{1,0:T(8,128)S(1)} %get-tuple-element.26), channel_id=1, source_target_pairs={{0,0},{1,5},{2,2},{3,7},{4,4},{5,1},{6,6},{7,3},{8,8},{9,13},{10,1... | collective-permute-start | bytes 12296 | tf_op jit(solution)/shard_map/ppermute | solution.py:173
  16.3 19.2 %collective-permute-start.12 = (f32[8,128]{1,0:T(8,128)S(1)}, f32[8,128]{1,0:T(8,128)S(1)}, u32[]{:S(2)}, u32[]{:S(2)}) collective-permute-start(f32[8,128]{1,0:T(8,128)S(1)} %add_add_fusion), channel_id=1, source_target_pairs={{0,1},{1,0},{2,3},{3,2},{4,5},{5,4},{6,7},{7,6},{8,9},{9,8},{10,11... | collective-permute-start | bytes 12296 | tf_op jit(solution)/shard_map/ppermute | solution.py:173

commit v8 on v5

--- a/solution.py
+++ b/solution.py
@@ -29,7 +29,8 @@
         return pltpu.make_async_copy(mid_hbm.at[at], mid_ref.at[at], mid_sem.at[n])
 
     def right_copy(q):
-        p = jnp.where(q < half, 2 * q + 1, 2 * q - groups)
+        k = jnp.where(q < half, q, q - half)
+        p = jnp.where(k == 0, 0, 2 * k + 1) ^ jnp.where(q < half, 1, 0)
         source = right_hbm.at[pl.ds((me ^ p) * blocks, blocks)]
         return pltpu.make_async_copy(source, right_ref.at[pl.ds(q * blocks, blocks)], right_sem.at[q])
 
@@ -156,7 +157,7 @@
     def swap(x, p):
         return lax.ppermute(x, "stem", [(s, s ^ p) for s in range(stems)])
 
-    pieces = [stem_tensor] + [swap(stem_tensor, p) for p in range(2, stems, 2)]
+    pieces = [stem_tensor] + [swap(stem_tensor, p) for p in range(3, stems, 2)]
     kept, *sent = branch_sums(mid_tensors, right_tensors, stems)
     got = [swap(x, 1) for x in sent]
     partial_sum = close(pieces, kept, got)
@@ -172,13 +173,13 @@
     high, low = cuts // 2, 2
     chip = [partial_sum, send(partial_sum, 0, 1)]
     own, *away = deal(chip, high, lambda: lax.axis_index("cuts") // low)
-    line = [own] + [send(x, low * m, 0) for m, x in enumerate(away, 1)]
+    line = [own] + [send(x, low * m, 1) for m, x in reversed(list(enumerate(away, 1)))]
     own, away = deal(line, low, lambda: lax.axis_index("cuts") % low)
     total = own
     for s in range(0, stems, 2):
-        total = total + send(away, 1, s)
+        total = total + send(away, 1, s ^ 1)
         if s:
-            total = total + send(own, 0, s)
+            total = total + send(own, 0, s ^ 1)
     return total.reshape(-1)
 
 

time: 29.1 us -> 26 us (0.89)
  waiting for transfers between devices: 10.2 us -> 8.26 us
  starting transfers between devices: 12.3 us -> 11.2 us
    ppermute x7, waiting for transfers between devices: 9.18 us -> 6.99 us  [send(): return lax.ppermute(x, ('cuts', 'stem'), pairs)]
    ppermute x7, starting transfers between devices: 8.27 us -> 7.42 us  [send(): return lax.ppermute(x, ('cuts', 'stem'), pairs)]
    ppermute x5, starting transfers between devices: 4.04 us -> 3.74 us  [swap(): return lax.ppermute(x, 'stem', [(s, s ^ p) for s in range(stems)])]
  transfers between devices with their start and end apart: 12 -> 12, of which waited for: 10 -> 10; matrix products, arithmetic and copies ran while one was open for 0% -> 0% of each run, Pallas kernels for 18% -> 21%
where the time goes in v8:
time: 26 us; the launch traced here: 25.8 us
  starting transfers between devices  11.2 us (43%)
  waiting for transfers between devices  8.26 us (32%)
  Pallas kernels  5.78 us (22%)
  other arithmetic  0.6 us (2%)
    ppermute x7, starting transfers between devices, send(): return lax.ppermute(x, ('cuts', 'stem'), pairs)  7.42 us
    ppermute x7, waiting for transfers between devices, send(): return lax.ppermute(x, ('cuts', 'stem'), pairs)  6.99 us
    pallas_call x1, Pallas kernels, branch_sums(): pl.pallas_call(branch_kernel, in_specs=[hbm, hbm], out_specs=[vmem] * (1...  5.34 us
    ppermute x5, starting transfers between devices, swap(): return lax.ppermute(x, 'stem', [(s, s ^ p) for s in range(stems)])  3.74 us
    ppermute x5, waiting for transfers between devices, swap(): return lax.ppermute(x, 'stem', [(s, s ^ p) for s in range(stems)])  1.27 us
    reshape x1, other arithmetic, on_device(): return total.reshape(-1)  0.6 us
  transfers between devices with their start and end apart: 12, of which 10 were waited for; matrix products, arithmetic and copies ran while one was open for 0% of the time, Pallas kernels for 21%

profile of v8, /device:TPU:0, one launch (start us, length us, event | category | flops | bytes accessed | tf_op | source)
XLA Modules:
  0.0 25.8 jit_solution(12294103541855164416)
XLA Ops:
  0.0 0.0 copy-start
  0.0 2.4 %collective-permute-start = (bf16[2,64,1024]{2,1,0:T(8,128)(2,1)}, bf16[2,64,1024]{2,1,0:T(8,128)(2,1)S(1)}, u32[]{:S(2)}, u32[]{:S(2)}) collective-permute-start(bf16[2,64,1024]{2,1,0:T(8,128)(2,1)} %refs_0_.1), channel_id=1, source_target_pairs={{0,3},{1,2},{2,1},{3,0},{4,7},{5,6},{6,5},{7,4},{8,11},{9,10},{10,... | collective-permute-start | bytes 786440 | tf_op jit(solution)/shard_map/ppermute | solution.py:158
  2.4 5.3 %branch_sums.1 = (f32[4,512,128]{2,1,0:T(8,128)S(1)}, bf16[512,128]{1,0:T(8,128)(2,1)S(1)}, bf16[512,128]{1,0:T(8,128)(2,1)S(1)}, bf16[512,128]{1,0:T(8,128)(2,1)S(1)}, bf16[512,128]{1,0:T(8,128)(2,1)S(1)}) custom-call(bf16[16,512,128]{2,1,0:T(8,128)(2,1)} %mid_hbm.1, bf16[8,16,64,128]{3,2,1,0:T(8,128)(2,1)} %right_hbm.1), custom_call_target="tpu_custom_call" | custom-call | flops 2147483648 | bytes 6291456 | tf_op jit(solution)/shard_map/branch_sums/pallas_call | solution.py:78
  7.8 0.7 %collective-permute-start.1 = (bf16[512,128]{1,0:T(8,128)(2,1)S(1)}, bf16[512,128]{1,0:T(8,128)(2,1)S(1)}, u32[]{:S(2)}, u32[]{:S(2)}) collective-permute-start(bf16[512,128]{1,0:T(8,128)(2,1)S(1)} %get-tuple-element.16), channel_id=1, source_target_pairs={{0,1},{1,0},{2,3},{3,2},{4,5},{5,4},{6,7},{7,6},{8,9},{9,8},{10,11... | collective-permute-start | bytes 393224 | tf_op jit(solution)/shard_map/ppermute | solution.py:158
  8.5 0.1 collective-permute-start.2
  8.6 0.4 %collective-permute-start.3 = (bf16[512,128]{1,0:T(8,128)(2,1)S(1)}, bf16[512,128]{1,0:T(8,128)(2,1)S(1)}, u32[]{:S(2)}, u32[]{:S(2)}) collective-permute-start(bf16[512,128]{1,0:T(8,128)(2,1)S(1)} %get-tuple-element.18), channel_id=1, source_target_pairs={{0,1},{1,0},{2,3},{3,2},{4,5},{5,4},{6,7},{7,6},{8,9},{9,8},{10,11... | collective-permute-start | bytes 393224 | tf_op jit(solution)/shard_map/ppermute | solution.py:158
  9.0 0.1 collective-permute-start.4
  9.1 0.4 %collective-permute-done.1.refs_2_ = bf16[512,128]{1,0:T(8,128)(2,1)S(1)} collective-permute-done((bf16[512,128]{1,0:T(8,128)(2,1)S(1)}, bf16[512,128]{1,0:T(8,128)(2,1)S(1)}, u32[]{:S(2)}, u32[]{:S(2)}) %collective-permute-start.1) | collective-permute-done | bytes 131104 | tf_op jit(solution)/shard_map/ppermute | solution.py:158
  9.5 0.4 %collective-permute-done.2.refs_3_ = bf16[512,128]{1,0:T(8,128)(2,1)S(1)} collective-permute-done((bf16[512,128]{1,0:T(8,128)(2,1)S(1)}, bf16[512,128]{1,0:T(8,128)(2,1)S(1)}, u32[]{:S(2)}, u32[]{:S(2)}) %collective-permute-start.2) | collective-permute-done | bytes 131104 | tf_op jit(solution)/shard_map/ppermute | solution.py:158
  9.8 0.2 collective-permute-done.3.refs_4_
  10.0 0.3 %collective-permute-done.4.refs_5_ = bf16[512,128]{1,0:T(8,128)(2,1)S(1)} collective-permute-done((bf16[512,128]{1,0:T(8,128)(2,1)S(1)}, bf16[512,128]{1,0:T(8,128)(2,1)S(1)}, u32[]{:S(2)}, u32[]{:S(2)}) %collective-permute-start.4) | collective-permute-done | bytes 131104 | tf_op jit(solution)/shard_map/ppermute | solution.py:158
  10.4 0.0 collective-permute-done.refs_1_
  10.4 0.0 copy-done
  10.4 0.4 %close.1.refs_0_ = f32[64,128]{1,0:T(8,128)S(1)} custom-call(bf16[2,64,1024]{2,1,0:T(8,128)(2,1)S(1)} %copy-done, bf16[2,64,1024]{2,1,0:T(8,128)(2,1)S(1)} %collective-permute-done.refs_1_, bf16[512,128]{1,0:T(8,128)(2,1)S(1)} %collective-permute-done.1.refs_2_, bf16[512,128]{1,0:T(8,128)(2,1)S(1)} %collective-permute-done.2.refs_3_, ...), custom_call_target="tpu_custom_call" | custom-call | flops 134217728 | bytes 1048576 | tf_op jit(solution)/shard_map/close/pallas_call | solution.py:123
  10.8 0.2 collective-permute-start.5
  11.1 1.0 %collective-permute-done.5.refs_1_ = f32[64,128]{1,0:T(8,128)S(1)} collective-permute-done((f32[64,128]{1,0:T(8,128)S(1)}, f32[64,128]{1,0:T(8,128)S(1)}, u32[]{:S(2)}, u32[]{:S(2)}) %collective-permute-start.5) | collective-permute-done | bytes 32800 | tf_op jit(solution)/shard_map/ppermute | solution.py:171
  12.1 3.4 %collective-permute-start.6 = (f32[16,128]{1,0:T(8,128)S(1)}, f32[16,128]{1,0:T(8,128)S(1)}, u32[]{:S(2)}, u32[]{:S(2)}) collective-permute-start(f32[16,128]{1,0:T(8,128)S(1)} %get-tuple-element.22), channel_id=1, source_target_pairs={{0,25},{1,24},{2,27},{3,26},{4,29},{5,28},{6,31},{7,30},{8,17},{9,... | collective-permute-start | bytes 24584 | tf_op jit(solution)/shard_map/ppermute | solution.py:171
  15.5 0.0 collective-permute-start.7
  15.5 0.6 %collective-permute-start.8 = (f32[16,128]{1,0:T(8,128)S(1)}, f32[16,128]{1,0:T(8,128)S(1)}, u32[]{:S(2)}, u32[]{:S(2)}) collective-permute-start(f32[16,128]{1,0:T(8,128)S(1)} %get-tuple-element.24), channel_id=1, source_target_pairs={{0,9},{1,8},{2,11},{3,10},{4,13},{5,12},{6,15},{7,14},{8,1},{9,0},... | collective-permute-start | bytes 24584 | tf_op jit(solution)/shard_map/ppermute | solution.py:171
  16.0 0.9 %collective-permute-done.6.refs_1_ = f32[16,128]{1,0:T(8,128)S(1)} collective-permute-done((f32[16,128]{1,0:T(8,128)S(1)}, f32[16,128]{1,0:T(8,128)S(1)}, u32[]{:S(2)}, u32[]{:S(2)}) %collective-permute-start.6) | collective-permute-done | bytes 8224 | tf_op jit(solution)/shard_map/ppermute | solution.py:171
  17.0 2.5 %collective-permute-done.7.refs_2_ = f32[16,128]{1,0:T(8,128)S(1)} collective-permute-done((f32[16,128]{1,0:T(8,128)S(1)}, f32[16,128]{1,0:T(8,128)S(1)}, u32[]{:S(2)}, u32[]{:S(2)}) %collective-permute-start.7) | collective-permute-done | bytes 8224 | tf_op jit(solution)/shard_map/ppermute | solution.py:171
  19.5 0.0 collective-permute-done.8.refs_3_
  19.5 2.3 %collective-permute-start.10 = (f32[8,128]{1,0:T(8,128)S(1)}, f32[8,128]{1,0:T(8,128)S(1)}, u32[]{:S(2)}, u32[]{:S(2)}) collective-permute-start(f32[8,128]{1,0:T(8,128)S(1)} %get-tuple-element.26), channel_id=1, source_target_pairs={{0,7},{1,6},{2,5},{3,4},{4,3},{5,2},{6,1},{7,0},{8,15},{9,14},{10,... | collective-permute-start | bytes 12296 | tf_op jit(solution)/shard_map/ppermute | solution.py:171
  21.8 0.4 %collective-permute-start.11 = (f32[8,128]{1,0:T(8,128)S(1)}, f32[8,128]{1,0:T(8,128)S(1)}, u32[]{:S(2)}, u32[]{:S(2)}) collective-permute-start(f32[8,128]{1,0:T(8,128)S(1)} %get-tuple-element.25), channel_id=1, source_target_pairs={{0,3},{1,2},{2,1},{3,0},{4,7},{5,6},{6,5},{7,4},{8,11},{9,10},{10,... | collective-permute-start | bytes 12296 | tf_op jit(solution)/shard_map/ppermute | solution.py:171
  22.2 0.5 %collective-permute-start.9 = (f32[8,128]{1,0:T(8,128)S(1)}, f32[8,128]{1,0:T(8,128)S(1)}, u32[]{:S(2)}, u32[]{:S(2)}) collective-permute-start(f32[8,128]{1,0:T(8,128)S(1)} %get-tuple-element.26), channel_id=1, source_target_pairs={{0,5},{1,4},{2,7},{3,6},{4,1},{5,0},{6,3},{7,2},{8,13},{9,12},{10,... | collective-permute-start | bytes 12296 | tf_op jit(solution)/shard_map/ppermute | solution.py:171
  22.7 0.8 %collective-permute-done.10 = f32[8,128]{1,0:T(8,128)S(1)} collective-permute-done((f32[8,128]{1,0:T(8,128)S(1)}, f32[8,128]{1,0:T(8,128)S(1)}, u32[]{:S(2)}, u32[]{:S(2)}) %collective-permute-start.10) | collective-permute-done | bytes 4128 | tf_op jit(solution)/shard_map/ppermute | solution.py:171
  23.5 1.4 %collective-permute-done.11 = f32[8,128]{1,0:T(8,128)S(1)} collective-permute-done((f32[8,128]{1,0:T(8,128)S(1)}, f32[8,128]{1,0:T(8,128)S(1)}, u32[]{:S(2)}, u32[]{:S(2)}) %collective-permute-start.11) | collective-permute-done | bytes 4128 | tf_op jit(solution)/shard_map/ppermute | solution.py:171
  24.8 0.4 %collective-permute-done.9 = f32[8,128]{1,0:T(8,128)S(1)} collective-permute-done((f32[8,128]{1,0:T(8,128)S(1)}, f32[8,128]{1,0:T(8,128)S(1)}, u32[]{:S(2)}, u32[]{:S(2)}) %collective-permute-start.9) | collective-permute-done | bytes 4128 | tf_op jit(solution)/shard_map/ppermute | solution.py:171
  25.2 0.6 %add_bitcast_fusion = f32[1024]{0:T(1024)} fusion(f32[8,128]{1,0:T(8,128)S(1)} %collective-permute-done.11, f32[8,128]{1,0:T(8,128)S(1)} %collective-permute-done.10, f32[8,128]{1,0:T(8,128)S(1)} %get-tuple-element.25, f32[8,128]{1,0:T(8,128)S(1)} %collective-permute-done.9), kind=kLoop, calls=%fused_computation | loop fusion | flops 3072 | bytes 20480 | tf_op jit(solution)/shard_map/reshape | solution.py:183
  (2 shorter events, 0.0 us)
Async XLA Ops:
  0.0 10.4 %copy-start = (bf16[2,64,1024]{2,1,0:T(8,128)(2,1)S(1)}, bf16[2,64,1024]{2,1,0:T(8,128)(2,1)}, u32[]{:S(2)}) copy-start(bf16[2,64,1024]{2,1,0:T(8,128)(2,1)} %refs_0_.1) | copy-start | bytes 786436
  0.0 10.4 %collective-permute-start = (bf16[2,64,1024]{2,1,0:T(8,128)(2,1)}, bf16[2,64,1024]{2,1,0:T(8,128)(2,1)S(1)}, u32[]{:S(2)}, u32[]{:S(2)}) collective-permute-start(bf16[2,64,1024]{2,1,0:T(8,128)(2,1)} %refs_0_.1), channel_id=1, source_target_pairs={{0,3},{1,2},{2,1},{3,0},{4,7},{5,6},{6,5},{7,4},{8,11},{9,10},{10,... | collective-permute-start | bytes 786440 | tf_op jit(solution)/shard_map/ppermute | solution.py:158
  7.8 1.7 %collective-permute-start.1 = (bf16[512,128]{1,0:T(8,128)(2,1)S(1)}, bf16[512,128]{1,0:T(8,128)(2,1)S(1)}, u32[]{:S(2)}, u32[]{:S(2)}) collective-permute-start(bf16[512,128]{1,0:T(8,128)(2,1)S(1)} %get-tuple-element.16), channel_id=1, source_target_pairs={{0,1},{1,0},{2,3},{3,2},{4,5},{5,4},{6,7},{7,6},{8,9},{9,8},{10,11... | collective-permute-start | bytes 393224 | tf_op jit(solution)/shard_map/ppermute | solution.py:158
  8.5 1.3 %collective-permute-start.2 = (bf16[512,128]{1,0:T(8,128)(2,1)S(1)}, bf16[512,128]{1,0:T(8,128)(2,1)S(1)}, u32[]{:S(2)}, u32[]{:S(2)}) collective-permute-start(bf16[512,128]{1,0:T(8,128)(2,1)S(1)} %get-tuple-element.17), channel_id=1, source_target_pairs={{0,1},{1,0},{2,3},{3,2},{4,5},{5,4},{6,7},{7,6},{8,9},{9,8},{10,11... | collective-permute-start | bytes 393224 | tf_op jit(solution)/shard_map/ppermute | solution.py:158
  8.6 1.5 %collective-permute-start.3 = (bf16[512,128]{1,0:T(8,128)(2,1)S(1)}, bf16[512,128]{1,0:T(8,128)(2,1)S(1)}, u32[]{:S(2)}, u32[]{:S(2)}) collective-permute-start(bf16[512,128]{1,0:T(8,128)(2,1)S(1)} %get-tuple-element.18), channel_id=1, source_target_pairs={{0,1},{1,0},{2,3},{3,2},{4,5},{5,4},{6,7},{7,6},{8,9},{9,8},{10,11... | collective-permute-start | bytes 393224 | tf_op jit(solution)/shard_map/ppermute | solution.py:158
  9.0 1.3 %collective-permute-start.4 = (bf16[512,128]{1,0:T(8,128)(2,1)S(1)}, bf16[512,128]{1,0:T(8,128)(2,1)S(1)}, u32[]{:S(2)}, u32[]{:S(2)}) collective-permute-start(bf16[512,128]{1,0:T(8,128)(2,1)S(1)} %get-tuple-element.19), channel_id=1, source_target_pairs={{0,1},{1,0},{2,3},{3,2},{4,5},{5,4},{6,7},{7,6},{8,9},{9,8},{10,11... | collective-permute-start | bytes 393224 | tf_op jit(solution)/shard_map/ppermute | solution.py:158
  10.8 1.3 %collective-permute-start.5 = (f32[64,128]{1,0:T(8,128)S(1)}, f32[64,128]{1,0:T(8,128)S(1)}, u32[]{:S(2)}, u32[]{:S(2)}) collective-permute-start(f32[64,128]{1,0:T(8,128)S(1)} %close.1.refs_0_), channel_id=1, source_target_pairs={{0,1},{1,0},{2,3},{3,2},{4,5},{5,4},{6,7},{7,6},{8,9},{9,8},{10,11... | collective-permute-start | bytes 98312 | tf_op jit(solution)/shard_map/ppermute | solution.py:171
  12.1 4.9 %collective-permute-start.6 = (f32[16,128]{1,0:T(8,128)S(1)}, f32[16,128]{1,0:T(8,128)S(1)}, u32[]{:S(2)}, u32[]{:S(2)}) collective-permute-start(f32[16,128]{1,0:T(8,128)S(1)} %get-tuple-element.22), channel_id=1, source_target_pairs={{0,25},{1,24},{2,27},{3,26},{4,29},{5,28},{6,31},{7,30},{8,17},{9,... | collective-permute-start | bytes 24584 | tf_op jit(solution)/shard_map/ppermute | solution.py:171
  15.5 4.0 %collective-permute-start.7 = (f32[16,128]{1,0:T(8,128)S(1)}, f32[16,128]{1,0:T(8,128)S(1)}, u32[]{:S(2)}, u32[]{:S(2)}) collective-permute-start(f32[16,128]{1,0:T(8,128)S(1)} %get-tuple-element.23), channel_id=1, source_target_pairs={{0,17},{1,16},{2,19},{3,18},{4,21},{5,20},{6,23},{7,22},{8,25},{9,... | collective-permute-start | bytes 24584 | tf_op jit(solution)/shard_map/ppermute | solution.py:171
  15.5 4.0 %collective-permute-start.8 = (f32[16,128]{1,0:T(8,128)S(1)}, f32[16,128]{1,0:T(8,128)S(1)}, u32[]{:S(2)}, u32[]{:S(2)}) collective-permute-start(f32[16,128]{1,0:T(8,128)S(1)} %get-tuple-element.24), channel_id=1, source_target_pairs={{0,9},{1,8},{2,11},{3,10},{4,13},{5,12},{6,15},{7,14},{8,1},{9,0},... | collective-permute-start | bytes 24584 | tf_op jit(solution)/shard_map/ppermute | solution.py:171
  19.5 4.0 %collective-permute-start.10 = (f32[8,128]{1,0:T(8,128)S(1)}, f32[8,128]{1,0:T(8,128)S(1)}, u32[]{:S(2)}, u32[]{:S(2)}) collective-permute-start(f32[8,128]{1,0:T(8,128)S(1)} %get-tuple-element.26), channel_id=1, source_target_pairs={{0,7},{1,6},{2,5},{3,4},{4,3},{5,2},{6,1},{7,0},{8,15},{9,14},{10,... | collective-permute-start | bytes 12296 | tf_op jit(solution)/shard_map/ppermute | solution.py:171
  21.8 3.0 %collective-permute-start.11 = (f32[8,128]{1,0:T(8,128)S(1)}, f32[8,128]{1,0:T(8,128)S(1)}, u32[]{:S(2)}, u32[]{:S(2)}) collective-permute-start(f32[8,128]{1,0:T(8,128)S(1)} %get-tuple-element.25), channel_id=1, source_target_pairs={{0,3},{1,2},{2,1},{3,0},{4,7},{5,6},{6,5},{7,4},{8,11},{9,10},{10,... | collective-permute-start | bytes 12296 | tf_op jit(solution)/shard_map/ppermute | solution.py:171
  22.2 3.0 %collective-permute-start.9 = (f32[8,128]{1,0:T(8,128)S(1)}, f32[8,128]{1,0:T(8,128)S(1)}, u32[]{:S(2)}, u32[]{:S(2)}) collective-permute-start(f32[8,128]{1,0:T(8,128)S(1)} %get-tuple-element.26), channel_id=1, source_target_pairs={{0,5},{1,4},{2,7},{3,6},{4,1},{5,0},{6,3},{7,2},{8,13},{9,12},{10,... | collective-permute-start | bytes 12296 | tf_op jit(solution)/shard_map/ppermute | solution.py:171

commit v9 on v3

--- a/solution.py
+++ b/solution.py
@@ -1,3 +1,5 @@
+import functools
+
 import jax
 import jax.numpy as jnp
 from jax import lax
@@ -15,12 +17,12 @@
     return jnp.where(lane < half, -rolled, rolled)
 
 
-def branch_kernel(mid_hbm, right_hbm, kept_ref, *refs):
-    *sent_refs, mid_ref, right_ref, mid_sem, right_sem = refs
-    pairs, depth, width = mid_ref.shape
-    groups = right_sem.shape[0]
-    half = groups // 2
-    blocks = right_ref.shape[0] // groups
+def branch_kernel(blocks, mid_hbm, right_hbm, kept_ref, *refs):
+    *sent_refs, mid_ref, wide_ref, mid_sem, right_sem = refs
+    pairs, _, width = mid_ref.shape
+    total, _, inner, _ = right_hbm.shape
+    groups = total // blocks
+    leaving = len(sent_refs) // blocks
     me = lax.axis_index("stem")
     chunk = pairs // mid_sem.shape[0]
 
@@ -29,40 +31,44 @@
         return pltpu.make_async_copy(mid_hbm.at[at], mid_ref.at[at], mid_sem.at[n])
 
     def right_copy(q):
-        p = jnp.where(q < half, 2 * q + 1, 2 * q - groups)
+        stays = q - leaving
+        p = jnp.where(stays < 0, 2 * q + 3, jnp.where(stays < 2, stays, 2 * stays - 2))
         source = right_hbm.at[pl.ds((me ^ p) * blocks, blocks)]
-        return pltpu.make_async_copy(source, right_ref.at[pl.ds(q * blocks, blocks)], right_sem.at[q])
+        target = wide_ref.at[pl.ds(q * blocks, blocks), :, pl.ds(0, inner)]
+        return pltpu.make_async_copy(source, target, right_sem.at[q])
 
+    for q in range(groups):
+        right_copy(q).start()
     for n in range(mid_sem.shape[0]):
         mid_copy(n).start()
-    for q in range(groups):
-        right_copy(q).start()
+
+    def widen(q, carry):
+        right_copy(q).wait()
+        for b in range(blocks):
+            for j in range(pairs):
+                upper = wide_ref[q * blocks + b, j, :inner]
+                wide_ref[q * blocks + b, j, inner:] = turn(upper.astype(jnp.float32)).astype(upper.dtype)
+        return carry
+
+    lax.fori_loop(0, groups, widen, 0)
     for n in range(mid_sem.shape[0]):
         mid_copy(n).wait()
 
     def group(q, carry):
-        right_copy(q).wait()
         left = jnp.concatenate([mid_ref[j] for j in range(pairs)], axis=1)
-        columns = []
-        for b in range(blocks):
-            rows = []
-            for j in range(pairs):
-                w = right_ref[q * blocks + b, j]
-                rows += [w, turn(w.astype(jnp.float32)).astype(w.dtype)]
-            columns.append(jnp.concatenate(rows, axis=0))
-        sums = jnp.dot(left, jnp.concatenate(columns, axis=1), preferred_element_type=jnp.float32)
-
-        for at in range(half):
+        right = [wide_ref[q * blocks + b].reshape(pairs * 2 * inner, width) for b in range(blocks)]
+        sums = jnp.dot(left, jnp.concatenate(right, axis=1), preferred_element_type=jnp.float32)
+        for at in range(leaving):
             @pl.when(q == at)
             def _():
                 for b in range(blocks):
                     part = sums[:, b * width:(b + 1) * width]
                     sent_refs[at * blocks + b][...] = part.astype(jnp.bfloat16)
 
-        @pl.when(q >= half)
+        @pl.when(q >= leaving)
         def _():
             for b in range(blocks):
-                kept_ref[(q - half) * blocks + b] = sums[:, b * width:(b + 1) * width]
+                kept_ref[(q - leaving) * blocks + b] = sums[:, b * width:(b + 1) * width]
 
         return carry
 
@@ -71,19 +77,21 @@
 
 def branch_sums(mid, right, groups):
     pairs, depth, width = mid.shape
-    total = right.shape[0]
+    total, _, inner, _ = right.shape
+    blocks = total // groups
+    leaving = (groups // 2 - 1) * blocks
     vmem = pl.BlockSpec(memory_space=pltpu.VMEM)
     hbm = pl.BlockSpec(memory_space=pltpu.HBM)
     return pl.pallas_call(
-        branch_kernel,
+        functools.partial(branch_kernel, blocks),
         in_specs=[hbm, hbm],
-        out_specs=[vmem] * (1 + total // 2),
+        out_specs=[vmem] * (1 + leaving),
         out_shape=[
-            jax.ShapeDtypeStruct((total // 2, depth, width), jnp.float32),
-        ] + [jax.ShapeDtypeStruct((depth, width), jnp.bfloat16)] * (total // 2),
+            jax.ShapeDtypeStruct((total - leaving, depth, width), jnp.float32),
+        ] + [jax.ShapeDtypeStruct((depth, width), jnp.bfloat16)] * leaving,
         scratch_shapes=[
             pltpu.VMEM(mid.shape, mid.dtype),
-            pltpu.VMEM(right.shape, right.dtype),
+            pltpu.VMEM((total, pairs, 2 * inner, width), right.dtype),
             pltpu.SemaphoreType.DMA((4,)),
             pltpu.SemaphoreType.DMA((groups,)),
         ],
@@ -95,9 +103,10 @@
     )(mid, right)
 
 
-def close_kernel(*refs):
+def close_kernel(count, *refs):
     *more, kept_ref, out_ref = refs
-    stem_refs, got_refs = more[:-kept_ref.shape[0]], more[-kept_ref.shape[0]:]
+    stem_refs, got_refs = more[:count], more[count:]
+    alone = kept_ref.shape[0] - len(got_refs)
     part = None
     at = 0
     for ref in stem_refs:
@@ -105,7 +114,9 @@
             block = ref[b]
             half = block.shape[-1] // 2
             rows = jnp.concatenate([block[:, :half], block[:, half:]], axis=0)
-            sums = kept_ref[at] + got_refs[at][...].astype(jnp.float32)
+            sums = kept_ref[at]
+            if at >= alone:
+                sums += got_refs[at - alone][...].astype(jnp.float32)
             high = sums.astype(jnp.bfloat16)
             low = (sums - high.astype(jnp.float32)).astype(jnp.bfloat16)
             term = jnp.dot(rows, jnp.concatenate([high, low], axis=1), preferred_element_type=jnp.float32)
@@ -129,7 +140,7 @@
     whole_tiles = rows % (8 * cuts) == 0
     shape = (cuts, copies, rows // cuts, width) if whole_tiles else (rows, width)
     out = pl.pallas_call(
-        close_kernel,
+        functools.partial(close_kernel, len(stems)),
         out_shape=jax.ShapeDtypeStruct(shape, jnp.float32),
         compiler_params=pltpu.CompilerParams(vmem_limit_bytes=24 * MIB),
         cost_estimate=pl.CostEstimate(flops=8 * rows * kept.size, bytes_accessed=MIB, transcendentals=0),
@@ -148,7 +159,8 @@
     def swap(x, p):
         return lax.ppermute(x, "stem", [(s, s ^ p) for s in range(stems)])
 
-    pieces = [stem_tensor] + [swap(stem_tensor, p) for p in range(2, stems, 2)]
+    far = [swap(stem_tensor, p) for p in range(2, stems, 2)]
+    pieces = [stem_tensor, swap(stem_tensor, 1)] + far
     kept, *sent = branch_sums(mid_tensors, right_tensors, stems)
     got = [swap(x, 1) for x in sent]
     spread = close(pieces, kept, got, cuts, stems)

time: 24.8 us -> 25.5 us (1.028)
  blocking collectives: 13.2 us -> 14.1 us
  starting transfers between devices: 4.04 us -> 3.61 us
  waiting for transfers between devices: 1.03 us -> 1.3 us
    all_to_all x1, blocking collectives: 13.2 us -> 14.1 us  [on_device(): parts = lax.all_to_all(spread, ('cuts', 'stem'), 0, 0, tiled=True)]
    ppermute x5 -> x4, starting transfers between devices: 4.04 us -> 3.61 us  [swap(): return lax.ppermute(x, 'stem', [(s, s ^ p) for s in range(stems)])]
    ppermute x5 -> x4, waiting for transfers between devices: 1.03 us -> 1.3 us  [swap(): return lax.ppermute(x, 'stem', [(s, s ^ p) for s in range(stems)])]
  transfers between devices with their start and end apart: 5 -> 4, of which waited for: 4 -> 3; matrix products, arithmetic and copies ran while one was open for 0% -> 0% of each run, Pallas kernels for 22% -> 21%
where the time goes in v9:
time: 25.5 us; the launch traced here: 25.4 us
  blocking collectives  14.1 us (55%)
  Pallas kernels  5.71 us (22%)
  starting transfers between devices  3.61 us (14%)
  waiting for transfers between devices  1.3 us (5%)
  other arithmetic  0.63 us (2%)
    all_to_all x1, blocking collectives, on_device(): parts = lax.all_to_all(spread, ('cuts', 'stem'), 0, 0, tiled=True)  14.1 us
    pallas_call x1, Pallas kernels, branch_sums(): pl.pallas_call(functools.partial(branch_kernel, blocks), in_specs=[hbm, h...  5.24 us
    ppermute x4, starting transfers between devices, swap(): return lax.ppermute(x, 'stem', [(s, s ^ p) for s in range(stems)])  3.61 us
    ppermute x4, waiting for transfers between devices, swap(): return lax.ppermute(x, 'stem', [(s, s ^ p) for s in range(stems)])  1.3 us
    reduce_sum x1, other arithmetic, on_device(): return jnp.sum(parts, axis=0).reshape(-1)  0.63 us
  transfers between devices with their start and end apart: 4, of which 3 were waited for; matrix products, arithmetic and copies ran while one was open for 0% of the time, Pallas kernels for 21%

profile of v9, /device:TPU:0, one launch (start us, length us, event | category | flops | bytes accessed | tf_op | source)
XLA Modules:
  0.0 25.4 jit_solution(14942554480247829899)
XLA Ops:
  0.0 0.0 copy-start
  0.0 0.5 %collective-permute-start = (bf16[2,64,1024]{2,1,0:T(8,128)(2,1)}, bf16[2,64,1024]{2,1,0:T(8,128)(2,1)S(1)}, u32[]{:S(2)}, u32[]{:S(2)}) collective-permute-start(bf16[2,64,1024]{2,1,0:T(8,128)(2,1)} %refs_0_.1), channel_id=1, source_target_pairs={{0,1},{1,0},{2,3},{3,2},{4,5},{5,4},{6,7},{7,6},{8,9},{9,8},{10,11... | collective-permute-start | bytes 786440 | tf_op jit(solution)/shard_map/ppermute | solution.py:160
  0.5 2.6 %collective-permute-start.1 = (bf16[2,64,1024]{2,1,0:T(8,128)(2,1)}, bf16[2,64,1024]{2,1,0:T(8,128)(2,1)S(1)}, u32[]{:S(2)}, u32[]{:S(2)}) collective-permute-start(bf16[2,64,1024]{2,1,0:T(8,128)(2,1)} %refs_0_.1), channel_id=1, source_target_pairs={{0,2},{1,3},{2,0},{3,1},{4,6},{5,7},{6,4},{7,5},{8,10},{9,11},{10,... | collective-permute-start | bytes 786440 | tf_op jit(solution)/shard_map/ppermute | solution.py:160
  3.0 5.2 %branch_sums.1 = (f32[6,512,128]{2,1,0:T(8,128)S(1)}, bf16[512,128]{1,0:T(8,128)(2,1)S(1)}, bf16[512,128]{1,0:T(8,128)(2,1)S(1)}) custom-call(bf16[16,512,128]{2,1,0:T(8,128)(2,1)} %mid_hbm.1, bf16[8,16,64,128]{3,2,1,0:T(8,128)(2,1)} %right_hbm.1), custom_call_target="tpu_custom_call" | custom-call | flops 2147483648 | bytes 6291456 | tf_op jit(solution)/shard_map/branch_sums/pallas_call | solution.py:85
  8.3 0.2 collective-permute-start.2
  8.5 0.3 %collective-permute-start.3 = (bf16[512,128]{1,0:T(8,128)(2,1)S(1)}, bf16[512,128]{1,0:T(8,128)(2,1)S(1)}, u32[]{:S(2)}, u32[]{:S(2)}) collective-permute-start(bf16[512,128]{1,0:T(8,128)(2,1)S(1)} %get-tuple-element.9), channel_id=1, source_target_pairs={{0,1},{1,0},{2,3},{3,2},{4,5},{5,4},{6,7},{7,6},{8,9},{9,8},{10,11... | collective-permute-start | bytes 393224 | tf_op jit(solution)/shard_map/ppermute | solution.py:160
  8.9 0.8 %collective-permute-done.2.refs_3_ = bf16[512,128]{1,0:T(8,128)(2,1)S(1)} collective-permute-done((bf16[512,128]{1,0:T(8,128)(2,1)S(1)}, bf16[512,128]{1,0:T(8,128)(2,1)S(1)}, u32[]{:S(2)}, u32[]{:S(2)}) %collective-permute-start.2) | collective-permute-done | bytes 131104 | tf_op jit(solution)/shard_map/ppermute | solution.py:160
  9.7 0.2 collective-permute-done.3.refs_4_
  9.9 0.0 collective-permute-done.refs_1_
  9.9 0.3 %collective-permute-done.1.refs_2_ = bf16[2,64,1024]{2,1,0:T(8,128)(2,1)S(1)} collective-permute-done((bf16[2,64,1024]{2,1,0:T(8,128)(2,1)}, bf16[2,64,1024]{2,1,0:T(8,128)(2,1)S(1)}, u32[]{:S(2)}, u32[]{:S(2)}) %collective-permute-start.1) | collective-permute-done | bytes 262176 | tf_op jit(solution)/shard_map/ppermute | solution.py:160
  10.2 0.0 copy-done
  10.2 0.5 %close.1 = f32[8,4,8,128]{3,2,1,0:T(8,128)S(1)} custom-call(bf16[2,64,1024]{2,1,0:T(8,128)(2,1)S(1)} %copy-done, bf16[2,64,1024]{2,1,0:T(8,128)(2,1)S(1)} %collective-permute-done.refs_1_, bf16[2,64,1024]{2,1,0:T(8,128)(2,1)S(1)} %collective-permute-done.1.refs_2_, bf16[512,128]{1,0:T(8,128)(2,1)S(1)} %collective-permute-done.2.refs_3_, ...), custom_call_target="tpu_custom_call" | custom-call | flops 201326592 | bytes 1048576 | tf_op jit(solution)/shard_map/close/pallas_call | solution.py:142
  10.6 14.1 %all_to_all.5 = f32[32,8,128]{2,1,0:T(8,128)S(1)} all-to-all(f32[32,8,128]{2,1,0:T(8,128)S(1)} %bitcast.2), channel_id=1, replica_groups=mesh['cuts'=8,'stem'=4] {'cuts','stem'}, dimensions={0} | all-to-all | bytes 262144 | tf_op jit(solution)/shard_map/all_to_all | solution.py:167
  24.7 0.6 %reduce_sum.9 = f32[8,128]{1,0:T(8,128)} reduce(f32[32,8,128]{2,1,0:T(8,128)S(1)} %all_to_all.5, f32[]{:T(128)} %constant.0.clone.1), dimensions={0}, to_apply=%region_0.0 | reduce | flops 31744 | bytes 135172 | tf_op jit(solution)/shard_map/reduce_sum | solution.py:168
Async XLA Ops:
  0.0 10.2 %copy-start = (bf16[2,64,1024]{2,1,0:T(8,128)(2,1)S(1)}, bf16[2,64,1024]{2,1,0:T(8,128)(2,1)}, u32[]{:S(2)}) copy-start(bf16[2,64,1024]{2,1,0:T(8,128)(2,1)} %refs_0_.1) | copy-start | bytes 786436
  0.0 9.9 %collective-permute-start = (bf16[2,64,1024]{2,1,0:T(8,128)(2,1)}, bf16[2,64,1024]{2,1,0:T(8,128)(2,1)S(1)}, u32[]{:S(2)}, u32[]{:S(2)}) collective-permute-start(bf16[2,64,1024]{2,1,0:T(8,128)(2,1)} %refs_0_.1), channel_id=1, source_target_pairs={{0,1},{1,0},{2,3},{3,2},{4,5},{5,4},{6,7},{7,6},{8,9},{9,8},{10,11... | collective-permute-start | bytes 786440 | tf_op jit(solution)/shard_map/ppermute | solution.py:160
  0.5 9.7 %collective-permute-start.1 = (bf16[2,64,1024]{2,1,0:T(8,128)(2,1)}, bf16[2,64,1024]{2,1,0:T(8,128)(2,1)S(1)}, u32[]{:S(2)}, u32[]{:S(2)}) collective-permute-start(bf16[2,64,1024]{2,1,0:T(8,128)(2,1)} %refs_0_.1), channel_id=1, source_target_pairs={{0,2},{1,3},{2,0},{3,1},{4,6},{5,7},{6,4},{7,5},{8,10},{9,11},{10,... | collective-permute-start | bytes 786440 | tf_op jit(solution)/shard_map/ppermute | solution.py:160
  8.3 1.4 %collective-permute-start.2 = (bf16[512,128]{1,0:T(8,128)(2,1)S(1)}, bf16[512,128]{1,0:T(8,128)(2,1)S(1)}, u32[]{:S(2)}, u32[]{:S(2)}) collective-permute-start(bf16[512,128]{1,0:T(8,128)(2,1)S(1)} %get-tuple-element.8), channel_id=1, source_target_pairs={{0,1},{1,0},{2,3},{3,2},{4,5},{5,4},{6,7},{7,6},{8,9},{9,8},{10,11... | collective-permute-start | bytes 393224 | tf_op jit(solution)/shard_map/ppermute | solution.py:160
  8.5 1.4 %collective-permute-start.3 = (bf16[512,128]{1,0:T(8,128)(2,1)S(1)}, bf16[512,128]{1,0:T(8,128)(2,1)S(1)}, u32[]{:S(2)}, u32[]{:S(2)}) collective-permute-start(bf16[512,128]{1,0:T(8,128)(2,1)S(1)} %get-tuple-element.9), channel_id=1, source_target_pairs={{0,1},{1,0},{2,3},{3,2},{4,5},{5,4},{6,7},{7,6},{8,9},{9,8},{10,11... | collective-permute-start | bytes 393224 | tf_op jit(solution)/shard_map/ppermute | solution.py:160

commit v10 on v3

v10 whole, which is shorter than its diff:
```python
import functools

import jax
import jax.numpy as jnp
from jax import lax
from jax.experimental import pallas as pl
from jax.experimental.pallas import tpu as pltpu
from jax.sharding import PartitionSpec as P

MIB = 1024 * 1024


def turn(x):
    half = x.shape[-1] // 2
    lane = lax.broadcasted_iota(jnp.int32, x.shape, x.ndim - 1)
    rolled = pltpu.roll(x, half, x.ndim - 1)
    return jnp.where(lane < half, -rolled, rolled)


def branch_kernel(blocks, mid_hbm, right_hbm, kept_ref, *refs):
    *sent_refs, sums_ref, mid_ref, right_ref, wide_ref, mid_sem, right_sem = refs
    width = mid_ref.shape[2]
    inner = right_ref.shape[3]
    groups = right_ref.shape[1] // blocks
    half = groups // 2
    chunks = mid_sem.shape[0]
    chunk = mid_ref.shape[0] // chunks
    steps = chunks * groups
    me = lax.axis_index("stem")

    def mid_copy(n):
        at = pl.ds(n * chunk, chunk)
        return pltpu.make_async_copy(mid_hbm.at[at], mid_ref.at[at], mid_sem.at[n])

    def right_copy(n):
        return pltpu.make_async_copy(right_hbm.at[:, pl.ds(n * chunk, chunk)], right_ref.at[n], right_sem.at[n])

    def widen(step):
        n, q = step // groups, step % groups
        p = jnp.where(q < half, 2 * q + 1, 2 * q - groups)
        slot = step % 2
        for b in range(blocks):
            cols = slice(b * width, (b + 1) * width)
            for j in range(chunk):
                w = right_ref[n, (me ^ p) * blocks + b, j]
                at = j * 2 * inner
                wide_ref[slot, at:at + inner, cols] = w
                wide_ref[slot, at + inner:at + 2 * inner, cols] = turn(w.astype(jnp.float32)).astype(w.dtype)

    for n in range(chunks):
        right_copy(n).start()
        mid_copy(n).start()
    sums_ref[...] = jnp.zeros_like(sums_ref)
    right_copy(0).wait()
    mid_copy(0).wait()
    widen(0)

    def multiply(step):
        n, q = step // groups, step % groups
        left = jnp.concatenate([mid_ref[n * chunk + j] for j in range(chunk)], axis=1)
        return q, jnp.dot(left, wide_ref[step % 2], preferred_element_type=jnp.float32)

    def advance(step, carry):
        @pl.when((step % groups == groups - 1) & (step < steps - 1))
        def _():
            right_copy(step // groups + 1).wait()
            mid_copy(step // groups + 1).wait()

        q, product = multiply(step)
        sums_ref[q] += product
        widen((step + 1) % steps)
        return carry

    lax.fori_loop(0, steps, advance, 0)
    for q in range(half):
        kept_ref[q] = sums_ref[q + half]
        for b in range(blocks):
            sent_refs[q * blocks + b][...] = sums_ref[q, :, b * width:(b + 1) * width].astype(jnp.bfloat16)


def branch_sums(mid, right, groups):
    pairs, depth, width = mid.shape
    total, _, inner, _ = right.shape
    blocks = total // groups
    chunks = 4
    vmem = pl.BlockSpec(memory_space=pltpu.VMEM)
    hbm = pl.BlockSpec(memory_space=pltpu.HBM)
    return pl.pallas_call(
        functools.partial(branch_kernel, blocks),
        in_specs=[hbm, hbm],
        out_specs=[vmem] * (1 + total // 2),
        out_shape=[
            jax.ShapeDtypeStruct((groups // 2, depth, blocks * width), jnp.float32),
        ] + [jax.ShapeDtypeStruct((depth, width), jnp.bfloat16)] * (total // 2),
        scratch_shapes=[
            pltpu.VMEM((groups, depth, blocks * width), jnp.float32),
            pltpu.VMEM(mid.shape, mid.dtype),
            pltpu.VMEM((chunks, total, pairs // chunks, inner, width), right.dtype),
            pltpu.VMEM((2, pairs // chunks * 2 * inner, blocks * width), right.dtype),
            pltpu.SemaphoreType.DMA((chunks,)),
            pltpu.SemaphoreType.DMA((chunks,)),
        ],
        compiler_params=pltpu.CompilerParams(vmem_limit_bytes=52 * MIB),
        cost_estimate=pl.CostEstimate(
            flops=2 * depth * pairs * width * total * width, bytes_accessed=6 * MIB, transcendentals=0
        ),
        name="branch_sums",
    )(mid, right)


def close_kernel(*refs):
    *more, sums_ref, out_ref = refs
    stem_refs, got_refs = more[:sums_ref.shape[0]], more[sums_ref.shape[0]:]
    part = None
    at = 0
    for q, ref in enumerate(stem_refs):
        for b in range(ref.shape[0]):
            block = ref[b]
            half = block.shape[-1] // 2
            rows = jnp.concatenate([block[:, :half], block[:, half:]], axis=0)
            width = got_refs[at].shape[1]
            sums = sums_ref[q, :, b * width:(b + 1) * width] + got_refs[at][...].astype(jnp.float32)
            high = sums.astype(jnp.bfloat16)
            low = (sums - high.astype(jnp.float32)).astype(jnp.bfloat16)
            term = jnp.dot(rows, jnp.concatenate([high, low], axis=1), preferred_element_type=jnp.float32)
            part = term if part is None else part + term
            at += 1
    width = part.shape[1] // 2
    part = part[:, :width] + part[:, width:]
    half = part.shape[0] // 2
    total = part[:half] + turn(part[half:])
    if len(out_ref.shape) == 2:
        out_ref[...] = total
    else:
        cuts, copies, rows, _ = out_ref.shape
        for c in range(cuts):
            for s in range(copies):
                out_ref[c, s] = total[c * rows:(c + 1) * rows]


def close(stems, sums, got, cuts, copies):
    rows, width = stems[0].shape[1], got[0].shape[1]
    whole_tiles = rows % (8 * cuts) == 0
    shape = (cuts, copies, rows // cuts, width) if whole_tiles else (rows, width)
    out = pl.pallas_call(
        close_kernel,
        out_shape=jax.ShapeDtypeStruct(shape, jnp.float32),
        compiler_params=pltpu.CompilerParams(vmem_limit_bytes=24 * MIB),
        cost_estimate=pl.CostEstimate(flops=8 * rows * sums.size, bytes_accessed=MIB, transcendentals=0),
        name="close",
    )(*stems, *got, sums)
    if whole_tiles:
        return out.reshape(cuts * copies, rows // cuts, width)
    out = out.reshape(cuts, 1, -1)
    return jnp.broadcast_to(out, (cuts, copies, out.shape[-1])).reshape(cuts * copies, -1)


def on_device(stem_tensor, mid_tensors, right_tensors):
    stems = lax.axis_size("stem")
    cuts = lax.axis_size("cuts")

    def swap(x, p):
        return lax.ppermute(x, "stem", [(s, s ^ p) for s in range(stems)])

    pieces = [stem_tensor] + [swap(stem_tensor, p) for p in range(2, stems, 2)]
    sums, *sent = branch_sums(mid_tensors, right_tensors, stems)
    got = [swap(x, 1) for x in sent]
    spread = close(pieces, sums, got, cuts, stems)
    parts = lax.all_to_all(spread, ("cuts", "stem"), 0, 0, tiled=True)
    return jnp.sum(parts, axis=0).reshape(-1)


def solution(mesh):
    return jax.shard_map(
        on_device,
        mesh=mesh,
        in_specs=(
            P("stem", None, None),
            P(("cuts", "stem"), None, None),
            P(None, ("cuts", "stem"), None, None),
        ),
        out_specs=P("cuts"),
        check_vma=False,
    )
```

time: 24.8 us -> 25.7 us (1.036)
  Pallas kernels: 5.77 us -> 6.89 us
  blocking collectives: 13.2 us -> 12.9 us
    pallas_call x1, Pallas kernels: 5.34 us -> 6.46 us  [branch_sums(): pl.pallas_call(functools.partial(branch_kernel, blocks), in_specs=[hbm, h...]
  transfers between devices with their start and end apart: 5 -> 5, of which waited for: 4 -> 4; matrix products, arithmetic and copies ran while one was open for 0% -> 0% of each run, Pallas kernels for 22% -> 25%
where the time goes in v10:
time: 25.7 us; the launch traced here: 25.6 us
  blocking collectives  12.9 us (50%)
  Pallas kernels  6.89 us (27%)
  starting transfers between devices  4.04 us (16%)
  waiting for transfers between devices  1.03 us (4%)
  other arithmetic  0.63 us (2%)
    all_to_all x1, blocking collectives, on_device(): parts = lax.all_to_all(spread, ('cuts', 'stem'), 0, 0, tiled=True)  12.9 us
    pallas_call x1, Pallas kernels, branch_sums(): pl.pallas_call(functools.partial(branch_kernel, blocks), in_specs=[hbm, h...  6.46 us
    ppermute x5, starting transfers between devices, swap(): return lax.ppermute(x, 'stem', [(s, s ^ p) for s in range(stems)])  4.04 us
    ppermute x5, waiting for transfers between devices, swap(): return lax.ppermute(x, 'stem', [(s, s ^ p) for s in range(stems)])  1.03 us
    reduce_sum x1, other arithmetic, on_device(): return jnp.sum(parts, axis=0).reshape(-1)  0.63 us
  transfers between devices with their start and end apart: 5, of which 4 were waited for; matrix products, arithmetic and copies ran while one was open for 0% of the time, Pallas kernels for 25%

profile of v10, /device:TPU:0, one launch (start us, length us, event | category | flops | bytes accessed | tf_op | source)
XLA Modules:
  0.0 25.6 jit_solution(6758670708873926604)
XLA Ops:
  0.0 0.0 copy-start
  0.0 3.0 %collective-permute-start = (bf16[2,64,1024]{2,1,0:T(8,128)(2,1)}, bf16[2,64,1024]{2,1,0:T(8,128)(2,1)S(1)}, u32[]{:S(2)}, u32[]{:S(2)}) collective-permute-start(bf16[2,64,1024]{2,1,0:T(8,128)(2,1)} %refs_0_.1), channel_id=1, source_target_pairs={{0,2},{1,3},{2,0},{3,1},{4,6},{5,7},{6,4},{7,5},{8,10},{9,11},{10,... | collective-permute-start | bytes 786440 | tf_op jit(solution)/shard_map/ppermute | solution.py:163
  3.0 6.5 %branch_sums.1 = (f32[2,512,256]{2,1,0:T(8,128)S(1)}, bf16[512,128]{1,0:T(8,128)(2,1)S(1)}, bf16[512,128]{1,0:T(8,128)(2,1)S(1)}, bf16[512,128]{1,0:T(8,128)(2,1)S(1)}, bf16[512,128]{1,0:T(8,128)(2,1)S(1)}) custom-call(bf16[16,512,128]{2,1,0:T(8,128)(2,1)} %mid_hbm.1, bf16[8,16,64,128]{3,2,1,0:T(8,128)(2,1)} %right_hbm.1), custom_call_target="tpu_custom_call" | custom-call | flops 2147483648 | bytes 6291456 | tf_op jit(solution)/shard_map/branch_sums/pallas_call | solution.py:88
  9.4 0.1 collective-permute-start.1
  9.5 0.5 %collective-permute-start.2 = (bf16[512,128]{1,0:T(8,128)(2,1)S(1)}, bf16[512,128]{1,0:T(8,128)(2,1)S(1)}, u32[]{:S(2)}, u32[]{:S(2)}) collective-permute-start(bf16[512,128]{1,0:T(8,128)(2,1)S(1)} %get-tuple-element.11), channel_id=1, source_target_pairs={{0,1},{1,0},{2,3},{3,2},{4,5},{5,4},{6,7},{7,6},{8,9},{9,8},{10,11... | collective-permute-start | bytes 393224 | tf_op jit(solution)/shard_map/ppermute | solution.py:163
  10.0 0.1 collective-permute-start.3
  10.1 0.4 %collective-permute-start.4 = (bf16[512,128]{1,0:T(8,128)(2,1)S(1)}, bf16[512,128]{1,0:T(8,128)(2,1)S(1)}, u32[]{:S(2)}, u32[]{:S(2)}) collective-permute-start(bf16[512,128]{1,0:T(8,128)(2,1)S(1)} %get-tuple-element.13), channel_id=1, source_target_pairs={{0,1},{1,0},{2,3},{3,2},{4,5},{5,4},{6,7},{7,6},{8,9},{9,8},{10,11... | collective-permute-start | bytes 393224 | tf_op jit(solution)/shard_map/ppermute | solution.py:163
  10.5 0.3 %collective-permute-done.1.refs_2_ = bf16[512,128]{1,0:T(8,128)(2,1)S(1)} collective-permute-done((bf16[512,128]{1,0:T(8,128)(2,1)S(1)}, bf16[512,128]{1,0:T(8,128)(2,1)S(1)}, u32[]{:S(2)}, u32[]{:S(2)}) %collective-permute-start.1) | collective-permute-done | bytes 131104 | tf_op jit(solution)/shard_map/ppermute | solution.py:163
  10.9 0.2 collective-permute-done.2.refs_3_
  11.0 0.3 %collective-permute-done.3.refs_4_ = bf16[512,128]{1,0:T(8,128)(2,1)S(1)} collective-permute-done((bf16[512,128]{1,0:T(8,128)(2,1)S(1)}, bf16[512,128]{1,0:T(8,128)(2,1)S(1)}, u32[]{:S(2)}, u32[]{:S(2)}) %collective-permute-start.3) | collective-permute-done | bytes 131104 | tf_op jit(solution)/shard_map/ppermute | solution.py:163
  11.4 0.2 collective-permute-done.4.refs_5_
  11.6 0.0 collective-permute-done.refs_1_
  11.6 0.0 copy-done
  11.6 0.4 %close.1 = f32[8,4,8,128]{3,2,1,0:T(8,128)S(1)} custom-call(bf16[2,64,1024]{2,1,0:T(8,128)(2,1)S(1)} %copy-done, bf16[2,64,1024]{2,1,0:T(8,128)(2,1)S(1)} %collective-permute-done.refs_1_, bf16[512,128]{1,0:T(8,128)(2,1)S(1)} %collective-permute-done.1.refs_2_, bf16[512,128]{1,0:T(8,128)(2,1)S(1)} %collective-permute-done.2.refs_3_, ...), custom_call_target="tpu_custom_call" | custom-call | flops 134217728 | bytes 1048576 | tf_op jit(solution)/shard_map/close/pallas_call | solution.py:145
  12.0 12.9 %all_to_all.5 = f32[32,8,128]{2,1,0:T(8,128)S(1)} all-to-all(f32[32,8,128]{2,1,0:T(8,128)S(1)} %bitcast.2), channel_id=1, replica_groups=mesh['cuts'=8,'stem'=4] {'cuts','stem'}, dimensions={0} | all-to-all | bytes 262144 | tf_op jit(solution)/shard_map/all_to_all | solution.py:169
  24.9 0.6 %reduce_sum.9 = f32[8,128]{1,0:T(8,128)} reduce(f32[32,8,128]{2,1,0:T(8,128)S(1)} %all_to_all.5, f32[]{:T(128)} %constant.0.clone.1), dimensions={0}, to_apply=%region_0.0 | reduce | flops 31744 | bytes 135172 | tf_op jit(solution)/shard_map/reduce_sum | solution.py:170
Async XLA Ops:
  0.0 11.6 %copy-start = (bf16[2,64,1024]{2,1,0:T(8,128)(2,1)S(1)}, bf16[2,64,1024]{2,1,0:T(8,128)(2,1)}, u32[]{:S(2)}) copy-start(bf16[2,64,1024]{2,1,0:T(8,128)(2,1)} %refs_0_.1) | copy-start | bytes 786436
  0.0 11.6 %collective-permute-start = (bf16[2,64,1024]{2,1,0:T(8,128)(2,1)}, bf16[2,64,1024]{2,1,0:T(8,128)(2,1)S(1)}, u32[]{:S(2)}, u32[]{:S(2)}) collective-permute-start(bf16[2,64,1024]{2,1,0:T(8,128)(2,1)} %refs_0_.1), channel_id=1, source_target_pairs={{0,2},{1,3},{2,0},{3,1},{4,6},{5,7},{6,4},{7,5},{8,10},{9,11},{10,... | collective-permute-start | bytes 786440 | tf_op jit(solution)/shard_map/ppermute | solution.py:163
  9.4 1.4 %collective-permute-start.1 = (bf16[512,128]{1,0:T(8,128)(2,1)S(1)}, bf16[512,128]{1,0:T(8,128)(2,1)S(1)}, u32[]{:S(2)}, u32[]{:S(2)}) collective-permute-start(bf16[512,128]{1,0:T(8,128)(2,1)S(1)} %get-tuple-element.10), channel_id=1, source_target_pairs={{0,1},{1,0},{2,3},{3,2},{4,5},{5,4},{6,7},{7,6},{8,9},{9,8},{10,11... | collective-permute-start | bytes 393224 | tf_op jit(solution)/shard_map/ppermute | solution.py:163
  9.5 1.5 %collective-permute-start.2 = (bf16[512,128]{1,0:T(8,128)(2,1)S(1)}, bf16[512,128]{1,0:T(8,128)(2,1)S(1)}, u32[]{:S(2)}, u32[]{:S(2)}) collective-permute-start(bf16[512,128]{1,0:T(8,128)(2,1)S(1)} %get-tuple-element.11), channel_id=1, source_target_pairs={{0,1},{1,0},{2,3},{3,2},{4,5},{5,4},{6,7},{7,6},{8,9},{9,8},{10,11... | collective-permute-start | bytes 393224 | tf_op jit(solution)/shard_map/ppermute | solution.py:163
  10.0 1.3 %collective-permute-start.3 = (bf16[512,128]{1,0:T(8,128)(2,1)S(1)}, bf16[512,128]{1,0:T(8,128)(2,1)S(1)}, u32[]{:S(2)}, u32[]{:S(2)}) collective-permute-start(bf16[512,128]{1,0:T(8,128)(2,1)S(1)} %get-tuple-element.12), channel_id=1, source_target_pairs={{0,1},{1,0},{2,3},{3,2},{4,5},{5,4},{6,7},{7,6},{8,9},{9,8},{10,11... | collective-permute-start | bytes 393224 | tf_op jit(solution)/shard_map/ppermute | solution.py:163
  10.1 1.5 %collective-permute-start.4 = (bf16[512,128]{1,0:T(8,128)(2,1)S(1)}, bf16[512,128]{1,0:T(8,128)(2,1)S(1)}, u32[]{:S(2)}, u32[]{:S(2)}) collective-permute-start(bf16[512,128]{1,0:T(8,128)(2,1)S(1)} %get-tuple-element.13), channel_id=1, source_target_pairs={{0,1},{1,0},{2,3},{3,2},{4,5},{5,4},{6,7},{7,6},{8,9},{9,8},{10,11... | collective-permute-start | bytes 393224 | tf_op jit(solution)/shard_map/ppermute | solution.py:163

commit v11 on v9

--- a/solution.py
+++ b/solution.py
@@ -18,11 +18,11 @@
 
 
 def branch_kernel(blocks, mid_hbm, right_hbm, kept_ref, *refs):
-    *sent_refs, mid_ref, wide_ref, mid_sem, right_sem = refs
+    *sent_refs, sums_ref, mid_ref, wide_ref, mid_sem, right_sem = refs
     pairs, _, width = mid_ref.shape
     total, _, inner, _ = right_hbm.shape
     groups = total // blocks
-    leaving = len(sent_refs) // blocks
+    half = groups // 2
     me = lax.axis_index("stem")
     chunk = pairs // mid_sem.shape[0]
 
@@ -31,8 +31,7 @@
         return pltpu.make_async_copy(mid_hbm.at[at], mid_ref.at[at], mid_sem.at[n])
 
     def right_copy(q):
-        stays = q - leaving
-        p = jnp.where(stays < 0, 2 * q + 3, jnp.where(stays < 2, stays, 2 * stays - 2))
+        p = jnp.where(q < half, 2 * q + 1, 2 * q - groups)
         source = right_hbm.at[pl.ds((me ^ p) * blocks, blocks)]
         target = wide_ref.at[pl.ds(q * blocks, blocks), :, pl.ds(0, inner)]
         return pltpu.make_async_copy(source, target, right_sem.at[q])
@@ -54,42 +53,33 @@
     for n in range(mid_sem.shape[0]):
         mid_copy(n).wait()
 
-    def group(q, carry):
+    def multiply(h, carry):
         left = jnp.concatenate([mid_ref[j] for j in range(pairs)], axis=1)
-        right = [wide_ref[q * blocks + b].reshape(pairs * 2 * inner, width) for b in range(blocks)]
-        sums = jnp.dot(left, jnp.concatenate(right, axis=1), preferred_element_type=jnp.float32)
-        for at in range(leaving):
-            @pl.when(q == at)
-            def _():
-                for b in range(blocks):
-                    part = sums[:, b * width:(b + 1) * width]
-                    sent_refs[at * blocks + b][...] = part.astype(jnp.bfloat16)
-
-        @pl.when(q >= leaving)
-        def _():
-            for b in range(blocks):
-                kept_ref[(q - leaving) * blocks + b] = sums[:, b * width:(b + 1) * width]
-
+        right = [wide_ref[h * (total // 2) + b].reshape(pairs * 2 * inner, width) for b in range(total // 2)]
+        sums_ref[h] = jnp.dot(left, jnp.concatenate(right, axis=1), preferred_element_type=jnp.float32)
         return carry
 
-    lax.fori_loop(0, groups, group, 0)
+    lax.fori_loop(0, 2, multiply, 0)
+    for b, ref in enumerate(sent_refs):
+        cols = slice(b * width, (b + 1) * width)
+        ref[...] = sums_ref[0, :, cols].astype(ref.dtype)
+        kept_ref[b] = sums_ref[1, :, cols]
 
 
 def branch_sums(mid, right, groups):
     pairs, depth, width = mid.shape
     total, _, inner, _ = right.shape
-    blocks = total // groups
-    leaving = (groups // 2 - 1) * blocks
     vmem = pl.BlockSpec(memory_space=pltpu.VMEM)
     hbm = pl.BlockSpec(memory_space=pltpu.HBM)
     return pl.pallas_call(
-        functools.partial(branch_kernel, blocks),
+        functools.partial(branch_kernel, total // groups),
         in_specs=[hbm, hbm],
-        out_specs=[vmem] * (1 + leaving),
+        out_specs=[vmem] * (1 + total // 2),
         out_shape=[
-            jax.ShapeDtypeStruct((total - leaving, depth, width), jnp.float32),
-        ] + [jax.ShapeDtypeStruct((depth, width), jnp.bfloat16)] * leaving,
+            jax.ShapeDtypeStruct((total // 2, depth, width), jnp.float32),
+        ] + [jax.ShapeDtypeStruct((depth, width), jnp.bfloat16)] * (total // 2),
         scratch_shapes=[
+            pltpu.VMEM((2, depth, total // 2 * width), jnp.float32),
             pltpu.VMEM(mid.shape, mid.dtype),
             pltpu.VMEM((total, pairs, 2 * inner, width), right.dtype),
             pltpu.SemaphoreType.DMA((4,)),
@@ -103,10 +93,9 @@
     )(mid, right)
 
 
-def close_kernel(count, *refs):
+def close_kernel(*refs):
     *more, kept_ref, out_ref = refs
-    stem_refs, got_refs = more[:count], more[count:]
-    alone = kept_ref.shape[0] - len(got_refs)
+    stem_refs, got_refs = more[:-kept_ref.shape[0]], more[-kept_ref.shape[0]:]
     part = None
     at = 0
     for ref in stem_refs:
@@ -114,9 +103,7 @@
             block = ref[b]
             half = block.shape[-1] // 2
             rows = jnp.concatenate([block[:, :half], block[:, half:]], axis=0)
-            sums = kept_ref[at]
-            if at >= alone:
-                sums += got_refs[at - alone][...].astype(jnp.float32)
+            sums = kept_ref[at] + got_refs[at][...].astype(jnp.float32)
             high = sums.astype(jnp.bfloat16)
             low = (sums - high.astype(jnp.float32)).astype(jnp.bfloat16)
             term = jnp.dot(rows, jnp.concatenate([high, low], axis=1), preferred_element_type=jnp.float32)
@@ -140,7 +127,7 @@
     whole_tiles = rows % (8 * cuts) == 0
     shape = (cuts, copies, rows // cuts, width) if whole_tiles else (rows, width)
     out = pl.pallas_call(
-        functools.partial(close_kernel, len(stems)),
+        close_kernel,
         out_shape=jax.ShapeDtypeStruct(shape, jnp.float32),
         compiler_params=pltpu.CompilerParams(vmem_limit_bytes=24 * MIB),
         cost_estimate=pl.CostEstimate(flops=8 * rows * kept.size, bytes_accessed=MIB, transcendentals=0),
@@ -159,8 +146,7 @@
     def swap(x, p):
         return lax.ppermute(x, "stem", [(s, s ^ p) for s in range(stems)])
 
-    far = [swap(stem_tensor, p) for p in range(2, stems, 2)]
-    pieces = [stem_tensor, swap(stem_tensor, 1)] + far
+    pieces = [stem_tensor] + [swap(stem_tensor, p) for p in range(2, stems, 2)]
     kept, *sent = branch_sums(mid_tensors, right_tensors, stems)
     got = [swap(x, 1) for x in sent]
     spread = close(pieces, kept, got, cuts, stems)

time: 25.5 us -> 24.8 us (0.973)
  blocking collectives: 14.1 us -> 13.6 us
  starting transfers between devices: 3.61 us -> 4.04 us
  Pallas kernels: 5.71 us -> 5.38 us
  waiting for transfers between devices: 1.3 us -> 1.03 us
    all_to_all x1, blocking collectives: 14.1 us -> 13.6 us  [on_device(): parts = lax.all_to_all(spread, ('cuts', 'stem'), 0, 0, tiled=True)]
    ppermute x4 -> x5, starting transfers between devices: 3.61 us -> 4.04 us  [swap(): return lax.ppermute(x, 'stem', [(s, s ^ p) for s in range(stems)])]
    pallas_call x2, Pallas kernels: 5.71 us -> 5.38 us  [the longest x1 4.95 us: branch_sums(): pl.pallas_call(functools.partial(branch_kernel, total // groups), in_spec...]
    ppermute x4 -> x5, waiting for transfers between devices: 1.3 us -> 1.03 us  [swap(): return lax.ppermute(x, 'stem', [(s, s ^ p) for s in range(stems)])]
  transfers between devices with their start and end apart: 4 -> 5, of which waited for: 3 -> 4; matrix products, arithmetic and copies ran while one was open for 0% -> 0% of each run, Pallas kernels for 21% -> 20%
where the time goes in v11:
time: 24.8 us; the launch traced here: 24.7 us
  blocking collectives  13.6 us (55%)
  Pallas kernels  5.38 us (22%)
  starting transfers between devices  4.04 us (16%)
  waiting for transfers between devices  1.03 us (4%)
  other arithmetic  0.63 us (3%)
    all_to_all x1, blocking collectives, on_device(): parts = lax.all_to_all(spread, ('cuts', 'stem'), 0, 0, tiled=True)  13.6 us
    pallas_call x1, Pallas kernels, branch_sums(): pl.pallas_call(functools.partial(branch_kernel, total // groups), in_spec...  4.95 us
    ppermute x5, starting transfers between devices, swap(): return lax.ppermute(x, 'stem', [(s, s ^ p) for s in range(stems)])  4.04 us
    ppermute x5, waiting for transfers between devices, swap(): return lax.ppermute(x, 'stem', [(s, s ^ p) for s in range(stems)])  1.03 us
    reduce_sum x1, other arithmetic, on_device(): return jnp.sum(parts, axis=0).reshape(-1)  0.63 us
  transfers between devices with their start and end apart: 5, of which 4 were waited for; matrix products, arithmetic and copies ran while one was open for 0% of the time, Pallas kernels for 20%

profile of v11, /device:TPU:0, one launch (start us, length us, event | category | flops | bytes accessed | tf_op | source)
XLA Modules:
  0.0 24.7 jit_solution(8403074627736285991)
XLA Ops:
  0.0 0.0 copy-start
  0.0 3.0 %collective-permute-start = (bf16[2,64,1024]{2,1,0:T(8,128)(2,1)}, bf16[2,64,1024]{2,1,0:T(8,128)(2,1)S(1)}, u32[]{:S(2)}, u32[]{:S(2)}) collective-permute-start(bf16[2,64,1024]{2,1,0:T(8,128)(2,1)} %refs_0_.1), channel_id=1, source_target_pairs={{0,2},{1,3},{2,0},{3,1},{4,6},{5,7},{6,4},{7,5},{8,10},{9,11},{10,... | collective-permute-start | bytes 786440 | tf_op jit(solution)/shard_map/ppermute | solution.py:147
  3.0 4.9 %branch_sums.1 = (f32[4,512,128]{2,1,0:T(8,128)S(1)}, bf16[512,128]{1,0:T(8,128)(2,1)S(1)}, bf16[512,128]{1,0:T(8,128)(2,1)S(1)}, bf16[512,128]{1,0:T(8,128)(2,1)S(1)}, bf16[512,128]{1,0:T(8,128)(2,1)S(1)}) custom-call(bf16[16,512,128]{2,1,0:T(8,128)(2,1)} %mid_hbm.1, bf16[8,16,64,128]{3,2,1,0:T(8,128)(2,1)} %right_hbm.1), custom_call_target="tpu_custom_call" | custom-call | flops 2147483648 | bytes 6291456 | tf_op jit(solution)/shard_map/branch_sums/pallas_call | solution.py:74
  7.9 0.1 collective-permute-start.1
  8.0 0.5 %collective-permute-start.2 = (bf16[512,128]{1,0:T(8,128)(2,1)S(1)}, bf16[512,128]{1,0:T(8,128)(2,1)S(1)}, u32[]{:S(2)}, u32[]{:S(2)}) collective-permute-start(bf16[512,128]{1,0:T(8,128)(2,1)S(1)} %get-tuple-element.11), channel_id=1, source_target_pairs={{0,1},{1,0},{2,3},{3,2},{4,5},{5,4},{6,7},{7,6},{8,9},{9,8},{10,11... | collective-permute-start | bytes 393224 | tf_op jit(solution)/shard_map/ppermute | solution.py:147
  8.5 0.1 collective-permute-start.3
  8.6 0.4 %collective-permute-start.4 = (bf16[512,128]{1,0:T(8,128)(2,1)S(1)}, bf16[512,128]{1,0:T(8,128)(2,1)S(1)}, u32[]{:S(2)}, u32[]{:S(2)}) collective-permute-start(bf16[512,128]{1,0:T(8,128)(2,1)S(1)} %get-tuple-element.13), channel_id=1, source_target_pairs={{0,1},{1,0},{2,3},{3,2},{4,5},{5,4},{6,7},{7,6},{8,9},{9,8},{10,11... | collective-permute-start | bytes 393224 | tf_op jit(solution)/shard_map/ppermute | solution.py:147
  9.0 0.3 %collective-permute-done.1.refs_2_ = bf16[512,128]{1,0:T(8,128)(2,1)S(1)} collective-permute-done((bf16[512,128]{1,0:T(8,128)(2,1)S(1)}, bf16[512,128]{1,0:T(8,128)(2,1)S(1)}, u32[]{:S(2)}, u32[]{:S(2)}) %collective-permute-start.1) | collective-permute-done | bytes 131104 | tf_op jit(solution)/shard_map/ppermute | solution.py:147
  9.3 0.2 collective-permute-done.2.refs_3_
  9.5 0.3 %collective-permute-done.3.refs_4_ = bf16[512,128]{1,0:T(8,128)(2,1)S(1)} collective-permute-done((bf16[512,128]{1,0:T(8,128)(2,1)S(1)}, bf16[512,128]{1,0:T(8,128)(2,1)S(1)}, u32[]{:S(2)}, u32[]{:S(2)}) %collective-permute-start.3) | collective-permute-done | bytes 131104 | tf_op jit(solution)/shard_map/ppermute | solution.py:147
  9.9 0.2 collective-permute-done.4.refs_5_
  10.0 0.0 collective-permute-done.refs_1_
  10.0 0.0 copy-done
  10.0 0.4 %close.1 = f32[8,4,8,128]{3,2,1,0:T(8,128)S(1)} custom-call(bf16[2,64,1024]{2,1,0:T(8,128)(2,1)S(1)} %copy-done, bf16[2,64,1024]{2,1,0:T(8,128)(2,1)S(1)} %collective-permute-done.refs_1_, bf16[512,128]{1,0:T(8,128)(2,1)S(1)} %collective-permute-done.1.refs_2_, bf16[512,128]{1,0:T(8,128)(2,1)S(1)} %collective-permute-done.2.refs_3_, ...), custom_call_target="tpu_custom_call" | custom-call | flops 134217728 | bytes 1048576 | tf_op jit(solution)/shard_map/close/pallas_call | solution.py:129
  10.5 13.6 %all_to_all.5 = f32[32,8,128]{2,1,0:T(8,128)S(1)} all-to-all(f32[32,8,128]{2,1,0:T(8,128)S(1)} %bitcast.2), channel_id=1, replica_groups=mesh['cuts'=8,'stem'=4] {'cuts','stem'}, dimensions={0} | all-to-all | bytes 262144 | tf_op jit(solution)/shard_map/all_to_all | solution.py:153
  24.0 0.6 %reduce_sum.9 = f32[8,128]{1,0:T(8,128)} reduce(f32[32,8,128]{2,1,0:T(8,128)S(1)} %all_to_all.5, f32[]{:T(128)} %constant.0.clone.1), dimensions={0}, to_apply=%region_0.0 | reduce | flops 31744 | bytes 135172 | tf_op jit(solution)/shard_map/reduce_sum | solution.py:154
Async XLA Ops:
  0.0 10.0 %copy-start = (bf16[2,64,1024]{2,1,0:T(8,128)(2,1)S(1)}, bf16[2,64,1024]{2,1,0:T(8,128)(2,1)}, u32[]{:S(2)}) copy-start(bf16[2,64,1024]{2,1,0:T(8,128)(2,1)} %refs_0_.1) | copy-start | bytes 786436
  0.0 10.0 %collective-permute-start = (bf16[2,64,1024]{2,1,0:T(8,128)(2,1)}, bf16[2,64,1024]{2,1,0:T(8,128)(2,1)S(1)}, u32[]{:S(2)}, u32[]{:S(2)}) collective-permute-start(bf16[2,64,1024]{2,1,0:T(8,128)(2,1)} %refs_0_.1), channel_id=1, source_target_pairs={{0,2},{1,3},{2,0},{3,1},{4,6},{5,7},{6,4},{7,5},{8,10},{9,11},{10,... | collective-permute-start | bytes 786440 | tf_op jit(solution)/shard_map/ppermute | solution.py:147
  7.9 1.4 %collective-permute-start.1 = (bf16[512,128]{1,0:T(8,128)(2,1)S(1)}, bf16[512,128]{1,0:T(8,128)(2,1)S(1)}, u32[]{:S(2)}, u32[]{:S(2)}) collective-permute-start(bf16[512,128]{1,0:T(8,128)(2,1)S(1)} %get-tuple-element.10), channel_id=1, source_target_pairs={{0,1},{1,0},{2,3},{3,2},{4,5},{5,4},{6,7},{7,6},{8,9},{9,8},{10,11... | collective-permute-start | bytes 393224 | tf_op jit(solution)/shard_map/ppermute | solution.py:147
  8.0 1.5 %collective-permute-start.2 = (bf16[512,128]{1,0:T(8,128)(2,1)S(1)}, bf16[512,128]{1,0:T(8,128)(2,1)S(1)}, u32[]{:S(2)}, u32[]{:S(2)}) collective-permute-start(bf16[512,128]{1,0:T(8,128)(2,1)S(1)} %get-tuple-element.11), channel_id=1, source_target_pairs={{0,1},{1,0},{2,3},{3,2},{4,5},{5,4},{6,7},{7,6},{8,9},{9,8},{10,11... | collective-permute-start | bytes 393224 | tf_op jit(solution)/shard_map/ppermute | solution.py:147
  8.5 1.3 %collective-permute-start.3 = (bf16[512,128]{1,0:T(8,128)(2,1)S(1)}, bf16[512,128]{1,0:T(8,128)(2,1)S(1)}, u32[]{:S(2)}, u32[]{:S(2)}) collective-permute-start(bf16[512,128]{1,0:T(8,128)(2,1)S(1)} %get-tuple-element.12), channel_id=1, source_target_pairs={{0,1},{1,0},{2,3},{3,2},{4,5},{5,4},{6,7},{7,6},{8,9},{9,8},{10,11... | collective-permute-start | bytes 393224 | tf_op jit(solution)/shard_map/ppermute | solution.py:147
  8.6 1.5 %collective-permute-start.4 = (bf16[512,128]{1,0:T(8,128)(2,1)S(1)}, bf16[512,128]{1,0:T(8,128)(2,1)S(1)}, u32[]{:S(2)}, u32[]{:S(2)}) collective-permute-start(bf16[512,128]{1,0:T(8,128)(2,1)S(1)} %get-tuple-element.13), channel_id=1, source_target_pairs={{0,1},{1,0},{2,3},{3,2},{4,5},{5,4},{6,7},{7,6},{8,9},{9,8},{10,11... | collective-permute-start | bytes 393224 | tf_op jit(solution)/shard_map/ppermute | solution.py:147

commit v12 on v11

--- a/solution.py
+++ b/solution.py
@@ -112,31 +112,51 @@
     width = part.shape[1] // 2
     part = part[:, :width] + part[:, width:]
     half = part.shape[0] // 2
-    total = part[:half] + turn(part[half:])
-    if len(out_ref.shape) == 2:
-        out_ref[...] = total
-    else:
-        cuts, copies, rows, _ = out_ref.shape
-        for c in range(cuts):
-            for s in range(copies):
-                out_ref[c, s] = total[c * rows:(c + 1) * rows]
-
-
-def close(stems, kept, got, cuts, copies):
+    out_ref[...] = part[:half] + turn(part[half:])
+
+
+def close(stems, kept, got):
     rows, width = stems[0].shape[1], kept.shape[2]
-    whole_tiles = rows % (8 * cuts) == 0
-    shape = (cuts, copies, rows // cuts, width) if whole_tiles else (rows, width)
-    out = pl.pallas_call(
+    return pl.pallas_call(
         close_kernel,
-        out_shape=jax.ShapeDtypeStruct(shape, jnp.float32),
+        out_shape=jax.ShapeDtypeStruct((rows, width), jnp.float32),
         compiler_params=pltpu.CompilerParams(vmem_limit_bytes=24 * MIB),
         cost_estimate=pl.CostEstimate(flops=8 * rows * kept.size, bytes_accessed=MIB, transcendentals=0),
         name="close",
     )(*stems, *got, kept)
-    if whole_tiles:
-        return out.reshape(cuts * copies, rows // cuts, width)
-    out = out.reshape(cuts, 1, -1)
-    return jnp.broadcast_to(out, (cuts, copies, out.shape[-1])).reshape(cuts * copies, -1)
+
+
+def deal(one, other, sections, places):
+    rows, width = one.shape
+    size = rows // sections
+    count = len(places)
+
+    def kernel(one_ref, other_ref, *out_refs):
+        for place, out_ref in zip(places, out_refs):
+            at = pl.ds(pl.multiple_of(place() * size, size), size)
+            out_ref[...] = one_ref[at] + other_ref[at]
+
+    return pl.pallas_call(
+        kernel,
+        out_shape=[jax.ShapeDtypeStruct((size, width), jnp.float32)] * count,
+        compiler_params=pltpu.CompilerParams(vmem_limit_bytes=24 * MIB),
+        cost_estimate=pl.CostEstimate(flops=2 * rows * width, bytes_accessed=8 * rows * width, transcendentals=0),
+        name="deal",
+    )(one, other)
+
+
+def half_line(own, near, far):
+    def kernel(own_ref, near_ref, far_ref, out_ref):
+        odd = lax.axis_index("stem") % 2 == 1
+        out_ref[...] = jnp.where(odd, own_ref[...], near_ref[...]) + far_ref[...]
+
+    return pl.pallas_call(
+        kernel,
+        out_shape=jax.ShapeDtypeStruct(own.shape, own.dtype),
+        compiler_params=pltpu.CompilerParams(vmem_limit_bytes=24 * MIB),
+        cost_estimate=pl.CostEstimate(flops=2 * own.size, bytes_accessed=16 * own.size, transcendentals=0),
+        name="half_line",
+    )(own, near, far)
 
 
 def on_device(stem_tensor, mid_tensors, right_tensors):
@@ -149,9 +169,37 @@
     pieces = [stem_tensor] + [swap(stem_tensor, p) for p in range(2, stems, 2)]
     kept, *sent = branch_sums(mid_tensors, right_tensors, stems)
     got = [swap(x, 1) for x in sent]
-    spread = close(pieces, kept, got, cuts, stems)
-    parts = lax.all_to_all(spread, ("cuts", "stem"), 0, 0, tiled=True)
-    return jnp.sum(parts, axis=0).reshape(-1)
+    partial_sum = close(pieces, kept, got)
+    rows = partial_sum.shape[0]
+    if cuts != 8 or stems != 4 or rows % 64:
+        parts = partial_sum.reshape(cuts, 1, -1)
+        parts = jnp.broadcast_to(parts, (cuts, stems, parts.shape[-1])).reshape(cuts * stems, -1)
+        return jnp.sum(lax.all_to_all(parts, ("cuts", "stem"), 0, 0, tiled=True), axis=0)
+
+    def send(x, mask):
+        pairs = []
+        for i in range(cuts):
+            for j in range(stems):
+                c, s = mask(j % 2)
+                pairs.append((i * stems + j, (i ^ c) * stems + (j ^ s)))
+        return lax.ppermute(x, ("cuts", "stem"), pairs)
+
+    def plane():
+        return lax.axis_index("cuts") // 2
+
+    def column():
+        return lax.axis_index("cuts") % 2
+
+    chip = send(partial_sum, lambda core: (0, 1))
+    own, near, far = deal(
+        partial_sum, chip, 4, (plane, lambda: plane() ^ 1, lambda: plane() ^ (2 + lax.axis_index("stem") % 2))
+    )
+    near = send(near, lambda core: (2, 1))
+    far = send(far, lambda core: (2 * (2 + core), 0))
+    line = half_line(own, near, far)
+    own, away = deal(line, send(line, lambda core: (0, 1)), 2, (column, lambda: column() ^ 1))
+    total = own + send(away, lambda core: (1, 1)) + send(away, lambda core: (1, 3)) + send(own, lambda core: (0, 3))
+    return total.reshape(-1)
 
 
 def solution(mesh):

time: 24.8 us -> 25.4 us (1.024)
  blocking collectives: 13.6 us -> 0 us
  starting transfers between devices: 4.04 us -> 11.5 us
  waiting for transfers between devices: 1.03 us -> 7.76 us
    all_to_all x1 -> x0, blocking collectives: 13.6 us -> none  [on_device(): parts = lax.all_to_all(spread, ('cuts', 'stem'), 0, 0, tiled=True)]
    ppermute x0 -> x7, starting transfers between devices: none -> 7.46 us  [send(): return lax.ppermute(x, ('cuts', 'stem'), pairs)]
    ppermute x0 -> x7, waiting for transfers between devices: none -> 6.73 us  [send(): return lax.ppermute(x, ('cuts', 'stem'), pairs)]
    reduce_sum x1 -> x0, other arithmetic: 0.63 us -> none  [on_device(): return jnp.sum(parts, axis=0).reshape(-1)]
    reshape x0 -> x1, other arithmetic: none -> 0.6 us  [on_device(): return total.reshape(-1)]
  transfers between devices with their start and end apart: 5 -> 12, of which waited for: 4 -> 10; matrix products, arithmetic and copies ran while one was open for 0% -> 0% of each run, Pallas kernels for 20% -> 20%
where the time goes in v12:
time: 25.4 us; the launch traced here: 25.3 us
  starting transfers between devices  11.5 us (45%)
  waiting for transfers between devices  7.76 us (31%)
  Pallas kernels  5.39 us (21%)
  other arithmetic  0.6 us (2%)
    ppermute x7, starting transfers between devices, send(): return lax.ppermute(x, ('cuts', 'stem'), pairs)  7.46 us
    ppermute x7, waiting for transfers between devices, send(): return lax.ppermute(x, ('cuts', 'stem'), pairs)  6.73 us
    pallas_call x1, Pallas kernels, branch_sums(): pl.pallas_call(functools.partial(branch_kernel, total // groups), in_spec...  4.95 us
    ppermute x5, starting transfers between devices, swap(): return lax.ppermute(x, 'stem', [(s, s ^ p) for s in range(stems)])  4.04 us
    ppermute x5, waiting for transfers between devices, swap(): return lax.ppermute(x, 'stem', [(s, s ^ p) for s in range(stems)])  1.03 us
    reshape x1, other arithmetic, on_device(): return total.reshape(-1)  0.6 us
  transfers between devices with their start and end apart: 12, of which 10 were waited for; matrix products, arithmetic and copies ran while one was open for 0% of the time, Pallas kernels for 20%

profile of v12, /device:TPU:0, one launch (start us, length us, event | category | flops | bytes accessed | tf_op | source)
XLA Modules:
  0.0 25.3 jit_solution(15206653346438176170)
XLA Ops:
  0.0 0.0 copy-start
  0.0 3.0 %collective-permute-start = (bf16[2,64,1024]{2,1,0:T(8,128)(2,1)}, bf16[2,64,1024]{2,1,0:T(8,128)(2,1)S(1)}, u32[]{:S(2)}, u32[]{:S(2)}) collective-permute-start(bf16[2,64,1024]{2,1,0:T(8,128)(2,1)} %refs_0_.1), channel_id=1, source_target_pairs={{0,2},{1,3},{2,0},{3,1},{4,6},{5,7},{6,4},{7,5},{8,10},{9,11},{10,... | collective-permute-start | bytes 786440 | tf_op jit(solution)/shard_map/ppermute | solution.py:167
  3.0 4.9 %branch_sums.1 = (f32[4,512,128]{2,1,0:T(8,128)S(1)}, bf16[512,128]{1,0:T(8,128)(2,1)S(1)}, bf16[512,128]{1,0:T(8,128)(2,1)S(1)}, bf16[512,128]{1,0:T(8,128)(2,1)S(1)}, bf16[512,128]{1,0:T(8,128)(2,1)S(1)}) custom-call(bf16[16,512,128]{2,1,0:T(8,128)(2,1)} %mid_hbm.1, bf16[8,16,64,128]{3,2,1,0:T(8,128)(2,1)} %right_hbm.1), custom_call_target="tpu_custom_call" | custom-call | flops 2147483648 | bytes 6291456 | tf_op jit(solution)/shard_map/branch_sums/pallas_call | solution.py:74
  7.9 0.1 collective-permute-start.1
  8.0 0.5 %collective-permute-start.2 = (bf16[512,128]{1,0:T(8,128)(2,1)S(1)}, bf16[512,128]{1,0:T(8,128)(2,1)S(1)}, u32[]{:S(2)}, u32[]{:S(2)}) collective-permute-start(bf16[512,128]{1,0:T(8,128)(2,1)S(1)} %get-tuple-element.16), channel_id=1, source_target_pairs={{0,1},{1,0},{2,3},{3,2},{4,5},{5,4},{6,7},{7,6},{8,9},{9,8},{10,11... | collective-permute-start | bytes 393224 | tf_op jit(solution)/shard_map/ppermute | solution.py:167
  8.5 0.1 collective-permute-start.3
  8.6 0.4 %collective-permute-start.4 = (bf16[512,128]{1,0:T(8,128)(2,1)S(1)}, bf16[512,128]{1,0:T(8,128)(2,1)S(1)}, u32[]{:S(2)}, u32[]{:S(2)}) collective-permute-start(bf16[512,128]{1,0:T(8,128)(2,1)S(1)} %get-tuple-element.18), channel_id=1, source_target_pairs={{0,1},{1,0},{2,3},{3,2},{4,5},{5,4},{6,7},{7,6},{8,9},{9,8},{10,11... | collective-permute-start | bytes 393224 | tf_op jit(solution)/shard_map/ppermute | solution.py:167
  9.0 0.3 %collective-permute-done.1.refs_2_ = bf16[512,128]{1,0:T(8,128)(2,1)S(1)} collective-permute-done((bf16[512,128]{1,0:T(8,128)(2,1)S(1)}, bf16[512,128]{1,0:T(8,128)(2,1)S(1)}, u32[]{:S(2)}, u32[]{:S(2)}) %collective-permute-start.1) | collective-permute-done | bytes 131104 | tf_op jit(solution)/shard_map/ppermute | solution.py:167
  9.3 0.2 collective-permute-done.2.refs_3_
  9.5 0.3 %collective-permute-done.3.refs_4_ = bf16[512,128]{1,0:T(8,128)(2,1)S(1)} collective-permute-done((bf16[512,128]{1,0:T(8,128)(2,1)S(1)}, bf16[512,128]{1,0:T(8,128)(2,1)S(1)}, u32[]{:S(2)}, u32[]{:S(2)}) %collective-permute-start.3) | collective-permute-done | bytes 131104 | tf_op jit(solution)/shard_map/ppermute | solution.py:167
  9.9 0.2 collective-permute-done.4.refs_5_
  10.0 0.0 collective-permute-done.refs_1_
  10.0 0.0 copy-done
  10.0 0.4 %close.1.one_ref = f32[64,128]{1,0:T(8,128)S(1)} custom-call(bf16[2,64,1024]{2,1,0:T(8,128)(2,1)S(1)} %copy-done, bf16[2,64,1024]{2,1,0:T(8,128)(2,1)S(1)} %collective-permute-done.refs_1_, bf16[512,128]{1,0:T(8,128)(2,1)S(1)} %collective-permute-done.1.refs_2_, bf16[512,128]{1,0:T(8,128)(2,1)S(1)} %collective-permute-done.2.refs_3_, ...), custom_call_target="tpu_custom_call" | custom-call | flops 134217728 | bytes 1048576 | tf_op jit(solution)/shard_map/close/pallas_call | solution.py:120
  10.5 0.4 %collective-permute-start.5 = (f32[64,128]{1,0:T(8,128)S(1)}, f32[64,128]{1,0:T(8,128)S(1)}, u32[]{:S(2)}, u32[]{:S(2)}) collective-permute-start(f32[64,128]{1,0:T(8,128)S(1)} %close.1.one_ref), channel_id=1, source_target_pairs={{0,1},{1,0},{2,3},{3,2},{4,5},{5,4},{6,7},{7,6},{8,9},{9,8},{10,11... | collective-permute-start | bytes 98312 | tf_op jit(solution)/shard_map/ppermute | solution.py:185
  10.9 0.9 %collective-permute-done.5.other_ref = f32[64,128]{1,0:T(8,128)S(1)} collective-permute-done((f32[64,128]{1,0:T(8,128)S(1)}, f32[64,128]{1,0:T(8,128)S(1)}, u32[]{:S(2)}, u32[]{:S(2)}) %collective-permute-start.5) | collective-permute-done | bytes 32800 | tf_op jit(solution)/shard_map/ppermute | solution.py:185
  11.8 1.5 %collective-permute-start.6 = (f32[16,128]{1,0:T(8,128)S(1)}, f32[16,128]{1,0:T(8,128)S(1)}, u32[]{:S(2)}, u32[]{:S(2)}) collective-permute-start(f32[16,128]{1,0:T(8,128)S(1)} %get-tuple-element.21), channel_id=1, source_target_pairs={{0,9},{1,8},{2,11},{3,10},{4,13},{5,12},{6,15},{7,14},{8,1},{9,0},... | collective-permute-start | bytes 24584 | tf_op jit(solution)/shard_map/ppermute | solution.py:185
  13.3 2.6 %collective-permute-start.7 = (f32[16,128]{1,0:T(8,128)S(1)}, f32[16,128]{1,0:T(8,128)S(1)}, u32[]{:S(2)}, u32[]{:S(2)}) collective-permute-start(f32[16,128]{1,0:T(8,128)S(1)} %get-tuple-element.22), channel_id=1, source_target_pairs={{0,16},{1,25},{2,18},{3,27},{4,20},{5,29},{6,22},{7,31},{8,24},{9,... | collective-permute-start | bytes 24584 | tf_op jit(solution)/shard_map/ppermute | solution.py:185
  15.9 0.0 collective-permute-done.6.near_ref
  15.9 2.0 %collective-permute-done.7.far_ref = f32[16,128]{1,0:T(8,128)S(1)} collective-permute-done((f32[16,128]{1,0:T(8,128)S(1)}, f32[16,128]{1,0:T(8,128)S(1)}, u32[]{:S(2)}, u32[]{:S(2)}) %collective-permute-start.7) | collective-permute-done | bytes 8224 | tf_op jit(solution)/shard_map/ppermute | solution.py:185
  17.8 0.0 collective-permute-start.8
  17.8 1.2 %collective-permute-done.8.other_ref = f32[16,128]{1,0:T(8,128)S(1)} collective-permute-done((f32[16,128]{1,0:T(8,128)S(1)}, f32[16,128]{1,0:T(8,128)S(1)}, u32[]{:S(2)}, u32[]{:S(2)}) %collective-permute-start.8) | collective-permute-done | bytes 8224 | tf_op jit(solution)/shard_map/ppermute | solution.py:185
  19.0 1.7 %collective-permute-start.10 = (f32[8,128]{1,0:T(8,128)S(1)}, f32[8,128]{1,0:T(8,128)S(1)}, u32[]{:S(2)}, u32[]{:S(2)}) collective-permute-start(f32[8,128]{1,0:T(8,128)S(1)} %get-tuple-element.24), channel_id=1, source_target_pairs={{0,7},{1,6},{2,5},{3,4},{4,3},{5,2},{6,1},{7,0},{8,15},{9,14},{10,... | collective-permute-start | bytes 12296 | tf_op jit(solution)/shard_map/ppermute | solution.py:185
  20.7 0.9 %collective-permute-start.11 = (f32[8,128]{1,0:T(8,128)S(1)}, f32[8,128]{1,0:T(8,128)S(1)}, u32[]{:S(2)}, u32[]{:S(2)}) collective-permute-start(f32[8,128]{1,0:T(8,128)S(1)} %get-tuple-element.23), channel_id=1, source_target_pairs={{0,3},{1,2},{2,1},{3,0},{4,7},{5,6},{6,5},{7,4},{8,11},{9,10},{10,... | collective-permute-start | bytes 12296 | tf_op jit(solution)/shard_map/ppermute | solution.py:185
  21.7 0.3 %collective-permute-start.9 = (f32[8,128]{1,0:T(8,128)S(1)}, f32[8,128]{1,0:T(8,128)S(1)}, u32[]{:S(2)}, u32[]{:S(2)}) collective-permute-start(f32[8,128]{1,0:T(8,128)S(1)} %get-tuple-element.24), channel_id=1, source_target_pairs={{0,5},{1,4},{2,7},{3,6},{4,1},{5,0},{6,3},{7,2},{8,13},{9,12},{10,... | collective-permute-start | bytes 12296 | tf_op jit(solution)/shard_map/ppermute | solution.py:185
  22.0 1.0 %collective-permute-done.10 = f32[8,128]{1,0:T(8,128)S(1)} collective-permute-done((f32[8,128]{1,0:T(8,128)S(1)}, f32[8,128]{1,0:T(8,128)S(1)}, u32[]{:S(2)}, u32[]{:S(2)}) %collective-permute-start.10) | collective-permute-done | bytes 4128 | tf_op jit(solution)/shard_map/ppermute | solution.py:185
  22.9 0.8 %collective-permute-done.11 = f32[8,128]{1,0:T(8,128)S(1)} collective-permute-done((f32[8,128]{1,0:T(8,128)S(1)}, f32[8,128]{1,0:T(8,128)S(1)}, u32[]{:S(2)}, u32[]{:S(2)}) %collective-permute-start.11) | collective-permute-done | bytes 4128 | tf_op jit(solution)/shard_map/ppermute | solution.py:185
  23.8 0.9 %collective-permute-done.9 = f32[8,128]{1,0:T(8,128)S(1)} collective-permute-done((f32[8,128]{1,0:T(8,128)S(1)}, f32[8,128]{1,0:T(8,128)S(1)}, u32[]{:S(2)}, u32[]{:S(2)}) %collective-permute-start.9) | collective-permute-done | bytes 4128 | tf_op jit(solution)/shard_map/ppermute | solution.py:185
  24.7 0.6 %add_bitcast_fusion = f32[1024]{0:T(1024)} fusion(f32[8,128]{1,0:T(8,128)S(1)} %collective-permute-done.11, f32[8,128]{1,0:T(8,128)S(1)} %collective-permute-done.10, f32[8,128]{1,0:T(8,128)S(1)} %get-tuple-element.23, f32[8,128]{1,0:T(8,128)S(1)} %collective-permute-done.9), kind=kLoop, calls=%fused_computation | loop fusion | flops 3072 | bytes 20480 | tf_op jit(solution)/shard_map/reshape | solution.py:202
  (3 shorter events, 0.0 us)
Async XLA Ops:
  0.0 10.0 %copy-start = (bf16[2,64,1024]{2,1,0:T(8,128)(2,1)S(1)}, bf16[2,64,1024]{2,1,0:T(8,128)(2,1)}, u32[]{:S(2)}) copy-start(bf16[2,64,1024]{2,1,0:T(8,128)(2,1)} %refs_0_.1) | copy-start | bytes 786436
  0.0 10.0 %collective-permute-start = (bf16[2,64,1024]{2,1,0:T(8,128)(2,1)}, bf16[2,64,1024]{2,1,0:T(8,128)(2,1)S(1)}, u32[]{:S(2)}, u32[]{:S(2)}) collective-permute-start(bf16[2,64,1024]{2,1,0:T(8,128)(2,1)} %refs_0_.1), channel_id=1, source_target_pairs={{0,2},{1,3},{2,0},{3,1},{4,6},{5,7},{6,4},{7,5},{8,10},{9,11},{10,... | collective-permute-start | bytes 786440 | tf_op jit(solution)/shard_map/ppermute | solution.py:167
  7.9 1.4 %collective-permute-start.1 = (bf16[512,128]{1,0:T(8,128)(2,1)S(1)}, bf16[512,128]{1,0:T(8,128)(2,1)S(1)}, u32[]{:S(2)}, u32[]{:S(2)}) collective-permute-start(bf16[512,128]{1,0:T(8,128)(2,1)S(1)} %get-tuple-element.15), channel_id=1, source_target_pairs={{0,1},{1,0},{2,3},{3,2},{4,5},{5,4},{6,7},{7,6},{8,9},{9,8},{10,11... | collective-permute-start | bytes 393224 | tf_op jit(solution)/shard_map/ppermute | solution.py:167
  8.0 1.5 %collective-permute-start.2 = (bf16[512,128]{1,0:T(8,128)(2,1)S(1)}, bf16[512,128]{1,0:T(8,128)(2,1)S(1)}, u32[]{:S(2)}, u32[]{:S(2)}) collective-permute-start(bf16[512,128]{1,0:T(8,128)(2,1)S(1)} %get-tuple-element.16), channel_id=1, source_target_pairs={{0,1},{1,0},{2,3},{3,2},{4,5},{5,4},{6,7},{7,6},{8,9},{9,8},{10,11... | collective-permute-start | bytes 393224 | tf_op jit(solution)/shard_map/ppermute | solution.py:167
  8.5 1.3 %collective-permute-start.3 = (bf16[512,128]{1,0:T(8,128)(2,1)S(1)}, bf16[512,128]{1,0:T(8,128)(2,1)S(1)}, u32[]{:S(2)}, u32[]{:S(2)}) collective-permute-start(bf16[512,128]{1,0:T(8,128)(2,1)S(1)} %get-tuple-element.17), channel_id=1, source_target_pairs={{0,1},{1,0},{2,3},{3,2},{4,5},{5,4},{6,7},{7,6},{8,9},{9,8},{10,11... | collective-permute-start | bytes 393224 | tf_op jit(solution)/shard_map/ppermute | solution.py:167
  8.6 1.5 %collective-permute-start.4 = (bf16[512,128]{1,0:T(8,128)(2,1)S(1)}, bf16[512,128]{1,0:T(8,128)(2,1)S(1)}, u32[]{:S(2)}, u32[]{:S(2)}) collective-permute-start(bf16[512,128]{1,0:T(8,128)(2,1)S(1)} %get-tuple-element.18), channel_id=1, source_target_pairs={{0,1},{1,0},{2,3},{3,2},{4,5},{5,4},{6,7},{7,6},{8,9},{9,8},{10,11... | collective-permute-start | bytes 393224 | tf_op jit(solution)/shard_map/ppermute | solution.py:167
  10.5 1.3 %collective-permute-start.5 = (f32[64,128]{1,0:T(8,128)S(1)}, f32[64,128]{1,0:T(8,128)S(1)}, u32[]{:S(2)}, u32[]{:S(2)}) collective-permute-start(f32[64,128]{1,0:T(8,128)S(1)} %close.1.one_ref), channel_id=1, source_target_pairs={{0,1},{1,0},{2,3},{3,2},{4,5},{5,4},{6,7},{7,6},{8,9},{9,8},{10,11... | collective-permute-start | bytes 98312 | tf_op jit(solution)/shard_map/ppermute | solution.py:185
  11.8 4.1 %collective-permute-start.6 = (f32[16,128]{1,0:T(8,128)S(1)}, f32[16,128]{1,0:T(8,128)S(1)}, u32[]{:S(2)}, u32[]{:S(2)}) collective-permute-start(f32[16,128]{1,0:T(8,128)S(1)} %get-tuple-element.21), channel_id=1, source_target_pairs={{0,9},{1,8},{2,11},{3,10},{4,13},{5,12},{6,15},{7,14},{8,1},{9,0},... | collective-permute-start | bytes 24584 | tf_op jit(solution)/shard_map/ppermute | solution.py:185
  13.3 4.5 %collective-permute-start.7 = (f32[16,128]{1,0:T(8,128)S(1)}, f32[16,128]{1,0:T(8,128)S(1)}, u32[]{:S(2)}, u32[]{:S(2)}) collective-permute-start(f32[16,128]{1,0:T(8,128)S(1)} %get-tuple-element.22), channel_id=1, source_target_pairs={{0,16},{1,25},{2,18},{3,27},{4,20},{5,29},{6,22},{7,31},{8,24},{9,... | collective-permute-start | bytes 24584 | tf_op jit(solution)/shard_map/ppermute | solution.py:185
  17.8 1.2 %collective-permute-start.8 = (f32[16,128]{1,0:T(8,128)S(1)}, f32[16,128]{1,0:T(8,128)S(1)}, u32[]{:S(2)}, u32[]{:S(2)}) collective-permute-start(f32[16,128]{1,0:T(8,128)S(1)} %half_line.1.one_ref), channel_id=1, source_target_pairs={{0,1},{1,0},{2,3},{3,2},{4,5},{5,4},{6,7},{7,6},{8,9},{9,8},{10,11... | collective-permute-start | bytes 24584 | tf_op jit(solution)/shard_map/ppermute | solution.py:185
  19.0 3.9 %collective-permute-start.10 = (f32[8,128]{1,0:T(8,128)S(1)}, f32[8,128]{1,0:T(8,128)S(1)}, u32[]{:S(2)}, u32[]{:S(2)}) collective-permute-start(f32[8,128]{1,0:T(8,128)S(1)} %get-tuple-element.24), channel_id=1, source_target_pairs={{0,7},{1,6},{2,5},{3,4},{4,3},{5,2},{6,1},{7,0},{8,15},{9,14},{10,... | collective-permute-start | bytes 12296 | tf_op jit(solution)/shard_map/ppermute | solution.py:185
  20.7 3.0 %collective-permute-start.11 = (f32[8,128]{1,0:T(8,128)S(1)}, f32[8,128]{1,0:T(8,128)S(1)}, u32[]{:S(2)}, u32[]{:S(2)}) collective-permute-start(f32[8,128]{1,0:T(8,128)S(1)} %get-tuple-element.23), channel_id=1, source_target_pairs={{0,3},{1,2},{2,1},{3,0},{4,7},{5,6},{6,5},{7,4},{8,11},{9,10},{10,... | collective-permute-start | bytes 12296 | tf_op jit(solution)/shard_map/ppermute | solution.py:185
  21.7 3.0 %collective-permute-start.9 = (f32[8,128]{1,0:T(8,128)S(1)}, f32[8,128]{1,0:T(8,128)S(1)}, u32[]{:S(2)}, u32[]{:S(2)}) collective-permute-start(f32[8,128]{1,0:T(8,128)S(1)} %get-tuple-element.24), channel_id=1, source_target_pairs={{0,5},{1,4},{2,7},{3,6},{4,1},{5,0},{6,3},{7,2},{8,13},{9,12},{10,... | collective-permute-start | bytes 12296 | tf_op jit(solution)/shard_map/ppermute | solution.py:185

commit v13 on v11

--- a/solution.py
+++ b/solution.py
@@ -116,16 +116,16 @@
     if len(out_ref.shape) == 2:
         out_ref[...] = total
     else:
-        cuts, copies, rows, _ = out_ref.shape
+        copies, cuts, rows, _ = out_ref.shape
         for c in range(cuts):
             for s in range(copies):
-                out_ref[c, s] = total[c * rows:(c + 1) * rows]
+                out_ref[s, c] = total[c * rows:(c + 1) * rows]
 
 
 def close(stems, kept, got, cuts, copies):
     rows, width = stems[0].shape[1], kept.shape[2]
     whole_tiles = rows % (8 * cuts) == 0
-    shape = (cuts, copies, rows // cuts, width) if whole_tiles else (rows, width)
+    shape = (copies, cuts, rows // cuts, width) if whole_tiles else (rows, width)
     out = pl.pallas_call(
         close_kernel,
         out_shape=jax.ShapeDtypeStruct(shape, jnp.float32),
@@ -135,8 +135,8 @@
     )(*stems, *got, kept)
     if whole_tiles:
         return out.reshape(cuts * copies, rows // cuts, width)
-    out = out.reshape(cuts, 1, -1)
-    return jnp.broadcast_to(out, (cuts, copies, out.shape[-1])).reshape(cuts * copies, -1)
+    out = out.reshape(1, cuts, -1)
+    return jnp.broadcast_to(out, (copies, cuts, out.shape[-1])).reshape(cuts * copies, -1)
 
 
 def on_device(stem_tensor, mid_tensors, right_tensors):
@@ -150,7 +150,7 @@
     kept, *sent = branch_sums(mid_tensors, right_tensors, stems)
     got = [swap(x, 1) for x in sent]
     spread = close(pieces, kept, got, cuts, stems)
-    parts = lax.all_to_all(spread, ("cuts", "stem"), 0, 0, tiled=True)
+    parts = lax.all_to_all(spread, ("stem", "cuts"), 0, 0, tiled=True)
     return jnp.sum(parts, axis=0).reshape(-1)
 
 

time: 24.8 us -> 24.3 us (0.980)
  blocking collectives: 13.6 us -> 13.1 us
    all_to_all x1, blocking collectives: 13.6 us -> 13.1 us  [on_device(): parts = lax.all_to_all(spread, ('stem', 'cuts'), 0, 0, tiled=True)]
where the time goes in v13:
time: 24.3 us; the launch traced here: 24.2 us
  blocking collectives  13.1 us (54%)
  Pallas kernels  5.38 us (22%)
  starting transfers between devices  4.04 us (17%)
  waiting for transfers between devices  1.03 us (4%)
  other arithmetic  0.63 us (3%)
    all_to_all x1, blocking collectives, on_device(): parts = lax.all_to_all(spread, ('stem', 'cuts'), 0, 0, tiled=True)  13.1 us
    pallas_call x1, Pallas kernels, branch_sums(): pl.pallas_call(functools.partial(branch_kernel, total // groups), in_spec...  4.95 us
    ppermute x5, starting transfers between devices, swap(): return lax.ppermute(x, 'stem', [(s, s ^ p) for s in range(stems)])  4.04 us
    ppermute x5, waiting for transfers between devices, swap(): return lax.ppermute(x, 'stem', [(s, s ^ p) for s in range(stems)])  1.03 us
    reduce_sum x1, other arithmetic, on_device(): return jnp.sum(parts, axis=0).reshape(-1)  0.63 us
  transfers between devices with their start and end apart: 5, of which 4 were waited for; matrix products, arithmetic and copies ran while one was open for 0% of the time, Pallas kernels for 20%

profile of v13, /device:TPU:0, one launch (start us, length us, event | category | flops | bytes accessed | tf_op | source)
XLA Modules:
  0.0 24.2 jit_solution(16933740418657693459)
XLA Ops:
  0.0 0.0 copy-start
  0.0 3.0 %collective-permute-start = (bf16[2,64,1024]{2,1,0:T(8,128)(2,1)}, bf16[2,64,1024]{2,1,0:T(8,128)(2,1)S(1)}, u32[]{:S(2)}, u32[]{:S(2)}) collective-permute-start(bf16[2,64,1024]{2,1,0:T(8,128)(2,1)} %refs_0_.1), channel_id=1, source_target_pairs={{0,2},{1,3},{2,0},{3,1},{4,6},{5,7},{6,4},{7,5},{8,10},{9,11},{10,... | collective-permute-start | bytes 786440 | tf_op jit(solution)/shard_map/ppermute | solution.py:147
  3.0 4.9 %branch_sums.1 = (f32[4,512,128]{2,1,0:T(8,128)S(1)}, bf16[512,128]{1,0:T(8,128)(2,1)S(1)}, bf16[512,128]{1,0:T(8,128)(2,1)S(1)}, bf16[512,128]{1,0:T(8,128)(2,1)S(1)}, bf16[512,128]{1,0:T(8,128)(2,1)S(1)}) custom-call(bf16[16,512,128]{2,1,0:T(8,128)(2,1)} %mid_hbm.1, bf16[8,16,64,128]{3,2,1,0:T(8,128)(2,1)} %right_hbm.1), custom_call_target="tpu_custom_call" | custom-call | flops 2147483648 | bytes 6291456 | tf_op jit(solution)/shard_map/branch_sums/pallas_call | solution.py:74
  7.9 0.1 collective-permute-start.1
  8.0 0.5 %collective-permute-start.2 = (bf16[512,128]{1,0:T(8,128)(2,1)S(1)}, bf16[512,128]{1,0:T(8,128)(2,1)S(1)}, u32[]{:S(2)}, u32[]{:S(2)}) collective-permute-start(bf16[512,128]{1,0:T(8,128)(2,1)S(1)} %get-tuple-element.11), channel_id=1, source_target_pairs={{0,1},{1,0},{2,3},{3,2},{4,5},{5,4},{6,7},{7,6},{8,9},{9,8},{10,11... | collective-permute-start | bytes 393224 | tf_op jit(solution)/shard_map/ppermute | solution.py:147
  8.5 0.1 collective-permute-start.3
  8.6 0.4 %collective-permute-start.4 = (bf16[512,128]{1,0:T(8,128)(2,1)S(1)}, bf16[512,128]{1,0:T(8,128)(2,1)S(1)}, u32[]{:S(2)}, u32[]{:S(2)}) collective-permute-start(bf16[512,128]{1,0:T(8,128)(2,1)S(1)} %get-tuple-element.13), channel_id=1, source_target_pairs={{0,1},{1,0},{2,3},{3,2},{4,5},{5,4},{6,7},{7,6},{8,9},{9,8},{10,11... | collective-permute-start | bytes 393224 | tf_op jit(solution)/shard_map/ppermute | solution.py:147
  9.0 0.3 %collective-permute-done.1.refs_2_ = bf16[512,128]{1,0:T(8,128)(2,1)S(1)} collective-permute-done((bf16[512,128]{1,0:T(8,128)(2,1)S(1)}, bf16[512,128]{1,0:T(8,128)(2,1)S(1)}, u32[]{:S(2)}, u32[]{:S(2)}) %collective-permute-start.1) | collective-permute-done | bytes 131104 | tf_op jit(solution)/shard_map/ppermute | solution.py:147
  9.3 0.2 collective-permute-done.2.refs_3_
  9.5 0.3 %collective-permute-done.3.refs_4_ = bf16[512,128]{1,0:T(8,128)(2,1)S(1)} collective-permute-done((bf16[512,128]{1,0:T(8,128)(2,1)S(1)}, bf16[512,128]{1,0:T(8,128)(2,1)S(1)}, u32[]{:S(2)}, u32[]{:S(2)}) %collective-permute-start.3) | collective-permute-done | bytes 131104 | tf_op jit(solution)/shard_map/ppermute | solution.py:147
  9.9 0.2 collective-permute-done.4.refs_5_
  10.0 0.0 collective-permute-done.refs_1_
  10.0 0.0 copy-done
  10.0 0.4 %close.1 = f32[4,8,8,128]{3,2,1,0:T(8,128)S(1)} custom-call(bf16[2,64,1024]{2,1,0:T(8,128)(2,1)S(1)} %copy-done, bf16[2,64,1024]{2,1,0:T(8,128)(2,1)S(1)} %collective-permute-done.refs_1_, bf16[512,128]{1,0:T(8,128)(2,1)S(1)} %collective-permute-done.1.refs_2_, bf16[512,128]{1,0:T(8,128)(2,1)S(1)} %collective-permute-done.2.refs_3_, ...), custom_call_target="tpu_custom_call" | custom-call | flops 134217728 | bytes 1048576 | tf_op jit(solution)/shard_map/close/pallas_call | solution.py:129
  10.5 13.1 %all_to_all.5 = f32[32,8,128]{2,1,0:T(8,128)S(1)} all-to-all(f32[32,8,128]{2,1,0:T(8,128)S(1)} %bitcast.2), channel_id=1, replica_groups=mesh['cuts'=8,'stem'=4] {'stem','cuts'}, dimensions={0} | all-to-all | bytes 262144 | tf_op jit(solution)/shard_map/all_to_all | solution.py:153
  23.5 0.6 %reduce_sum.9 = f32[8,128]{1,0:T(8,128)} reduce(f32[32,8,128]{2,1,0:T(8,128)S(1)} %all_to_all.5, f32[]{:T(128)} %constant.0.clone.1), dimensions={0}, to_apply=%region_0.0 | reduce | flops 31744 | bytes 135172 | tf_op jit(solution)/shard_map/reduce_sum | solution.py:154
Async XLA Ops:
  0.0 10.0 %copy-start = (bf16[2,64,1024]{2,1,0:T(8,128)(2,1)S(1)}, bf16[2,64,1024]{2,1,0:T(8,128)(2,1)}, u32[]{:S(2)}) copy-start(bf16[2,64,1024]{2,1,0:T(8,128)(2,1)} %refs_0_.1) | copy-start | bytes 786436
  0.0 10.0 %collective-permute-start = (bf16[2,64,1024]{2,1,0:T(8,128)(2,1)}, bf16[2,64,1024]{2,1,0:T(8,128)(2,1)S(1)}, u32[]{:S(2)}, u32[]{:S(2)}) collective-permute-start(bf16[2,64,1024]{2,1,0:T(8,128)(2,1)} %refs_0_.1), channel_id=1, source_target_pairs={{0,2},{1,3},{2,0},{3,1},{4,6},{5,7},{6,4},{7,5},{8,10},{9,11},{10,... | collective-permute-start | bytes 786440 | tf_op jit(solution)/shard_map/ppermute | solution.py:147
  7.9 1.4 %collective-permute-start.1 = (bf16[512,128]{1,0:T(8,128)(2,1)S(1)}, bf16[512,128]{1,0:T(8,128)(2,1)S(1)}, u32[]{:S(2)}, u32[]{:S(2)}) collective-permute-start(bf16[512,128]{1,0:T(8,128)(2,1)S(1)} %get-tuple-element.10), channel_id=1, source_target_pairs={{0,1},{1,0},{2,3},{3,2},{4,5},{5,4},{6,7},{7,6},{8,9},{9,8},{10,11... | collective-permute-start | bytes 393224 | tf_op jit(solution)/shard_map/ppermute | solution.py:147
  8.0 1.5 %collective-permute-start.2 = (bf16[512,128]{1,0:T(8,128)(2,1)S(1)}, bf16[512,128]{1,0:T(8,128)(2,1)S(1)}, u32[]{:S(2)}, u32[]{:S(2)}) collective-permute-start(bf16[512,128]{1,0:T(8,128)(2,1)S(1)} %get-tuple-element.11), channel_id=1, source_target_pairs={{0,1},{1,0},{2,3},{3,2},{4,5},{5,4},{6,7},{7,6},{8,9},{9,8},{10,11... | collective-permute-start | bytes 393224 | tf_op jit(solution)/shard_map/ppermute | solution.py:147
  8.5 1.3 %collective-permute-start.3 = (bf16[512,128]{1,0:T(8,128)(2,1)S(1)}, bf16[512,128]{1,0:T(8,128)(2,1)S(1)}, u32[]{:S(2)}, u32[]{:S(2)}) collective-permute-start(bf16[512,128]{1,0:T(8,128)(2,1)S(1)} %get-tuple-element.12), channel_id=1, source_target_pairs={{0,1},{1,0},{2,3},{3,2},{4,5},{5,4},{6,7},{7,6},{8,9},{9,8},{10,11... | collective-permute-start | bytes 393224 | tf_op jit(solution)/shard_map/ppermute | solution.py:147
  8.6 1.5 %collective-permute-start.4 = (bf16[512,128]{1,0:T(8,128)(2,1)S(1)}, bf16[512,128]{1,0:T(8,128)(2,1)S(1)}, u32[]{:S(2)}, u32[]{:S(2)}) collective-permute-start(bf16[512,128]{1,0:T(8,128)(2,1)S(1)} %get-tuple-element.13), channel_id=1, source_target_pairs={{0,1},{1,0},{2,3},{3,2},{4,5},{5,4},{6,7},{7,6},{8,9},{9,8},{10,11... | collective-permute-start | bytes 393224 | tf_op jit(solution)/shard_map/ppermute | solution.py:147

commit v14 on v13

--- a/solution.py
+++ b/solution.py
@@ -2,11 +2,15 @@
 
 import jax
 import jax.numpy as jnp
+import numpy as np
 from jax import lax
 from jax.experimental import pallas as pl
 from jax.experimental.pallas import tpu as pltpu
-from jax.sharding import PartitionSpec as P
+from jax.sharding import Mesh, PartitionSpec as P
 
+CUTS = ("plane", "column")
+STEM = ("side", "core")
+ORDER = ("side", "core", "column", "plane")
 MIB = 1024 * 1024
 
 
@@ -23,7 +27,7 @@
     total, _, inner, _ = right_hbm.shape
     groups = total // blocks
     half = groups // 2
-    me = lax.axis_index("stem")
+    me = lax.axis_index("side") * lax.axis_size("core") + lax.axis_index("core")
     chunk = pairs // mid_sem.shape[0]
 
     def mid_copy(n):
@@ -93,7 +97,7 @@
     )(mid, right)
 
 
-def close_kernel(*refs):
+def close_kernel(targets, *refs):
     *more, kept_ref, out_ref = refs
     stem_refs, got_refs = more[:-kept_ref.shape[0]], more[-kept_ref.shape[0]:]
     part = None
@@ -113,56 +117,53 @@
     part = part[:, :width] + part[:, width:]
     half = part.shape[0] // 2
     total = part[:half] + turn(part[half:])
-    if len(out_ref.shape) == 2:
+    if targets is None:
         out_ref[...] = total
     else:
-        copies, cuts, rows, _ = out_ref.shape
-        for c in range(cuts):
-            for s in range(copies):
-                out_ref[s, c] = total[c * rows:(c + 1) * rows]
+        rows = out_ref.shape[1]
+        for at, c in enumerate(targets):
+            out_ref[at] = total[c * rows:(c + 1) * rows]
 
 
-def close(stems, kept, got, cuts, copies):
+def close(stems, kept, got):
     rows, width = stems[0].shape[1], kept.shape[2]
+    cuts = lax.axis_size(CUTS)
+    sizes = [lax.axis_size(name) for name in ORDER]
+    places = np.arange(cuts).reshape([lax.axis_size(name) for name in CUTS])
+    targets = [int(places[at[ORDER.index("plane")], at[ORDER.index("column")]]) for at in np.ndindex(*sizes)]
     whole_tiles = rows % (8 * cuts) == 0
-    shape = (copies, cuts, rows // cuts, width) if whole_tiles else (rows, width)
+    shape = (len(targets), rows // cuts, width) if whole_tiles else (rows, width)
     out = pl.pallas_call(
-        close_kernel,
+        functools.partial(close_kernel, targets if whole_tiles else None),
         out_shape=jax.ShapeDtypeStruct(shape, jnp.float32),
         compiler_params=pltpu.CompilerParams(vmem_limit_bytes=24 * MIB),
         cost_estimate=pl.CostEstimate(flops=8 * rows * kept.size, bytes_accessed=MIB, transcendentals=0),
         name="close",
     )(*stems, *got, kept)
-    if whole_tiles:
-        return out.reshape(cuts * copies, rows // cuts, width)
-    out = out.reshape(1, cuts, -1)
-    return jnp.broadcast_to(out, (copies, cuts, out.shape[-1])).reshape(cuts * copies, -1)
+    return out if whole_tiles else out.reshape(cuts, -1)[np.array(targets)]
 
 
 def on_device(stem_tensor, mid_tensors, right_tensors):
-    stems = lax.axis_size("stem")
-    cuts = lax.axis_size("cuts")
+    stems = lax.axis_size(STEM)
 
     def swap(x, p):
-        return lax.ppermute(x, "stem", [(s, s ^ p) for s in range(stems)])
+        return lax.ppermute(x, STEM, [(s, s ^ p) for s in range(stems)])
 
     pieces = [stem_tensor] + [swap(stem_tensor, p) for p in range(2, stems, 2)]
     kept, *sent = branch_sums(mid_tensors, right_tensors, stems)
     got = [swap(x, 1) for x in sent]
-    spread = close(pieces, kept, got, cuts, stems)
-    parts = lax.all_to_all(spread, ("stem", "cuts"), 0, 0, tiled=True)
+    spread = close(pieces, kept, got)
+    parts = lax.all_to_all(spread, ORDER, 0, 0, tiled=True)
     return jnp.sum(parts, axis=0).reshape(-1)
 
 
 def solution(mesh):
+    cuts, stems = mesh.devices.shape
+    fine = Mesh(mesh.devices.reshape(cuts // 2, 2, stems // 2, 2), CUTS + STEM)
     return jax.shard_map(
         on_device,
-        mesh=mesh,
-        in_specs=(
-            P("stem", None, None),
-            P(("cuts", "stem"), None, None),
-            P(None, ("cuts", "stem"), None, None),
-        ),
-        out_specs=P("cuts"),
+        mesh=fine,
+        in_specs=(P(STEM, None, None), P(CUTS + STEM, None, None), P(None, CUTS + STEM, None, None)),
+        out_specs=P(CUTS),
         check_vma=False,
     )

time: 24.3 us -> 24.3 us (level)
  no operation moved by 1% of the time
where the time goes in v14:
time: 24.3 us; the launch traced here: 24.2 us
  blocking collectives  13.1 us (54%)
  Pallas kernels  5.38 us (22%)
  starting transfers between devices  4.04 us (17%)
  waiting for transfers between devices  1.03 us (4%)
  other arithmetic  0.63 us (3%)
    all_to_all x1, blocking collectives, on_device(): parts = lax.all_to_all(spread, ORDER, 0, 0, tiled=True)  13.1 us
    pallas_call x1, Pallas kernels, branch_sums(): pl.pallas_call(functools.partial(branch_kernel, total // groups), in_spec...  4.95 us
    ppermute x5, starting transfers between devices, swap(): return lax.ppermute(x, STEM, [(s, s ^ p) for s in range(stems)])  4.04 us
    ppermute x5, waiting for transfers between devices, swap(): return lax.ppermute(x, STEM, [(s, s ^ p) for s in range(stems)])  1.03 us
    reduce_sum x1, other arithmetic, on_device(): return jnp.sum(parts, axis=0).reshape(-1)  0.63 us
  transfers between devices with their start and end apart: 5, of which 4 were waited for; matrix products, arithmetic and copies ran while one was open for 0% of the time, Pallas kernels for 20%

profile of v14, /device:TPU:0, one launch (start us, length us, event | category | flops | bytes accessed | tf_op | source)
XLA Modules:
  0.0 24.2 jit_solution(11878174988900189127)
XLA Ops:
  0.0 0.0 copy-start
  0.0 3.0 %collective-permute-start = (bf16[2,64,1024]{2,1,0:T(8,128)(2,1)}, bf16[2,64,1024]{2,1,0:T(8,128)(2,1)S(1)}, u32[]{:S(2)}, u32[]{:S(2)}) collective-permute-start(bf16[2,64,1024]{2,1,0:T(8,128)(2,1)} %refs_0_.1), channel_id=1, source_target_pairs={{0,2},{1,3},{2,0},{3,1},{4,6},{5,7},{6,4},{7,5},{8,10},{9,11},{10,... | collective-permute-start | bytes 786440 | tf_op jit(solution)/shard_map/ppermute | solution.py:150
  3.0 4.9 %branch_sums.1 = (f32[4,512,128]{2,1,0:T(8,128)S(1)}, bf16[512,128]{1,0:T(8,128)(2,1)S(1)}, bf16[512,128]{1,0:T(8,128)(2,1)S(1)}, bf16[512,128]{1,0:T(8,128)(2,1)S(1)}, bf16[512,128]{1,0:T(8,128)(2,1)S(1)}) custom-call(bf16[16,512,128]{2,1,0:T(8,128)(2,1)} %mid_hbm.1, bf16[8,16,64,128]{3,2,1,0:T(8,128)(2,1)} %right_hbm.1), custom_call_target="tpu_custom_call" | custom-call | flops 2147483648 | bytes 6291456 | tf_op jit(solution)/shard_map/branch_sums/pallas_call | solution.py:78
  7.9 0.1 collective-permute-start.1
  8.0 0.5 %collective-permute-start.2 = (bf16[512,128]{1,0:T(8,128)(2,1)S(1)}, bf16[512,128]{1,0:T(8,128)(2,1)S(1)}, u32[]{:S(2)}, u32[]{:S(2)}) collective-permute-start(bf16[512,128]{1,0:T(8,128)(2,1)S(1)} %get-tuple-element.11), channel_id=1, source_target_pairs={{0,1},{1,0},{2,3},{3,2},{4,5},{5,4},{6,7},{7,6},{8,9},{9,8},{10,11... | collective-permute-start | bytes 393224 | tf_op jit(solution)/shard_map/ppermute | solution.py:150
  8.5 0.1 collective-permute-start.3
  8.6 0.4 %collective-permute-start.4 = (bf16[512,128]{1,0:T(8,128)(2,1)S(1)}, bf16[512,128]{1,0:T(8,128)(2,1)S(1)}, u32[]{:S(2)}, u32[]{:S(2)}) collective-permute-start(bf16[512,128]{1,0:T(8,128)(2,1)S(1)} %get-tuple-element.13), channel_id=1, source_target_pairs={{0,1},{1,0},{2,3},{3,2},{4,5},{5,4},{6,7},{7,6},{8,9},{9,8},{10,11... | collective-permute-start | bytes 393224 | tf_op jit(solution)/shard_map/ppermute | solution.py:150
  9.0 0.3 %collective-permute-done.1.refs_2_ = bf16[512,128]{1,0:T(8,128)(2,1)S(1)} collective-permute-done((bf16[512,128]{1,0:T(8,128)(2,1)S(1)}, bf16[512,128]{1,0:T(8,128)(2,1)S(1)}, u32[]{:S(2)}, u32[]{:S(2)}) %collective-permute-start.1) | collective-permute-done | bytes 131104 | tf_op jit(solution)/shard_map/ppermute | solution.py:150
  9.3 0.2 collective-permute-done.2.refs_3_
  9.5 0.3 %collective-permute-done.3.refs_4_ = bf16[512,128]{1,0:T(8,128)(2,1)S(1)} collective-permute-done((bf16[512,128]{1,0:T(8,128)(2,1)S(1)}, bf16[512,128]{1,0:T(8,128)(2,1)S(1)}, u32[]{:S(2)}, u32[]{:S(2)}) %collective-permute-start.3) | collective-permute-done | bytes 131104 | tf_op jit(solution)/shard_map/ppermute | solution.py:150
  9.9 0.2 collective-permute-done.4.refs_5_
  10.0 0.0 collective-permute-done.refs_1_
  10.0 0.0 copy-done
  10.0 0.4 %close.1 = f32[32,8,128]{2,1,0:T(8,128)S(1)} custom-call(bf16[2,64,1024]{2,1,0:T(8,128)(2,1)S(1)} %copy-done, bf16[2,64,1024]{2,1,0:T(8,128)(2,1)S(1)} %collective-permute-done.refs_1_, bf16[512,128]{1,0:T(8,128)(2,1)S(1)} %collective-permute-done.1.refs_2_, bf16[512,128]{1,0:T(8,128)(2,1)S(1)} %collective-permute-done.2.refs_3_, ...), custom_call_target="tpu_custom_call" | custom-call | flops 134217728 | bytes 1048576 | tf_op jit(solution)/shard_map/close/pallas_call | solution.py:136
  10.5 13.1 %all_to_all.5 = f32[32,8,128]{2,1,0:T(8,128)S(1)} all-to-all(f32[32,8,128]{2,1,0:T(8,128)S(1)} %close.1), channel_id=1, replica_groups=mesh['plane'=4,'column'=2,'side'=2,'core'=2] {'side','core','column','pl..., dimensions={0} | all-to-all | bytes 262144 | tf_op jit(solution)/shard_map/all_to_all | solution.py:156
  23.6 0.6 %reduce_sum.9 = f32[8,128]{1,0:T(8,128)} reduce(f32[32,8,128]{2,1,0:T(8,128)S(1)} %all_to_all.5, f32[]{:T(128)} %constant.0.clone.1), dimensions={0}, to_apply=%region_0.0 | reduce | flops 31744 | bytes 135172 | tf_op jit(solution)/shard_map/reduce_sum | solution.py:157
Async XLA Ops:
  0.0 10.0 %copy-start = (bf16[2,64,1024]{2,1,0:T(8,128)(2,1)S(1)}, bf16[2,64,1024]{2,1,0:T(8,128)(2,1)}, u32[]{:S(2)}) copy-start(bf16[2,64,1024]{2,1,0:T(8,128)(2,1)} %refs_0_.1) | copy-start | bytes 786436
  0.0 10.0 %collective-permute-start = (bf16[2,64,1024]{2,1,0:T(8,128)(2,1)}, bf16[2,64,1024]{2,1,0:T(8,128)(2,1)S(1)}, u32[]{:S(2)}, u32[]{:S(2)}) collective-permute-start(bf16[2,64,1024]{2,1,0:T(8,128)(2,1)} %refs_0_.1), channel_id=1, source_target_pairs={{0,2},{1,3},{2,0},{3,1},{4,6},{5,7},{6,4},{7,5},{8,10},{9,11},{10,... | collective-permute-start | bytes 786440 | tf_op jit(solution)/shard_map/ppermute | solution.py:150
  7.9 1.4 %collective-permute-start.1 = (bf16[512,128]{1,0:T(8,128)(2,1)S(1)}, bf16[512,128]{1,0:T(8,128)(2,1)S(1)}, u32[]{:S(2)}, u32[]{:S(2)}) collective-permute-start(bf16[512,128]{1,0:T(8,128)(2,1)S(1)} %get-tuple-element.10), channel_id=1, source_target_pairs={{0,1},{1,0},{2,3},{3,2},{4,5},{5,4},{6,7},{7,6},{8,9},{9,8},{10,11... | collective-permute-start | bytes 393224 | tf_op jit(solution)/shard_map/ppermute | solution.py:150
  8.0 1.5 %collective-permute-start.2 = (bf16[512,128]{1,0:T(8,128)(2,1)S(1)}, bf16[512,128]{1,0:T(8,128)(2,1)S(1)}, u32[]{:S(2)}, u32[]{:S(2)}) collective-permute-start(bf16[512,128]{1,0:T(8,128)(2,1)S(1)} %get-tuple-element.11), channel_id=1, source_target_pairs={{0,1},{1,0},{2,3},{3,2},{4,5},{5,4},{6,7},{7,6},{8,9},{9,8},{10,11... | collective-permute-start | bytes 393224 | tf_op jit(solution)/shard_map/ppermute | solution.py:150
  8.5 1.3 %collective-permute-start.3 = (bf16[512,128]{1,0:T(8,128)(2,1)S(1)}, bf16[512,128]{1,0:T(8,128)(2,1)S(1)}, u32[]{:S(2)}, u32[]{:S(2)}) collective-permute-start(bf16[512,128]{1,0:T(8,128)(2,1)S(1)} %get-tuple-element.12), channel_id=1, source_target_pairs={{0,1},{1,0},{2,3},{3,2},{4,5},{5,4},{6,7},{7,6},{8,9},{9,8},{10,11... | collective-permute-start | bytes 393224 | tf_op jit(solution)/shard_map/ppermute | solution.py:150
  8.6 1.5 %collective-permute-start.4 = (bf16[512,128]{1,0:T(8,128)(2,1)S(1)}, bf16[512,128]{1,0:T(8,128)(2,1)S(1)}, u32[]{:S(2)}, u32[]{:S(2)}) collective-permute-start(bf16[512,128]{1,0:T(8,128)(2,1)S(1)} %get-tuple-element.13), channel_id=1, source_target_pairs={{0,1},{1,0},{2,3},{3,2},{4,5},{5,4},{6,7},{7,6},{8,9},{9,8},{10,11... | collective-permute-start | bytes 393224 | tf_op jit(solution)/shard_map/ppermute | solution.py:150

commit v15 on v12

--- a/solution.py
+++ b/solution.py
@@ -2,11 +2,15 @@
 
 import jax
 import jax.numpy as jnp
+import numpy as np
 from jax import lax
 from jax.experimental import pallas as pl
 from jax.experimental.pallas import tpu as pltpu
-from jax.sharding import PartitionSpec as P
-
+from jax.sharding import Mesh, PartitionSpec as P
+
+CUTS = ("plane", "column")
+STEM = ("side", "core")
+PLANE = ("side", "core", "column")
 MIB = 1024 * 1024
 
 
@@ -23,7 +27,7 @@
     total, _, inner, _ = right_hbm.shape
     groups = total // blocks
     half = groups // 2
-    me = lax.axis_index("stem")
+    me = lax.axis_index("side") * lax.axis_size("core") + lax.axis_index("core")
     chunk = pairs // mid_sem.shape[0]
 
     def mid_copy(n):
@@ -145,72 +149,67 @@
     )(one, other)
 
 
-def half_line(own, near, far):
+def half_line(own, near, far, columns):
+    size = own.shape[0] // (max(columns) + 1)
+
     def kernel(own_ref, near_ref, far_ref, out_ref):
-        odd = lax.axis_index("stem") % 2 == 1
-        out_ref[...] = jnp.where(odd, own_ref[...], near_ref[...]) + far_ref[...]
+        odd = lax.axis_index("core") == 1
+        total = jnp.where(odd, own_ref[...], near_ref[...]) + far_ref[...]
+        for at, column in enumerate(columns):
+            out_ref[at] = total[column * size:(column + 1) * size]
 
     return pl.pallas_call(
         kernel,
-        out_shape=jax.ShapeDtypeStruct(own.shape, own.dtype),
+        out_shape=jax.ShapeDtypeStruct((len(columns), size, own.shape[1]), own.dtype),
         compiler_params=pltpu.CompilerParams(vmem_limit_bytes=24 * MIB),
-        cost_estimate=pl.CostEstimate(flops=2 * own.size, bytes_accessed=16 * own.size, transcendentals=0),
+        cost_estimate=pl.CostEstimate(flops=2 * own.size, bytes_accessed=32 * own.size, transcendentals=0),
         name="half_line",
     )(own, near, far)
 
 
 def on_device(stem_tensor, mid_tensors, right_tensors):
-    stems = lax.axis_size("stem")
-    cuts = lax.axis_size("cuts")
+    stems = lax.axis_size(STEM)
 
     def swap(x, p):
-        return lax.ppermute(x, "stem", [(s, s ^ p) for s in range(stems)])
+        return lax.ppermute(x, STEM, [(s, s ^ p) for s in range(stems)])
 
     pieces = [stem_tensor] + [swap(stem_tensor, p) for p in range(2, stems, 2)]
     kept, *sent = branch_sums(mid_tensors, right_tensors, stems)
     got = [swap(x, 1) for x in sent]
     partial_sum = close(pieces, kept, got)
-    rows = partial_sum.shape[0]
-    if cuts != 8 or stems != 4 or rows % 64:
-        parts = partial_sum.reshape(cuts, 1, -1)
-        parts = jnp.broadcast_to(parts, (cuts, stems, parts.shape[-1])).reshape(cuts * stems, -1)
-        return jnp.sum(lax.all_to_all(parts, ("cuts", "stem"), 0, 0, tiled=True), axis=0)
-
-    def send(x, mask):
+    cuts = lax.axis_size(CUTS)
+    if cuts != 8 or stems != 4 or partial_sum.shape[0] % 64:
+        parts = partial_sum.reshape(1, cuts, -1)
+        parts = jnp.broadcast_to(parts, (stems, cuts, parts.shape[-1])).reshape(cuts * stems, -1)
+        return jnp.sum(lax.all_to_all(parts, STEM + CUTS, 0, 0, tiled=True), axis=0)
+
+    def send(x, flips):
         pairs = []
-        for i in range(cuts):
-            for j in range(stems):
-                c, s = mask(j % 2)
-                pairs.append((i * stems + j, (i ^ c) * stems + (j ^ s)))
-        return lax.ppermute(x, ("cuts", "stem"), pairs)
+        for i in range(cuts * stems):
+            plane, core = flips(i % 2)
+            pairs.append((i, i ^ (plane * 8 + core)))
+        return lax.ppermute(x, CUTS + STEM, pairs)
 
     def plane():
-        return lax.axis_index("cuts") // 2
-
-    def column():
-        return lax.axis_index("cuts") % 2
+        return lax.axis_index("plane")
 
     chip = send(partial_sum, lambda core: (0, 1))
     own, near, far = deal(
-        partial_sum, chip, 4, (plane, lambda: plane() ^ 1, lambda: plane() ^ (2 + lax.axis_index("stem") % 2))
+        partial_sum, chip, 4, (plane, lambda: plane() ^ 1, lambda: plane() ^ (2 + lax.axis_index("core")))
     )
-    near = send(near, lambda core: (2, 1))
-    far = send(far, lambda core: (2 * (2 + core), 0))
-    line = half_line(own, near, far)
-    own, away = deal(line, send(line, lambda core: (0, 1)), 2, (column, lambda: column() ^ 1))
-    total = own + send(away, lambda core: (1, 1)) + send(away, lambda core: (1, 3)) + send(own, lambda core: (0, 3))
-    return total.reshape(-1)
+    near = send(near, lambda core: (1, 1))
+    far = send(far, lambda core: (2 + core, 0))
+    parts = half_line(own, near, far, [at[2] for at in np.ndindex(2, 2, 2)])
+    return jnp.sum(lax.all_to_all(parts, PLANE, 0, 0, tiled=True), axis=0).reshape(-1)
 
 
 def solution(mesh):
+    cuts, stems = mesh.devices.shape
+    fine = Mesh(mesh.devices.reshape(cuts // 2, 2, stems // 2, 2), CUTS + STEM)
     return jax.shard_map(
         on_device,
-        mesh=mesh,
-        in_specs=(
-            P("stem", None, None),
-            P(("cuts", "stem"), None, None),
-            P(None, ("cuts", "stem"), None, None),
-        ),
-        out_specs=P("cuts"),
+        mesh=fine,
+        in_specs=(P(STEM, None, None), P(CUTS + STEM, None, None), P(None, CUTS + STEM, None, None)),
+        out_specs=P(CUTS),
         check_vma=False,
     )

time: 25.4 us -> 26.4 us (1.039)
  blocking collectives: 0 us -> 7.77 us
  waiting for transfers between devices: 7.76 us -> 3.87 us
  starting transfers between devices: 11.5 us -> 8.53 us
    all_to_all x0 -> x1, blocking collectives: none -> 7.77 us  [on_device(): lax.all_to_all(parts, PLANE, 0, 0, tiled=True)]
    ppermute x12 -> x8, waiting for transfers between devices: 7.76 us -> 3.87 us  [the longest x3 2.84 us: send(): return lax.ppermute(x, CUTS + STEM, pairs)]
    ppermute x12 -> x8, starting transfers between devices: 11.5 us -> 8.53 us  [the longest x3 4.48 us: send(): return lax.ppermute(x, CUTS + STEM, pairs)]
    reduce_sum x0 -> x1, other arithmetic: none -> 0.6 us  [on_device(): jnp.sum(lax.all_to_all(parts, PLANE, 0, 0, tiled=True), axis=0).reshape(-1)]
    reshape x1 -> x0, other arithmetic: 0.6 us -> none  [on_device(): return total.reshape(-1)]
  transfers between devices with their start and end apart: 12 -> 8, of which waited for: 10 -> 6; matrix products, arithmetic and copies ran while one was open for 0% -> 0% of each run, Pallas kernels for 20% -> 19%
where the time goes in v15:
time: 26.4 us; the launch traced here: 26.2 us
  starting transfers between devices  8.53 us (32%)
  blocking collectives  7.77 us (29%)
  Pallas kernels  5.39 us (20%)
  waiting for transfers between devices  3.87 us (15%)
  other arithmetic  0.6 us (2%)
    all_to_all x1, blocking collectives, on_device(): lax.all_to_all(parts, PLANE, 0, 0, tiled=True)  7.77 us
    pallas_call x1, Pallas kernels, branch_sums(): pl.pallas_call(functools.partial(branch_kernel, total // groups), in_spec...  4.95 us
    ppermute x3, starting transfers between devices, send(): return lax.ppermute(x, CUTS + STEM, pairs)  4.48 us
    ppermute x5, starting transfers between devices, swap(): return lax.ppermute(x, STEM, [(s, s ^ p) for s in range(stems)])  4.04 us
    ppermute x3, waiting for transfers between devices, send(): return lax.ppermute(x, CUTS + STEM, pairs)  2.84 us
    ppermute x5, waiting for transfers between devices, swap(): return lax.ppermute(x, STEM, [(s, s ^ p) for s in range(stems)])  1.03 us
    reduce_sum x1, other arithmetic, on_device(): jnp.sum(lax.all_to_all(parts, PLANE, 0, 0, tiled=True), axis=0).reshape(-1)  0.6 us
  transfers between devices with their start and end apart: 8, of which 6 were waited for; matrix products, arithmetic and copies ran while one was open for 0% of the time, Pallas kernels for 19%

profile of v15, /device:TPU:0, one launch (start us, length us, event | category | flops | bytes accessed | tf_op | source)
XLA Modules:
  0.0 26.2 jit_solution(9259391404865424131)
XLA Ops:
  0.0 0.0 copy-start
  0.0 3.0 %collective-permute-start = (bf16[2,64,1024]{2,1,0:T(8,128)(2,1)}, bf16[2,64,1024]{2,1,0:T(8,128)(2,1)S(1)}, u32[]{:S(2)}, u32[]{:S(2)}) collective-permute-start(bf16[2,64,1024]{2,1,0:T(8,128)(2,1)} %refs_0_.1), channel_id=1, source_target_pairs={{0,2},{1,3},{2,0},{3,1},{4,6},{5,7},{6,4},{7,5},{8,10},{9,11},{10,... | collective-permute-start | bytes 786440 | tf_op jit(solution)/shard_map/ppermute | solution.py:174
  3.0 4.9 %branch_sums.1 = (f32[4,512,128]{2,1,0:T(8,128)S(1)}, bf16[512,128]{1,0:T(8,128)(2,1)S(1)}, bf16[512,128]{1,0:T(8,128)(2,1)S(1)}, bf16[512,128]{1,0:T(8,128)(2,1)S(1)}, bf16[512,128]{1,0:T(8,128)(2,1)S(1)}) custom-call(bf16[16,512,128]{2,1,0:T(8,128)(2,1)} %mid_hbm.1, bf16[8,16,64,128]{3,2,1,0:T(8,128)(2,1)} %right_hbm.1), custom_call_target="tpu_custom_call" | custom-call | flops 2147483648 | bytes 6291456 | tf_op jit(solution)/shard_map/branch_sums/pallas_call | solution.py:78
  7.9 0.1 collective-permute-start.1
  8.0 0.5 %collective-permute-start.2 = (bf16[512,128]{1,0:T(8,128)(2,1)S(1)}, bf16[512,128]{1,0:T(8,128)(2,1)S(1)}, u32[]{:S(2)}, u32[]{:S(2)}) collective-permute-start(bf16[512,128]{1,0:T(8,128)(2,1)S(1)} %get-tuple-element.14), channel_id=1, source_target_pairs={{0,1},{1,0},{2,3},{3,2},{4,5},{5,4},{6,7},{7,6},{8,9},{9,8},{10,11... | collective-permute-start | bytes 393224 | tf_op jit(solution)/shard_map/ppermute | solution.py:174
  8.5 0.1 collective-permute-start.3
  8.6 0.4 %collective-permute-start.4 = (bf16[512,128]{1,0:T(8,128)(2,1)S(1)}, bf16[512,128]{1,0:T(8,128)(2,1)S(1)}, u32[]{:S(2)}, u32[]{:S(2)}) collective-permute-start(bf16[512,128]{1,0:T(8,128)(2,1)S(1)} %get-tuple-element.16), channel_id=1, source_target_pairs={{0,1},{1,0},{2,3},{3,2},{4,5},{5,4},{6,7},{7,6},{8,9},{9,8},{10,11... | collective-permute-start | bytes 393224 | tf_op jit(solution)/shard_map/ppermute | solution.py:174
  9.0 0.3 %collective-permute-done.1.refs_2_ = bf16[512,128]{1,0:T(8,128)(2,1)S(1)} collective-permute-done((bf16[512,128]{1,0:T(8,128)(2,1)S(1)}, bf16[512,128]{1,0:T(8,128)(2,1)S(1)}, u32[]{:S(2)}, u32[]{:S(2)}) %collective-permute-start.1) | collective-permute-done | bytes 131104 | tf_op jit(solution)/shard_map/ppermute | solution.py:174
  9.3 0.2 collective-permute-done.2.refs_3_
  9.5 0.3 %collective-permute-done.3.refs_4_ = bf16[512,128]{1,0:T(8,128)(2,1)S(1)} collective-permute-done((bf16[512,128]{1,0:T(8,128)(2,1)S(1)}, bf16[512,128]{1,0:T(8,128)(2,1)S(1)}, u32[]{:S(2)}, u32[]{:S(2)}) %collective-permute-start.3) | collective-permute-done | bytes 131104 | tf_op jit(solution)/shard_map/ppermute | solution.py:174
  9.9 0.2 collective-permute-done.4.refs_5_
  10.0 0.0 collective-permute-done.refs_1_
  10.0 0.0 copy-done
  10.0 0.4 %close.1.one_ref = f32[64,128]{1,0:T(8,128)S(1)} custom-call(bf16[2,64,1024]{2,1,0:T(8,128)(2,1)S(1)} %copy-done, bf16[2,64,1024]{2,1,0:T(8,128)(2,1)S(1)} %collective-permute-done.refs_1_, bf16[512,128]{1,0:T(8,128)(2,1)S(1)} %collective-permute-done.1.refs_2_, bf16[512,128]{1,0:T(8,128)(2,1)S(1)} %collective-permute-done.2.refs_3_, ...), custom_call_target="tpu_custom_call" | custom-call | flops 134217728 | bytes 1048576 | tf_op jit(solution)/shard_map/close/pallas_call | solution.py:124
  10.5 0.4 %collective-permute-start.5 = (f32[64,128]{1,0:T(8,128)S(1)}, f32[64,128]{1,0:T(8,128)S(1)}, u32[]{:S(2)}, u32[]{:S(2)}) collective-permute-start(f32[64,128]{1,0:T(8,128)S(1)} %close.1.one_ref), channel_id=1, source_target_pairs={{0,1},{1,0},{2,3},{3,2},{4,5},{5,4},{6,7},{7,6},{8,9},{9,8},{10,11... | collective-permute-start | bytes 98312 | tf_op jit(solution)/shard_map/ppermute | solution.py:191
  10.9 0.9 %collective-permute-done.5.other_ref = f32[64,128]{1,0:T(8,128)S(1)} collective-permute-done((f32[64,128]{1,0:T(8,128)S(1)}, f32[64,128]{1,0:T(8,128)S(1)}, u32[]{:S(2)}, u32[]{:S(2)}) %collective-permute-start.5) | collective-permute-done | bytes 32800 | tf_op jit(solution)/shard_map/ppermute | solution.py:191
  11.8 1.5 %collective-permute-start.6 = (f32[16,128]{1,0:T(8,128)S(1)}, f32[16,128]{1,0:T(8,128)S(1)}, u32[]{:S(2)}, u32[]{:S(2)}) collective-permute-start(f32[16,128]{1,0:T(8,128)S(1)} %get-tuple-element.19), channel_id=1, source_target_pairs={{0,9},{1,8},{2,11},{3,10},{4,13},{5,12},{6,15},{7,14},{8,1},{9,0},... | collective-permute-start | bytes 24584 | tf_op jit(solution)/shard_map/ppermute | solution.py:191
  13.3 2.6 %collective-permute-start.7 = (f32[16,128]{1,0:T(8,128)S(1)}, f32[16,128]{1,0:T(8,128)S(1)}, u32[]{:S(2)}, u32[]{:S(2)}) collective-permute-start(f32[16,128]{1,0:T(8,128)S(1)} %get-tuple-element.20), channel_id=1, source_target_pairs={{0,16},{1,25},{2,18},{3,27},{4,20},{5,29},{6,22},{7,31},{8,24},{9,... | collective-permute-start | bytes 24584 | tf_op jit(solution)/shard_map/ppermute | solution.py:191
  15.9 0.0 collective-permute-done.6.near_ref
  15.9 2.0 %collective-permute-done.7.far_ref = f32[16,128]{1,0:T(8,128)S(1)} collective-permute-done((f32[16,128]{1,0:T(8,128)S(1)}, f32[16,128]{1,0:T(8,128)S(1)}, u32[]{:S(2)}, u32[]{:S(2)}) %collective-permute-start.7) | collective-permute-done | bytes 8224 | tf_op jit(solution)/shard_map/ppermute | solution.py:191
  17.8 7.8 %all_to_all.5 = f32[8,8,128]{2,1,0:T(8,128)S(1)} all-to-all(f32[8,8,128]{2,1,0:T(8,128)S(1)} %half_line.1), channel_id=1, replica_groups=mesh['plane'=4,'column'=2,'side'=2,'core'=2] {'side','core','column'}, dimensions={0} | all-to-all | bytes 65536 | tf_op jit(solution)/shard_map/all_to_all | solution.py:203
  25.6 0.6 %reduce_sum.9 = f32[8,128]{1,0:T(8,128)} reduce(f32[8,8,128]{2,1,0:T(8,128)S(1)} %all_to_all.5, f32[]{:T(128)} %constant.0.clone.1), dimensions={0}, to_apply=%region_0.0 | reduce | flops 7168 | bytes 36868 | tf_op jit(solution)/shard_map/reduce_sum | solution.py:203
  (2 shorter events, 0.0 us)
Async XLA Ops:
  0.0 10.0 %copy-start = (bf16[2,64,1024]{2,1,0:T(8,128)(2,1)S(1)}, bf16[2,64,1024]{2,1,0:T(8,128)(2,1)}, u32[]{:S(2)}) copy-start(bf16[2,64,1024]{2,1,0:T(8,128)(2,1)} %refs_0_.1) | copy-start | bytes 786436
  0.0 10.0 %collective-permute-start = (bf16[2,64,1024]{2,1,0:T(8,128)(2,1)}, bf16[2,64,1024]{2,1,0:T(8,128)(2,1)S(1)}, u32[]{:S(2)}, u32[]{:S(2)}) collective-permute-start(bf16[2,64,1024]{2,1,0:T(8,128)(2,1)} %refs_0_.1), channel_id=1, source_target_pairs={{0,2},{1,3},{2,0},{3,1},{4,6},{5,7},{6,4},{7,5},{8,10},{9,11},{10,... | collective-permute-start | bytes 786440 | tf_op jit(solution)/shard_map/ppermute | solution.py:174
  7.9 1.4 %collective-permute-start.1 = (bf16[512,128]{1,0:T(8,128)(2,1)S(1)}, bf16[512,128]{1,0:T(8,128)(2,1)S(1)}, u32[]{:S(2)}, u32[]{:S(2)}) collective-permute-start(bf16[512,128]{1,0:T(8,128)(2,1)S(1)} %get-tuple-element.13), channel_id=1, source_target_pairs={{0,1},{1,0},{2,3},{3,2},{4,5},{5,4},{6,7},{7,6},{8,9},{9,8},{10,11... | collective-permute-start | bytes 393224 | tf_op jit(solution)/shard_map/ppermute | solution.py:174
  8.0 1.5 %collective-permute-start.2 = (bf16[512,128]{1,0:T(8,128)(2,1)S(1)}, bf16[512,128]{1,0:T(8,128)(2,1)S(1)}, u32[]{:S(2)}, u32[]{:S(2)}) collective-permute-start(bf16[512,128]{1,0:T(8,128)(2,1)S(1)} %get-tuple-element.14), channel_id=1, source_target_pairs={{0,1},{1,0},{2,3},{3,2},{4,5},{5,4},{6,7},{7,6},{8,9},{9,8},{10,11... | collective-permute-start | bytes 393224 | tf_op jit(solution)/shard_map/ppermute | solution.py:174
  8.5 1.3 %collective-permute-start.3 = (bf16[512,128]{1,0:T(8,128)(2,1)S(1)}, bf16[512,128]{1,0:T(8,128)(2,1)S(1)}, u32[]{:S(2)}, u32[]{:S(2)}) collective-permute-start(bf16[512,128]{1,0:T(8,128)(2,1)S(1)} %get-tuple-element.15), channel_id=1, source_target_pairs={{0,1},{1,0},{2,3},{3,2},{4,5},{5,4},{6,7},{7,6},{8,9},{9,8},{10,11... | collective-permute-start | bytes 393224 | tf_op jit(solution)/shard_map/ppermute | solution.py:174
  8.6 1.5 %collective-permute-start.4 = (bf16[512,128]{1,0:T(8,128)(2,1)S(1)}, bf16[512,128]{1,0:T(8,128)(2,1)S(1)}, u32[]{:S(2)}, u32[]{:S(2)}) collective-permute-start(bf16[512,128]{1,0:T(8,128)(2,1)S(1)} %get-tuple-element.16), channel_id=1, source_target_pairs={{0,1},{1,0},{2,3},{3,2},{4,5},{5,4},{6,7},{7,6},{8,9},{9,8},{10,11... | collective-permute-start | bytes 393224 | tf_op jit(solution)/shard_map/ppermute | solution.py:174
  10.5 1.3 %collective-permute-start.5 = (f32[64,128]{1,0:T(8,128)S(1)}, f32[64,128]{1,0:T(8,128)S(1)}, u32[]{:S(2)}, u32[]{:S(2)}) collective-permute-start(f32[64,128]{1,0:T(8,128)S(1)} %close.1.one_ref), channel_id=1, source_target_pairs={{0,1},{1,0},{2,3},{3,2},{4,5},{5,4},{6,7},{7,6},{8,9},{9,8},{10,11... | collective-permute-start | bytes 98312 | tf_op jit(solution)/shard_map/ppermute | solution.py:191
  11.8 4.1 %collective-permute-start.6 = (f32[16,128]{1,0:T(8,128)S(1)}, f32[16,128]{1,0:T(8,128)S(1)}, u32[]{:S(2)}, u32[]{:S(2)}) collective-permute-start(f32[16,128]{1,0:T(8,128)S(1)} %get-tuple-element.19), channel_id=1, source_target_pairs={{0,9},{1,8},{2,11},{3,10},{4,13},{5,12},{6,15},{7,14},{8,1},{9,0},... | collective-permute-start | bytes 24584 | tf_op jit(solution)/shard_map/ppermute | solution.py:191
  13.3 4.5 %collective-permute-start.7 = (f32[16,128]{1,0:T(8,128)S(1)}, f32[16,128]{1,0:T(8,128)S(1)}, u32[]{:S(2)}, u32[]{:S(2)}) collective-permute-start(f32[16,128]{1,0:T(8,128)S(1)} %get-tuple-element.20), channel_id=1, source_target_pairs={{0,16},{1,25},{2,18},{3,27},{4,20},{5,29},{6,22},{7,31},{8,24},{9,... | collective-permute-start | bytes 24584 | tf_op jit(solution)/shard_map/ppermute | solution.py:191

commit v16 on v13

--- a/solution.py
+++ b/solution.py
@@ -119,7 +119,7 @@
         copies, cuts, rows, _ = out_ref.shape
         for c in range(cuts):
             for s in range(copies):
-                out_ref[s, c] = total[c * rows:(c + 1) * rows]
+                out_ref[s, c] = total[c * rows:(c + 1) * rows].astype(out_ref.dtype)
 
 
 def close(stems, kept, got, cuts, copies):
@@ -128,7 +128,7 @@
     shape = (copies, cuts, rows // cuts, width) if whole_tiles else (rows, width)
     out = pl.pallas_call(
         close_kernel,
-        out_shape=jax.ShapeDtypeStruct(shape, jnp.float32),
+        out_shape=jax.ShapeDtypeStruct(shape, jnp.bfloat16 if whole_tiles else jnp.float32),
         compiler_params=pltpu.CompilerParams(vmem_limit_bytes=24 * MIB),
         cost_estimate=pl.CostEstimate(flops=8 * rows * kept.size, bytes_accessed=MIB, transcendentals=0),
         name="close",
@@ -151,7 +151,7 @@
     got = [swap(x, 1) for x in sent]
     spread = close(pieces, kept, got, cuts, stems)
     parts = lax.all_to_all(spread, ("stem", "cuts"), 0, 0, tiled=True)
-    return jnp.sum(parts, axis=0).reshape(-1)
+    return jnp.sum(parts.astype(jnp.float32), axis=0).reshape(-1)
 
 
 def solution(mesh):

time: 24.3 us -> 23.9 us (0.984)
  blocking collectives: 13.1 us -> 12.6 us
    all_to_all x1, blocking collectives: 13.1 us -> 12.6 us  [on_device(): parts = lax.all_to_all(spread, ('stem', 'cuts'), 0, 0, tiled=True)]
  transfers between devices with their start and end apart: 5 -> 5, of which waited for: 4 -> 4; matrix products, arithmetic and copies ran while one was open for 0% -> 0% of each run, Pallas kernels for 20% -> 21%
where the time goes in v16:
time: 23.9 us; the launch traced here: 23.7 us
  blocking collectives  12.6 us (53%)
  Pallas kernels  5.38 us (23%)
  starting transfers between devices  4.04 us (17%)
  waiting for transfers between devices  1.03 us (4%)
  other arithmetic  0.63 us (3%)
    all_to_all x1, blocking collectives, on_device(): parts = lax.all_to_all(spread, ('stem', 'cuts'), 0, 0, tiled=True)  12.6 us
    pallas_call x1, Pallas kernels, branch_sums(): pl.pallas_call(functools.partial(branch_kernel, total // groups), in_spec...  4.95 us
    ppermute x5, starting transfers between devices, swap(): return lax.ppermute(x, 'stem', [(s, s ^ p) for s in range(stems)])  4.04 us
    ppermute x5, waiting for transfers between devices, swap(): return lax.ppermute(x, 'stem', [(s, s ^ p) for s in range(stems)])  1.03 us
    reduce_sum x1, other arithmetic, on_device(): return jnp.sum(parts.astype(jnp.float32), axis=0).reshape(-1)  0.63 us
  transfers between devices with their start and end apart: 5, of which 4 were waited for; matrix products, arithmetic and copies ran while one was open for 0% of the time, Pallas kernels for 21%

profile of v16, /device:TPU:0, one launch (start us, length us, event | category | flops | bytes accessed | tf_op | source)
XLA Modules:
  0.0 23.7 jit_solution(3542600144473692614)
XLA Ops:
  0.0 0.0 copy-start
  0.0 3.0 %collective-permute-start = (bf16[2,64,1024]{2,1,0:T(8,128)(2,1)}, bf16[2,64,1024]{2,1,0:T(8,128)(2,1)S(1)}, u32[]{:S(2)}, u32[]{:S(2)}) collective-permute-start(bf16[2,64,1024]{2,1,0:T(8,128)(2,1)} %refs_0_.1), channel_id=1, source_target_pairs={{0,2},{1,3},{2,0},{3,1},{4,6},{5,7},{6,4},{7,5},{8,10},{9,11},{10,... | collective-permute-start | bytes 786440 | tf_op jit(solution)/shard_map/ppermute | solution.py:147
  3.0 4.9 %branch_sums.1 = (f32[4,512,128]{2,1,0:T(8,128)S(1)}, bf16[512,128]{1,0:T(8,128)(2,1)S(1)}, bf16[512,128]{1,0:T(8,128)(2,1)S(1)}, bf16[512,128]{1,0:T(8,128)(2,1)S(1)}, bf16[512,128]{1,0:T(8,128)(2,1)S(1)}) custom-call(bf16[16,512,128]{2,1,0:T(8,128)(2,1)} %mid_hbm.1, bf16[8,16,64,128]{3,2,1,0:T(8,128)(2,1)} %right_hbm.1), custom_call_target="tpu_custom_call" | custom-call | flops 2147483648 | bytes 6291456 | tf_op jit(solution)/shard_map/branch_sums/pallas_call | solution.py:74
  7.9 0.1 collective-permute-start.1
  8.0 0.5 %collective-permute-start.2 = (bf16[512,128]{1,0:T(8,128)(2,1)S(1)}, bf16[512,128]{1,0:T(8,128)(2,1)S(1)}, u32[]{:S(2)}, u32[]{:S(2)}) collective-permute-start(bf16[512,128]{1,0:T(8,128)(2,1)S(1)} %get-tuple-element.11), channel_id=1, source_target_pairs={{0,1},{1,0},{2,3},{3,2},{4,5},{5,4},{6,7},{7,6},{8,9},{9,8},{10,11... | collective-permute-start | bytes 393224 | tf_op jit(solution)/shard_map/ppermute | solution.py:147
  8.5 0.1 collective-permute-start.3
  8.6 0.4 %collective-permute-start.4 = (bf16[512,128]{1,0:T(8,128)(2,1)S(1)}, bf16[512,128]{1,0:T(8,128)(2,1)S(1)}, u32[]{:S(2)}, u32[]{:S(2)}) collective-permute-start(bf16[512,128]{1,0:T(8,128)(2,1)S(1)} %get-tuple-element.13), channel_id=1, source_target_pairs={{0,1},{1,0},{2,3},{3,2},{4,5},{5,4},{6,7},{7,6},{8,9},{9,8},{10,11... | collective-permute-start | bytes 393224 | tf_op jit(solution)/shard_map/ppermute | solution.py:147
  9.0 0.3 %collective-permute-done.1.refs_2_ = bf16[512,128]{1,0:T(8,128)(2,1)S(1)} collective-permute-done((bf16[512,128]{1,0:T(8,128)(2,1)S(1)}, bf16[512,128]{1,0:T(8,128)(2,1)S(1)}, u32[]{:S(2)}, u32[]{:S(2)}) %collective-permute-start.1) | collective-permute-done | bytes 131104 | tf_op jit(solution)/shard_map/ppermute | solution.py:147
  9.3 0.2 collective-permute-done.2.refs_3_
  9.5 0.3 %collective-permute-done.3.refs_4_ = bf16[512,128]{1,0:T(8,128)(2,1)S(1)} collective-permute-done((bf16[512,128]{1,0:T(8,128)(2,1)S(1)}, bf16[512,128]{1,0:T(8,128)(2,1)S(1)}, u32[]{:S(2)}, u32[]{:S(2)}) %collective-permute-start.3) | collective-permute-done | bytes 131104 | tf_op jit(solution)/shard_map/ppermute | solution.py:147
  9.9 0.2 collective-permute-done.4.refs_5_
  10.0 0.0 collective-permute-done.refs_1_
  10.0 0.0 copy-done
  10.0 0.4 %close.1 = bf16[4,8,8,128]{3,2,1,0:T(8,128)(2,1)S(1)} custom-call(bf16[2,64,1024]{2,1,0:T(8,128)(2,1)S(1)} %copy-done, bf16[2,64,1024]{2,1,0:T(8,128)(2,1)S(1)} %collective-permute-done.refs_1_, bf16[512,128]{1,0:T(8,128)(2,1)S(1)} %collective-permute-done.1.refs_2_, bf16[512,128]{1,0:T(8,128)(2,1)S(1)} %collective-permute-done.2.refs_3_, ...), custom_call_target="tpu_custom_call" | custom-call | flops 134217728 | bytes 1048576 | tf_op jit(solution)/shard_map/close/pallas_call | solution.py:129
  10.5 12.6 %all_to_all.5 = bf16[32,8,128]{2,1,0:T(8,128)(2,1)S(1)} all-to-all(bf16[32,8,128]{2,1,0:T(8,128)(2,1)S(1)} %bitcast.2), channel_id=1, replica_groups=mesh['cuts'=8,'stem'=4] {'stem','cuts'}, dimensions={0} | all-to-all | bytes 131072 | tf_op jit(solution)/shard_map/all_to_all | solution.py:153
  23.1 0.6 %convert_reduce_fusion = f32[8,128]{1,0:T(8,128)} fusion(bf16[32,8,128]{2,1,0:T(8,128)(2,1)S(1)} %all_to_all.5), kind=kLoop, calls=%fused_computation | loop fusion | flops 64512 | bytes 69632 | tf_op jit(solution)/shard_map/reduce_sum | solution.py:154
Async XLA Ops:
  0.0 10.0 %copy-start = (bf16[2,64,1024]{2,1,0:T(8,128)(2,1)S(1)}, bf16[2,64,1024]{2,1,0:T(8,128)(2,1)}, u32[]{:S(2)}) copy-start(bf16[2,64,1024]{2,1,0:T(8,128)(2,1)} %refs_0_.1) | copy-start | bytes 786436
  0.0 10.0 %collective-permute-start = (bf16[2,64,1024]{2,1,0:T(8,128)(2,1)}, bf16[2,64,1024]{2,1,0:T(8,128)(2,1)S(1)}, u32[]{:S(2)}, u32[]{:S(2)}) collective-permute-start(bf16[2,64,1024]{2,1,0:T(8,128)(2,1)} %refs_0_.1), channel_id=1, source_target_pairs={{0,2},{1,3},{2,0},{3,1},{4,6},{5,7},{6,4},{7,5},{8,10},{9,11},{10,... | collective-permute-start | bytes 786440 | tf_op jit(solution)/shard_map/ppermute | solution.py:147
  7.9 1.4 %collective-permute-start.1 = (bf16[512,128]{1,0:T(8,128)(2,1)S(1)}, bf16[512,128]{1,0:T(8,128)(2,1)S(1)}, u32[]{:S(2)}, u32[]{:S(2)}) collective-permute-start(bf16[512,128]{1,0:T(8,128)(2,1)S(1)} %get-tuple-element.10), channel_id=1, source_target_pairs={{0,1},{1,0},{2,3},{3,2},{4,5},{5,4},{6,7},{7,6},{8,9},{9,8},{10,11... | collective-permute-start | bytes 393224 | tf_op jit(solution)/shard_map/ppermute | solution.py:147
  8.0 1.5 %collective-permute-start.2 = (bf16[512,128]{1,0:T(8,128)(2,1)S(1)}, bf16[512,128]{1,0:T(8,128)(2,1)S(1)}, u32[]{:S(2)}, u32[]{:S(2)}) collective-permute-start(bf16[512,128]{1,0:T(8,128)(2,1)S(1)} %get-tuple-element.11), channel_id=1, source_target_pairs={{0,1},{1,0},{2,3},{3,2},{4,5},{5,4},{6,7},{7,6},{8,9},{9,8},{10,11... | collective-permute-start | bytes 393224 | tf_op jit(solution)/shard_map/ppermute | solution.py:147
  8.5 1.3 %collective-permute-start.3 = (bf16[512,128]{1,0:T(8,128)(2,1)S(1)}, bf16[512,128]{1,0:T(8,128)(2,1)S(1)}, u32[]{:S(2)}, u32[]{:S(2)}) collective-permute-start(bf16[512,128]{1,0:T(8,128)(2,1)S(1)} %get-tuple-element.12), channel_id=1, source_target_pairs={{0,1},{1,0},{2,3},{3,2},{4,5},{5,4},{6,7},{7,6},{8,9},{9,8},{10,11... | collective-permute-start | bytes 393224 | tf_op jit(solution)/shard_map/ppermute | solution.py:147
  8.6 1.5 %collective-permute-start.4 = (bf16[512,128]{1,0:T(8,128)(2,1)S(1)}, bf16[512,128]{1,0:T(8,128)(2,1)S(1)}, u32[]{:S(2)}, u32[]{:S(2)}) collective-permute-start(bf16[512,128]{1,0:T(8,128)(2,1)S(1)} %get-tuple-element.13), channel_id=1, source_target_pairs={{0,1},{1,0},{2,3},{3,2},{4,5},{5,4},{6,7},{7,6},{8,9},{9,8},{10,11... | collective-permute-start | bytes 393224 | tf_op jit(solution)/shard_map/ppermute | solution.py:147

commit v17 on v16

--- a/solution.py
+++ b/solution.py
@@ -119,7 +119,8 @@
         copies, cuts, rows, _ = out_ref.shape
         for c in range(cuts):
             for s in range(copies):
-                out_ref[s, c] = total[c * rows:(c + 1) * rows].astype(out_ref.dtype)
+                at = (cuts - 1 - c) * rows
+                out_ref[s, c] = total[at:at + rows].astype(out_ref.dtype)
 
 
 def close(stems, kept, got, cuts, copies):
@@ -135,7 +136,7 @@
     )(*stems, *got, kept)
     if whole_tiles:
         return out.reshape(cuts * copies, rows // cuts, width)
-    out = out.reshape(1, cuts, -1)
+    out = out.reshape(1, cuts, -1)[:, ::-1]
     return jnp.broadcast_to(out, (copies, cuts, out.shape[-1])).reshape(cuts * copies, -1)
 
 
@@ -150,7 +151,8 @@
     kept, *sent = branch_sums(mid_tensors, right_tensors, stems)
     got = [swap(x, 1) for x in sent]
     spread = close(pieces, kept, got, cuts, stems)
-    parts = lax.all_to_all(spread, ("stem", "cuts"), 0, 0, tiled=True)
+    backwards = [list(range(stems * lax.axis_size("cuts") - 1, -1, -1))]
+    parts = lax.all_to_all(spread, ("stem", "cuts"), 0, 0, tiled=True, axis_index_groups=backwards)
     return jnp.sum(parts.astype(jnp.float32), axis=0).reshape(-1)
 
 

time: 23.9 us -> 24.1 us (level)
  no operation moved by 1% of the time
where the time goes in v17:
time: 24.1 us; the launch traced here: 23.9 us
  blocking collectives  12.8 us (53%)
  Pallas kernels  5.38 us (22%)
  starting transfers between devices  4.04 us (17%)
  waiting for transfers between devices  1.03 us (4%)
  other arithmetic  0.63 us (3%)
    all_to_all x1, blocking collectives, on_device(): lax.all_to_all(spread, ('stem', 'cuts'), 0, 0, tiled=True, axis_index_gro...  12.8 us
    pallas_call x1, Pallas kernels, branch_sums(): pl.pallas_call(functools.partial(branch_kernel, total // groups), in_spec...  4.95 us
    ppermute x5, starting transfers between devices, swap(): return lax.ppermute(x, 'stem', [(s, s ^ p) for s in range(stems)])  4.04 us
    ppermute x5, waiting for transfers between devices, swap(): return lax.ppermute(x, 'stem', [(s, s ^ p) for s in range(stems)])  1.03 us
    reduce_sum x1, other arithmetic, on_device(): return jnp.sum(parts.astype(jnp.float32), axis=0).reshape(-1)  0.63 us
  transfers between devices with their start and end apart: 5, of which 4 were waited for; matrix products, arithmetic and copies ran while one was open for 0% of the time, Pallas kernels for 21%

profile of v17, /device:TPU:0, one launch (start us, length us, event | category | flops | bytes accessed | tf_op | source)
XLA Modules:
  0.0 23.9 jit_solution(10964757912897342543)
XLA Ops:
  0.0 0.0 copy-start
  0.0 3.0 %collective-permute-start = (bf16[2,64,1024]{2,1,0:T(8,128)(2,1)}, bf16[2,64,1024]{2,1,0:T(8,128)(2,1)S(1)}, u32[]{:S(2)}, u32[]{:S(2)}) collective-permute-start(bf16[2,64,1024]{2,1,0:T(8,128)(2,1)} %refs_0_.1), channel_id=1, source_target_pairs={{0,2},{1,3},{2,0},{3,1},{4,6},{5,7},{6,4},{7,5},{8,10},{9,11},{10,... | collective-permute-start | bytes 786440 | tf_op jit(solution)/shard_map/ppermute | solution.py:148
  3.0 4.9 %branch_sums.1 = (f32[4,512,128]{2,1,0:T(8,128)S(1)}, bf16[512,128]{1,0:T(8,128)(2,1)S(1)}, bf16[512,128]{1,0:T(8,128)(2,1)S(1)}, bf16[512,128]{1,0:T(8,128)(2,1)S(1)}, bf16[512,128]{1,0:T(8,128)(2,1)S(1)}) custom-call(bf16[16,512,128]{2,1,0:T(8,128)(2,1)} %mid_hbm.1, bf16[8,16,64,128]{3,2,1,0:T(8,128)(2,1)} %right_hbm.1), custom_call_target="tpu_custom_call" | custom-call | flops 2147483648 | bytes 6291456 | tf_op jit(solution)/shard_map/branch_sums/pallas_call | solution.py:74
  7.9 0.1 collective-permute-start.1
  8.0 0.5 %collective-permute-start.2 = (bf16[512,128]{1,0:T(8,128)(2,1)S(1)}, bf16[512,128]{1,0:T(8,128)(2,1)S(1)}, u32[]{:S(2)}, u32[]{:S(2)}) collective-permute-start(bf16[512,128]{1,0:T(8,128)(2,1)S(1)} %get-tuple-element.11), channel_id=1, source_target_pairs={{0,1},{1,0},{2,3},{3,2},{4,5},{5,4},{6,7},{7,6},{8,9},{9,8},{10,11... | collective-permute-start | bytes 393224 | tf_op jit(solution)/shard_map/ppermute | solution.py:148
  8.5 0.1 collective-permute-start.3
  8.6 0.4 %collective-permute-start.4 = (bf16[512,128]{1,0:T(8,128)(2,1)S(1)}, bf16[512,128]{1,0:T(8,128)(2,1)S(1)}, u32[]{:S(2)}, u32[]{:S(2)}) collective-permute-start(bf16[512,128]{1,0:T(8,128)(2,1)S(1)} %get-tuple-element.13), channel_id=1, source_target_pairs={{0,1},{1,0},{2,3},{3,2},{4,5},{5,4},{6,7},{7,6},{8,9},{9,8},{10,11... | collective-permute-start | bytes 393224 | tf_op jit(solution)/shard_map/ppermute | solution.py:148
  9.0 0.3 %collective-permute-done.1.refs_2_ = bf16[512,128]{1,0:T(8,128)(2,1)S(1)} collective-permute-done((bf16[512,128]{1,0:T(8,128)(2,1)S(1)}, bf16[512,128]{1,0:T(8,128)(2,1)S(1)}, u32[]{:S(2)}, u32[]{:S(2)}) %collective-permute-start.1) | collective-permute-done | bytes 131104 | tf_op jit(solution)/shard_map/ppermute | solution.py:148
  9.3 0.2 collective-permute-done.2.refs_3_
  9.5 0.3 %collective-permute-done.3.refs_4_ = bf16[512,128]{1,0:T(8,128)(2,1)S(1)} collective-permute-done((bf16[512,128]{1,0:T(8,128)(2,1)S(1)}, bf16[512,128]{1,0:T(8,128)(2,1)S(1)}, u32[]{:S(2)}, u32[]{:S(2)}) %collective-permute-start.3) | collective-permute-done | bytes 131104 | tf_op jit(solution)/shard_map/ppermute | solution.py:148
  9.9 0.2 collective-permute-done.4.refs_5_
  10.0 0.0 collective-permute-done.refs_1_
  10.0 0.0 copy-done
  10.0 0.4 %close.1 = bf16[4,8,8,128]{3,2,1,0:T(8,128)(2,1)S(1)} custom-call(bf16[2,64,1024]{2,1,0:T(8,128)(2,1)S(1)} %copy-done, bf16[2,64,1024]{2,1,0:T(8,128)(2,1)S(1)} %collective-permute-done.refs_1_, bf16[512,128]{1,0:T(8,128)(2,1)S(1)} %collective-permute-done.1.refs_2_, bf16[512,128]{1,0:T(8,128)(2,1)S(1)} %collective-permute-done.2.refs_3_, ...), custom_call_target="tpu_custom_call" | custom-call | flops 134217728 | bytes 1048576 | tf_op jit(solution)/shard_map/close/pallas_call | solution.py:130
  10.5 12.8 %all_to_all.5 = bf16[32,8,128]{2,1,0:T(8,128)(2,1)S(1)} all-to-all(bf16[32,8,128]{2,1,0:T(8,128)(2,1)S(1)} %bitcast.2), channel_id=1, replica_groups={{31,27,23,19,15,11,7,3,30,26,22,18,14,10,6,2,29,25,21,17,13,9,5,1,28,24..., dimensions={0} | all-to-all | bytes 131072 | tf_op jit(solution)/shard_map/all_to_all | solution.py:155
  23.3 0.6 %convert_reduce_fusion = f32[8,128]{1,0:T(8,128)} fusion(bf16[32,8,128]{2,1,0:T(8,128)(2,1)S(1)} %all_to_all.5), kind=kLoop, calls=%fused_computation | loop fusion | flops 64512 | bytes 69632 | tf_op jit(solution)/shard_map/reduce_sum | solution.py:156
Async XLA Ops:
  0.0 10.0 %copy-start = (bf16[2,64,1024]{2,1,0:T(8,128)(2,1)S(1)}, bf16[2,64,1024]{2,1,0:T(8,128)(2,1)}, u32[]{:S(2)}) copy-start(bf16[2,64,1024]{2,1,0:T(8,128)(2,1)} %refs_0_.1) | copy-start | bytes 786436
  0.0 10.0 %collective-permute-start = (bf16[2,64,1024]{2,1,0:T(8,128)(2,1)}, bf16[2,64,1024]{2,1,0:T(8,128)(2,1)S(1)}, u32[]{:S(2)}, u32[]{:S(2)}) collective-permute-start(bf16[2,64,1024]{2,1,0:T(8,128)(2,1)} %refs_0_.1), channel_id=1, source_target_pairs={{0,2},{1,3},{2,0},{3,1},{4,6},{5,7},{6,4},{7,5},{8,10},{9,11},{10,... | collective-permute-start | bytes 786440 | tf_op jit(solution)/shard_map/ppermute | solution.py:148
  7.9 1.4 %collective-permute-start.1 = (bf16[512,128]{1,0:T(8,128)(2,1)S(1)}, bf16[512,128]{1,0:T(8,128)(2,1)S(1)}, u32[]{:S(2)}, u32[]{:S(2)}) collective-permute-start(bf16[512,128]{1,0:T(8,128)(2,1)S(1)} %get-tuple-element.10), channel_id=1, source_target_pairs={{0,1},{1,0},{2,3},{3,2},{4,5},{5,4},{6,7},{7,6},{8,9},{9,8},{10,11... | collective-permute-start | bytes 393224 | tf_op jit(solution)/shard_map/ppermute | solution.py:148
  8.0 1.5 %collective-permute-start.2 = (bf16[512,128]{1,0:T(8,128)(2,1)S(1)}, bf16[512,128]{1,0:T(8,128)(2,1)S(1)}, u32[]{:S(2)}, u32[]{:S(2)}) collective-permute-start(bf16[512,128]{1,0:T(8,128)(2,1)S(1)} %get-tuple-element.11), channel_id=1, source_target_pairs={{0,1},{1,0},{2,3},{3,2},{4,5},{5,4},{6,7},{7,6},{8,9},{9,8},{10,11... | collective-permute-start | bytes 393224 | tf_op jit(solution)/shard_map/ppermute | solution.py:148
  8.5 1.3 %collective-permute-start.3 = (bf16[512,128]{1,0:T(8,128)(2,1)S(1)}, bf16[512,128]{1,0:T(8,128)(2,1)S(1)}, u32[]{:S(2)}, u32[]{:S(2)}) collective-permute-start(bf16[512,128]{1,0:T(8,128)(2,1)S(1)} %get-tuple-element.12), channel_id=1, source_target_pairs={{0,1},{1,0},{2,3},{3,2},{4,5},{5,4},{6,7},{7,6},{8,9},{9,8},{10,11... | collective-permute-start | bytes 393224 | tf_op jit(solution)/shard_map/ppermute | solution.py:148
  8.6 1.5 %collective-permute-start.4 = (bf16[512,128]{1,0:T(8,128)(2,1)S(1)}, bf16[512,128]{1,0:T(8,128)(2,1)S(1)}, u32[]{:S(2)}, u32[]{:S(2)}) collective-permute-start(bf16[512,128]{1,0:T(8,128)(2,1)S(1)} %get-tuple-element.13), channel_id=1, source_target_pairs={{0,1},{1,0},{2,3},{3,2},{4,5},{5,4},{6,7},{7,6},{8,9},{9,8},{10,11... | collective-permute-start | bytes 393224 | tf_op jit(solution)/shard_map/ppermute | solution.py:148

commit v18 on v13

--- a/solution.py
+++ b/solution.py
@@ -2,6 +2,7 @@
 
 import jax
 import jax.numpy as jnp
+import numpy as np
 from jax import lax
 from jax.experimental import pallas as pl
 from jax.experimental.pallas import tpu as pltpu
@@ -93,7 +94,7 @@
     )(mid, right)
 
 
-def close_kernel(*refs):
+def close_kernel(targets, *refs):
     *more, kept_ref, out_ref = refs
     stem_refs, got_refs = more[:-kept_ref.shape[0]], more[-kept_ref.shape[0]:]
     part = None
@@ -113,30 +114,26 @@
     part = part[:, :width] + part[:, width:]
     half = part.shape[0] // 2
     total = part[:half] + turn(part[half:])
-    if len(out_ref.shape) == 2:
+    if targets is None:
         out_ref[...] = total
     else:
-        copies, cuts, rows, _ = out_ref.shape
-        for c in range(cuts):
-            for s in range(copies):
-                out_ref[s, c] = total[c * rows:(c + 1) * rows]
+        rows = out_ref.shape[1]
+        for at, c in enumerate(targets):
+            out_ref[at] = total[c * rows:(c + 1) * rows]
 
 
-def close(stems, kept, got, cuts, copies):
+def close(stems, kept, got, cuts, targets):
     rows, width = stems[0].shape[1], kept.shape[2]
     whole_tiles = rows % (8 * cuts) == 0
-    shape = (copies, cuts, rows // cuts, width) if whole_tiles else (rows, width)
+    shape = (len(targets), rows // cuts, width) if whole_tiles else (rows, width)
     out = pl.pallas_call(
-        close_kernel,
+        functools.partial(close_kernel, targets if whole_tiles else None),
         out_shape=jax.ShapeDtypeStruct(shape, jnp.float32),
         compiler_params=pltpu.CompilerParams(vmem_limit_bytes=24 * MIB),
         cost_estimate=pl.CostEstimate(flops=8 * rows * kept.size, bytes_accessed=MIB, transcendentals=0),
         name="close",
     )(*stems, *got, kept)
-    if whole_tiles:
-        return out.reshape(cuts * copies, rows // cuts, width)
-    out = out.reshape(1, cuts, -1)
-    return jnp.broadcast_to(out, (copies, cuts, out.shape[-1])).reshape(cuts * copies, -1)
+    return out if whole_tiles else out.reshape(cuts, -1)[np.array(targets)]
 
 
 def on_device(stem_tensor, mid_tensors, right_tensors):
@@ -149,9 +146,14 @@
     pieces = [stem_tensor] + [swap(stem_tensor, p) for p in range(2, stems, 2)]
     kept, *sent = branch_sums(mid_tensors, right_tensors, stems)
     got = [swap(x, 1) for x in sent]
-    spread = close(pieces, kept, got, cuts, stems)
-    parts = lax.all_to_all(spread, ("stem", "cuts"), 0, 0, tiled=True)
-    return jnp.sum(parts, axis=0).reshape(-1)
+    groups = [
+        [s * cuts + c for s in range(stems - 2 + core, -1, -2) for c in range(cuts - 1, -1, -1)] for core in range(2)
+    ]
+    targets = [at % cuts for at in groups[0]]
+    spread = close(pieces, kept, got, cuts, targets)
+    parts = lax.all_to_all(spread, ("stem", "cuts"), 0, 0, tiled=True, axis_index_groups=groups)
+    total = jnp.sum(parts, axis=0).reshape(-1)
+    return total + swap(total, 1)
 
 
 def solution(mesh):

time: 24.3 us -> 23 us (0.947)
  blocking collectives: 13.1 us -> 10.5 us
  waiting for transfers between devices: 1.03 us -> 2.18 us
    all_to_all x1, blocking collectives: 13.1 us -> 10.5 us  [on_device(): lax.all_to_all(spread, ('stem', 'cuts'), 0, 0, tiled=True, axis_index_gro...]
    ppermute x5 -> x6, waiting for transfers between devices: 1.03 us -> 2.18 us  [swap(): return lax.ppermute(x, 'stem', [(s, s ^ p) for s in range(stems)])]
    reduce_sum x1, other arithmetic: 0.63 us -> 0.02 us  [on_device(): total = jnp.sum(parts, axis=0).reshape(-1)]
    add x0 -> x1, other arithmetic: none -> 0.6 us  [on_device(): return total + swap(total, 1)]
    ppermute x5 -> x6, starting transfers between devices: 4.04 us -> 4.11 us  [swap(): return lax.ppermute(x, 'stem', [(s, s ^ p) for s in range(stems)])]
  transfers between devices with their start and end apart: 5 -> 6, of which waited for: 4 -> 5; matrix products, arithmetic and copies ran while one was open for 0% -> 0% of each run, Pallas kernels for 20% -> 22%
where the time goes in v18:
time: 23 us; the launch traced here: 22.8 us
  blocking collectives  10.5 us (46%)
  Pallas kernels  5.37 us (23%)
  starting transfers between devices  4.11 us (18%)
  waiting for transfers between devices  2.18 us (9%)
  other arithmetic  0.61 us (3%)
    all_to_all x1, blocking collectives, on_device(): lax.all_to_all(spread, ('stem', 'cuts'), 0, 0, tiled=True, axis_index_gro...  10.5 us
    pallas_call x1, Pallas kernels, branch_sums(): pl.pallas_call(functools.partial(branch_kernel, total // groups), in_spec...  4.95 us
    ppermute x6, starting transfers between devices, swap(): return lax.ppermute(x, 'stem', [(s, s ^ p) for s in range(stems)])  4.11 us
    ppermute x6, waiting for transfers between devices, swap(): return lax.ppermute(x, 'stem', [(s, s ^ p) for s in range(stems)])  2.18 us
    add x1, other arithmetic, on_device(): return total + swap(total, 1)  0.6 us
  transfers between devices with their start and end apart: 6, of which 5 were waited for; matrix products, arithmetic and copies ran while one was open for 0% of the time, Pallas kernels for 22%

profile of v18, /device:TPU:0, one launch (start us, length us, event | category | flops | bytes accessed | tf_op | source)
XLA Modules:
  0.0 22.8 jit_solution(7918996425181664290)
XLA Ops:
  0.0 0.0 copy-start
  0.0 3.0 %collective-permute-start = (bf16[2,64,1024]{2,1,0:T(8,128)(2,1)}, bf16[2,64,1024]{2,1,0:T(8,128)(2,1)S(1)}, u32[]{:S(2)}, u32[]{:S(2)}) collective-permute-start(bf16[2,64,1024]{2,1,0:T(8,128)(2,1)} %refs_0_.1), channel_id=1, source_target_pairs={{0,2},{1,3},{2,0},{3,1},{4,6},{5,7},{6,4},{7,5},{8,10},{9,11},{10,... | collective-permute-start | bytes 786440 | tf_op jit(solution)/shard_map/ppermute | solution.py:144
  3.0 4.9 %branch_sums.1 = (f32[4,512,128]{2,1,0:T(8,128)S(1)}, bf16[512,128]{1,0:T(8,128)(2,1)S(1)}, bf16[512,128]{1,0:T(8,128)(2,1)S(1)}, bf16[512,128]{1,0:T(8,128)(2,1)S(1)}, bf16[512,128]{1,0:T(8,128)(2,1)S(1)}) custom-call(bf16[16,512,128]{2,1,0:T(8,128)(2,1)} %mid_hbm.1, bf16[8,16,64,128]{3,2,1,0:T(8,128)(2,1)} %right_hbm.1), custom_call_target="tpu_custom_call" | custom-call | flops 2147483648 | bytes 6291456 | tf_op jit(solution)/shard_map/branch_sums/pallas_call | solution.py:75
  7.9 0.1 collective-permute-start.1
  8.0 0.5 %collective-permute-start.2 = (bf16[512,128]{1,0:T(8,128)(2,1)S(1)}, bf16[512,128]{1,0:T(8,128)(2,1)S(1)}, u32[]{:S(2)}, u32[]{:S(2)}) collective-permute-start(bf16[512,128]{1,0:T(8,128)(2,1)S(1)} %get-tuple-element.11), channel_id=1, source_target_pairs={{0,1},{1,0},{2,3},{3,2},{4,5},{5,4},{6,7},{7,6},{8,9},{9,8},{10,11... | collective-permute-start | bytes 393224 | tf_op jit(solution)/shard_map/ppermute | solution.py:144
  8.5 0.1 collective-permute-start.3
  8.6 0.4 %collective-permute-start.4 = (bf16[512,128]{1,0:T(8,128)(2,1)S(1)}, bf16[512,128]{1,0:T(8,128)(2,1)S(1)}, u32[]{:S(2)}, u32[]{:S(2)}) collective-permute-start(bf16[512,128]{1,0:T(8,128)(2,1)S(1)} %get-tuple-element.13), channel_id=1, source_target_pairs={{0,1},{1,0},{2,3},{3,2},{4,5},{5,4},{6,7},{7,6},{8,9},{9,8},{10,11... | collective-permute-start | bytes 393224 | tf_op jit(solution)/shard_map/ppermute | solution.py:144
  9.0 0.3 %collective-permute-done.1.refs_2_ = bf16[512,128]{1,0:T(8,128)(2,1)S(1)} collective-permute-done((bf16[512,128]{1,0:T(8,128)(2,1)S(1)}, bf16[512,128]{1,0:T(8,128)(2,1)S(1)}, u32[]{:S(2)}, u32[]{:S(2)}) %collective-permute-start.1) | collective-permute-done | bytes 131104 | tf_op jit(solution)/shard_map/ppermute | solution.py:144
  9.3 0.2 collective-permute-done.2.refs_3_
  9.5 0.3 %collective-permute-done.3.refs_4_ = bf16[512,128]{1,0:T(8,128)(2,1)S(1)} collective-permute-done((bf16[512,128]{1,0:T(8,128)(2,1)S(1)}, bf16[512,128]{1,0:T(8,128)(2,1)S(1)}, u32[]{:S(2)}, u32[]{:S(2)}) %collective-permute-start.3) | collective-permute-done | bytes 131104 | tf_op jit(solution)/shard_map/ppermute | solution.py:144
  9.9 0.2 collective-permute-done.4.refs_5_
  10.0 0.0 collective-permute-done.refs_1_
  10.0 0.0 copy-done
  10.0 0.4 %close.1 = f32[16,8,128]{2,1,0:T(8,128)S(1)} custom-call(bf16[2,64,1024]{2,1,0:T(8,128)(2,1)S(1)} %copy-done, bf16[2,64,1024]{2,1,0:T(8,128)(2,1)S(1)} %collective-permute-done.refs_1_, bf16[512,128]{1,0:T(8,128)(2,1)S(1)} %collective-permute-done.1.refs_2_, bf16[512,128]{1,0:T(8,128)(2,1)S(1)} %collective-permute-done.2.refs_3_, ...), custom_call_target="tpu_custom_call" | custom-call | flops 134217728 | bytes 1048576 | tf_op jit(solution)/shard_map/close/pallas_call | solution.py:129
  10.5 10.5 %all_to_all.5 = f32[16,8,128]{2,1,0:T(8,128)S(1)} all-to-all(f32[16,8,128]{2,1,0:T(8,128)S(1)} %close.1), channel_id=1, replica_groups={{30,26,22,18,14,10,6,2,28,24,20,16,12,8,4,0},{31,27,23,19,15,11,7,3,29,..., dimensions={0} | all-to-all | bytes 131072 | tf_op jit(solution)/shard_map/all_to_all | solution.py:154
  21.0 0.1 collective-permute-start.5
  21.0 1.2 %collective-permute-done.5 = f32[1024]{0:T(1024)S(1)} collective-permute-done((f32[1024]{0:T(1024)S(1)}, f32[1024]{0:T(1024)S(1)}, u32[]{:S(2)}, u32[]{:S(2)}) %collective-permute-start.5) | collective-permute-done | bytes 4128 | tf_op jit(solution)/shard_map/ppermute | solution.py:144
  22.2 0.6 %bitcast_add_fusion = f32[1024]{0:T(1024)} fusion(f32[1024]{0:T(1024)S(1)} %collective-permute-done.5, f32[8,128]{1,0:T(8,128)S(1)} %reduce_sum.9), kind=kLoop, calls=%fused_computation | loop fusion | flops 1024 | bytes 12288 | tf_op jit(solution)/shard_map/add | solution.py:156
  (1 shorter events, 0.0 us)
Async XLA Ops:
  0.0 10.0 %copy-start = (bf16[2,64,1024]{2,1,0:T(8,128)(2,1)S(1)}, bf16[2,64,1024]{2,1,0:T(8,128)(2,1)}, u32[]{:S(2)}) copy-start(bf16[2,64,1024]{2,1,0:T(8,128)(2,1)} %refs_0_.1) | copy-start | bytes 786436
  0.0 10.0 %collective-permute-start = (bf16[2,64,1024]{2,1,0:T(8,128)(2,1)}, bf16[2,64,1024]{2,1,0:T(8,128)(2,1)S(1)}, u32[]{:S(2)}, u32[]{:S(2)}) collective-permute-start(bf16[2,64,1024]{2,1,0:T(8,128)(2,1)} %refs_0_.1), channel_id=1, source_target_pairs={{0,2},{1,3},{2,0},{3,1},{4,6},{5,7},{6,4},{7,5},{8,10},{9,11},{10,... | collective-permute-start | bytes 786440 | tf_op jit(solution)/shard_map/ppermute | solution.py:144
  7.9 1.4 %collective-permute-start.1 = (bf16[512,128]{1,0:T(8,128)(2,1)S(1)}, bf16[512,128]{1,0:T(8,128)(2,1)S(1)}, u32[]{:S(2)}, u32[]{:S(2)}) collective-permute-start(bf16[512,128]{1,0:T(8,128)(2,1)S(1)} %get-tuple-element.10), channel_id=1, source_target_pairs={{0,1},{1,0},{2,3},{3,2},{4,5},{5,4},{6,7},{7,6},{8,9},{9,8},{10,11... | collective-permute-start | bytes 393224 | tf_op jit(solution)/shard_map/ppermute | solution.py:144
  8.0 1.5 %collective-permute-start.2 = (bf16[512,128]{1,0:T(8,128)(2,1)S(1)}, bf16[512,128]{1,0:T(8,128)(2,1)S(1)}, u32[]{:S(2)}, u32[]{:S(2)}) collective-permute-start(bf16[512,128]{1,0:T(8,128)(2,1)S(1)} %get-tuple-element.11), channel_id=1, source_target_pairs={{0,1},{1,0},{2,3},{3,2},{4,5},{5,4},{6,7},{7,6},{8,9},{9,8},{10,11... | collective-permute-start | bytes 393224 | tf_op jit(solution)/shard_map/ppermute | solution.py:144
  8.5 1.3 %collective-permute-start.3 = (bf16[512,128]{1,0:T(8,128)(2,1)S(1)}, bf16[512,128]{1,0:T(8,128)(2,1)S(1)}, u32[]{:S(2)}, u32[]{:S(2)}) collective-permute-start(bf16[512,128]{1,0:T(8,128)(2,1)S(1)} %get-tuple-element.12), channel_id=1, source_target_pairs={{0,1},{1,0},{2,3},{3,2},{4,5},{5,4},{6,7},{7,6},{8,9},{9,8},{10,11... | collective-permute-start | bytes 393224 | tf_op jit(solution)/shard_map/ppermute | solution.py:144
  8.6 1.5 %collective-permute-start.4 = (bf16[512,128]{1,0:T(8,128)(2,1)S(1)}, bf16[512,128]{1,0:T(8,128)(2,1)S(1)}, u32[]{:S(2)}, u32[]{:S(2)}) collective-permute-start(bf16[512,128]{1,0:T(8,128)(2,1)S(1)} %get-tuple-element.13), channel_id=1, source_target_pairs={{0,1},{1,0},{2,3},{3,2},{4,5},{5,4},{6,7},{7,6},{8,9},{9,8},{10,11... | collective-permute-start | bytes 393224 | tf_op jit(solution)/shard_map/ppermute | solution.py:144
  21.0 1.2 %collective-permute-start.5 = (f32[1024]{0:T(1024)S(1)}, f32[1024]{0:T(1024)S(1)}, u32[]{:S(2)}, u32[]{:S(2)}) collective-permute-start(f32[1024]{0:T(1024)S(1)} %bitcast.2), channel_id=1, source_target_pairs={{0,1},{1,0},{2,3},{3,2},{4,5},{5,4},{6,7},{7,6},{8,9},{9,8},{10,11... | collective-permute-start | bytes 12296 | tf_op jit(solution)/shard_map/ppermute | solution.py:144

commit v19 on v18

--- a/solution.py
+++ b/solution.py
@@ -146,10 +146,15 @@
     pieces = [stem_tensor] + [swap(stem_tensor, p) for p in range(2, stems, 2)]
     kept, *sent = branch_sums(mid_tensors, right_tensors, stems)
     got = [swap(x, 1) for x in sent]
-    groups = [
-        [s * cuts + c for s in range(stems - 2 + core, -1, -2) for c in range(cuts - 1, -1, -1)] for core in range(2)
-    ]
+    planes = [n // 2 if n % 2 else cuts // 2 - 1 - n // 2 for n in range(cuts // 2)]
+    groups = []
+    for group, sides in enumerate((range(stems // 2 - 1, -1, -1), range(stems // 2))):
+        groups.append([
+            (2 * side + (column + side + 1 + group) % 2) * cuts + 2 * plane + column
+            for side in sides for column in (1, 0) for plane in planes
+        ])
     targets = [at % cuts for at in groups[0]]
+    assert targets == [at % cuts for at in groups[1]]
     spread = close(pieces, kept, got, cuts, targets)
     parts = lax.all_to_all(spread, ("stem", "cuts"), 0, 0, tiled=True, axis_index_groups=groups)
     total = jnp.sum(parts, axis=0).reshape(-1)

time: 23 us -> 23.2 us (level)
    all_to_all x1, blocking collectives: 10.5 us -> 10.7 us  [on_device(): lax.all_to_all(spread, ('stem', 'cuts'), 0, 0, tiled=True, axis_index_gro...]
  transfers between devices with their start and end apart: 6 -> 6, of which waited for: 5 -> 5; matrix products, arithmetic and copies ran while one was open for 0% -> 0% of each run, Pallas kernels for 22% -> 21%
where the time goes in v19:
time: 23.2 us; the launch traced here: 23.1 us
  blocking collectives  10.7 us (46%)
  Pallas kernels  5.37 us (23%)
  starting transfers between devices  4.11 us (18%)
  waiting for transfers between devices  2.18 us (9%)
  other arithmetic  0.61 us (3%)
    all_to_all x1, blocking collectives, on_device(): lax.all_to_all(spread, ('stem', 'cuts'), 0, 0, tiled=True, axis_index_gro...  10.7 us
    pallas_call x1, Pallas kernels, branch_sums(): pl.pallas_call(functools.partial(branch_kernel, total // groups), in_spec...  4.95 us
    ppermute x6, starting transfers between devices, swap(): return lax.ppermute(x, 'stem', [(s, s ^ p) for s in range(stems)])  4.11 us
    ppermute x6, waiting for transfers between devices, swap(): return lax.ppermute(x, 'stem', [(s, s ^ p) for s in range(stems)])  2.18 us
    add x1, other arithmetic, on_device(): return total + swap(total, 1)  0.6 us
  transfers between devices with their start and end apart: 6, of which 5 were waited for; matrix products, arithmetic and copies ran while one was open for 0% of the time, Pallas kernels for 21%

profile of v19, /device:TPU:0, one launch (start us, length us, event | category | flops | bytes accessed | tf_op | source)
XLA Modules:
  0.0 23.1 jit_solution(4452897835586634986)
XLA Ops:
  0.0 0.0 copy-start
  0.0 3.0 %collective-permute-start = (bf16[2,64,1024]{2,1,0:T(8,128)(2,1)}, bf16[2,64,1024]{2,1,0:T(8,128)(2,1)S(1)}, u32[]{:S(2)}, u32[]{:S(2)}) collective-permute-start(bf16[2,64,1024]{2,1,0:T(8,128)(2,1)} %refs_0_.1), channel_id=1, source_target_pairs={{0,2},{1,3},{2,0},{3,1},{4,6},{5,7},{6,4},{7,5},{8,10},{9,11},{10,... | collective-permute-start | bytes 786440 | tf_op jit(solution)/shard_map/ppermute | solution.py:144
  3.0 4.9 %branch_sums.1 = (f32[4,512,128]{2,1,0:T(8,128)S(1)}, bf16[512,128]{1,0:T(8,128)(2,1)S(1)}, bf16[512,128]{1,0:T(8,128)(2,1)S(1)}, bf16[512,128]{1,0:T(8,128)(2,1)S(1)}, bf16[512,128]{1,0:T(8,128)(2,1)S(1)}) custom-call(bf16[16,512,128]{2,1,0:T(8,128)(2,1)} %mid_hbm.1, bf16[8,16,64,128]{3,2,1,0:T(8,128)(2,1)} %right_hbm.1), custom_call_target="tpu_custom_call" | custom-call | flops 2147483648 | bytes 6291456 | tf_op jit(solution)/shard_map/branch_sums/pallas_call | solution.py:75
  7.9 0.1 collective-permute-start.1
  8.0 0.5 %collective-permute-start.2 = (bf16[512,128]{1,0:T(8,128)(2,1)S(1)}, bf16[512,128]{1,0:T(8,128)(2,1)S(1)}, u32[]{:S(2)}, u32[]{:S(2)}) collective-permute-start(bf16[512,128]{1,0:T(8,128)(2,1)S(1)} %get-tuple-element.11), channel_id=1, source_target_pairs={{0,1},{1,0},{2,3},{3,2},{4,5},{5,4},{6,7},{7,6},{8,9},{9,8},{10,11... | collective-permute-start | bytes 393224 | tf_op jit(solution)/shard_map/ppermute | solution.py:144
  8.5 0.1 collective-permute-start.3
  8.6 0.4 %collective-permute-start.4 = (bf16[512,128]{1,0:T(8,128)(2,1)S(1)}, bf16[512,128]{1,0:T(8,128)(2,1)S(1)}, u32[]{:S(2)}, u32[]{:S(2)}) collective-permute-start(bf16[512,128]{1,0:T(8,128)(2,1)S(1)} %get-tuple-element.13), channel_id=1, source_target_pairs={{0,1},{1,0},{2,3},{3,2},{4,5},{5,4},{6,7},{7,6},{8,9},{9,8},{10,11... | collective-permute-start | bytes 393224 | tf_op jit(solution)/shard_map/ppermute | solution.py:144
  9.0 0.3 %collective-permute-done.1.refs_2_ = bf16[512,128]{1,0:T(8,128)(2,1)S(1)} collective-permute-done((bf16[512,128]{1,0:T(8,128)(2,1)S(1)}, bf16[512,128]{1,0:T(8,128)(2,1)S(1)}, u32[]{:S(2)}, u32[]{:S(2)}) %collective-permute-start.1) | collective-permute-done | bytes 131104 | tf_op jit(solution)/shard_map/ppermute | solution.py:144
  9.3 0.2 collective-permute-done.2.refs_3_
  9.5 0.3 %collective-permute-done.3.refs_4_ = bf16[512,128]{1,0:T(8,128)(2,1)S(1)} collective-permute-done((bf16[512,128]{1,0:T(8,128)(2,1)S(1)}, bf16[512,128]{1,0:T(8,128)(2,1)S(1)}, u32[]{:S(2)}, u32[]{:S(2)}) %collective-permute-start.3) | collective-permute-done | bytes 131104 | tf_op jit(solution)/shard_map/ppermute | solution.py:144
  9.9 0.2 collective-permute-done.4.refs_5_
  10.0 0.0 collective-permute-done.refs_1_
  10.0 0.0 copy-done
  10.0 0.4 %close.1 = f32[16,8,128]{2,1,0:T(8,128)S(1)} custom-call(bf16[2,64,1024]{2,1,0:T(8,128)(2,1)S(1)} %copy-done, bf16[2,64,1024]{2,1,0:T(8,128)(2,1)S(1)} %collective-permute-done.refs_1_, bf16[512,128]{1,0:T(8,128)(2,1)S(1)} %collective-permute-done.1.refs_2_, bf16[512,128]{1,0:T(8,128)(2,1)S(1)} %collective-permute-done.2.refs_3_, ...), custom_call_target="tpu_custom_call" | custom-call | flops 134217728 | bytes 1048576 | tf_op jit(solution)/shard_map/close/pallas_call | solution.py:129
  10.5 10.7 %all_to_all.5 = f32[16,8,128]{2,1,0:T(8,128)S(1)} all-to-all(f32[16,8,128]{2,1,0:T(8,128)S(1)} %close.1), channel_id=1, replica_groups={{31,7,23,15,26,2,18,10,28,4,20,12,25,1,17,9},{29,5,21,13,24,0,16,8,30,6..., dimensions={0} | all-to-all | bytes 131072 | tf_op jit(solution)/shard_map/all_to_all | solution.py:159
  21.2 0.1 collective-permute-start.5
  21.3 1.2 %collective-permute-done.5 = f32[1024]{0:T(1024)S(1)} collective-permute-done((f32[1024]{0:T(1024)S(1)}, f32[1024]{0:T(1024)S(1)}, u32[]{:S(2)}, u32[]{:S(2)}) %collective-permute-start.5) | collective-permute-done | bytes 4128 | tf_op jit(solution)/shard_map/ppermute | solution.py:144
  22.5 0.6 %bitcast_add_fusion = f32[1024]{0:T(1024)} fusion(f32[1024]{0:T(1024)S(1)} %collective-permute-done.5, f32[8,128]{1,0:T(8,128)S(1)} %reduce_sum.9), kind=kLoop, calls=%fused_computation | loop fusion | flops 1024 | bytes 12288 | tf_op jit(solution)/shard_map/add | solution.py:161
  (1 shorter events, 0.0 us)
Async XLA Ops:
  0.0 10.0 %copy-start = (bf16[2,64,1024]{2,1,0:T(8,128)(2,1)S(1)}, bf16[2,64,1024]{2,1,0:T(8,128)(2,1)}, u32[]{:S(2)}) copy-start(bf16[2,64,1024]{2,1,0:T(8,128)(2,1)} %refs_0_.1) | copy-start | bytes 786436
  0.0 10.0 %collective-permute-start = (bf16[2,64,1024]{2,1,0:T(8,128)(2,1)}, bf16[2,64,1024]{2,1,0:T(8,128)(2,1)S(1)}, u32[]{:S(2)}, u32[]{:S(2)}) collective-permute-start(bf16[2,64,1024]{2,1,0:T(8,128)(2,1)} %refs_0_.1), channel_id=1, source_target_pairs={{0,2},{1,3},{2,0},{3,1},{4,6},{5,7},{6,4},{7,5},{8,10},{9,11},{10,... | collective-permute-start | bytes 786440 | tf_op jit(solution)/shard_map/ppermute | solution.py:144
  7.9 1.4 %collective-permute-start.1 = (bf16[512,128]{1,0:T(8,128)(2,1)S(1)}, bf16[512,128]{1,0:T(8,128)(2,1)S(1)}, u32[]{:S(2)}, u32[]{:S(2)}) collective-permute-start(bf16[512,128]{1,0:T(8,128)(2,1)S(1)} %get-tuple-element.10), channel_id=1, source_target_pairs={{0,1},{1,0},{2,3},{3,2},{4,5},{5,4},{6,7},{7,6},{8,9},{9,8},{10,11... | collective-permute-start | bytes 393224 | tf_op jit(solution)/shard_map/ppermute | solution.py:144
  8.0 1.5 %collective-permute-start.2 = (bf16[512,128]{1,0:T(8,128)(2,1)S(1)}, bf16[512,128]{1,0:T(8,128)(2,1)S(1)}, u32[]{:S(2)}, u32[]{:S(2)}) collective-permute-start(bf16[512,128]{1,0:T(8,128)(2,1)S(1)} %get-tuple-element.11), channel_id=1, source_target_pairs={{0,1},{1,0},{2,3},{3,2},{4,5},{5,4},{6,7},{7,6},{8,9},{9,8},{10,11... | collective-permute-start | bytes 393224 | tf_op jit(solution)/shard_map/ppermute | solution.py:144
  8.5 1.3 %collective-permute-start.3 = (bf16[512,128]{1,0:T(8,128)(2,1)S(1)}, bf16[512,128]{1,0:T(8,128)(2,1)S(1)}, u32[]{:S(2)}, u32[]{:S(2)}) collective-permute-start(bf16[512,128]{1,0:T(8,128)(2,1)S(1)} %get-tuple-element.12), channel_id=1, source_target_pairs={{0,1},{1,0},{2,3},{3,2},{4,5},{5,4},{6,7},{7,6},{8,9},{9,8},{10,11... | collective-permute-start | bytes 393224 | tf_op jit(solution)/shard_map/ppermute | solution.py:144
  8.6 1.5 %collective-permute-start.4 = (bf16[512,128]{1,0:T(8,128)(2,1)S(1)}, bf16[512,128]{1,0:T(8,128)(2,1)S(1)}, u32[]{:S(2)}, u32[]{:S(2)}) collective-permute-start(bf16[512,128]{1,0:T(8,128)(2,1)S(1)} %get-tuple-element.13), channel_id=1, source_target_pairs={{0,1},{1,0},{2,3},{3,2},{4,5},{5,4},{6,7},{7,6},{8,9},{9,8},{10,11... | collective-permute-start | bytes 393224 | tf_op jit(solution)/shard_map/ppermute | solution.py:144
  21.2 1.2 %collective-permute-start.5 = (f32[1024]{0:T(1024)S(1)}, f32[1024]{0:T(1024)S(1)}, u32[]{:S(2)}, u32[]{:S(2)}) collective-permute-start(f32[1024]{0:T(1024)S(1)} %bitcast.2), channel_id=1, source_target_pairs={{0,1},{1,0},{2,3},{3,2},{4,5},{5,4},{6,7},{7,6},{8,9},{9,8},{10,11... | collective-permute-start | bytes 12296 | tf_op jit(solution)/shard_map/ppermute | solution.py:144

commit v20 on v19

--- a/solution.py
+++ b/solution.py
@@ -146,12 +146,12 @@
     pieces = [stem_tensor] + [swap(stem_tensor, p) for p in range(2, stems, 2)]
     kept, *sent = branch_sums(mid_tensors, right_tensors, stems)
     got = [swap(x, 1) for x in sent]
-    planes = [n // 2 if n % 2 else cuts // 2 - 1 - n // 2 for n in range(cuts // 2)]
+    planes = [cuts // 2 - 1, *range(cuts // 2 - 1)]
     groups = []
     for group, sides in enumerate((range(stems // 2 - 1, -1, -1), range(stems // 2))):
         groups.append([
             (2 * side + (column + side + 1 + group) % 2) * cuts + 2 * plane + column
-            for side in sides for column in (1, 0) for plane in planes
+            for plane in planes for side in sides for column in (1, 0)
         ])
     targets = [at % cuts for at in groups[0]]
     assert targets == [at % cuts for at in groups[1]]

time: 23.2 us -> 23.1 us (level)
  transfers between devices with their start and end apart: 6 -> 6, of which waited for: 5 -> 5; matrix products, arithmetic and copies ran while one was open for 0% -> 0% of each run, Pallas kernels for 21% -> 22%
where the time goes in v20:
time: 23.1 us; the launch traced here: 23 us
  blocking collectives  10.6 us (46%)
  Pallas kernels  5.37 us (23%)
  starting transfers between devices  4.11 us (18%)
  waiting for transfers between devices  2.18 us (9%)
  other arithmetic  0.61 us (3%)
    all_to_all x1, blocking collectives, on_device(): lax.all_to_all(spread, ('stem', 'cuts'), 0, 0, tiled=True, axis_index_gro...  10.6 us
    pallas_call x1, Pallas kernels, branch_sums(): pl.pallas_call(functools.partial(branch_kernel, total // groups), in_spec...  4.95 us
    ppermute x6, starting transfers between devices, swap(): return lax.ppermute(x, 'stem', [(s, s ^ p) for s in range(stems)])  4.11 us
    ppermute x6, waiting for transfers between devices, swap(): return lax.ppermute(x, 'stem', [(s, s ^ p) for s in range(stems)])  2.18 us
    add x1, other arithmetic, on_device(): return total + swap(total, 1)  0.6 us
  transfers between devices with their start and end apart: 6, of which 5 were waited for; matrix products, arithmetic and copies ran while one was open for 0% of the time, Pallas kernels for 22%

profile of v20, /device:TPU:0, one launch (start us, length us, event | category | flops | bytes accessed | tf_op | source)
XLA Modules:
  0.0 23.0 jit_solution(3563526528092275881)
XLA Ops:
  0.0 0.0 copy-start
  0.0 3.0 %collective-permute-start = (bf16[2,64,1024]{2,1,0:T(8,128)(2,1)}, bf16[2,64,1024]{2,1,0:T(8,128)(2,1)S(1)}, u32[]{:S(2)}, u32[]{:S(2)}) collective-permute-start(bf16[2,64,1024]{2,1,0:T(8,128)(2,1)} %refs_0_.1), channel_id=1, source_target_pairs={{0,2},{1,3},{2,0},{3,1},{4,6},{5,7},{6,4},{7,5},{8,10},{9,11},{10,... | collective-permute-start | bytes 786440 | tf_op jit(solution)/shard_map/ppermute | solution.py:144
  3.0 4.9 %branch_sums.1 = (f32[4,512,128]{2,1,0:T(8,128)S(1)}, bf16[512,128]{1,0:T(8,128)(2,1)S(1)}, bf16[512,128]{1,0:T(8,128)(2,1)S(1)}, bf16[512,128]{1,0:T(8,128)(2,1)S(1)}, bf16[512,128]{1,0:T(8,128)(2,1)S(1)}) custom-call(bf16[16,512,128]{2,1,0:T(8,128)(2,1)} %mid_hbm.1, bf16[8,16,64,128]{3,2,1,0:T(8,128)(2,1)} %right_hbm.1), custom_call_target="tpu_custom_call" | custom-call | flops 2147483648 | bytes 6291456 | tf_op jit(solution)/shard_map/branch_sums/pallas_call | solution.py:75
  7.9 0.1 collective-permute-start.1
  8.0 0.5 %collective-permute-start.2 = (bf16[512,128]{1,0:T(8,128)(2,1)S(1)}, bf16[512,128]{1,0:T(8,128)(2,1)S(1)}, u32[]{:S(2)}, u32[]{:S(2)}) collective-permute-start(bf16[512,128]{1,0:T(8,128)(2,1)S(1)} %get-tuple-element.11), channel_id=1, source_target_pairs={{0,1},{1,0},{2,3},{3,2},{4,5},{5,4},{6,7},{7,6},{8,9},{9,8},{10,11... | collective-permute-start | bytes 393224 | tf_op jit(solution)/shard_map/ppermute | solution.py:144
  8.5 0.1 collective-permute-start.3
  8.6 0.4 %collective-permute-start.4 = (bf16[512,128]{1,0:T(8,128)(2,1)S(1)}, bf16[512,128]{1,0:T(8,128)(2,1)S(1)}, u32[]{:S(2)}, u32[]{:S(2)}) collective-permute-start(bf16[512,128]{1,0:T(8,128)(2,1)S(1)} %get-tuple-element.13), channel_id=1, source_target_pairs={{0,1},{1,0},{2,3},{3,2},{4,5},{5,4},{6,7},{7,6},{8,9},{9,8},{10,11... | collective-permute-start | bytes 393224 | tf_op jit(solution)/shard_map/ppermute | solution.py:144
  9.0 0.3 %collective-permute-done.1.refs_2_ = bf16[512,128]{1,0:T(8,128)(2,1)S(1)} collective-permute-done((bf16[512,128]{1,0:T(8,128)(2,1)S(1)}, bf16[512,128]{1,0:T(8,128)(2,1)S(1)}, u32[]{:S(2)}, u32[]{:S(2)}) %collective-permute-start.1) | collective-permute-done | bytes 131104 | tf_op jit(solution)/shard_map/ppermute | solution.py:144
  9.3 0.2 collective-permute-done.2.refs_3_
  9.5 0.3 %collective-permute-done.3.refs_4_ = bf16[512,128]{1,0:T(8,128)(2,1)S(1)} collective-permute-done((bf16[512,128]{1,0:T(8,128)(2,1)S(1)}, bf16[512,128]{1,0:T(8,128)(2,1)S(1)}, u32[]{:S(2)}, u32[]{:S(2)}) %collective-permute-start.3) | collective-permute-done | bytes 131104 | tf_op jit(solution)/shard_map/ppermute | solution.py:144
  9.9 0.2 collective-permute-done.4.refs_5_
  10.0 0.0 collective-permute-done.refs_1_
  10.0 0.0 copy-done
  10.0 0.4 %close.1 = f32[16,8,128]{2,1,0:T(8,128)S(1)} custom-call(bf16[2,64,1024]{2,1,0:T(8,128)(2,1)S(1)} %copy-done, bf16[2,64,1024]{2,1,0:T(8,128)(2,1)S(1)} %collective-permute-done.refs_1_, bf16[512,128]{1,0:T(8,128)(2,1)S(1)} %collective-permute-done.1.refs_2_, bf16[512,128]{1,0:T(8,128)(2,1)S(1)} %collective-permute-done.2.refs_3_, ...), custom_call_target="tpu_custom_call" | custom-call | flops 134217728 | bytes 1048576 | tf_op jit(solution)/shard_map/close/pallas_call | solution.py:129
  10.5 10.6 %all_to_all.5 = f32[16,8,128]{2,1,0:T(8,128)S(1)} all-to-all(f32[16,8,128]{2,1,0:T(8,128)S(1)} %close.1), channel_id=1, replica_groups={{31,26,28,25,7,2,4,1,15,10,12,9,23,18,20,17},{29,24,30,27,5,0,6,3,13,8,..., dimensions={0} | all-to-all | bytes 131072 | tf_op jit(solution)/shard_map/all_to_all | solution.py:159
  21.1 0.1 collective-permute-start.5
  21.2 1.2 %collective-permute-done.5 = f32[1024]{0:T(1024)S(1)} collective-permute-done((f32[1024]{0:T(1024)S(1)}, f32[1024]{0:T(1024)S(1)}, u32[]{:S(2)}, u32[]{:S(2)}) %collective-permute-start.5) | collective-permute-done | bytes 4128 | tf_op jit(solution)/shard_map/ppermute | solution.py:144
  22.4 0.6 %bitcast_add_fusion = f32[1024]{0:T(1024)} fusion(f32[1024]{0:T(1024)S(1)} %collective-permute-done.5, f32[8,128]{1,0:T(8,128)S(1)} %reduce_sum.9), kind=kLoop, calls=%fused_computation | loop fusion | flops 1024 | bytes 12288 | tf_op jit(solution)/shard_map/add | solution.py:161
  (1 shorter events, 0.0 us)
Async XLA Ops:
  0.0 10.0 %copy-start = (bf16[2,64,1024]{2,1,0:T(8,128)(2,1)S(1)}, bf16[2,64,1024]{2,1,0:T(8,128)(2,1)}, u32[]{:S(2)}) copy-start(bf16[2,64,1024]{2,1,0:T(8,128)(2,1)} %refs_0_.1) | copy-start | bytes 786436
  0.0 10.0 %collective-permute-start = (bf16[2,64,1024]{2,1,0:T(8,128)(2,1)}, bf16[2,64,1024]{2,1,0:T(8,128)(2,1)S(1)}, u32[]{:S(2)}, u32[]{:S(2)}) collective-permute-start(bf16[2,64,1024]{2,1,0:T(8,128)(2,1)} %refs_0_.1), channel_id=1, source_target_pairs={{0,2},{1,3},{2,0},{3,1},{4,6},{5,7},{6,4},{7,5},{8,10},{9,11},{10,... | collective-permute-start | bytes 786440 | tf_op jit(solution)/shard_map/ppermute | solution.py:144
  7.9 1.4 %collective-permute-start.1 = (bf16[512,128]{1,0:T(8,128)(2,1)S(1)}, bf16[512,128]{1,0:T(8,128)(2,1)S(1)}, u32[]{:S(2)}, u32[]{:S(2)}) collective-permute-start(bf16[512,128]{1,0:T(8,128)(2,1)S(1)} %get-tuple-element.10), channel_id=1, source_target_pairs={{0,1},{1,0},{2,3},{3,2},{4,5},{5,4},{6,7},{7,6},{8,9},{9,8},{10,11... | collective-permute-start | bytes 393224 | tf_op jit(solution)/shard_map/ppermute | solution.py:144
  8.0 1.5 %collective-permute-start.2 = (bf16[512,128]{1,0:T(8,128)(2,1)S(1)}, bf16[512,128]{1,0:T(8,128)(2,1)S(1)}, u32[]{:S(2)}, u32[]{:S(2)}) collective-permute-start(bf16[512,128]{1,0:T(8,128)(2,1)S(1)} %get-tuple-element.11), channel_id=1, source_target_pairs={{0,1},{1,0},{2,3},{3,2},{4,5},{5,4},{6,7},{7,6},{8,9},{9,8},{10,11... | collective-permute-start | bytes 393224 | tf_op jit(solution)/shard_map/ppermute | solution.py:144
  8.5 1.3 %collective-permute-start.3 = (bf16[512,128]{1,0:T(8,128)(2,1)S(1)}, bf16[512,128]{1,0:T(8,128)(2,1)S(1)}, u32[]{:S(2)}, u32[]{:S(2)}) collective-permute-start(bf16[512,128]{1,0:T(8,128)(2,1)S(1)} %get-tuple-element.12), channel_id=1, source_target_pairs={{0,1},{1,0},{2,3},{3,2},{4,5},{5,4},{6,7},{7,6},{8,9},{9,8},{10,11... | collective-permute-start | bytes 393224 | tf_op jit(solution)/shard_map/ppermute | solution.py:144
  8.6 1.5 %collective-permute-start.4 = (bf16[512,128]{1,0:T(8,128)(2,1)S(1)}, bf16[512,128]{1,0:T(8,128)(2,1)S(1)}, u32[]{:S(2)}, u32[]{:S(2)}) collective-permute-start(bf16[512,128]{1,0:T(8,128)(2,1)S(1)} %get-tuple-element.13), channel_id=1, source_target_pairs={{0,1},{1,0},{2,3},{3,2},{4,5},{5,4},{6,7},{7,6},{8,9},{9,8},{10,11... | collective-permute-start | bytes 393224 | tf_op jit(solution)/shard_map/ppermute | solution.py:144
  21.1 1.2 %collective-permute-start.5 = (f32[1024]{0:T(1024)S(1)}, f32[1024]{0:T(1024)S(1)}, u32[]{:S(2)}, u32[]{:S(2)}) collective-permute-start(f32[1024]{0:T(1024)S(1)} %bitcast.2), channel_id=1, source_target_pairs={{0,1},{1,0},{2,3},{3,2},{4,5},{5,4},{6,7},{7,6},{8,9},{9,8},{10,11... | collective-permute-start | bytes 12296 | tf_op jit(solution)/shard_map/ppermute | solution.py:144

commit v21 on v19

--- a/solution.py
+++ b/solution.py
@@ -119,7 +119,7 @@
     else:
         rows = out_ref.shape[1]
         for at, c in enumerate(targets):
-            out_ref[at] = total[c * rows:(c + 1) * rows]
+            out_ref[at] = total[c * rows:(c + 1) * rows].astype(out_ref.dtype)
 
 
 def close(stems, kept, got, cuts, targets):
@@ -128,7 +128,7 @@
     shape = (len(targets), rows // cuts, width) if whole_tiles else (rows, width)
     out = pl.pallas_call(
         functools.partial(close_kernel, targets if whole_tiles else None),
-        out_shape=jax.ShapeDtypeStruct(shape, jnp.float32),
+        out_shape=jax.ShapeDtypeStruct(shape, jnp.bfloat16 if whole_tiles else jnp.float32),
         compiler_params=pltpu.CompilerParams(vmem_limit_bytes=24 * MIB),
         cost_estimate=pl.CostEstimate(flops=8 * rows * kept.size, bytes_accessed=MIB, transcendentals=0),
         name="close",
@@ -157,7 +157,7 @@
     assert targets == [at % cuts for at in groups[1]]
     spread = close(pieces, kept, got, cuts, targets)
     parts = lax.all_to_all(spread, ("stem", "cuts"), 0, 0, tiled=True, axis_index_groups=groups)
-    total = jnp.sum(parts, axis=0).reshape(-1)
+    total = jnp.sum(parts.astype(jnp.float32), axis=0).reshape(-1)
     return total + swap(total, 1)
 
 

time: 23.2 us -> 22.9 us (0.987)
  blocking collectives: 10.7 us -> 10.4 us
    all_to_all x1, blocking collectives: 10.7 us -> 10.4 us  [on_device(): lax.all_to_all(spread, ('stem', 'cuts'), 0, 0, tiled=True, axis_index_gro...]
  transfers between devices with their start and end apart: 6 -> 6, of which waited for: 5 -> 5; matrix products, arithmetic and copies ran while one was open for 0% -> 0% of each run, Pallas kernels for 21% -> 22%
where the time goes in v21:
time: 22.9 us; the launch traced here: 22.7 us
  blocking collectives  10.4 us (45%)
  Pallas kernels  5.38 us (23%)
  starting transfers between devices  4.11 us (18%)
  waiting for transfers between devices  2.18 us (10%)
  other arithmetic  0.61 us (3%)
    all_to_all x1, blocking collectives, on_device(): lax.all_to_all(spread, ('stem', 'cuts'), 0, 0, tiled=True, axis_index_gro...  10.4 us
    pallas_call x1, Pallas kernels, branch_sums(): pl.pallas_call(functools.partial(branch_kernel, total // groups), in_spec...  4.95 us
    ppermute x6, starting transfers between devices, swap(): return lax.ppermute(x, 'stem', [(s, s ^ p) for s in range(stems)])  4.11 us
    ppermute x6, waiting for transfers between devices, swap(): return lax.ppermute(x, 'stem', [(s, s ^ p) for s in range(stems)])  2.18 us
    add x1, other arithmetic, on_device(): return total + swap(total, 1)  0.6 us
  transfers between devices with their start and end apart: 6, of which 5 were waited for; matrix products, arithmetic and copies ran while one was open for 0% of the time, Pallas kernels for 22%

profile of v21, /device:TPU:0, one launch (start us, length us, event | category | flops | bytes accessed | tf_op | source)
XLA Modules:
  0.0 22.7 jit_solution(979932182950428052)
XLA Ops:
  0.0 0.0 copy-start
  0.0 3.0 %collective-permute-start = (bf16[2,64,1024]{2,1,0:T(8,128)(2,1)}, bf16[2,64,1024]{2,1,0:T(8,128)(2,1)S(1)}, u32[]{:S(2)}, u32[]{:S(2)}) collective-permute-start(bf16[2,64,1024]{2,1,0:T(8,128)(2,1)} %refs_0_.1), channel_id=1, source_target_pairs={{0,2},{1,3},{2,0},{3,1},{4,6},{5,7},{6,4},{7,5},{8,10},{9,11},{10,... | collective-permute-start | bytes 786440 | tf_op jit(solution)/shard_map/ppermute | solution.py:144
  3.0 4.9 %branch_sums.1 = (f32[4,512,128]{2,1,0:T(8,128)S(1)}, bf16[512,128]{1,0:T(8,128)(2,1)S(1)}, bf16[512,128]{1,0:T(8,128)(2,1)S(1)}, bf16[512,128]{1,0:T(8,128)(2,1)S(1)}, bf16[512,128]{1,0:T(8,128)(2,1)S(1)}) custom-call(bf16[16,512,128]{2,1,0:T(8,128)(2,1)} %mid_hbm.1, bf16[8,16,64,128]{3,2,1,0:T(8,128)(2,1)} %right_hbm.1), custom_call_target="tpu_custom_call" | custom-call | flops 2147483648 | bytes 6291456 | tf_op jit(solution)/shard_map/branch_sums/pallas_call | solution.py:75
  7.9 0.1 collective-permute-start.1
  8.0 0.5 %collective-permute-start.2 = (bf16[512,128]{1,0:T(8,128)(2,1)S(1)}, bf16[512,128]{1,0:T(8,128)(2,1)S(1)}, u32[]{:S(2)}, u32[]{:S(2)}) collective-permute-start(bf16[512,128]{1,0:T(8,128)(2,1)S(1)} %get-tuple-element.11), channel_id=1, source_target_pairs={{0,1},{1,0},{2,3},{3,2},{4,5},{5,4},{6,7},{7,6},{8,9},{9,8},{10,11... | collective-permute-start | bytes 393224 | tf_op jit(solution)/shard_map/ppermute | solution.py:144
  8.5 0.1 collective-permute-start.3
  8.6 0.4 %collective-permute-start.4 = (bf16[512,128]{1,0:T(8,128)(2,1)S(1)}, bf16[512,128]{1,0:T(8,128)(2,1)S(1)}, u32[]{:S(2)}, u32[]{:S(2)}) collective-permute-start(bf16[512,128]{1,0:T(8,128)(2,1)S(1)} %get-tuple-element.13), channel_id=1, source_target_pairs={{0,1},{1,0},{2,3},{3,2},{4,5},{5,4},{6,7},{7,6},{8,9},{9,8},{10,11... | collective-permute-start | bytes 393224 | tf_op jit(solution)/shard_map/ppermute | solution.py:144
  9.0 0.3 %collective-permute-done.1.refs_2_ = bf16[512,128]{1,0:T(8,128)(2,1)S(1)} collective-permute-done((bf16[512,128]{1,0:T(8,128)(2,1)S(1)}, bf16[512,128]{1,0:T(8,128)(2,1)S(1)}, u32[]{:S(2)}, u32[]{:S(2)}) %collective-permute-start.1) | collective-permute-done | bytes 131104 | tf_op jit(solution)/shard_map/ppermute | solution.py:144
  9.3 0.2 collective-permute-done.2.refs_3_
  9.5 0.3 %collective-permute-done.3.refs_4_ = bf16[512,128]{1,0:T(8,128)(2,1)S(1)} collective-permute-done((bf16[512,128]{1,0:T(8,128)(2,1)S(1)}, bf16[512,128]{1,0:T(8,128)(2,1)S(1)}, u32[]{:S(2)}, u32[]{:S(2)}) %collective-permute-start.3) | collective-permute-done | bytes 131104 | tf_op jit(solution)/shard_map/ppermute | solution.py:144
  9.9 0.2 collective-permute-done.4.refs_5_
  10.0 0.0 collective-permute-done.refs_1_
  10.0 0.0 copy-done
  10.0 0.4 %close.1 = bf16[16,8,128]{2,1,0:T(8,128)(2,1)S(1)} custom-call(bf16[2,64,1024]{2,1,0:T(8,128)(2,1)S(1)} %copy-done, bf16[2,64,1024]{2,1,0:T(8,128)(2,1)S(1)} %collective-permute-done.refs_1_, bf16[512,128]{1,0:T(8,128)(2,1)S(1)} %collective-permute-done.1.refs_2_, bf16[512,128]{1,0:T(8,128)(2,1)S(1)} %collective-permute-done.2.refs_3_, ...), custom_call_target="tpu_custom_call" | custom-call | flops 134217728 | bytes 1048576 | tf_op jit(solution)/shard_map/close/pallas_call | solution.py:129
  10.5 10.4 %all_to_all.5 = bf16[16,8,128]{2,1,0:T(8,128)(2,1)S(1)} all-to-all(bf16[16,8,128]{2,1,0:T(8,128)(2,1)S(1)} %close.1), channel_id=1, replica_groups={{31,7,23,15,26,2,18,10,28,4,20,12,25,1,17,9},{29,5,21,13,24,0,16,8,30,6..., dimensions={0} | all-to-all | bytes 65536 | tf_op jit(solution)/shard_map/all_to_all | solution.py:159
  20.9 0.1 collective-permute-start.5
  21.0 1.2 %collective-permute-done.5 = f32[1024]{0:T(1024)S(1)} collective-permute-done((f32[1024]{0:T(1024)S(1)}, f32[1024]{0:T(1024)S(1)}, u32[]{:S(2)}, u32[]{:S(2)}) %collective-permute-start.5) | collective-permute-done | bytes 4128 | tf_op jit(solution)/shard_map/ppermute | solution.py:144
  22.1 0.6 %bitcast_add_fusion = f32[1024]{0:T(1024)} fusion(f32[1024]{0:T(1024)S(1)} %collective-permute-done.5, f32[8,128]{1,0:T(8,128)S(1)} %convert_reduce_fusion), kind=kLoop, calls=%fused_computation.1 | loop fusion | flops 1024 | bytes 12288 | tf_op jit(solution)/shard_map/add | solution.py:161
  (1 shorter events, 0.0 us)
Async XLA Ops:
  0.0 10.0 %copy-start = (bf16[2,64,1024]{2,1,0:T(8,128)(2,1)S(1)}, bf16[2,64,1024]{2,1,0:T(8,128)(2,1)}, u32[]{:S(2)}) copy-start(bf16[2,64,1024]{2,1,0:T(8,128)(2,1)} %refs_0_.1) | copy-start | bytes 786436
  0.0 10.0 %collective-permute-start = (bf16[2,64,1024]{2,1,0:T(8,128)(2,1)}, bf16[2,64,1024]{2,1,0:T(8,128)(2,1)S(1)}, u32[]{:S(2)}, u32[]{:S(2)}) collective-permute-start(bf16[2,64,1024]{2,1,0:T(8,128)(2,1)} %refs_0_.1), channel_id=1, source_target_pairs={{0,2},{1,3},{2,0},{3,1},{4,6},{5,7},{6,4},{7,5},{8,10},{9,11},{10,... | collective-permute-start | bytes 786440 | tf_op jit(solution)/shard_map/ppermute | solution.py:144
  7.9 1.4 %collective-permute-start.1 = (bf16[512,128]{1,0:T(8,128)(2,1)S(1)}, bf16[512,128]{1,0:T(8,128)(2,1)S(1)}, u32[]{:S(2)}, u32[]{:S(2)}) collective-permute-start(bf16[512,128]{1,0:T(8,128)(2,1)S(1)} %get-tuple-element.10), channel_id=1, source_target_pairs={{0,1},{1,0},{2,3},{3,2},{4,5},{5,4},{6,7},{7,6},{8,9},{9,8},{10,11... | collective-permute-start | bytes 393224 | tf_op jit(solution)/shard_map/ppermute | solution.py:144
  8.0 1.5 %collective-permute-start.2 = (bf16[512,128]{1,0:T(8,128)(2,1)S(1)}, bf16[512,128]{1,0:T(8,128)(2,1)S(1)}, u32[]{:S(2)}, u32[]{:S(2)}) collective-permute-start(bf16[512,128]{1,0:T(8,128)(2,1)S(1)} %get-tuple-element.11), channel_id=1, source_target_pairs={{0,1},{1,0},{2,3},{3,2},{4,5},{5,4},{6,7},{7,6},{8,9},{9,8},{10,11... | collective-permute-start | bytes 393224 | tf_op jit(solution)/shard_map/ppermute | solution.py:144
  8.5 1.3 %collective-permute-start.3 = (bf16[512,128]{1,0:T(8,128)(2,1)S(1)}, bf16[512,128]{1,0:T(8,128)(2,1)S(1)}, u32[]{:S(2)}, u32[]{:S(2)}) collective-permute-start(bf16[512,128]{1,0:T(8,128)(2,1)S(1)} %get-tuple-element.12), channel_id=1, source_target_pairs={{0,1},{1,0},{2,3},{3,2},{4,5},{5,4},{6,7},{7,6},{8,9},{9,8},{10,11... | collective-permute-start | bytes 393224 | tf_op jit(solution)/shard_map/ppermute | solution.py:144
  8.6 1.5 %collective-permute-start.4 = (bf16[512,128]{1,0:T(8,128)(2,1)S(1)}, bf16[512,128]{1,0:T(8,128)(2,1)S(1)}, u32[]{:S(2)}, u32[]{:S(2)}) collective-permute-start(bf16[512,128]{1,0:T(8,128)(2,1)S(1)} %get-tuple-element.13), channel_id=1, source_target_pairs={{0,1},{1,0},{2,3},{3,2},{4,5},{5,4},{6,7},{7,6},{8,9},{9,8},{10,11... | collective-permute-start | bytes 393224 | tf_op jit(solution)/shard_map/ppermute | solution.py:144
  20.9 1.2 %collective-permute-start.5 = (f32[1024]{0:T(1024)S(1)}, f32[1024]{0:T(1024)S(1)}, u32[]{:S(2)}, u32[]{:S(2)}) collective-permute-start(f32[1024]{0:T(1024)S(1)} %bitcast.2), channel_id=1, source_target_pairs={{0,1},{1,0},{2,3},{3,2},{4,5},{5,4},{6,7},{7,6},{8,9},{9,8},{10,11... | collective-permute-start | bytes 12296 | tf_op jit(solution)/shard_map/ppermute | solution.py:144

commit v22 on v18

--- a/solution.py
+++ b/solution.py
@@ -147,7 +147,11 @@
     kept, *sent = branch_sums(mid_tensors, right_tensors, stems)
     got = [swap(x, 1) for x in sent]
     groups = [
-        [s * cuts + c for s in range(stems - 2 + core, -1, -2) for c in range(cuts - 1, -1, -1)] for core in range(2)
+        [
+            (2 * side + (plane + group) % 2) * cuts + 2 * plane + column
+            for side in range(stems // 2 - 1, -1, -1) for plane in range(cuts // 2 - 1, -1, -1) for column in (1, 0)
+        ]
+        for group in (0, 1)
     ]
     targets = [at % cuts for at in groups[0]]
     spread = close(pieces, kept, got, cuts, targets)

time: 23 us -> 22.4 us (0.974)
  blocking collectives: 10.5 us -> 9.9 us
    all_to_all x1, blocking collectives: 10.5 us -> 9.9 us  [on_device(): lax.all_to_all(spread, ('stem', 'cuts'), 0, 0, tiled=True, axis_index_gro...]
where the time goes in v22:
time: 22.4 us; the launch traced here: 22.2 us
  blocking collectives  9.9 us (44%)
  Pallas kernels  5.37 us (24%)
  starting transfers between devices  4.28 us (19%)
  waiting for transfers between devices  2.02 us (9%)
  other arithmetic  0.61 us (3%)
    all_to_all x1, blocking collectives, on_device(): lax.all_to_all(spread, ('stem', 'cuts'), 0, 0, tiled=True, axis_index_gro...  9.9 us
    pallas_call x1, Pallas kernels, branch_sums(): pl.pallas_call(functools.partial(branch_kernel, total // groups), in_spec...  4.95 us
    ppermute x6, starting transfers between devices, swap(): return lax.ppermute(x, 'stem', [(s, s ^ p) for s in range(stems)])  4.28 us
    ppermute x6, waiting for transfers between devices, swap(): return lax.ppermute(x, 'stem', [(s, s ^ p) for s in range(stems)])  2.02 us
    add x1, other arithmetic, on_device(): return total + swap(total, 1)  0.6 us
  transfers between devices with their start and end apart: 6, of which 5 were waited for; matrix products, arithmetic and copies ran while one was open for 0% of the time, Pallas kernels for 22%

profile of v22, /device:TPU:0, one launch (start us, length us, event | category | flops | bytes accessed | tf_op | source)
XLA Modules:
  0.0 22.2 jit_solution(183770564244268908)
XLA Ops:
  0.0 0.0 copy-start
  0.0 3.0 %collective-permute-start = (bf16[2,64,1024]{2,1,0:T(8,128)(2,1)}, bf16[2,64,1024]{2,1,0:T(8,128)(2,1)S(1)}, u32[]{:S(2)}, u32[]{:S(2)}) collective-permute-start(bf16[2,64,1024]{2,1,0:T(8,128)(2,1)} %refs_0_.1), channel_id=1, source_target_pairs={{0,2},{1,3},{2,0},{3,1},{4,6},{5,7},{6,4},{7,5},{8,10},{9,11},{10,... | collective-permute-start | bytes 786440 | tf_op jit(solution)/shard_map/ppermute | solution.py:144
  3.0 4.9 %branch_sums.1 = (f32[4,512,128]{2,1,0:T(8,128)S(1)}, bf16[512,128]{1,0:T(8,128)(2,1)S(1)}, bf16[512,128]{1,0:T(8,128)(2,1)S(1)}, bf16[512,128]{1,0:T(8,128)(2,1)S(1)}, bf16[512,128]{1,0:T(8,128)(2,1)S(1)}) custom-call(bf16[16,512,128]{2,1,0:T(8,128)(2,1)} %mid_hbm.1, bf16[8,16,64,128]{3,2,1,0:T(8,128)(2,1)} %right_hbm.1), custom_call_target="tpu_custom_call" | custom-call | flops 2147483648 | bytes 6291456 | tf_op jit(solution)/shard_map/branch_sums/pallas_call | solution.py:75
  7.9 0.1 collective-permute-start.1
  8.0 0.5 %collective-permute-start.2 = (bf16[512,128]{1,0:T(8,128)(2,1)S(1)}, bf16[512,128]{1,0:T(8,128)(2,1)S(1)}, u32[]{:S(2)}, u32[]{:S(2)}) collective-permute-start(bf16[512,128]{1,0:T(8,128)(2,1)S(1)} %get-tuple-element.11), channel_id=1, source_target_pairs={{0,1},{1,0},{2,3},{3,2},{4,5},{5,4},{6,7},{7,6},{8,9},{9,8},{10,11... | collective-permute-start | bytes 393224 | tf_op jit(solution)/shard_map/ppermute | solution.py:144
  8.5 0.1 collective-permute-start.3
  8.6 0.4 %collective-permute-start.4 = (bf16[512,128]{1,0:T(8,128)(2,1)S(1)}, bf16[512,128]{1,0:T(8,128)(2,1)S(1)}, u32[]{:S(2)}, u32[]{:S(2)}) collective-permute-start(bf16[512,128]{1,0:T(8,128)(2,1)S(1)} %get-tuple-element.13), channel_id=1, source_target_pairs={{0,1},{1,0},{2,3},{3,2},{4,5},{5,4},{6,7},{7,6},{8,9},{9,8},{10,11... | collective-permute-start | bytes 393224 | tf_op jit(solution)/shard_map/ppermute | solution.py:144
  9.0 0.3 %collective-permute-done.1.refs_2_ = bf16[512,128]{1,0:T(8,128)(2,1)S(1)} collective-permute-done((bf16[512,128]{1,0:T(8,128)(2,1)S(1)}, bf16[512,128]{1,0:T(8,128)(2,1)S(1)}, u32[]{:S(2)}, u32[]{:S(2)}) %collective-permute-start.1) | collective-permute-done | bytes 131104 | tf_op jit(solution)/shard_map/ppermute | solution.py:144
  9.3 0.2 collective-permute-done.2.refs_3_
  9.5 0.3 %collective-permute-done.3.refs_4_ = bf16[512,128]{1,0:T(8,128)(2,1)S(1)} collective-permute-done((bf16[512,128]{1,0:T(8,128)(2,1)S(1)}, bf16[512,128]{1,0:T(8,128)(2,1)S(1)}, u32[]{:S(2)}, u32[]{:S(2)}) %collective-permute-start.3) | collective-permute-done | bytes 131104 | tf_op jit(solution)/shard_map/ppermute | solution.py:144
  9.9 0.2 collective-permute-done.4.refs_5_
  10.0 0.0 collective-permute-done.refs_1_
  10.0 0.0 copy-done
  10.0 0.4 %close.1 = f32[16,8,128]{2,1,0:T(8,128)S(1)} custom-call(bf16[2,64,1024]{2,1,0:T(8,128)(2,1)S(1)} %copy-done, bf16[2,64,1024]{2,1,0:T(8,128)(2,1)S(1)} %collective-permute-done.refs_1_, bf16[512,128]{1,0:T(8,128)(2,1)S(1)} %collective-permute-done.1.refs_2_, bf16[512,128]{1,0:T(8,128)(2,1)S(1)} %collective-permute-done.2.refs_3_, ...), custom_call_target="tpu_custom_call" | custom-call | flops 134217728 | bytes 1048576 | tf_op jit(solution)/shard_map/close/pallas_call | solution.py:129
  10.5 9.9 %all_to_all.5 = f32[16,8,128]{2,1,0:T(8,128)S(1)} all-to-all(f32[16,8,128]{2,1,0:T(8,128)S(1)} %close.1), channel_id=1, replica_groups={{31,27,22,18,15,11,6,2,29,25,20,16,13,9,4,0},{30,26,23,19,14,10,7,3,28,..., dimensions={0} | all-to-all | bytes 131072 | tf_op jit(solution)/shard_map/all_to_all | solution.py:158
  20.4 0.2 %collective-permute-start.5 = (f32[1024]{0:T(1024)S(1)}, f32[1024]{0:T(1024)S(1)}, u32[]{:S(2)}, u32[]{:S(2)}) collective-permute-start(f32[1024]{0:T(1024)S(1)} %bitcast.2), channel_id=1, source_target_pairs={{0,1},{1,0},{2,3},{3,2},{4,5},{5,4},{6,7},{7,6},{8,9},{9,8},{10,11... | collective-permute-start | bytes 12296 | tf_op jit(solution)/shard_map/ppermute | solution.py:144
  20.6 1.0 %collective-permute-done.5 = f32[1024]{0:T(1024)S(1)} collective-permute-done((f32[1024]{0:T(1024)S(1)}, f32[1024]{0:T(1024)S(1)}, u32[]{:S(2)}, u32[]{:S(2)}) %collective-permute-start.5) | collective-permute-done | bytes 4128 | tf_op jit(solution)/shard_map/ppermute | solution.py:144
  21.6 0.6 %bitcast_add_fusion = f32[1024]{0:T(1024)} fusion(f32[1024]{0:T(1024)S(1)} %collective-permute-done.5, f32[8,128]{1,0:T(8,128)S(1)} %reduce_sum.9), kind=kLoop, calls=%fused_computation | loop fusion | flops 1024 | bytes 12288 | tf_op jit(solution)/shard_map/add | solution.py:160
  (1 shorter events, 0.0 us)
Async XLA Ops:
  0.0 10.0 %copy-start = (bf16[2,64,1024]{2,1,0:T(8,128)(2,1)S(1)}, bf16[2,64,1024]{2,1,0:T(8,128)(2,1)}, u32[]{:S(2)}) copy-start(bf16[2,64,1024]{2,1,0:T(8,128)(2,1)} %refs_0_.1) | copy-start | bytes 786436
  0.0 10.0 %collective-permute-start = (bf16[2,64,1024]{2,1,0:T(8,128)(2,1)}, bf16[2,64,1024]{2,1,0:T(8,128)(2,1)S(1)}, u32[]{:S(2)}, u32[]{:S(2)}) collective-permute-start(bf16[2,64,1024]{2,1,0:T(8,128)(2,1)} %refs_0_.1), channel_id=1, source_target_pairs={{0,2},{1,3},{2,0},{3,1},{4,6},{5,7},{6,4},{7,5},{8,10},{9,11},{10,... | collective-permute-start | bytes 786440 | tf_op jit(solution)/shard_map/ppermute | solution.py:144
  7.9 1.4 %collective-permute-start.1 = (bf16[512,128]{1,0:T(8,128)(2,1)S(1)}, bf16[512,128]{1,0:T(8,128)(2,1)S(1)}, u32[]{:S(2)}, u32[]{:S(2)}) collective-permute-start(bf16[512,128]{1,0:T(8,128)(2,1)S(1)} %get-tuple-element.10), channel_id=1, source_target_pairs={{0,1},{1,0},{2,3},{3,2},{4,5},{5,4},{6,7},{7,6},{8,9},{9,8},{10,11... | collective-permute-start | bytes 393224 | tf_op jit(solution)/shard_map/ppermute | solution.py:144
  8.0 1.5 %collective-permute-start.2 = (bf16[512,128]{1,0:T(8,128)(2,1)S(1)}, bf16[512,128]{1,0:T(8,128)(2,1)S(1)}, u32[]{:S(2)}, u32[]{:S(2)}) collective-permute-start(bf16[512,128]{1,0:T(8,128)(2,1)S(1)} %get-tuple-element.11), channel_id=1, source_target_pairs={{0,1},{1,0},{2,3},{3,2},{4,5},{5,4},{6,7},{7,6},{8,9},{9,8},{10,11... | collective-permute-start | bytes 393224 | tf_op jit(solution)/shard_map/ppermute | solution.py:144
  8.5 1.3 %collective-permute-start.3 = (bf16[512,128]{1,0:T(8,128)(2,1)S(1)}, bf16[512,128]{1,0:T(8,128)(2,1)S(1)}, u32[]{:S(2)}, u32[]{:S(2)}) collective-permute-start(bf16[512,128]{1,0:T(8,128)(2,1)S(1)} %get-tuple-element.12), channel_id=1, source_target_pairs={{0,1},{1,0},{2,3},{3,2},{4,5},{5,4},{6,7},{7,6},{8,9},{9,8},{10,11... | collective-permute-start | bytes 393224 | tf_op jit(solution)/shard_map/ppermute | solution.py:144
  8.6 1.5 %collective-permute-start.4 = (bf16[512,128]{1,0:T(8,128)(2,1)S(1)}, bf16[512,128]{1,0:T(8,128)(2,1)S(1)}, u32[]{:S(2)}, u32[]{:S(2)}) collective-permute-start(bf16[512,128]{1,0:T(8,128)(2,1)S(1)} %get-tuple-element.13), channel_id=1, source_target_pairs={{0,1},{1,0},{2,3},{3,2},{4,5},{5,4},{6,7},{7,6},{8,9},{9,8},{10,11... | collective-permute-start | bytes 393224 | tf_op jit(solution)/shard_map/ppermute | solution.py:144
  20.4 1.2 %collective-permute-start.5 = (f32[1024]{0:T(1024)S(1)}, f32[1024]{0:T(1024)S(1)}, u32[]{:S(2)}, u32[]{:S(2)}) collective-permute-start(f32[1024]{0:T(1024)S(1)} %bitcast.2), channel_id=1, source_target_pairs={{0,1},{1,0},{2,3},{3,2},{4,5},{5,4},{6,7},{7,6},{8,9},{9,8},{10,11... | collective-permute-start | bytes 12296 | tf_op jit(solution)/shard_map/ppermute | solution.py:144

commit v23 on v22

--- a/solution.py
+++ b/solution.py
@@ -149,7 +149,7 @@
     groups = [
         [
             (2 * side + (plane + group) % 2) * cuts + 2 * plane + column
-            for side in range(stems // 2 - 1, -1, -1) for plane in range(cuts // 2 - 1, -1, -1) for column in (1, 0)
+            for plane in range(cuts // 2 - 1, -1, -1) for side in range(stems // 2 - 1, -1, -1) for column in (1, 0)
         ]
         for group in (0, 1)
     ]

time: 22.4 us -> 22.5 us (level)
  no operation moved by 1% of the time
where the time goes in v23:
time: 22.5 us; the launch traced here: 22.3 us
  blocking collectives  10 us (44%)
  Pallas kernels  5.37 us (24%)
  starting transfers between devices  4.25 us (19%)
  waiting for transfers between devices  2.05 us (9%)
  other arithmetic  0.61 us (3%)
    all_to_all x1, blocking collectives, on_device(): lax.all_to_all(spread, ('stem', 'cuts'), 0, 0, tiled=True, axis_index_gro...  10 us
    pallas_call x1, Pallas kernels, branch_sums(): pl.pallas_call(functools.partial(branch_kernel, total // groups), in_spec...  4.95 us
    ppermute x6, starting transfers between devices, swap(): return lax.ppermute(x, 'stem', [(s, s ^ p) for s in range(stems)])  4.25 us
    ppermute x6, waiting for transfers between devices, swap(): return lax.ppermute(x, 'stem', [(s, s ^ p) for s in range(stems)])  2.05 us
    add x1, other arithmetic, on_device(): return total + swap(total, 1)  0.6 us
  transfers between devices with their start and end apart: 6, of which 5 were waited for; matrix products, arithmetic and copies ran while one was open for 0% of the time, Pallas kernels for 22%

profile of v23, /device:TPU:0, one launch (start us, length us, event | category | flops | bytes accessed | tf_op | source)
XLA Modules:
  0.0 22.3 jit_solution(3242361011125490911)
XLA Ops:
  0.0 0.0 copy-start
  0.0 3.0 %collective-permute-start = (bf16[2,64,1024]{2,1,0:T(8,128)(2,1)}, bf16[2,64,1024]{2,1,0:T(8,128)(2,1)S(1)}, u32[]{:S(2)}, u32[]{:S(2)}) collective-permute-start(bf16[2,64,1024]{2,1,0:T(8,128)(2,1)} %refs_0_.1), channel_id=1, source_target_pairs={{0,2},{1,3},{2,0},{3,1},{4,6},{5,7},{6,4},{7,5},{8,10},{9,11},{10,... | collective-permute-start | bytes 786440 | tf_op jit(solution)/shard_map/ppermute | solution.py:144
  3.0 4.9 %branch_sums.1 = (f32[4,512,128]{2,1,0:T(8,128)S(1)}, bf16[512,128]{1,0:T(8,128)(2,1)S(1)}, bf16[512,128]{1,0:T(8,128)(2,1)S(1)}, bf16[512,128]{1,0:T(8,128)(2,1)S(1)}, bf16[512,128]{1,0:T(8,128)(2,1)S(1)}) custom-call(bf16[16,512,128]{2,1,0:T(8,128)(2,1)} %mid_hbm.1, bf16[8,16,64,128]{3,2,1,0:T(8,128)(2,1)} %right_hbm.1), custom_call_target="tpu_custom_call" | custom-call | flops 2147483648 | bytes 6291456 | tf_op jit(solution)/shard_map/branch_sums/pallas_call | solution.py:75
  7.9 0.1 collective-permute-start.1
  8.0 0.5 %collective-permute-start.2 = (bf16[512,128]{1,0:T(8,128)(2,1)S(1)}, bf16[512,128]{1,0:T(8,128)(2,1)S(1)}, u32[]{:S(2)}, u32[]{:S(2)}) collective-permute-start(bf16[512,128]{1,0:T(8,128)(2,1)S(1)} %get-tuple-element.11), channel_id=1, source_target_pairs={{0,1},{1,0},{2,3},{3,2},{4,5},{5,4},{6,7},{7,6},{8,9},{9,8},{10,11... | collective-permute-start | bytes 393224 | tf_op jit(solution)/shard_map/ppermute | solution.py:144
  8.5 0.1 collective-permute-start.3
  8.6 0.4 %collective-permute-start.4 = (bf16[512,128]{1,0:T(8,128)(2,1)S(1)}, bf16[512,128]{1,0:T(8,128)(2,1)S(1)}, u32[]{:S(2)}, u32[]{:S(2)}) collective-permute-start(bf16[512,128]{1,0:T(8,128)(2,1)S(1)} %get-tuple-element.13), channel_id=1, source_target_pairs={{0,1},{1,0},{2,3},{3,2},{4,5},{5,4},{6,7},{7,6},{8,9},{9,8},{10,11... | collective-permute-start | bytes 393224 | tf_op jit(solution)/shard_map/ppermute | solution.py:144
  9.0 0.3 %collective-permute-done.1.refs_2_ = bf16[512,128]{1,0:T(8,128)(2,1)S(1)} collective-permute-done((bf16[512,128]{1,0:T(8,128)(2,1)S(1)}, bf16[512,128]{1,0:T(8,128)(2,1)S(1)}, u32[]{:S(2)}, u32[]{:S(2)}) %collective-permute-start.1) | collective-permute-done | bytes 131104 | tf_op jit(solution)/shard_map/ppermute | solution.py:144
  9.3 0.2 collective-permute-done.2.refs_3_
  9.5 0.3 %collective-permute-done.3.refs_4_ = bf16[512,128]{1,0:T(8,128)(2,1)S(1)} collective-permute-done((bf16[512,128]{1,0:T(8,128)(2,1)S(1)}, bf16[512,128]{1,0:T(8,128)(2,1)S(1)}, u32[]{:S(2)}, u32[]{:S(2)}) %collective-permute-start.3) | collective-permute-done | bytes 131104 | tf_op jit(solution)/shard_map/ppermute | solution.py:144
  9.9 0.2 collective-permute-done.4.refs_5_
  10.0 0.0 collective-permute-done.refs_1_
  10.0 0.0 copy-done
  10.0 0.4 %close.1 = f32[16,8,128]{2,1,0:T(8,128)S(1)} custom-call(bf16[2,64,1024]{2,1,0:T(8,128)(2,1)S(1)} %copy-done, bf16[2,64,1024]{2,1,0:T(8,128)(2,1)S(1)} %collective-permute-done.refs_1_, bf16[512,128]{1,0:T(8,128)(2,1)S(1)} %collective-permute-done.1.refs_2_, bf16[512,128]{1,0:T(8,128)(2,1)S(1)} %collective-permute-done.2.refs_3_, ...), custom_call_target="tpu_custom_call" | custom-call | flops 134217728 | bytes 1048576 | tf_op jit(solution)/shard_map/close/pallas_call | solution.py:129
  10.5 10.0 %all_to_all.5 = f32[16,8,128]{2,1,0:T(8,128)S(1)} all-to-all(f32[16,8,128]{2,1,0:T(8,128)S(1)} %close.1), channel_id=1, replica_groups={{31,27,29,25,22,18,20,16,15,11,13,9,6,2,4,0},{30,26,28,24,23,19,21,17,1..., dimensions={0} | all-to-all | bytes 131072 | tf_op jit(solution)/shard_map/all_to_all | solution.py:158
  20.5 0.2 collective-permute-start.5
  20.7 1.0 %collective-permute-done.5 = f32[1024]{0:T(1024)S(1)} collective-permute-done((f32[1024]{0:T(1024)S(1)}, f32[1024]{0:T(1024)S(1)}, u32[]{:S(2)}, u32[]{:S(2)}) %collective-permute-start.5) | collective-permute-done | bytes 4128 | tf_op jit(solution)/shard_map/ppermute | solution.py:144
  21.7 0.6 %bitcast_add_fusion = f32[1024]{0:T(1024)} fusion(f32[1024]{0:T(1024)S(1)} %collective-permute-done.5, f32[8,128]{1,0:T(8,128)S(1)} %reduce_sum.9), kind=kLoop, calls=%fused_computation | loop fusion | flops 1024 | bytes 12288 | tf_op jit(solution)/shard_map/add | solution.py:160
  (1 shorter events, 0.0 us)
Async XLA Ops:
  0.0 10.0 %copy-start = (bf16[2,64,1024]{2,1,0:T(8,128)(2,1)S(1)}, bf16[2,64,1024]{2,1,0:T(8,128)(2,1)}, u32[]{:S(2)}) copy-start(bf16[2,64,1024]{2,1,0:T(8,128)(2,1)} %refs_0_.1) | copy-start | bytes 786436
  0.0 10.0 %collective-permute-start = (bf16[2,64,1024]{2,1,0:T(8,128)(2,1)}, bf16[2,64,1024]{2,1,0:T(8,128)(2,1)S(1)}, u32[]{:S(2)}, u32[]{:S(2)}) collective-permute-start(bf16[2,64,1024]{2,1,0:T(8,128)(2,1)} %refs_0_.1), channel_id=1, source_target_pairs={{0,2},{1,3},{2,0},{3,1},{4,6},{5,7},{6,4},{7,5},{8,10},{9,11},{10,... | collective-permute-start | bytes 786440 | tf_op jit(solution)/shard_map/ppermute | solution.py:144
  7.9 1.4 %collective-permute-start.1 = (bf16[512,128]{1,0:T(8,128)(2,1)S(1)}, bf16[512,128]{1,0:T(8,128)(2,1)S(1)}, u32[]{:S(2)}, u32[]{:S(2)}) collective-permute-start(bf16[512,128]{1,0:T(8,128)(2,1)S(1)} %get-tuple-element.10), channel_id=1, source_target_pairs={{0,1},{1,0},{2,3},{3,2},{4,5},{5,4},{6,7},{7,6},{8,9},{9,8},{10,11... | collective-permute-start | bytes 393224 | tf_op jit(solution)/shard_map/ppermute | solution.py:144
  8.0 1.5 %collective-permute-start.2 = (bf16[512,128]{1,0:T(8,128)(2,1)S(1)}, bf16[512,128]{1,0:T(8,128)(2,1)S(1)}, u32[]{:S(2)}, u32[]{:S(2)}) collective-permute-start(bf16[512,128]{1,0:T(8,128)(2,1)S(1)} %get-tuple-element.11), channel_id=1, source_target_pairs={{0,1},{1,0},{2,3},{3,2},{4,5},{5,4},{6,7},{7,6},{8,9},{9,8},{10,11... | collective-permute-start | bytes 393224 | tf_op jit(solution)/shard_map/ppermute | solution.py:144
  8.5 1.3 %collective-permute-start.3 = (bf16[512,128]{1,0:T(8,128)(2,1)S(1)}, bf16[512,128]{1,0:T(8,128)(2,1)S(1)}, u32[]{:S(2)}, u32[]{:S(2)}) collective-permute-start(bf16[512,128]{1,0:T(8,128)(2,1)S(1)} %get-tuple-element.12), channel_id=1, source_target_pairs={{0,1},{1,0},{2,3},{3,2},{4,5},{5,4},{6,7},{7,6},{8,9},{9,8},{10,11... | collective-permute-start | bytes 393224 | tf_op jit(solution)/shard_map/ppermute | solution.py:144
  8.6 1.5 %collective-permute-start.4 = (bf16[512,128]{1,0:T(8,128)(2,1)S(1)}, bf16[512,128]{1,0:T(8,128)(2,1)S(1)}, u32[]{:S(2)}, u32[]{:S(2)}) collective-permute-start(bf16[512,128]{1,0:T(8,128)(2,1)S(1)} %get-tuple-element.13), channel_id=1, source_target_pairs={{0,1},{1,0},{2,3},{3,2},{4,5},{5,4},{6,7},{7,6},{8,9},{9,8},{10,11... | collective-permute-start | bytes 393224 | tf_op jit(solution)/shard_map/ppermute | solution.py:144
  20.5 1.2 %collective-permute-start.5 = (f32[1024]{0:T(1024)S(1)}, f32[1024]{0:T(1024)S(1)}, u32[]{:S(2)}, u32[]{:S(2)}) collective-permute-start(f32[1024]{0:T(1024)S(1)} %bitcast.2), channel_id=1, source_target_pairs={{0,1},{1,0},{2,3},{3,2},{4,5},{5,4},{6,7},{7,6},{8,9},{9,8},{10,11... | collective-permute-start | bytes 12296 | tf_op jit(solution)/shard_map/ppermute | solution.py:144

commit v24 on v22

--- a/solution.py
+++ b/solution.py
@@ -148,7 +148,7 @@
     got = [swap(x, 1) for x in sent]
     groups = [
         [
-            (2 * side + (plane + group) % 2) * cuts + 2 * plane + column
+            (2 * side + ((plane > 0) ^ group)) * cuts + 2 * plane + column
             for side in range(stems // 2 - 1, -1, -1) for plane in range(cuts // 2 - 1, -1, -1) for column in (1, 0)
         ]
         for group in (0, 1)

time: 22.4 us -> 22.4 us (level)
  starting transfers between devices: 4.28 us -> 5.12 us
  blocking collectives: 9.9 us -> 9.28 us
    ppermute x6, starting transfers between devices: 4.28 us -> 5.12 us  [swap(): return lax.ppermute(x, 'stem', [(s, s ^ p) for s in range(stems)])]
    all_to_all x1, blocking collectives: 9.9 us -> 9.28 us  [on_device(): lax.all_to_all(spread, ('stem', 'cuts'), 0, 0, tiled=True, axis_index_gro...]
where the time goes in v24:
time: 22.4 us; the launch traced here: 22.3 us
  blocking collectives  9.28 us (41%)
  Pallas kernels  5.37 us (24%)
  starting transfers between devices  5.12 us (23%)
  waiting for transfers between devices  1.85 us (8%)
  other arithmetic  0.61 us (3%)
    all_to_all x1, blocking collectives, on_device(): lax.all_to_all(spread, ('stem', 'cuts'), 0, 0, tiled=True, axis_index_gro...  9.28 us
    ppermute x6, starting transfers between devices, swap(): return lax.ppermute(x, 'stem', [(s, s ^ p) for s in range(stems)])  5.12 us
    pallas_call x1, Pallas kernels, branch_sums(): pl.pallas_call(functools.partial(branch_kernel, total // groups), in_spec...  4.95 us
    ppermute x6, waiting for transfers between devices, swap(): return lax.ppermute(x, 'stem', [(s, s ^ p) for s in range(stems)])  1.85 us
    add x1, other arithmetic, on_device(): return total + swap(total, 1)  0.59 us
  transfers between devices with their start and end apart: 6, of which 5 were waited for; matrix products, arithmetic and copies ran while one was open for 0% of the time, Pallas kernels for 22%

profile of v24, /device:TPU:0, one launch (start us, length us, event | category | flops | bytes accessed | tf_op | source)
XLA Modules:
  0.0 22.3 jit_solution(12699749884863524637)
XLA Ops:
  0.0 0.0 copy-start
  0.0 3.0 %collective-permute-start = (bf16[2,64,1024]{2,1,0:T(8,128)(2,1)}, bf16[2,64,1024]{2,1,0:T(8,128)(2,1)S(1)}, u32[]{:S(2)}, u32[]{:S(2)}) collective-permute-start(bf16[2,64,1024]{2,1,0:T(8,128)(2,1)} %refs_0_.1), channel_id=1, source_target_pairs={{0,2},{1,3},{2,0},{3,1},{4,6},{5,7},{6,4},{7,5},{8,10},{9,11},{10,... | collective-permute-start | bytes 786440 | tf_op jit(solution)/shard_map/ppermute | solution.py:144
  3.0 4.9 %branch_sums.1 = (f32[4,512,128]{2,1,0:T(8,128)S(1)}, bf16[512,128]{1,0:T(8,128)(2,1)S(1)}, bf16[512,128]{1,0:T(8,128)(2,1)S(1)}, bf16[512,128]{1,0:T(8,128)(2,1)S(1)}, bf16[512,128]{1,0:T(8,128)(2,1)S(1)}) custom-call(bf16[16,512,128]{2,1,0:T(8,128)(2,1)} %mid_hbm.1, bf16[8,16,64,128]{3,2,1,0:T(8,128)(2,1)} %right_hbm.1), custom_call_target="tpu_custom_call" | custom-call | flops 2147483648 | bytes 6291456 | tf_op jit(solution)/shard_map/branch_sums/pallas_call | solution.py:75
  7.9 0.1 collective-permute-start.1
  8.0 0.5 %collective-permute-start.2 = (bf16[512,128]{1,0:T(8,128)(2,1)S(1)}, bf16[512,128]{1,0:T(8,128)(2,1)S(1)}, u32[]{:S(2)}, u32[]{:S(2)}) collective-permute-start(bf16[512,128]{1,0:T(8,128)(2,1)S(1)} %get-tuple-element.11), channel_id=1, source_target_pairs={{0,1},{1,0},{2,3},{3,2},{4,5},{5,4},{6,7},{7,6},{8,9},{9,8},{10,11... | collective-permute-start | bytes 393224 | tf_op jit(solution)/shard_map/ppermute | solution.py:144
  8.5 0.1 collective-permute-start.3
  8.6 0.4 %collective-permute-start.4 = (bf16[512,128]{1,0:T(8,128)(2,1)S(1)}, bf16[512,128]{1,0:T(8,128)(2,1)S(1)}, u32[]{:S(2)}, u32[]{:S(2)}) collective-permute-start(bf16[512,128]{1,0:T(8,128)(2,1)S(1)} %get-tuple-element.13), channel_id=1, source_target_pairs={{0,1},{1,0},{2,3},{3,2},{4,5},{5,4},{6,7},{7,6},{8,9},{9,8},{10,11... | collective-permute-start | bytes 393224 | tf_op jit(solution)/shard_map/ppermute | solution.py:144
  9.0 0.3 %collective-permute-done.1.refs_2_ = bf16[512,128]{1,0:T(8,128)(2,1)S(1)} collective-permute-done((bf16[512,128]{1,0:T(8,128)(2,1)S(1)}, bf16[512,128]{1,0:T(8,128)(2,1)S(1)}, u32[]{:S(2)}, u32[]{:S(2)}) %collective-permute-start.1) | collective-permute-done | bytes 131104 | tf_op jit(solution)/shard_map/ppermute | solution.py:144
  9.3 0.2 collective-permute-done.2.refs_3_
  9.5 0.3 %collective-permute-done.3.refs_4_ = bf16[512,128]{1,0:T(8,128)(2,1)S(1)} collective-permute-done((bf16[512,128]{1,0:T(8,128)(2,1)S(1)}, bf16[512,128]{1,0:T(8,128)(2,1)S(1)}, u32[]{:S(2)}, u32[]{:S(2)}) %collective-permute-start.3) | collective-permute-done | bytes 131104 | tf_op jit(solution)/shard_map/ppermute | solution.py:144
  9.9 0.2 collective-permute-done.4.refs_5_
  10.0 0.0 collective-permute-done.refs_1_
  10.0 0.0 copy-done
  10.0 0.4 %close.1 = f32[16,8,128]{2,1,0:T(8,128)S(1)} custom-call(bf16[2,64,1024]{2,1,0:T(8,128)(2,1)S(1)} %copy-done, bf16[2,64,1024]{2,1,0:T(8,128)(2,1)S(1)} %collective-permute-done.refs_1_, bf16[512,128]{1,0:T(8,128)(2,1)S(1)} %collective-permute-done.1.refs_2_, bf16[512,128]{1,0:T(8,128)(2,1)S(1)} %collective-permute-done.2.refs_3_, ...), custom_call_target="tpu_custom_call" | custom-call | flops 134217728 | bytes 1048576 | tf_op jit(solution)/shard_map/close/pallas_call | solution.py:129
  10.5 9.3 %all_to_all.5 = f32[16,8,128]{2,1,0:T(8,128)S(1)} all-to-all(f32[16,8,128]{2,1,0:T(8,128)S(1)} %close.1), channel_id=1, replica_groups={{31,27,23,19,15,11,6,2,29,25,21,17,13,9,4,0},{30,26,22,18,14,10,7,3,28,..., dimensions={0} | all-to-all | bytes 131072 | tf_op jit(solution)/shard_map/all_to_all | solution.py:158
  19.8 1.1 %collective-permute-start.5 = (f32[1024]{0:T(1024)S(1)}, f32[1024]{0:T(1024)S(1)}, u32[]{:S(2)}, u32[]{:S(2)}) collective-permute-start(f32[1024]{0:T(1024)S(1)} %bitcast.2), channel_id=1, source_target_pairs={{0,1},{1,0},{2,3},{3,2},{4,5},{5,4},{6,7},{7,6},{8,9},{9,8},{10,11... | collective-permute-start | bytes 12296 | tf_op jit(solution)/shard_map/ppermute | solution.py:144
  20.9 0.8 %collective-permute-done.5 = f32[1024]{0:T(1024)S(1)} collective-permute-done((f32[1024]{0:T(1024)S(1)}, f32[1024]{0:T(1024)S(1)}, u32[]{:S(2)}, u32[]{:S(2)}) %collective-permute-start.5) | collective-permute-done | bytes 4128 | tf_op jit(solution)/shard_map/ppermute | solution.py:144
  21.7 0.6 %bitcast_add_fusion = f32[1024]{0:T(1024)} fusion(f32[1024]{0:T(1024)S(1)} %collective-permute-done.5, f32[8,128]{1,0:T(8,128)S(1)} %reduce_sum.9), kind=kLoop, calls=%fused_computation | loop fusion | flops 1024 | bytes 12288 | tf_op jit(solution)/shard_map/add | solution.py:160
  (1 shorter events, 0.0 us)
Async XLA Ops:
  0.0 10.0 %copy-start = (bf16[2,64,1024]{2,1,0:T(8,128)(2,1)S(1)}, bf16[2,64,1024]{2,1,0:T(8,128)(2,1)}, u32[]{:S(2)}) copy-start(bf16[2,64,1024]{2,1,0:T(8,128)(2,1)} %refs_0_.1) | copy-start | bytes 786436
  0.0 10.0 %collective-permute-start = (bf16[2,64,1024]{2,1,0:T(8,128)(2,1)}, bf16[2,64,1024]{2,1,0:T(8,128)(2,1)S(1)}, u32[]{:S(2)}, u32[]{:S(2)}) collective-permute-start(bf16[2,64,1024]{2,1,0:T(8,128)(2,1)} %refs_0_.1), channel_id=1, source_target_pairs={{0,2},{1,3},{2,0},{3,1},{4,6},{5,7},{6,4},{7,5},{8,10},{9,11},{10,... | collective-permute-start | bytes 786440 | tf_op jit(solution)/shard_map/ppermute | solution.py:144
  7.9 1.4 %collective-permute-start.1 = (bf16[512,128]{1,0:T(8,128)(2,1)S(1)}, bf16[512,128]{1,0:T(8,128)(2,1)S(1)}, u32[]{:S(2)}, u32[]{:S(2)}) collective-permute-start(bf16[512,128]{1,0:T(8,128)(2,1)S(1)} %get-tuple-element.10), channel_id=1, source_target_pairs={{0,1},{1,0},{2,3},{3,2},{4,5},{5,4},{6,7},{7,6},{8,9},{9,8},{10,11... | collective-permute-start | bytes 393224 | tf_op jit(solution)/shard_map/ppermute | solution.py:144
  8.0 1.5 %collective-permute-start.2 = (bf16[512,128]{1,0:T(8,128)(2,1)S(1)}, bf16[512,128]{1,0:T(8,128)(2,1)S(1)}, u32[]{:S(2)}, u32[]{:S(2)}) collective-permute-start(bf16[512,128]{1,0:T(8,128)(2,1)S(1)} %get-tuple-element.11), channel_id=1, source_target_pairs={{0,1},{1,0},{2,3},{3,2},{4,5},{5,4},{6,7},{7,6},{8,9},{9,8},{10,11... | collective-permute-start | bytes 393224 | tf_op jit(solution)/shard_map/ppermute | solution.py:144
  8.5 1.3 %collective-permute-start.3 = (bf16[512,128]{1,0:T(8,128)(2,1)S(1)}, bf16[512,128]{1,0:T(8,128)(2,1)S(1)}, u32[]{:S(2)}, u32[]{:S(2)}) collective-permute-start(bf16[512,128]{1,0:T(8,128)(2,1)S(1)} %get-tuple-element.12), channel_id=1, source_target_pairs={{0,1},{1,0},{2,3},{3,2},{4,5},{5,4},{6,7},{7,6},{8,9},{9,8},{10,11... | collective-permute-start | bytes 393224 | tf_op jit(solution)/shard_map/ppermute | solution.py:144
  8.6 1.5 %collective-permute-start.4 = (bf16[512,128]{1,0:T(8,128)(2,1)S(1)}, bf16[512,128]{1,0:T(8,128)(2,1)S(1)}, u32[]{:S(2)}, u32[]{:S(2)}) collective-permute-start(bf16[512,128]{1,0:T(8,128)(2,1)S(1)} %get-tuple-element.13), channel_id=1, source_target_pairs={{0,1},{1,0},{2,3},{3,2},{4,5},{5,4},{6,7},{7,6},{8,9},{9,8},{10,11... | collective-permute-start | bytes 393224 | tf_op jit(solution)/shard_map/ppermute | solution.py:144
  19.8 1.9 %collective-permute-start.5 = (f32[1024]{0:T(1024)S(1)}, f32[1024]{0:T(1024)S(1)}, u32[]{:S(2)}, u32[]{:S(2)}) collective-permute-start(f32[1024]{0:T(1024)S(1)} %bitcast.2), channel_id=1, source_target_pairs={{0,1},{1,0},{2,3},{3,2},{4,5},{5,4},{6,7},{7,6},{8,9},{9,8},{10,11... | collective-permute-start | bytes 12296 | tf_op jit(solution)/shard_map/ppermute | solution.py:144

commit v25 on v22

--- a/solution.py
+++ b/solution.py
@@ -16,6 +16,23 @@
     lane = lax.broadcasted_iota(jnp.int32, x.shape, x.ndim - 1)
     rolled = pltpu.roll(x, half, x.ndim - 1)
     return jnp.where(lane < half, -rolled, rolled)
+
+
+def segments(blocks, depth, sizes):
+    out, row = [], 0
+    for piece, size in enumerate(sizes):
+        end = row + size
+        first = row
+        while row < end:
+            count = min(end, (row // depth + 1) * depth) - row
+            out.append((row // depth, row % depth, piece, row - first, count))
+            row += count
+    return out
+
+
+def piece_sizes(rows, count):
+    size = -(-rows // (16 * count)) * 16
+    return [min(size, rows - at) for at in range(0, rows, size)]
 
 
 def branch_kernel(blocks, mid_hbm, right_hbm, kept_ref, *refs):
@@ -61,24 +78,27 @@
         return carry
 
     lax.fori_loop(0, 2, multiply, 0)
-    for b, ref in enumerate(sent_refs):
-        cols = slice(b * width, (b + 1) * width)
-        ref[...] = sums_ref[0, :, cols].astype(ref.dtype)
-        kept_ref[b] = sums_ref[1, :, cols]
+    sizes = [ref.shape[0] for ref in sent_refs]
+    for b, row, piece, at, count in segments(total // 2, sums_ref.shape[1], sizes):
+        part = sums_ref[0, row:row + count, b * width:(b + 1) * width]
+        sent_refs[piece][at:at + count] = part.astype(jnp.bfloat16)
+    for b in range(total // 2):
+        kept_ref[b] = sums_ref[1, :, b * width:(b + 1) * width]
 
 
 def branch_sums(mid, right, groups):
     pairs, depth, width = mid.shape
     total, _, inner, _ = right.shape
+    sizes = piece_sizes(total // 2 * depth, 3)
     vmem = pl.BlockSpec(memory_space=pltpu.VMEM)
     hbm = pl.BlockSpec(memory_space=pltpu.HBM)
     return pl.pallas_call(
         functools.partial(branch_kernel, total // groups),
         in_specs=[hbm, hbm],
-        out_specs=[vmem] * (1 + total // 2),
+        out_specs=[vmem] * (1 + len(sizes)),
         out_shape=[
             jax.ShapeDtypeStruct((total // 2, depth, width), jnp.float32),
-        ] + [jax.ShapeDtypeStruct((depth, width), jnp.bfloat16)] * (total // 2),
+        ] + [jax.ShapeDtypeStruct((size, width), jnp.bfloat16) for size in sizes],
         scratch_shapes=[
             pltpu.VMEM((2, depth, total // 2 * width), jnp.float32),
             pltpu.VMEM(mid.shape, mid.dtype),
@@ -94,21 +114,53 @@
     )(mid, right)
 
 
+def stacked(block):
+    half = block.shape[-1] // 2
+    return jnp.concatenate([block[:, :half], block[:, half:]], axis=0)
+
+
+def fold_kernel(own_ref, kept_ref, *refs):
+    *got_refs, part_ref, far_ref = refs
+    blocks, depth, width = kept_ref.shape
+    own = own_ref.shape[0]
+    pieces = segments(blocks, depth, [ref.shape[0] for ref in got_refs])
+    part = None
+    for b in range(blocks):
+        got = [got_refs[piece][at:at + count] for block, _, piece, at, count in pieces if block == b]
+        sums = kept_ref[b] + jnp.concatenate(got, axis=0).astype(jnp.float32)
+        high = sums.astype(jnp.bfloat16)
+        low = (sums - high.astype(jnp.float32)).astype(jnp.bfloat16)
+        both = jnp.concatenate([high, low], axis=1)
+        if b < own:
+            term = jnp.dot(stacked(own_ref[b]), both, preferred_element_type=jnp.float32)
+            part = term if part is None else part + term
+        else:
+            far_ref[b - own] = both
+    part_ref[...] = part
+
+
+def fold(own, kept, got):
+    count, rows, _ = own.shape
+    blocks, depth, width = kept.shape
+    return pl.pallas_call(
+        fold_kernel,
+        out_shape=[
+            jax.ShapeDtypeStruct((2 * rows, 2 * width), jnp.float32),
+            jax.ShapeDtypeStruct((blocks - count, depth, 2 * width), jnp.bfloat16),
+        ],
+        compiler_params=pltpu.CompilerParams(vmem_limit_bytes=24 * MIB),
+        cost_estimate=pl.CostEstimate(flops=8 * rows * kept.size, bytes_accessed=MIB, transcendentals=0),
+        name="fold",
+    )(own, kept, *got)
+
+
 def close_kernel(targets, *refs):
-    *more, kept_ref, out_ref = refs
-    stem_refs, got_refs = more[:-kept_ref.shape[0]], more[-kept_ref.shape[0]:]
-    part = None
+    *stem_refs, part_ref, far_ref, out_ref = refs
+    part = part_ref[...]
     at = 0
     for ref in stem_refs:
         for b in range(ref.shape[0]):
-            block = ref[b]
-            half = block.shape[-1] // 2
-            rows = jnp.concatenate([block[:, :half], block[:, half:]], axis=0)
-            sums = kept_ref[at] + got_refs[at][...].astype(jnp.float32)
-            high = sums.astype(jnp.bfloat16)
-            low = (sums - high.astype(jnp.float32)).astype(jnp.bfloat16)
-            term = jnp.dot(rows, jnp.concatenate([high, low], axis=1), preferred_element_type=jnp.float32)
-            part = term if part is None else part + term
+            part += jnp.dot(stacked(ref[b]), far_ref[at], preferred_element_type=jnp.float32)
             at += 1
     width = part.shape[1] // 2
     part = part[:, :width] + part[:, width:]
@@ -122,17 +174,17 @@
             out_ref[at] = total[c * rows:(c + 1) * rows]
 
 
-def close(stems, kept, got, cuts, targets):
-    rows, width = stems[0].shape[1], kept.shape[2]
+def close(stems, part, far, cuts, targets):
+    rows, width = part.shape[0] // 2, part.shape[1] // 2
     whole_tiles = rows % (8 * cuts) == 0
     shape = (len(targets), rows // cuts, width) if whole_tiles else (rows, width)
     out = pl.pallas_call(
         functools.partial(close_kernel, targets if whole_tiles else None),
         out_shape=jax.ShapeDtypeStruct(shape, jnp.float32),
         compiler_params=pltpu.CompilerParams(vmem_limit_bytes=24 * MIB),
-        cost_estimate=pl.CostEstimate(flops=8 * rows * kept.size, bytes_accessed=MIB, transcendentals=0),
+        cost_estimate=pl.CostEstimate(flops=4 * rows * far.size, bytes_accessed=MIB, transcendentals=0),
         name="close",
-    )(*stems, *got, kept)
+    )(*stems, part, far)
     return out if whole_tiles else out.reshape(cuts, -1)[np.array(targets)]
 
 
@@ -143,7 +195,7 @@
     def swap(x, p):
         return lax.ppermute(x, "stem", [(s, s ^ p) for s in range(stems)])
 
-    pieces = [stem_tensor] + [swap(stem_tensor, p) for p in range(2, stems, 2)]
+    stems_far = [swap(stem_tensor, p) for p in range(2, stems, 2)]
     kept, *sent = branch_sums(mid_tensors, right_tensors, stems)
     got = [swap(x, 1) for x in sent]
     groups = [
@@ -154,7 +206,8 @@
         for group in (0, 1)
     ]
     targets = [at % cuts for at in groups[0]]
-    spread = close(pieces, kept, got, cuts, targets)
+    part, far = fold(stem_tensor, kept, got)
+    spread = close(stems_far, part, far, cuts, targets)
     parts = lax.all_to_all(spread, ("stem", "cuts"), 0, 0, tiled=True, axis_index_groups=groups)
     total = jnp.sum(parts, axis=0).reshape(-1)
     return total + swap(total, 1)

time: 22.4 us -> 22.5 us (level)
  starting transfers between devices: 4.28 us -> 3.75 us
  waiting for transfers between devices: 2.02 us -> 2.43 us
    ppermute x6 -> x5, starting transfers between devices: 4.28 us -> 3.75 us  [swap(): return lax.ppermute(x, 'stem', [(s, s ^ p) for s in range(stems)])]
    ppermute x6 -> x5, waiting for transfers between devices: 2.02 us -> 2.43 us  [swap(): return lax.ppermute(x, 'stem', [(s, s ^ p) for s in range(stems)])]
    pallas_call x0 -> x1, Pallas kernels: none -> 0.33 us  [fold(): pl.pallas_call(fold_kernel, out_shape=[jax.ShapeDtypeStruct((2 * rows, 2...]
  transfers between devices with their start and end apart: 6 -> 5, of which waited for: 5 -> 2; matrix products, arithmetic and copies ran while one was open for 0% -> 0% of each run, Pallas kernels for 22% -> 23%
where the time goes in v25:
time: 22.5 us; the launch traced here: 22.4 us
  blocking collectives  9.98 us (44%)
  Pallas kernels  5.55 us (25%)
  starting transfers between devices  3.75 us (17%)
  waiting for transfers between devices  2.43 us (11%)
  other arithmetic  0.61 us (3%)
    all_to_all x1, blocking collectives, on_device(): lax.all_to_all(spread, ('stem', 'cuts'), 0, 0, tiled=True, axis_index_gro...  9.98 us
    pallas_call x1, Pallas kernels, branch_sums(): pl.pallas_call(functools.partial(branch_kernel, total // groups), in_spec...  4.92 us
    ppermute x5, starting transfers between devices, swap(): return lax.ppermute(x, 'stem', [(s, s ^ p) for s in range(stems)])  3.75 us
    ppermute x5, waiting for transfers between devices, swap(): return lax.ppermute(x, 'stem', [(s, s ^ p) for s in range(stems)])  2.43 us
    add x1, other arithmetic, on_device(): return total + swap(total, 1)  0.6 us
  transfers between devices with their start and end apart: 5, of which 2 were waited for; matrix products, arithmetic and copies ran while one was open for 0% of the time, Pallas kernels for 23%

profile of v25, /device:TPU:0, one launch (start us, length us, event | category | flops | bytes accessed | tf_op | source)
XLA Modules:
  0.0 22.4 jit_solution(3630655584423102193)
XLA Ops:
  0.0 0.0 copy-start
  0.0 3.0 %collective-permute-start = (bf16[2,64,1024]{2,1,0:T(8,128)(2,1)}, bf16[2,64,1024]{2,1,0:T(8,128)(2,1)S(1)}, u32[]{:S(2)}, u32[]{:S(2)}) collective-permute-start(bf16[2,64,1024]{2,1,0:T(8,128)(2,1)} %own_ref.1), channel_id=1, source_target_pairs={{0,2},{1,3},{2,0},{3,1},{4,6},{5,7},{6,4},{7,5},{8,10},{9,11},{10,... | collective-permute-start | bytes 786440 | tf_op jit(solution)/shard_map/ppermute | solution.py:196
  3.0 4.9 %branch_sums.1 = (f32[4,512,128]{2,1,0:T(8,128)S(1)}, bf16[688,128]{1,0:T(8,128)(2,1)S(1)}, bf16[688,128]{1,0:T(8,128)(2,1)S(1)}, bf16[672,128]{1,0:T(8,128)(2,1)S(1)}) custom-call(bf16[16,512,128]{2,1,0:T(8,128)(2,1)} %mid_hbm.1, bf16[8,16,64,128]{3,2,1,0:T(8,128)(2,1)} %right_hbm.1), custom_call_target="tpu_custom_call" | custom-call | flops 2147483648 | bytes 6291456 | tf_op jit(solution)/shard_map/branch_sums/pallas_call | solution.py:95
  7.9 0.1 collective-permute-start.1
  8.0 0.5 %collective-permute-start.2 = (bf16[688,128]{1,0:T(8,128)(2,1)S(1)}, bf16[688,128]{1,0:T(8,128)(2,1)S(1)}, u32[]{:S(2)}, u32[]{:S(2)}) collective-permute-start(bf16[688,128]{1,0:T(8,128)(2,1)S(1)} %get-tuple-element.13), channel_id=1, source_target_pairs={{0,1},{1,0},{2,3},{3,2},{4,5},{5,4},{6,7},{7,6},{8,9},{9,8},{10,11... | collective-permute-start | bytes 528392 | tf_op jit(solution)/shard_map/ppermute | solution.py:196
  8.5 0.1 collective-permute-start.3
  8.6 1.3 %collective-permute-done.3.refs_2_ = bf16[672,128]{1,0:T(8,128)(2,1)S(1)} collective-permute-done((bf16[672,128]{1,0:T(8,128)(2,1)S(1)}, bf16[672,128]{1,0:T(8,128)(2,1)S(1)}, u32[]{:S(2)}, u32[]{:S(2)}) %collective-permute-start.3) | collective-permute-done | bytes 172064 | tf_op jit(solution)/shard_map/ppermute | solution.py:196
  9.9 0.0 collective-permute-done.1.refs_0_
  9.9 0.0 collective-permute-done.2.refs_1_
  9.9 0.0 copy-done
  9.9 0.3 %fold.1 = (f32[128,256]{1,0:T(8,128)S(1)}, bf16[2,512,256]{2,1,0:T(8,128)(2,1)S(1)}) custom-call(bf16[2,64,1024]{2,1,0:T(8,128)(2,1)S(1)} %copy-done, f32[4,512,128]{2,1,0:T(8,128)S(1)} %get-tuple-element.11.kept_ref, bf16[688,128]{1,0:T(8,128)(2,1)S(1)} %collective-permute-done.1.refs_0_, bf16[688,128]{1,0:T(8,128)(2,1)S(1)} %collective-permute-done.2.refs_1_, ...), custom_call_target="tpu_custom_call" | custom-call | flops 134217728 | bytes 1048576 | tf_op jit(solution)/shard_map/fold/pallas_call | solution.py:145
  10.2 0.0 collective-permute-done.refs_0_
  10.2 0.3 %close.1 = f32[16,8,128]{2,1,0:T(8,128)S(1)} custom-call(bf16[2,64,1024]{2,1,0:T(8,128)(2,1)S(1)} %collective-permute-done.refs_0_, f32[128,256]{1,0:T(8,128)S(1)} %get-tuple-element.15.refs_1_, bf16[2,512,256]{2,1,0:T(8,128)(2,1)S(1)} %get-tuple-element.16.refs_2_), custom_call_target="tpu_custom_call" | custom-call | flops 67108864 | bytes 1048576 | tf_op jit(solution)/shard_map/close/pallas_call | solution.py:181
  10.5 10.0 %all_to_all.5 = f32[16,8,128]{2,1,0:T(8,128)S(1)} all-to-all(f32[16,8,128]{2,1,0:T(8,128)S(1)} %close.1), channel_id=1, replica_groups={{31,27,22,18,15,11,6,2,29,25,20,16,13,9,4,0},{30,26,23,19,14,10,7,3,28,..., dimensions={0} | all-to-all | bytes 131072 | tf_op jit(solution)/shard_map/all_to_all | solution.py:211
  20.5 0.1 collective-permute-start.4
  20.7 1.1 %collective-permute-done.4 = f32[1024]{0:T(1024)S(1)} collective-permute-done((f32[1024]{0:T(1024)S(1)}, f32[1024]{0:T(1024)S(1)}, u32[]{:S(2)}, u32[]{:S(2)}) %collective-permute-start.4) | collective-permute-done | bytes 4128 | tf_op jit(solution)/shard_map/ppermute | solution.py:196
  21.8 0.6 %bitcast_add_fusion = f32[1024]{0:T(1024)} fusion(f32[1024]{0:T(1024)S(1)} %collective-permute-done.4, f32[8,128]{1,0:T(8,128)S(1)} %reduce_sum.9), kind=kLoop, calls=%fused_computation | loop fusion | flops 1024 | bytes 12288 | tf_op jit(solution)/shard_map/add | solution.py:213
  (1 shorter events, 0.0 us)
Async XLA Ops:
  0.0 9.9 %copy-start = (bf16[2,64,1024]{2,1,0:T(8,128)(2,1)S(1)}, bf16[2,64,1024]{2,1,0:T(8,128)(2,1)}, u32[]{:S(2)}) copy-start(bf16[2,64,1024]{2,1,0:T(8,128)(2,1)} %own_ref.1) | copy-start | bytes 786436
  0.0 10.2 %collective-permute-start = (bf16[2,64,1024]{2,1,0:T(8,128)(2,1)}, bf16[2,64,1024]{2,1,0:T(8,128)(2,1)S(1)}, u32[]{:S(2)}, u32[]{:S(2)}) collective-permute-start(bf16[2,64,1024]{2,1,0:T(8,128)(2,1)} %own_ref.1), channel_id=1, source_target_pairs={{0,2},{1,3},{2,0},{3,1},{4,6},{5,7},{6,4},{7,5},{8,10},{9,11},{10,... | collective-permute-start | bytes 786440 | tf_op jit(solution)/shard_map/ppermute | solution.py:196
  7.9 2.0 %collective-permute-start.1 = (bf16[688,128]{1,0:T(8,128)(2,1)S(1)}, bf16[688,128]{1,0:T(8,128)(2,1)S(1)}, u32[]{:S(2)}, u32[]{:S(2)}) collective-permute-start(bf16[688,128]{1,0:T(8,128)(2,1)S(1)} %get-tuple-element.12), channel_id=1, source_target_pairs={{0,1},{1,0},{2,3},{3,2},{4,5},{5,4},{6,7},{7,6},{8,9},{9,8},{10,11... | collective-permute-start | bytes 528392 | tf_op jit(solution)/shard_map/ppermute | solution.py:196
  8.0 1.9 %collective-permute-start.2 = (bf16[688,128]{1,0:T(8,128)(2,1)S(1)}, bf16[688,128]{1,0:T(8,128)(2,1)S(1)}, u32[]{:S(2)}, u32[]{:S(2)}) collective-permute-start(bf16[688,128]{1,0:T(8,128)(2,1)S(1)} %get-tuple-element.13), channel_id=1, source_target_pairs={{0,1},{1,0},{2,3},{3,2},{4,5},{5,4},{6,7},{7,6},{8,9},{9,8},{10,11... | collective-permute-start | bytes 528392 | tf_op jit(solution)/shard_map/ppermute | solution.py:196
  8.5 1.4 %collective-permute-start.3 = (bf16[672,128]{1,0:T(8,128)(2,1)S(1)}, bf16[672,128]{1,0:T(8,128)(2,1)S(1)}, u32[]{:S(2)}, u32[]{:S(2)}) collective-permute-start(bf16[672,128]{1,0:T(8,128)(2,1)S(1)} %get-tuple-element.14), channel_id=1, source_target_pairs={{0,1},{1,0},{2,3},{3,2},{4,5},{5,4},{6,7},{7,6},{8,9},{9,8},{10,11... | collective-permute-start | bytes 516104 | tf_op jit(solution)/shard_map/ppermute | solution.py:196
  20.5 1.2 %collective-permute-start.4 = (f32[1024]{0:T(1024)S(1)}, f32[1024]{0:T(1024)S(1)}, u32[]{:S(2)}, u32[]{:S(2)}) collective-permute-start(f32[1024]{0:T(1024)S(1)} %bitcast.2), channel_id=1, source_target_pairs={{0,1},{1,0},{2,3},{3,2},{4,5},{5,4},{6,7},{7,6},{8,9},{9,8},{10,11... | collective-permute-start | bytes 12296 | tf_op jit(solution)/shard_map/ppermute | solution.py:196

commit v26 on v22

--- a/solution.py
+++ b/solution.py
@@ -16,6 +16,23 @@
     lane = lax.broadcasted_iota(jnp.int32, x.shape, x.ndim - 1)
     rolled = pltpu.roll(x, half, x.ndim - 1)
     return jnp.where(lane < half, -rolled, rolled)
+
+
+def segments(blocks, depth, sizes):
+    out, row = [], 0
+    for piece, size in enumerate(sizes):
+        end = row + size
+        first = row
+        while row < end:
+            count = min(end, (row // depth + 1) * depth) - row
+            out.append((row // depth, row % depth, piece, row - first, count))
+            row += count
+    return out
+
+
+def piece_sizes(rows, count):
+    size = -(-rows // (16 * count)) * 16
+    return [min(size, rows - at) for at in range(0, rows, size)]
 
 
 def branch_kernel(blocks, mid_hbm, right_hbm, kept_ref, *refs):
@@ -32,8 +49,9 @@
         return pltpu.make_async_copy(mid_hbm.at[at], mid_ref.at[at], mid_sem.at[n])
 
     def right_copy(q):
-        p = jnp.where(q < half, 2 * q + 1, 2 * q - groups)
-        source = right_hbm.at[pl.ds((me ^ p) * blocks, blocks)]
+        stays = jnp.where(q < half, 0, 1)
+        side = (me // 2) ^ (me % 2) ^ stays ^ 1
+        source = right_hbm.at[pl.ds((2 * side + q % 2) * blocks, blocks)]
         target = wide_ref.at[pl.ds(q * blocks, blocks), :, pl.ds(0, inner)]
         return pltpu.make_async_copy(source, target, right_sem.at[q])
 
@@ -61,24 +79,27 @@
         return carry
 
     lax.fori_loop(0, 2, multiply, 0)
-    for b, ref in enumerate(sent_refs):
-        cols = slice(b * width, (b + 1) * width)
-        ref[...] = sums_ref[0, :, cols].astype(ref.dtype)
-        kept_ref[b] = sums_ref[1, :, cols]
+    sizes = [ref.shape[0] for ref in sent_refs]
+    for b, row, piece, at, count in segments(total // 2, sums_ref.shape[1], sizes):
+        part = sums_ref[0, row:row + count, b * width:(b + 1) * width]
+        sent_refs[piece][at:at + count] = part.astype(jnp.bfloat16)
+    for b in range(total // 2):
+        kept_ref[b] = sums_ref[1, :, b * width:(b + 1) * width]
 
 
 def branch_sums(mid, right, groups):
     pairs, depth, width = mid.shape
     total, _, inner, _ = right.shape
+    sizes = piece_sizes(total // 2 * depth, 3)
     vmem = pl.BlockSpec(memory_space=pltpu.VMEM)
     hbm = pl.BlockSpec(memory_space=pltpu.HBM)
     return pl.pallas_call(
         functools.partial(branch_kernel, total // groups),
         in_specs=[hbm, hbm],
-        out_specs=[vmem] * (1 + total // 2),
+        out_specs=[vmem] * (1 + len(sizes)),
         out_shape=[
             jax.ShapeDtypeStruct((total // 2, depth, width), jnp.float32),
-        ] + [jax.ShapeDtypeStruct((depth, width), jnp.bfloat16)] * (total // 2),
+        ] + [jax.ShapeDtypeStruct((size, width), jnp.bfloat16) for size in sizes],
         scratch_shapes=[
             pltpu.VMEM((2, depth, total // 2 * width), jnp.float32),
             pltpu.VMEM(mid.shape, mid.dtype),
@@ -95,16 +116,18 @@
 
 
 def close_kernel(targets, *refs):
-    *more, kept_ref, out_ref = refs
-    stem_refs, got_refs = more[:-kept_ref.shape[0]], more[-kept_ref.shape[0]:]
+    own_ref, cross_ref, cycle_ref, *got_refs, kept_ref, out_ref = refs
+    first_core = lax.axis_index("stem") % 2 == 0
+    pieces = segments(kept_ref.shape[0], kept_ref.shape[1], [ref.shape[0] for ref in got_refs])
     part = None
     at = 0
-    for ref in stem_refs:
-        for b in range(ref.shape[0]):
-            block = ref[b]
+    for when_first, when_second in ((own_ref, cycle_ref), (cycle_ref, cross_ref)):
+        for b in range(own_ref.shape[0]):
+            block = jnp.where(first_core, when_first[b], when_second[b])
             half = block.shape[-1] // 2
             rows = jnp.concatenate([block[:, :half], block[:, half:]], axis=0)
-            sums = kept_ref[at] + got_refs[at][...].astype(jnp.float32)
+            got = [got_refs[piece][row:row + count] for block_at, _, piece, row, count in pieces if block_at == at]
+            sums = kept_ref[at] + jnp.concatenate(got, axis=0).astype(jnp.float32)
             high = sums.astype(jnp.bfloat16)
             low = (sums - high.astype(jnp.float32)).astype(jnp.bfloat16)
             term = jnp.dot(rows, jnp.concatenate([high, low], axis=1), preferred_element_type=jnp.float32)
@@ -143,7 +166,17 @@
     def swap(x, p):
         return lax.ppermute(x, "stem", [(s, s ^ p) for s in range(stems)])
 
-    pieces = [stem_tensor] + [swap(stem_tensor, p) for p in range(2, stems, 2)]
+    def route(target):
+        pairs = []
+        for at in np.ndindex(cuts, 2, 2):
+            cut, side, core = target(*at)
+            pairs.append((at[0] * 4 + at[1] * 2 + at[2], cut * 4 + side * 2 + core))
+        return lax.ppermute(stem_tensor, ("cuts", "stem"), pairs)
+
+    assert stems == 4
+    cross = route(lambda cut, side, core: (cut, 1 - side, 1) if core else (cut ^ 1, side, 0))
+    cycle = route(lambda cut, side, core: (cut, side, 0) if core else (cut, 1 - side, 1))
+    pieces = [stem_tensor, cross, cycle]
     kept, *sent = branch_sums(mid_tensors, right_tensors, stems)
     got = [swap(x, 1) for x in sent]
     groups = [

time: 22.4 us -> 22.9 us (1.022)
  blocking collectives: 9.9 us -> 10.3 us
  waiting for transfers between devices: 2.02 us -> 2.31 us
    ppermute x6 -> x4, starting transfers between devices: 4.28 us -> 1.15 us  [swap(): return lax.ppermute(x, 'stem', [(s, s ^ p) for s in range(stems)])]
    ppermute x0 -> x2, starting transfers between devices: none -> 2.94 us  [route(): return lax.ppermute(stem_tensor, ('cuts', 'stem'), pairs)]
    all_to_all x1, blocking collectives: 9.9 us -> 10.3 us  [on_device(): lax.all_to_all(spread, ('stem', 'cuts'), 0, 0, tiled=True, axis_index_gro...]
    ppermute x6 -> x4, waiting for transfers between devices: 2.02 us -> 2.31 us  [swap(): return lax.ppermute(x, 'stem', [(s, s ^ p) for s in range(stems)])]
  transfers between devices with their start and end apart: 6 -> 6, of which waited for: 5 -> 2; matrix products, arithmetic and copies ran while one was open for 0% -> 0% of each run, Pallas kernels for 22% -> 22%
where the time goes in v26:
time: 22.9 us; the launch traced here: 22.7 us
  blocking collectives  10.3 us (45%)
  Pallas kernels  5.38 us (23%)
  starting transfers between devices  4.09 us (18%)
  waiting for transfers between devices  2.31 us (10%)
  other arithmetic  0.61 us (3%)
    all_to_all x1, blocking collectives, on_device(): lax.all_to_all(spread, ('stem', 'cuts'), 0, 0, tiled=True, axis_index_gro...  10.3 us
    pallas_call x1, Pallas kernels, branch_sums(): pl.pallas_call(functools.partial(branch_kernel, total // groups), in_spec...  4.93 us
    ppermute x2, starting transfers between devices, route(): return lax.ppermute(stem_tensor, ('cuts', 'stem'), pairs)  2.94 us
    ppermute x4, waiting for transfers between devices, swap(): return lax.ppermute(x, 'stem', [(s, s ^ p) for s in range(stems)])  2.31 us
    ppermute x4, starting transfers between devices, swap(): return lax.ppermute(x, 'stem', [(s, s ^ p) for s in range(stems)])  1.15 us
    add x1, other arithmetic, on_device(): return total + swap(total, 1)  0.6 us
  transfers between devices with their start and end apart: 6, of which 2 were waited for; matrix products, arithmetic and copies ran while one was open for 0% of the time, Pallas kernels for 22%

profile of v26, /device:TPU:0, one launch (start us, length us, event | category | flops | bytes accessed | tf_op | source)
XLA Modules:
  0.0 22.7 jit_solution(16216005280926541747)
XLA Ops:
  0.0 0.0 copy-start
  0.0 2.9 %collective-permute-start = (bf16[2,64,1024]{2,1,0:T(8,128)(2,1)}, bf16[2,64,1024]{2,1,0:T(8,128)(2,1)S(1)}, u32[]{:S(2)}, u32[]{:S(2)}) collective-permute-start(bf16[2,64,1024]{2,1,0:T(8,128)(2,1)} %refs_0_.1), channel_id=1, source_target_pairs={{0,4},{1,3},{2,6},{3,1},{4,0},{5,7},{6,2},{7,5},{8,12},{9,11},{10,... | collective-permute-start | bytes 786440 | tf_op jit(solution)/shard_map/ppermute | solution.py:174
  2.9 0.0 collective-permute-start.1
  2.9 4.9 %branch_sums.1 = (f32[4,512,128]{2,1,0:T(8,128)S(1)}, bf16[688,128]{1,0:T(8,128)(2,1)S(1)}, bf16[688,128]{1,0:T(8,128)(2,1)S(1)}, bf16[672,128]{1,0:T(8,128)(2,1)S(1)}) custom-call(bf16[16,512,128]{2,1,0:T(8,128)(2,1)} %mid_hbm.1, bf16[8,16,64,128]{3,2,1,0:T(8,128)(2,1)} %right_hbm.1), custom_call_target="tpu_custom_call" | custom-call | flops 2147483648 | bytes 6291456 | tf_op jit(solution)/shard_map/branch_sums/pallas_call | solution.py:96
  7.9 0.6 %collective-permute-start.2 = (bf16[688,128]{1,0:T(8,128)(2,1)S(1)}, bf16[688,128]{1,0:T(8,128)(2,1)S(1)}, u32[]{:S(2)}, u32[]{:S(2)}) collective-permute-start(bf16[688,128]{1,0:T(8,128)(2,1)S(1)} %get-tuple-element.9), channel_id=1, source_target_pairs={{0,1},{1,0},{2,3},{3,2},{4,5},{5,4},{6,7},{7,6},{8,9},{9,8},{10,11... | collective-permute-start | bytes 528392 | tf_op jit(solution)/shard_map/ppermute | solution.py:167
  8.5 0.1 collective-permute-start.3
  8.5 0.4 %collective-permute-start.4 = (bf16[672,128]{1,0:T(8,128)(2,1)S(1)}, bf16[672,128]{1,0:T(8,128)(2,1)S(1)}, u32[]{:S(2)}, u32[]{:S(2)}) collective-permute-start(bf16[672,128]{1,0:T(8,128)(2,1)S(1)} %get-tuple-element.11), channel_id=1, source_target_pairs={{0,1},{1,0},{2,3},{3,2},{4,5},{5,4},{6,7},{7,6},{8,9},{9,8},{10,11... | collective-permute-start | bytes 516104 | tf_op jit(solution)/shard_map/ppermute | solution.py:167
  9.0 1.1 %collective-permute-done.4.refs_5_ = bf16[672,128]{1,0:T(8,128)(2,1)S(1)} collective-permute-done((bf16[672,128]{1,0:T(8,128)(2,1)S(1)}, bf16[672,128]{1,0:T(8,128)(2,1)S(1)}, u32[]{:S(2)}, u32[]{:S(2)}) %collective-permute-start.4) | collective-permute-done | bytes 172064 | tf_op jit(solution)/shard_map/ppermute | solution.py:167
  10.1 0.0 collective-permute-done.2.refs_3_
  10.1 0.0 collective-permute-done.3.refs_4_
  10.1 0.0 collective-permute-done.refs_1_
  10.1 0.0 collective-permute-done.1.refs_2_
  10.1 0.0 copy-done
  10.2 0.4 %close.1 = f32[16,8,128]{2,1,0:T(8,128)S(1)} custom-call(bf16[2,64,1024]{2,1,0:T(8,128)(2,1)S(1)} %copy-done, bf16[2,64,1024]{2,1,0:T(8,128)(2,1)S(1)} %collective-permute-done.refs_1_, bf16[2,64,1024]{2,1,0:T(8,128)(2,1)S(1)} %collective-permute-done.1.refs_2_, bf16[688,128]{1,0:T(8,128)(2,1)S(1)} %collective-permute-done.2.refs_3_, ...), custom_call_target="tpu_custom_call" | custom-call | flops 134217728 | bytes 1048576 | tf_op jit(solution)/shard_map/close/pallas_call | solution.py:152
  10.6 10.3 %all_to_all.5 = f32[16,8,128]{2,1,0:T(8,128)S(1)} all-to-all(f32[16,8,128]{2,1,0:T(8,128)S(1)} %close.1), channel_id=1, replica_groups={{31,27,22,18,15,11,6,2,29,25,20,16,13,9,4,0},{30,26,23,19,14,10,7,3,28,..., dimensions={0} | all-to-all | bytes 131072 | tf_op jit(solution)/shard_map/all_to_all | solution.py:191
  20.9 0.1 collective-permute-start.5
  21.0 1.2 %collective-permute-done.5 = f32[1024]{0:T(1024)S(1)} collective-permute-done((f32[1024]{0:T(1024)S(1)}, f32[1024]{0:T(1024)S(1)}, u32[]{:S(2)}, u32[]{:S(2)}) %collective-permute-start.5) | collective-permute-done | bytes 4128 | tf_op jit(solution)/shard_map/ppermute | solution.py:167
  22.1 0.6 %bitcast_add_fusion = f32[1024]{0:T(1024)} fusion(f32[1024]{0:T(1024)S(1)} %collective-permute-done.5, f32[8,128]{1,0:T(8,128)S(1)} %reduce_sum.9), kind=kLoop, calls=%fused_computation | loop fusion | flops 1024 | bytes 12288 | tf_op jit(solution)/shard_map/add | solution.py:193
  (1 shorter events, 0.0 us)
Async XLA Ops:
  0.0 10.1 %copy-start = (bf16[2,64,1024]{2,1,0:T(8,128)(2,1)S(1)}, bf16[2,64,1024]{2,1,0:T(8,128)(2,1)}, u32[]{:S(2)}) copy-start(bf16[2,64,1024]{2,1,0:T(8,128)(2,1)} %refs_0_.1) | copy-start | bytes 786436
  0.0 10.1 %collective-permute-start = (bf16[2,64,1024]{2,1,0:T(8,128)(2,1)}, bf16[2,64,1024]{2,1,0:T(8,128)(2,1)S(1)}, u32[]{:S(2)}, u32[]{:S(2)}) collective-permute-start(bf16[2,64,1024]{2,1,0:T(8,128)(2,1)} %refs_0_.1), channel_id=1, source_target_pairs={{0,4},{1,3},{2,6},{3,1},{4,0},{5,7},{6,2},{7,5},{8,12},{9,11},{10,... | collective-permute-start | bytes 786440 | tf_op jit(solution)/shard_map/ppermute | solution.py:174
  2.9 7.2 %collective-permute-start.1 = (bf16[2,64,1024]{2,1,0:T(8,128)(2,1)}, bf16[2,64,1024]{2,1,0:T(8,128)(2,1)S(1)}, u32[]{:S(2)}, u32[]{:S(2)}) collective-permute-start(bf16[2,64,1024]{2,1,0:T(8,128)(2,1)} %refs_0_.1), channel_id=1, source_target_pairs={{0,3},{1,0},{2,1},{3,2},{4,7},{5,4},{6,5},{7,6},{8,11},{9,8},{10,9... | collective-permute-start | bytes 786440 | tf_op jit(solution)/shard_map/ppermute | solution.py:174
  7.9 2.2 %collective-permute-start.2 = (bf16[688,128]{1,0:T(8,128)(2,1)S(1)}, bf16[688,128]{1,0:T(8,128)(2,1)S(1)}, u32[]{:S(2)}, u32[]{:S(2)}) collective-permute-start(bf16[688,128]{1,0:T(8,128)(2,1)S(1)} %get-tuple-element.9), channel_id=1, source_target_pairs={{0,1},{1,0},{2,3},{3,2},{4,5},{5,4},{6,7},{7,6},{8,9},{9,8},{10,11... | collective-permute-start | bytes 528392 | tf_op jit(solution)/shard_map/ppermute | solution.py:167
  8.5 1.7 %collective-permute-start.3 = (bf16[688,128]{1,0:T(8,128)(2,1)S(1)}, bf16[688,128]{1,0:T(8,128)(2,1)S(1)}, u32[]{:S(2)}, u32[]{:S(2)}) collective-permute-start(bf16[688,128]{1,0:T(8,128)(2,1)S(1)} %get-tuple-element.10), channel_id=1, source_target_pairs={{0,1},{1,0},{2,3},{3,2},{4,5},{5,4},{6,7},{7,6},{8,9},{9,8},{10,11... | collective-permute-start | bytes 528392 | tf_op jit(solution)/shard_map/ppermute | solution.py:167
  8.5 1.6 %collective-permute-start.4 = (bf16[672,128]{1,0:T(8,128)(2,1)S(1)}, bf16[672,128]{1,0:T(8,128)(2,1)S(1)}, u32[]{:S(2)}, u32[]{:S(2)}) collective-permute-start(bf16[672,128]{1,0:T(8,128)(2,1)S(1)} %get-tuple-element.11), channel_id=1, source_target_pairs={{0,1},{1,0},{2,3},{3,2},{4,5},{5,4},{6,7},{7,6},{8,9},{9,8},{10,11... | collective-permute-start | bytes 516104 | tf_op jit(solution)/shard_map/ppermute | solution.py:167
  20.9 1.2 %collective-permute-start.5 = (f32[1024]{0:T(1024)S(1)}, f32[1024]{0:T(1024)S(1)}, u32[]{:S(2)}, u32[]{:S(2)}) collective-permute-start(f32[1024]{0:T(1024)S(1)} %bitcast.2), channel_id=1, source_target_pairs={{0,1},{1,0},{2,3},{3,2},{4,5},{5,4},{6,7},{7,6},{8,9},{9,8},{10,11... | collective-permute-start | bytes 12296 | tf_op jit(solution)/shard_map/ppermute | solution.py:167

commit v27 on v26

--- a/solution.py
+++ b/solution.py
@@ -9,6 +9,7 @@
 from jax.sharding import PartitionSpec as P
 
 MIB = 1024 * 1024
+LEAVE_MIB = 48
 
 
 def turn(x):
@@ -35,9 +36,17 @@
     return [min(size, rows - at) for at in range(0, rows, size)]
 
 
-def branch_kernel(blocks, mid_hbm, right_hbm, kept_ref, *refs):
-    *sent_refs, sums_ref, mid_ref, wide_ref, mid_sem, right_sem = refs
-    pairs, _, width = mid_ref.shape
+def product(mid_ref, wide_ref):
+    pairs = mid_ref.shape[0]
+    left = jnp.concatenate([mid_ref[j] for j in range(pairs)], axis=1)
+    blocks, _, rows, width = wide_ref.shape
+    right = [wide_ref[b].reshape(pairs * rows, width) for b in range(blocks)]
+    return jnp.dot(left, jnp.concatenate(right, axis=1), preferred_element_type=jnp.float32)
+
+
+def leave_kernel(blocks, mid_hbm, right_hbm, mid_ref, stay_ref, *refs):
+    *sent_refs, leave_ref, mid_sem, right_sem = refs
+    pairs, depth, width = mid_ref.shape
     total, _, inner, _ = right_hbm.shape
     groups = total // blocks
     half = groups // 2
@@ -48,71 +57,84 @@
         at = pl.ds(n * chunk, chunk)
         return pltpu.make_async_copy(mid_hbm.at[at], mid_ref.at[at], mid_sem.at[n])
 
-    def right_copy(q):
-        stays = jnp.where(q < half, 0, 1)
+    def right_copy(q, wide_ref, stays):
         side = (me // 2) ^ (me % 2) ^ stays ^ 1
-        source = right_hbm.at[pl.ds((2 * side + q % 2) * blocks, blocks)]
+        source = right_hbm.at[pl.ds((2 * side + q) * blocks, blocks)]
         target = wide_ref.at[pl.ds(q * blocks, blocks), :, pl.ds(0, inner)]
-        return pltpu.make_async_copy(source, target, right_sem.at[q])
-
-    for q in range(groups):
-        right_copy(q).start()
+        return pltpu.make_async_copy(source, target, right_sem.at[stays * half + q])
+
+    for q in range(half):
+        right_copy(q, leave_ref, 0).start()
     for n in range(mid_sem.shape[0]):
         mid_copy(n).start()
-
-    def widen(q, carry):
-        right_copy(q).wait()
-        for b in range(blocks):
-            for j in range(pairs):
-                upper = wide_ref[q * blocks + b, j, :inner]
-                wide_ref[q * blocks + b, j, inner:] = turn(upper.astype(jnp.float32)).astype(upper.dtype)
-        return carry
-
-    lax.fori_loop(0, groups, widen, 0)
+    for q in range(half):
+        right_copy(q, stay_ref, 1).start()
+
+    def widen(wide_ref, stays):
+        def step(q, carry):
+            right_copy(q, wide_ref, stays).wait()
+            for b in range(blocks):
+                for j in range(pairs):
+                    upper = wide_ref[q * blocks + b, j, :inner]
+                    wide_ref[q * blocks + b, j, inner:] = turn(upper.astype(jnp.float32)).astype(upper.dtype)
+            return carry
+
+        lax.fori_loop(0, half, step, 0)
+
+    widen(leave_ref, 0)
     for n in range(mid_sem.shape[0]):
         mid_copy(n).wait()
-
-    def multiply(h, carry):
-        left = jnp.concatenate([mid_ref[j] for j in range(pairs)], axis=1)
-        right = [wide_ref[h * (total // 2) + b].reshape(pairs * 2 * inner, width) for b in range(total // 2)]
-        sums_ref[h] = jnp.dot(left, jnp.concatenate(right, axis=1), preferred_element_type=jnp.float32)
-        return carry
-
-    lax.fori_loop(0, 2, multiply, 0)
+    sums = product(mid_ref, leave_ref)
     sizes = [ref.shape[0] for ref in sent_refs]
-    for b, row, piece, at, count in segments(total // 2, sums_ref.shape[1], sizes):
-        part = sums_ref[0, row:row + count, b * width:(b + 1) * width]
+    for b, row, piece, at, count in segments(total // 2, depth, sizes):
+        part = sums[row:row + count, b * width:(b + 1) * width]
         sent_refs[piece][at:at + count] = part.astype(jnp.bfloat16)
-    for b in range(total // 2):
-        kept_ref[b] = sums_ref[1, :, b * width:(b + 1) * width]
+    widen(stay_ref, 1)
+
+
+def stay_kernel(mid_ref, wide_ref, kept_ref):
+    sums = product(mid_ref, wide_ref)
+    width = kept_ref.shape[2]
+    for b in range(kept_ref.shape[0]):
+        kept_ref[b] = sums[:, b * width:(b + 1) * width]
 
 
 def branch_sums(mid, right, groups):
     pairs, depth, width = mid.shape
     total, _, inner, _ = right.shape
-    sizes = piece_sizes(total // 2 * depth, 3)
+    half = total // 2
+    sizes = piece_sizes(half * depth, 3)
+    wide = (half, pairs, 2 * inner, width)
     vmem = pl.BlockSpec(memory_space=pltpu.VMEM)
     hbm = pl.BlockSpec(memory_space=pltpu.HBM)
-    return pl.pallas_call(
-        functools.partial(branch_kernel, total // groups),
+    cost = pl.CostEstimate(
+        flops=depth * pairs * width * total * width, bytes_accessed=4 * MIB, transcendentals=0
+    )
+    mid_here, wide_here, *sent = pl.pallas_call(
+        functools.partial(leave_kernel, total // groups),
         in_specs=[hbm, hbm],
-        out_specs=[vmem] * (1 + len(sizes)),
+        out_specs=[vmem] * (2 + len(sizes)),
         out_shape=[
-            jax.ShapeDtypeStruct((total // 2, depth, width), jnp.float32),
+            jax.ShapeDtypeStruct(mid.shape, mid.dtype),
+            jax.ShapeDtypeStruct(wide, right.dtype),
         ] + [jax.ShapeDtypeStruct((size, width), jnp.bfloat16) for size in sizes],
         scratch_shapes=[
-            pltpu.VMEM((2, depth, total // 2 * width), jnp.float32),
-            pltpu.VMEM(mid.shape, mid.dtype),
-            pltpu.VMEM((total, pairs, 2 * inner, width), right.dtype),
+            pltpu.VMEM(wide, right.dtype),
             pltpu.SemaphoreType.DMA((4,)),
             pltpu.SemaphoreType.DMA((groups,)),
         ],
-        compiler_params=pltpu.CompilerParams(vmem_limit_bytes=52 * MIB),
-        cost_estimate=pl.CostEstimate(
-            flops=2 * depth * pairs * width * total * width, bytes_accessed=6 * MIB, transcendentals=0
-        ),
-        name="branch_sums",
+        compiler_params=pltpu.CompilerParams(vmem_limit_bytes=LEAVE_MIB * MIB),
+        cost_estimate=cost,
+        name="leave",
     )(mid, right)
+    kept = pl.pallas_call(
+        stay_kernel,
+        out_shape=jax.ShapeDtypeStruct((half, depth, width), jnp.float32),
+        compiler_params=pltpu.CompilerParams(vmem_limit_bytes=24 * MIB),
+        cost_estimate=cost,
+        name="stay",
+    )(mid_here, wide_here)
+    return kept, *sent
 
 
 def close_kernel(targets, *refs):

time: 22.9 us -> 22.2 us (0.969)
  waiting for transfers between devices: 2.31 us -> 1.17 us
  blocking collectives: 10.3 us -> 10.7 us
    ppermute x4, waiting for transfers between devices: 2.31 us -> 1.16 us  [swap(): return lax.ppermute(x, 'stem', [(s, s ^ p) for s in range(stems)])]
    all_to_all x1, blocking collectives: 10.3 us -> 10.7 us  [on_device(): lax.all_to_all(spread, ('stem', 'cuts'), 0, 0, tiled=True, axis_index_gro...]
    pallas_call x1 -> x2, Pallas kernels: 4.93 us -> 4.97 us  [the longest x1 3.72 us: branch_sums(): pl.pallas_call(functools.partial(leave_kernel, total // groups), in_specs...]
  transfers between devices with their start and end apart: 6 -> 6, of which waited for: 2 -> 1; matrix products, arithmetic and copies ran while one was open for 0% -> 0% of each run, Pallas kernels for 22% -> 22%
where the time goes in v27:
time: 22.2 us; the launch traced here: 22.1 us
  blocking collectives  10.7 us (48%)
  Pallas kernels  5.42 us (24%)
  starting transfers between devices  4.09 us (18%)
  waiting for transfers between devices  1.17 us (5%)
  other arithmetic  0.61 us (3%)
    all_to_all x1, blocking collectives, on_device(): lax.all_to_all(spread, ('stem', 'cuts'), 0, 0, tiled=True, axis_index_gro...  10.7 us
    pallas_call x1, Pallas kernels, branch_sums(): pl.pallas_call(functools.partial(leave_kernel, total // groups), in_specs...  3.72 us
    ppermute x2, starting transfers between devices, route(): return lax.ppermute(stem_tensor, ('cuts', 'stem'), pairs)  2.94 us
    pallas_call x1, Pallas kernels, branch_sums(): pl.pallas_call(stay_kernel, out_shape=jax.ShapeDtypeStruct((half, depth,...  1.24 us
    ppermute x4, waiting for transfers between devices, swap(): return lax.ppermute(x, 'stem', [(s, s ^ p) for s in range(stems)])  1.16 us
    ppermute x4, starting transfers between devices, swap(): return lax.ppermute(x, 'stem', [(s, s ^ p) for s in range(stems)])  1.15 us
    add x1, other arithmetic, on_device(): return total + swap(total, 1)  0.6 us
    pallas_call x1, Pallas kernels, close(): pl.pallas_call(functools.partial(close_kernel, targets if whole_tiles els...  0.46 us
  transfers between devices with their start and end apart: 6, of which 1 were waited for; matrix products, arithmetic and copies ran while one was open for 0% of the time, Pallas kernels for 22%

profile of v27, /device:TPU:0, one launch (start us, length us, event | category | flops | bytes accessed | tf_op | source)
XLA Modules:
  0.0 22.1 jit_solution(5568361150372122319)
XLA Ops:
  0.0 2.9 %collective-permute-start = (bf16[2,64,1024]{2,1,0:T(8,128)(2,1)}, bf16[2,64,1024]{2,1,0:T(8,128)(2,1)S(1)}, u32[]{:S(2)}, u32[]{:S(2)}) collective-permute-start(bf16[2,64,1024]{2,1,0:T(8,128)(2,1)} %refs_0_.1), channel_id=1, source_target_pairs={{0,4},{1,3},{2,6},{3,1},{4,0},{5,7},{6,2},{7,5},{8,12},{9,11},{10,... | collective-permute-start | bytes 786440 | tf_op jit(solution)/shard_map/ppermute | solution.py:196
  2.9 0.0 collective-permute-start.1
  2.9 3.7 %leave.1 = (bf16[16,512,128]{2,1,0:T(8,128)(2,1)S(1)}, bf16[4,16,128,128]{3,2,1,0:T(8,128)(2,1)S(1)}, bf16[688,128]{1,0:T(8,128)(2,1)S(1)}, bf16[688,128]{1,0:T(8,128)(2,1)S(1)}, bf16[672,128]{1,0:T(8,128)(2,1)S(1)}) custom-call(bf16[16,512,128]{2,1,0:T(8,128)(2,1)} %mid_hbm.1, bf16[8,16,64,128]{3,2,1,0:T(8,128)(2,1)} %right_hbm.1), custom_call_target="tpu_custom_call" | custom-call | flops 1073741824 | bytes 4194304 | tf_op jit(solution)/shard_map/leave/pallas_call | solution.py:113
  6.7 0.6 %collective-permute-start.2 = (bf16[688,128]{1,0:T(8,128)(2,1)S(1)}, bf16[688,128]{1,0:T(8,128)(2,1)S(1)}, u32[]{:S(2)}, u32[]{:S(2)}) collective-permute-start(bf16[688,128]{1,0:T(8,128)(2,1)S(1)} %get-tuple-element.10), channel_id=1, source_target_pairs={{0,1},{1,0},{2,3},{3,2},{4,5},{5,4},{6,7},{7,6},{8,9},{9,8},{10,11... | collective-permute-start | bytes 528392 | tf_op jit(solution)/shard_map/ppermute | solution.py:189
  7.2 0.1 collective-permute-start.3
  7.3 0.4 %collective-permute-start.4 = (bf16[672,128]{1,0:T(8,128)(2,1)S(1)}, bf16[672,128]{1,0:T(8,128)(2,1)S(1)}, u32[]{:S(2)}, u32[]{:S(2)}) collective-permute-start(bf16[672,128]{1,0:T(8,128)(2,1)S(1)} %get-tuple-element.12), channel_id=1, source_target_pairs={{0,1},{1,0},{2,3},{3,2},{4,5},{5,4},{6,7},{7,6},{8,9},{9,8},{10,11... | collective-permute-start | bytes 516104 | tf_op jit(solution)/shard_map/ppermute | solution.py:189
  7.8 0.0 copy-start
  7.8 1.2 %stay.1.refs_6_ = f32[4,512,128]{2,1,0:T(8,128)S(1)} custom-call(bf16[16,512,128]{2,1,0:T(8,128)(2,1)S(1)} %get-tuple-element.13.mid_ref, bf16[4,16,128,128]{3,2,1,0:T(8,128)(2,1)S(1)} %get-tuple-element.14.wide_ref), custom_call_target="tpu_custom_call" | custom-call | flops 1073741824 | bytes 4194304 | tf_op jit(solution)/shard_map/stay/pallas_call | solution.py:130
  9.0 0.0 collective-permute-done.4.refs_5_
  9.0 0.0 collective-permute-done.2.refs_3_
  9.0 0.0 collective-permute-done.3.refs_4_
  9.0 0.0 collective-permute-done.refs_1_
  9.1 0.0 collective-permute-done.1.refs_2_
  9.1 0.0 copy-done
  9.1 0.5 %close.1 = f32[16,8,128]{2,1,0:T(8,128)S(1)} custom-call(bf16[2,64,1024]{2,1,0:T(8,128)(2,1)S(1)} %copy-done, bf16[2,64,1024]{2,1,0:T(8,128)(2,1)S(1)} %collective-permute-done.refs_1_, bf16[2,64,1024]{2,1,0:T(8,128)(2,1)S(1)} %collective-permute-done.1.refs_2_, bf16[688,128]{1,0:T(8,128)(2,1)S(1)} %collective-permute-done.2.refs_3_, ...), custom_call_target="tpu_custom_call" | custom-call | flops 134217728 | bytes 1048576 | tf_op jit(solution)/shard_map/close/pallas_call | solution.py:174
  9.5 10.7 %all_to_all.5 = f32[16,8,128]{2,1,0:T(8,128)S(1)} all-to-all(f32[16,8,128]{2,1,0:T(8,128)S(1)} %close.1), channel_id=1, replica_groups={{31,27,22,18,15,11,6,2,29,25,20,16,13,9,4,0},{30,26,23,19,14,10,7,3,28,..., dimensions={0} | all-to-all | bytes 131072 | tf_op jit(solution)/shard_map/all_to_all | solution.py:213
  20.2 0.1 collective-permute-start.5
  20.3 1.2 %collective-permute-done.5 = f32[1024]{0:T(1024)S(1)} collective-permute-done((f32[1024]{0:T(1024)S(1)}, f32[1024]{0:T(1024)S(1)}, u32[]{:S(2)}, u32[]{:S(2)}) %collective-permute-start.5) | collective-permute-done | bytes 4128 | tf_op jit(solution)/shard_map/ppermute | solution.py:189
  21.5 0.6 %bitcast_add_fusion = f32[1024]{0:T(1024)} fusion(f32[1024]{0:T(1024)S(1)} %collective-permute-done.5, f32[8,128]{1,0:T(8,128)S(1)} %reduce_sum.9), kind=kLoop, calls=%fused_computation | loop fusion | flops 1024 | bytes 12288 | tf_op jit(solution)/shard_map/add | solution.py:215
  (1 shorter events, 0.0 us)
Async XLA Ops:
  0.0 9.0 %collective-permute-start = (bf16[2,64,1024]{2,1,0:T(8,128)(2,1)}, bf16[2,64,1024]{2,1,0:T(8,128)(2,1)S(1)}, u32[]{:S(2)}, u32[]{:S(2)}) collective-permute-start(bf16[2,64,1024]{2,1,0:T(8,128)(2,1)} %refs_0_.1), channel_id=1, source_target_pairs={{0,4},{1,3},{2,6},{3,1},{4,0},{5,7},{6,2},{7,5},{8,12},{9,11},{10,... | collective-permute-start | bytes 786440 | tf_op jit(solution)/shard_map/ppermute | solution.py:196
  2.9 6.1 %collective-permute-start.1 = (bf16[2,64,1024]{2,1,0:T(8,128)(2,1)}, bf16[2,64,1024]{2,1,0:T(8,128)(2,1)S(1)}, u32[]{:S(2)}, u32[]{:S(2)}) collective-permute-start(bf16[2,64,1024]{2,1,0:T(8,128)(2,1)} %refs_0_.1), channel_id=1, source_target_pairs={{0,3},{1,0},{2,1},{3,2},{4,7},{5,4},{6,5},{7,6},{8,11},{9,8},{10,9... | collective-permute-start | bytes 786440 | tf_op jit(solution)/shard_map/ppermute | solution.py:196
  6.7 2.3 %collective-permute-start.2 = (bf16[688,128]{1,0:T(8,128)(2,1)S(1)}, bf16[688,128]{1,0:T(8,128)(2,1)S(1)}, u32[]{:S(2)}, u32[]{:S(2)}) collective-permute-start(bf16[688,128]{1,0:T(8,128)(2,1)S(1)} %get-tuple-element.10), channel_id=1, source_target_pairs={{0,1},{1,0},{2,3},{3,2},{4,5},{5,4},{6,7},{7,6},{8,9},{9,8},{10,11... | collective-permute-start | bytes 528392 | tf_op jit(solution)/shard_map/ppermute | solution.py:189
  7.2 1.8 %collective-permute-start.3 = (bf16[688,128]{1,0:T(8,128)(2,1)S(1)}, bf16[688,128]{1,0:T(8,128)(2,1)S(1)}, u32[]{:S(2)}, u32[]{:S(2)}) collective-permute-start(bf16[688,128]{1,0:T(8,128)(2,1)S(1)} %get-tuple-element.11), channel_id=1, source_target_pairs={{0,1},{1,0},{2,3},{3,2},{4,5},{5,4},{6,7},{7,6},{8,9},{9,8},{10,11... | collective-permute-start | bytes 528392 | tf_op jit(solution)/shard_map/ppermute | solution.py:189
  7.3 1.7 %collective-permute-start.4 = (bf16[672,128]{1,0:T(8,128)(2,1)S(1)}, bf16[672,128]{1,0:T(8,128)(2,1)S(1)}, u32[]{:S(2)}, u32[]{:S(2)}) collective-permute-start(bf16[672,128]{1,0:T(8,128)(2,1)S(1)} %get-tuple-element.12), channel_id=1, source_target_pairs={{0,1},{1,0},{2,3},{3,2},{4,5},{5,4},{6,7},{7,6},{8,9},{9,8},{10,11... | collective-permute-start | bytes 516104 | tf_op jit(solution)/shard_map/ppermute | solution.py:189
  7.8 1.3 %copy-start = (bf16[2,64,1024]{2,1,0:T(8,128)(2,1)S(1)}, bf16[2,64,1024]{2,1,0:T(8,128)(2,1)}, u32[]{:S(2)}) copy-start(bf16[2,64,1024]{2,1,0:T(8,128)(2,1)} %refs_0_.1) | copy-start | bytes 786436
  20.2 1.2 %collective-permute-start.5 = (f32[1024]{0:T(1024)S(1)}, f32[1024]{0:T(1024)S(1)}, u32[]{:S(2)}, u32[]{:S(2)}) collective-permute-start(f32[1024]{0:T(1024)S(1)} %bitcast.2), channel_id=1, source_target_pairs={{0,1},{1,0},{2,3},{3,2},{4,5},{5,4},{6,7},{7,6},{8,9},{9,8},{10,11... | collective-permute-start | bytes 12296 | tf_op jit(solution)/shard_map/ppermute | solution.py:189

commit v28 on v27

--- a/solution.py
+++ b/solution.py
@@ -203,7 +203,7 @@
     got = [swap(x, 1) for x in sent]
     groups = [
         [
-            (2 * side + (plane + group) % 2) * cuts + 2 * plane + column
+            (2 * side + group) * cuts + 2 * plane + column
             for side in range(stems // 2 - 1, -1, -1) for plane in range(cuts // 2 - 1, -1, -1) for column in (1, 0)
         ]
         for group in (0, 1)

time: 22.2 us -> 22.2 us (level)
  transfers between devices with their start and end apart: 6 -> 6, of which waited for: 1 -> 1; matrix products, arithmetic and copies ran while one was open for 0% -> 0% of each run, Pallas kernels for 22% -> 23%
where the time goes in v28:
time: 22.2 us; the launch traced here: 22 us
  blocking collectives  10.6 us (48%)
  Pallas kernels  5.42 us (24%)
  starting transfers between devices  4.2 us (19%)
  waiting for transfers between devices  1.06 us (5%)
  other arithmetic  0.61 us (3%)
    all_to_all x1, blocking collectives, on_device(): lax.all_to_all(spread, ('stem', 'cuts'), 0, 0, tiled=True, axis_index_gro...  10.6 us
    pallas_call x1, Pallas kernels, branch_sums(): pl.pallas_call(functools.partial(leave_kernel, total // groups), in_specs...  3.72 us
    ppermute x2, starting transfers between devices, route(): return lax.ppermute(stem_tensor, ('cuts', 'stem'), pairs)  2.94 us
    ppermute x4, starting transfers between devices, swap(): return lax.ppermute(x, 'stem', [(s, s ^ p) for s in range(stems)])  1.26 us
    pallas_call x1, Pallas kernels, branch_sums(): pl.pallas_call(stay_kernel, out_shape=jax.ShapeDtypeStruct((half, depth,...  1.24 us
    ppermute x4, waiting for transfers between devices, swap(): return lax.ppermute(x, 'stem', [(s, s ^ p) for s in range(stems)])  1.06 us
    add x1, other arithmetic, on_device(): return total + swap(total, 1)  0.6 us
    pallas_call x1, Pallas kernels, close(): pl.pallas_call(functools.partial(close_kernel, targets if whole_tiles els...  0.46 us
  transfers between devices with their start and end apart: 6, of which 1 were waited for; matrix products, arithmetic and copies ran while one was open for 0% of the time, Pallas kernels for 23%

profile of v28, /device:TPU:0, one launch (start us, length us, event | category | flops | bytes accessed | tf_op | source)
XLA Modules:
  0.0 22.0 jit_solution(18309878559811379804)
XLA Ops:
  0.0 2.9 %collective-permute-start = (bf16[2,64,1024]{2,1,0:T(8,128)(2,1)}, bf16[2,64,1024]{2,1,0:T(8,128)(2,1)S(1)}, u32[]{:S(2)}, u32[]{:S(2)}) collective-permute-start(bf16[2,64,1024]{2,1,0:T(8,128)(2,1)} %refs_0_.1), channel_id=1, source_target_pairs={{0,4},{1,3},{2,6},{3,1},{4,0},{5,7},{6,2},{7,5},{8,12},{9,11},{10,... | collective-permute-start | bytes 786440 | tf_op jit(solution)/shard_map/ppermute | solution.py:196
  2.9 0.0 collective-permute-start.1
  2.9 3.7 %leave.1 = (bf16[16,512,128]{2,1,0:T(8,128)(2,1)S(1)}, bf16[4,16,128,128]{3,2,1,0:T(8,128)(2,1)S(1)}, bf16[688,128]{1,0:T(8,128)(2,1)S(1)}, bf16[688,128]{1,0:T(8,128)(2,1)S(1)}, bf16[672,128]{1,0:T(8,128)(2,1)S(1)}) custom-call(bf16[16,512,128]{2,1,0:T(8,128)(2,1)} %mid_hbm.1, bf16[8,16,64,128]{3,2,1,0:T(8,128)(2,1)} %right_hbm.1), custom_call_target="tpu_custom_call" | custom-call | flops 1073741824 | bytes 4194304 | tf_op jit(solution)/shard_map/leave/pallas_call | solution.py:113
  6.7 0.6 %collective-permute-start.2 = (bf16[688,128]{1,0:T(8,128)(2,1)S(1)}, bf16[688,128]{1,0:T(8,128)(2,1)S(1)}, u32[]{:S(2)}, u32[]{:S(2)}) collective-permute-start(bf16[688,128]{1,0:T(8,128)(2,1)S(1)} %get-tuple-element.10), channel_id=1, source_target_pairs={{0,1},{1,0},{2,3},{3,2},{4,5},{5,4},{6,7},{7,6},{8,9},{9,8},{10,11... | collective-permute-start | bytes 528392 | tf_op jit(solution)/shard_map/ppermute | solution.py:189
  7.2 0.1 collective-permute-start.3
  7.3 0.4 %collective-permute-start.4 = (bf16[672,128]{1,0:T(8,128)(2,1)S(1)}, bf16[672,128]{1,0:T(8,128)(2,1)S(1)}, u32[]{:S(2)}, u32[]{:S(2)}) collective-permute-start(bf16[672,128]{1,0:T(8,128)(2,1)S(1)} %get-tuple-element.12), channel_id=1, source_target_pairs={{0,1},{1,0},{2,3},{3,2},{4,5},{5,4},{6,7},{7,6},{8,9},{9,8},{10,11... | collective-permute-start | bytes 516104 | tf_op jit(solution)/shard_map/ppermute | solution.py:189
  7.8 0.0 copy-start
  7.8 1.2 %stay.1.refs_6_ = f32[4,512,128]{2,1,0:T(8,128)S(1)} custom-call(bf16[16,512,128]{2,1,0:T(8,128)(2,1)S(1)} %get-tuple-element.13.mid_ref, bf16[4,16,128,128]{3,2,1,0:T(8,128)(2,1)S(1)} %get-tuple-element.14.wide_ref), custom_call_target="tpu_custom_call" | custom-call | flops 1073741824 | bytes 4194304 | tf_op jit(solution)/shard_map/stay/pallas_call | solution.py:130
  9.0 0.0 collective-permute-done.4.refs_5_
  9.0 0.0 collective-permute-done.2.refs_3_
  9.0 0.0 collective-permute-done.3.refs_4_
  9.0 0.0 collective-permute-done.refs_1_
  9.1 0.0 collective-permute-done.1.refs_2_
  9.1 0.0 copy-done
  9.1 0.5 %close.1 = f32[16,8,128]{2,1,0:T(8,128)S(1)} custom-call(bf16[2,64,1024]{2,1,0:T(8,128)(2,1)S(1)} %copy-done, bf16[2,64,1024]{2,1,0:T(8,128)(2,1)S(1)} %collective-permute-done.refs_1_, bf16[2,64,1024]{2,1,0:T(8,128)(2,1)S(1)} %collective-permute-done.1.refs_2_, bf16[688,128]{1,0:T(8,128)(2,1)S(1)} %collective-permute-done.2.refs_3_, ...), custom_call_target="tpu_custom_call" | custom-call | flops 134217728 | bytes 1048576 | tf_op jit(solution)/shard_map/close/pallas_call | solution.py:174
  9.5 10.6 %all_to_all.5 = f32[16,8,128]{2,1,0:T(8,128)S(1)} all-to-all(f32[16,8,128]{2,1,0:T(8,128)S(1)} %close.1), channel_id=1, replica_groups={{30,26,22,18,14,10,6,2,28,24,20,16,12,8,4,0},{31,27,23,19,15,11,7,3,29,..., dimensions={0} | all-to-all | bytes 131072 | tf_op jit(solution)/shard_map/all_to_all | solution.py:213
  20.2 0.2 collective-permute-start.5
  20.4 1.1 %collective-permute-done.5 = f32[1024]{0:T(1024)S(1)} collective-permute-done((f32[1024]{0:T(1024)S(1)}, f32[1024]{0:T(1024)S(1)}, u32[]{:S(2)}, u32[]{:S(2)}) %collective-permute-start.5) | collective-permute-done | bytes 4128 | tf_op jit(solution)/shard_map/ppermute | solution.py:189
  21.4 0.6 %bitcast_add_fusion = f32[1024]{0:T(1024)} fusion(f32[1024]{0:T(1024)S(1)} %collective-permute-done.5, f32[8,128]{1,0:T(8,128)S(1)} %reduce_sum.9), kind=kLoop, calls=%fused_computation | loop fusion | flops 1024 | bytes 12288 | tf_op jit(solution)/shard_map/add | solution.py:215
  (1 shorter events, 0.0 us)
Async XLA Ops:
  0.0 9.0 %collective-permute-start = (bf16[2,64,1024]{2,1,0:T(8,128)(2,1)}, bf16[2,64,1024]{2,1,0:T(8,128)(2,1)S(1)}, u32[]{:S(2)}, u32[]{:S(2)}) collective-permute-start(bf16[2,64,1024]{2,1,0:T(8,128)(2,1)} %refs_0_.1), channel_id=1, source_target_pairs={{0,4},{1,3},{2,6},{3,1},{4,0},{5,7},{6,2},{7,5},{8,12},{9,11},{10,... | collective-permute-start | bytes 786440 | tf_op jit(solution)/shard_map/ppermute | solution.py:196
  2.9 6.1 %collective-permute-start.1 = (bf16[2,64,1024]{2,1,0:T(8,128)(2,1)}, bf16[2,64,1024]{2,1,0:T(8,128)(2,1)S(1)}, u32[]{:S(2)}, u32[]{:S(2)}) collective-permute-start(bf16[2,64,1024]{2,1,0:T(8,128)(2,1)} %refs_0_.1), channel_id=1, source_target_pairs={{0,3},{1,0},{2,1},{3,2},{4,7},{5,4},{6,5},{7,6},{8,11},{9,8},{10,9... | collective-permute-start | bytes 786440 | tf_op jit(solution)/shard_map/ppermute | solution.py:196
  6.7 2.3 %collective-permute-start.2 = (bf16[688,128]{1,0:T(8,128)(2,1)S(1)}, bf16[688,128]{1,0:T(8,128)(2,1)S(1)}, u32[]{:S(2)}, u32[]{:S(2)}) collective-permute-start(bf16[688,128]{1,0:T(8,128)(2,1)S(1)} %get-tuple-element.10), channel_id=1, source_target_pairs={{0,1},{1,0},{2,3},{3,2},{4,5},{5,4},{6,7},{7,6},{8,9},{9,8},{10,11... | collective-permute-start | bytes 528392 | tf_op jit(solution)/shard_map/ppermute | solution.py:189
  7.2 1.8 %collective-permute-start.3 = (bf16[688,128]{1,0:T(8,128)(2,1)S(1)}, bf16[688,128]{1,0:T(8,128)(2,1)S(1)}, u32[]{:S(2)}, u32[]{:S(2)}) collective-permute-start(bf16[688,128]{1,0:T(8,128)(2,1)S(1)} %get-tuple-element.11), channel_id=1, source_target_pairs={{0,1},{1,0},{2,3},{3,2},{4,5},{5,4},{6,7},{7,6},{8,9},{9,8},{10,11... | collective-permute-start | bytes 528392 | tf_op jit(solution)/shard_map/ppermute | solution.py:189
  7.3 1.7 %collective-permute-start.4 = (bf16[672,128]{1,0:T(8,128)(2,1)S(1)}, bf16[672,128]{1,0:T(8,128)(2,1)S(1)}, u32[]{:S(2)}, u32[]{:S(2)}) collective-permute-start(bf16[672,128]{1,0:T(8,128)(2,1)S(1)} %get-tuple-element.12), channel_id=1, source_target_pairs={{0,1},{1,0},{2,3},{3,2},{4,5},{5,4},{6,7},{7,6},{8,9},{9,8},{10,11... | collective-permute-start | bytes 516104 | tf_op jit(solution)/shard_map/ppermute | solution.py:189
  7.8 1.3 %copy-start = (bf16[2,64,1024]{2,1,0:T(8,128)(2,1)S(1)}, bf16[2,64,1024]{2,1,0:T(8,128)(2,1)}, u32[]{:S(2)}) copy-start(bf16[2,64,1024]{2,1,0:T(8,128)(2,1)} %refs_0_.1) | copy-start | bytes 786436
  20.2 1.2 %collective-permute-start.5 = (f32[1024]{0:T(1024)S(1)}, f32[1024]{0:T(1024)S(1)}, u32[]{:S(2)}, u32[]{:S(2)}) collective-permute-start(f32[1024]{0:T(1024)S(1)} %bitcast.2), channel_id=1, source_target_pairs={{0,1},{1,0},{2,3},{3,2},{4,5},{5,4},{6,7},{7,6},{8,9},{9,8},{10,11... | collective-permute-start | bytes 12296 | tf_op jit(solution)/shard_map/ppermute | solution.py:189

commit v29 on v28

--- a/solution.py
+++ b/solution.py
@@ -196,7 +196,7 @@
         return lax.ppermute(stem_tensor, ("cuts", "stem"), pairs)
 
     assert stems == 4
-    cross = route(lambda cut, side, core: (cut, 1 - side, 1) if core else (cut ^ 1, side, 0))
+    cross = route(lambda cut, side, core: (cut, 1 - side, 1) if core else (cut ^ 2, side, 0))
     cycle = route(lambda cut, side, core: (cut, side, 0) if core else (cut, 1 - side, 1))
     pieces = [stem_tensor, cross, cycle]
     kept, *sent = branch_sums(mid_tensors, right_tensors, stems)

time: 22.2 us -> 22.2 us (level)
  no operation moved by 1% of the time
where the time goes in v29:
time: 22.2 us; the launch traced here: 22 us
  blocking collectives  10.6 us (48%)
  Pallas kernels  5.42 us (24%)
  starting transfers between devices  4.29 us (19%)
  waiting for transfers between devices  1.06 us (5%)
  other arithmetic  0.61 us (3%)
    all_to_all x1, blocking collectives, on_device(): lax.all_to_all(spread, ('stem', 'cuts'), 0, 0, tiled=True, axis_index_gro...  10.6 us
    pallas_call x1, Pallas kernels, branch_sums(): pl.pallas_call(functools.partial(leave_kernel, total // groups), in_specs...  3.72 us
    ppermute x2, starting transfers between devices, route(): return lax.ppermute(stem_tensor, ('cuts', 'stem'), pairs)  3.03 us
    ppermute x4, starting transfers between devices, swap(): return lax.ppermute(x, 'stem', [(s, s ^ p) for s in range(stems)])  1.26 us
    pallas_call x1, Pallas kernels, branch_sums(): pl.pallas_call(stay_kernel, out_shape=jax.ShapeDtypeStruct((half, depth,...  1.24 us
    ppermute x4, waiting for transfers between devices, swap(): return lax.ppermute(x, 'stem', [(s, s ^ p) for s in range(stems)])  1.06 us
    add x1, other arithmetic, on_device(): return total + swap(total, 1)  0.6 us
    pallas_call x1, Pallas kernels, close(): pl.pallas_call(functools.partial(close_kernel, targets if whole_tiles els...  0.46 us
  transfers between devices with their start and end apart: 6, of which 1 were waited for; matrix products, arithmetic and copies ran while one was open for 0% of the time, Pallas kernels for 23%

profile of v29, /device:TPU:0, one launch (start us, length us, event | category | flops | bytes accessed | tf_op | source)
XLA Modules:
  0.0 22.0 jit_solution(11375839730261444236)
XLA Ops:
  0.0 3.0 %collective-permute-start = (bf16[2,64,1024]{2,1,0:T(8,128)(2,1)}, bf16[2,64,1024]{2,1,0:T(8,128)(2,1)S(1)}, u32[]{:S(2)}, u32[]{:S(2)}) collective-permute-start(bf16[2,64,1024]{2,1,0:T(8,128)(2,1)} %refs_0_.1), channel_id=1, source_target_pairs={{0,8},{1,3},{2,10},{3,1},{4,12},{5,7},{6,14},{7,5},{8,0},{9,11},{1... | collective-permute-start | bytes 786440 | tf_op jit(solution)/shard_map/ppermute | solution.py:196
  3.0 0.0 collective-permute-start.1
  3.0 3.7 %leave.1 = (bf16[16,512,128]{2,1,0:T(8,128)(2,1)S(1)}, bf16[4,16,128,128]{3,2,1,0:T(8,128)(2,1)S(1)}, bf16[688,128]{1,0:T(8,128)(2,1)S(1)}, bf16[688,128]{1,0:T(8,128)(2,1)S(1)}, bf16[672,128]{1,0:T(8,128)(2,1)S(1)}) custom-call(bf16[16,512,128]{2,1,0:T(8,128)(2,1)} %mid_hbm.1, bf16[8,16,64,128]{3,2,1,0:T(8,128)(2,1)} %right_hbm.1), custom_call_target="tpu_custom_call" | custom-call | flops 1073741824 | bytes 4194304 | tf_op jit(solution)/shard_map/leave/pallas_call | solution.py:113
  6.8 0.6 %collective-permute-start.2 = (bf16[688,128]{1,0:T(8,128)(2,1)S(1)}, bf16[688,128]{1,0:T(8,128)(2,1)S(1)}, u32[]{:S(2)}, u32[]{:S(2)}) collective-permute-start(bf16[688,128]{1,0:T(8,128)(2,1)S(1)} %get-tuple-element.10), channel_id=1, source_target_pairs={{0,1},{1,0},{2,3},{3,2},{4,5},{5,4},{6,7},{7,6},{8,9},{9,8},{10,11... | collective-permute-start | bytes 528392 | tf_op jit(solution)/shard_map/ppermute | solution.py:189
  7.3 0.1 collective-permute-start.3
  7.4 0.4 %collective-permute-start.4 = (bf16[672,128]{1,0:T(8,128)(2,1)S(1)}, bf16[672,128]{1,0:T(8,128)(2,1)S(1)}, u32[]{:S(2)}, u32[]{:S(2)}) collective-permute-start(bf16[672,128]{1,0:T(8,128)(2,1)S(1)} %get-tuple-element.12), channel_id=1, source_target_pairs={{0,1},{1,0},{2,3},{3,2},{4,5},{5,4},{6,7},{7,6},{8,9},{9,8},{10,11... | collective-permute-start | bytes 516104 | tf_op jit(solution)/shard_map/ppermute | solution.py:189
  7.8 0.0 copy-start
  7.8 1.2 %stay.1.refs_6_ = f32[4,512,128]{2,1,0:T(8,128)S(1)} custom-call(bf16[16,512,128]{2,1,0:T(8,128)(2,1)S(1)} %get-tuple-element.13.mid_ref, bf16[4,16,128,128]{3,2,1,0:T(8,128)(2,1)S(1)} %get-tuple-element.14.wide_ref), custom_call_target="tpu_custom_call" | custom-call | flops 1073741824 | bytes 4194304 | tf_op jit(solution)/shard_map/stay/pallas_call | solution.py:130
  9.1 0.0 collective-permute-done.4.refs_5_
  9.1 0.0 collective-permute-done.2.refs_3_
  9.1 0.0 collective-permute-done.3.refs_4_
  9.1 0.0 collective-permute-done.refs_1_
  9.1 0.0 collective-permute-done.1.refs_2_
  9.1 0.0 copy-done
  9.2 0.5 %close.1 = f32[16,8,128]{2,1,0:T(8,128)S(1)} custom-call(bf16[2,64,1024]{2,1,0:T(8,128)(2,1)S(1)} %copy-done, bf16[2,64,1024]{2,1,0:T(8,128)(2,1)S(1)} %collective-permute-done.refs_1_, bf16[2,64,1024]{2,1,0:T(8,128)(2,1)S(1)} %collective-permute-done.1.refs_2_, bf16[688,128]{1,0:T(8,128)(2,1)S(1)} %collective-permute-done.2.refs_3_, ...), custom_call_target="tpu_custom_call" | custom-call | flops 134217728 | bytes 1048576 | tf_op jit(solution)/shard_map/close/pallas_call | solution.py:174
  9.6 10.6 %all_to_all.5 = f32[16,8,128]{2,1,0:T(8,128)S(1)} all-to-all(f32[16,8,128]{2,1,0:T(8,128)S(1)} %close.1), channel_id=1, replica_groups={{30,26,22,18,14,10,6,2,28,24,20,16,12,8,4,0},{31,27,23,19,15,11,7,3,29,..., dimensions={0} | all-to-all | bytes 131072 | tf_op jit(solution)/shard_map/all_to_all | solution.py:213
  20.2 0.2 collective-permute-start.5
  20.4 1.1 %collective-permute-done.5 = f32[1024]{0:T(1024)S(1)} collective-permute-done((f32[1024]{0:T(1024)S(1)}, f32[1024]{0:T(1024)S(1)}, u32[]{:S(2)}, u32[]{:S(2)}) %collective-permute-start.5) | collective-permute-done | bytes 4128 | tf_op jit(solution)/shard_map/ppermute | solution.py:189
  21.4 0.6 %bitcast_add_fusion = f32[1024]{0:T(1024)} fusion(f32[1024]{0:T(1024)S(1)} %collective-permute-done.5, f32[8,128]{1,0:T(8,128)S(1)} %reduce_sum.9), kind=kLoop, calls=%fused_computation | loop fusion | flops 1024 | bytes 12288 | tf_op jit(solution)/shard_map/add | solution.py:215
  (1 shorter events, 0.0 us)
Async XLA Ops:
  0.0 9.1 %collective-permute-start = (bf16[2,64,1024]{2,1,0:T(8,128)(2,1)}, bf16[2,64,1024]{2,1,0:T(8,128)(2,1)S(1)}, u32[]{:S(2)}, u32[]{:S(2)}) collective-permute-start(bf16[2,64,1024]{2,1,0:T(8,128)(2,1)} %refs_0_.1), channel_id=1, source_target_pairs={{0,8},{1,3},{2,10},{3,1},{4,12},{5,7},{6,14},{7,5},{8,0},{9,11},{1... | collective-permute-start | bytes 786440 | tf_op jit(solution)/shard_map/ppermute | solution.py:196
  3.0 6.1 %collective-permute-start.1 = (bf16[2,64,1024]{2,1,0:T(8,128)(2,1)}, bf16[2,64,1024]{2,1,0:T(8,128)(2,1)S(1)}, u32[]{:S(2)}, u32[]{:S(2)}) collective-permute-start(bf16[2,64,1024]{2,1,0:T(8,128)(2,1)} %refs_0_.1), channel_id=1, source_target_pairs={{0,3},{1,0},{2,1},{3,2},{4,7},{5,4},{6,5},{7,6},{8,11},{9,8},{10,9... | collective-permute-start | bytes 786440 | tf_op jit(solution)/shard_map/ppermute | solution.py:196
  6.8 2.3 %collective-permute-start.2 = (bf16[688,128]{1,0:T(8,128)(2,1)S(1)}, bf16[688,128]{1,0:T(8,128)(2,1)S(1)}, u32[]{:S(2)}, u32[]{:S(2)}) collective-permute-start(bf16[688,128]{1,0:T(8,128)(2,1)S(1)} %get-tuple-element.10), channel_id=1, source_target_pairs={{0,1},{1,0},{2,3},{3,2},{4,5},{5,4},{6,7},{7,6},{8,9},{9,8},{10,11... | collective-permute-start | bytes 528392 | tf_op jit(solution)/shard_map/ppermute | solution.py:189
  7.3 1.8 %collective-permute-start.3 = (bf16[688,128]{1,0:T(8,128)(2,1)S(1)}, bf16[688,128]{1,0:T(8,128)(2,1)S(1)}, u32[]{:S(2)}, u32[]{:S(2)}) collective-permute-start(bf16[688,128]{1,0:T(8,128)(2,1)S(1)} %get-tuple-element.11), channel_id=1, source_target_pairs={{0,1},{1,0},{2,3},{3,2},{4,5},{5,4},{6,7},{7,6},{8,9},{9,8},{10,11... | collective-permute-start | bytes 528392 | tf_op jit(solution)/shard_map/ppermute | solution.py:189
  7.4 1.7 %collective-permute-start.4 = (bf16[672,128]{1,0:T(8,128)(2,1)S(1)}, bf16[672,128]{1,0:T(8,128)(2,1)S(1)}, u32[]{:S(2)}, u32[]{:S(2)}) collective-permute-start(bf16[672,128]{1,0:T(8,128)(2,1)S(1)} %get-tuple-element.12), channel_id=1, source_target_pairs={{0,1},{1,0},{2,3},{3,2},{4,5},{5,4},{6,7},{7,6},{8,9},{9,8},{10,11... | collective-permute-start | bytes 516104 | tf_op jit(solution)/shard_map/ppermute | solution.py:189
  7.8 1.3 %copy-start = (bf16[2,64,1024]{2,1,0:T(8,128)(2,1)S(1)}, bf16[2,64,1024]{2,1,0:T(8,128)(2,1)}, u32[]{:S(2)}) copy-start(bf16[2,64,1024]{2,1,0:T(8,128)(2,1)} %refs_0_.1) | copy-start | bytes 786436
  20.2 1.2 %collective-permute-start.5 = (f32[1024]{0:T(1024)S(1)}, f32[1024]{0:T(1024)S(1)}, u32[]{:S(2)}, u32[]{:S(2)}) collective-permute-start(f32[1024]{0:T(1024)S(1)} %bitcast.2), channel_id=1, source_target_pairs={{0,1},{1,0},{2,3},{3,2},{4,5},{5,4},{6,7},{7,6},{8,9},{9,8},{10,11... | collective-permute-start | bytes 12296 | tf_op jit(solution)/shard_map/ppermute | solution.py:189

commit v30 on v29

--- a/solution.py
+++ b/solution.py
@@ -164,7 +164,7 @@
     else:
         rows = out_ref.shape[1]
         for at, c in enumerate(targets):
-            out_ref[at] = total[c * rows:(c + 1) * rows]
+            out_ref[at] = total[c * rows:(c + 1) * rows].astype(out_ref.dtype)
 
 
 def close(stems, kept, got, cuts, targets):
@@ -173,7 +173,7 @@
     shape = (len(targets), rows // cuts, width) if whole_tiles else (rows, width)
     out = pl.pallas_call(
         functools.partial(close_kernel, targets if whole_tiles else None),
-        out_shape=jax.ShapeDtypeStruct(shape, jnp.float32),
+        out_shape=jax.ShapeDtypeStruct(shape, jnp.bfloat16 if whole_tiles else jnp.float32),
         compiler_params=pltpu.CompilerParams(vmem_limit_bytes=24 * MIB),
         cost_estimate=pl.CostEstimate(flops=8 * rows * kept.size, bytes_accessed=MIB, transcendentals=0),
         name="close",
@@ -211,7 +211,7 @@
     targets = [at % cuts for at in groups[0]]
     spread = close(pieces, kept, got, cuts, targets)
     parts = lax.all_to_all(spread, ("stem", "cuts"), 0, 0, tiled=True, axis_index_groups=groups)
-    total = jnp.sum(parts, axis=0).reshape(-1)
+    total = jnp.sum(parts.astype(jnp.float32), axis=0).reshape(-1)
     return total + swap(total, 1)
 
 

time: 22.2 us -> 21.6 us (0.973)
  blocking collectives: 10.6 us -> 9.97 us
    all_to_all x1, blocking collectives: 10.6 us -> 9.97 us  [on_device(): lax.all_to_all(spread, ('stem', 'cuts'), 0, 0, tiled=True, axis_index_gro...]
where the time goes in v30:
time: 21.6 us; the launch traced here: 21.4 us
  blocking collectives  9.97 us (46%)
  Pallas kernels  5.43 us (25%)
  starting transfers between devices  4.29 us (20%)
  waiting for transfers between devices  1.06 us (5%)
  other arithmetic  0.61 us (3%)
    all_to_all x1, blocking collectives, on_device(): lax.all_to_all(spread, ('stem', 'cuts'), 0, 0, tiled=True, axis_index_gro...  9.97 us
    pallas_call x1, Pallas kernels, branch_sums(): pl.pallas_call(functools.partial(leave_kernel, total // groups), in_specs...  3.72 us
    ppermute x2, starting transfers between devices, route(): return lax.ppermute(stem_tensor, ('cuts', 'stem'), pairs)  3.03 us
    ppermute x4, starting transfers between devices, swap(): return lax.ppermute(x, 'stem', [(s, s ^ p) for s in range(stems)])  1.26 us
    pallas_call x1, Pallas kernels, branch_sums(): pl.pallas_call(stay_kernel, out_shape=jax.ShapeDtypeStruct((half, depth,...  1.24 us
    ppermute x4, waiting for transfers between devices, swap(): return lax.ppermute(x, 'stem', [(s, s ^ p) for s in range(stems)])  1.06 us
    add x1, other arithmetic, on_device(): return total + swap(total, 1)  0.6 us
    pallas_call x1, Pallas kernels, close(): pl.pallas_call(functools.partial(close_kernel, targets if whole_tiles els...  0.46 us
  transfers between devices with their start and end apart: 6, of which 1 were waited for; matrix products, arithmetic and copies ran while one was open for 0% of the time, Pallas kernels for 23%

profile of v30, /device:TPU:0, one launch (start us, length us, event | category | flops | bytes accessed | tf_op | source)
XLA Modules:
  0.0 21.4 jit_solution(14783603681264345326)
XLA Ops:
  0.0 3.0 %collective-permute-start = (bf16[2,64,1024]{2,1,0:T(8,128)(2,1)}, bf16[2,64,1024]{2,1,0:T(8,128)(2,1)S(1)}, u32[]{:S(2)}, u32[]{:S(2)}) collective-permute-start(bf16[2,64,1024]{2,1,0:T(8,128)(2,1)} %refs_0_.1), channel_id=1, source_target_pairs={{0,8},{1,3},{2,10},{3,1},{4,12},{5,7},{6,14},{7,5},{8,0},{9,11},{1... | collective-permute-start | bytes 786440 | tf_op jit(solution)/shard_map/ppermute | solution.py:196
  3.0 0.0 collective-permute-start.1
  3.0 3.7 %leave.1 = (bf16[16,512,128]{2,1,0:T(8,128)(2,1)S(1)}, bf16[4,16,128,128]{3,2,1,0:T(8,128)(2,1)S(1)}, bf16[688,128]{1,0:T(8,128)(2,1)S(1)}, bf16[688,128]{1,0:T(8,128)(2,1)S(1)}, bf16[672,128]{1,0:T(8,128)(2,1)S(1)}) custom-call(bf16[16,512,128]{2,1,0:T(8,128)(2,1)} %mid_hbm.1, bf16[8,16,64,128]{3,2,1,0:T(8,128)(2,1)} %right_hbm.1), custom_call_target="tpu_custom_call" | custom-call | flops 1073741824 | bytes 4194304 | tf_op jit(solution)/shard_map/leave/pallas_call | solution.py:113
  6.8 0.6 %collective-permute-start.2 = (bf16[688,128]{1,0:T(8,128)(2,1)S(1)}, bf16[688,128]{1,0:T(8,128)(2,1)S(1)}, u32[]{:S(2)}, u32[]{:S(2)}) collective-permute-start(bf16[688,128]{1,0:T(8,128)(2,1)S(1)} %get-tuple-element.10), channel_id=1, source_target_pairs={{0,1},{1,0},{2,3},{3,2},{4,5},{5,4},{6,7},{7,6},{8,9},{9,8},{10,11... | collective-permute-start | bytes 528392 | tf_op jit(solution)/shard_map/ppermute | solution.py:189
  7.3 0.1 collective-permute-start.3
  7.4 0.4 %collective-permute-start.4 = (bf16[672,128]{1,0:T(8,128)(2,1)S(1)}, bf16[672,128]{1,0:T(8,128)(2,1)S(1)}, u32[]{:S(2)}, u32[]{:S(2)}) collective-permute-start(bf16[672,128]{1,0:T(8,128)(2,1)S(1)} %get-tuple-element.12), channel_id=1, source_target_pairs={{0,1},{1,0},{2,3},{3,2},{4,5},{5,4},{6,7},{7,6},{8,9},{9,8},{10,11... | collective-permute-start | bytes 516104 | tf_op jit(solution)/shard_map/ppermute | solution.py:189
  7.8 0.0 copy-start
  7.8 1.2 %stay.1.refs_6_ = f32[4,512,128]{2,1,0:T(8,128)S(1)} custom-call(bf16[16,512,128]{2,1,0:T(8,128)(2,1)S(1)} %get-tuple-element.13.mid_ref, bf16[4,16,128,128]{3,2,1,0:T(8,128)(2,1)S(1)} %get-tuple-element.14.wide_ref), custom_call_target="tpu_custom_call" | custom-call | flops 1073741824 | bytes 4194304 | tf_op jit(solution)/shard_map/stay/pallas_call | solution.py:130
  9.1 0.0 collective-permute-done.4.refs_5_
  9.1 0.0 collective-permute-done.2.refs_3_
  9.1 0.0 collective-permute-done.3.refs_4_
  9.1 0.0 collective-permute-done.refs_1_
  9.1 0.0 collective-permute-done.1.refs_2_
  9.1 0.0 copy-done
  9.2 0.5 %close.1 = bf16[16,8,128]{2,1,0:T(8,128)(2,1)S(1)} custom-call(bf16[2,64,1024]{2,1,0:T(8,128)(2,1)S(1)} %copy-done, bf16[2,64,1024]{2,1,0:T(8,128)(2,1)S(1)} %collective-permute-done.refs_1_, bf16[2,64,1024]{2,1,0:T(8,128)(2,1)S(1)} %collective-permute-done.1.refs_2_, bf16[688,128]{1,0:T(8,128)(2,1)S(1)} %collective-permute-done.2.refs_3_, ...), custom_call_target="tpu_custom_call" | custom-call | flops 134217728 | bytes 1048576 | tf_op jit(solution)/shard_map/close/pallas_call | solution.py:174
  9.6 10.0 %all_to_all.5 = bf16[16,8,128]{2,1,0:T(8,128)(2,1)S(1)} all-to-all(bf16[16,8,128]{2,1,0:T(8,128)(2,1)S(1)} %close.1), channel_id=1, replica_groups={{30,26,22,18,14,10,6,2,28,24,20,16,12,8,4,0},{31,27,23,19,15,11,7,3,29,..., dimensions={0} | all-to-all | bytes 65536 | tf_op jit(solution)/shard_map/all_to_all | solution.py:213
  19.6 0.2 collective-permute-start.5
  19.8 1.1 %collective-permute-done.5 = f32[1024]{0:T(1024)S(1)} collective-permute-done((f32[1024]{0:T(1024)S(1)}, f32[1024]{0:T(1024)S(1)}, u32[]{:S(2)}, u32[]{:S(2)}) %collective-permute-start.5) | collective-permute-done | bytes 4128 | tf_op jit(solution)/shard_map/ppermute | solution.py:189
  20.8 0.6 %bitcast_add_fusion = f32[1024]{0:T(1024)} fusion(f32[1024]{0:T(1024)S(1)} %collective-permute-done.5, f32[8,128]{1,0:T(8,128)S(1)} %convert_reduce_fusion), kind=kLoop, calls=%fused_computation.1 | loop fusion | flops 1024 | bytes 12288 | tf_op jit(solution)/shard_map/add | solution.py:215
  (1 shorter events, 0.0 us)
Async XLA Ops:
  0.0 9.1 %collective-permute-start = (bf16[2,64,1024]{2,1,0:T(8,128)(2,1)}, bf16[2,64,1024]{2,1,0:T(8,128)(2,1)S(1)}, u32[]{:S(2)}, u32[]{:S(2)}) collective-permute-start(bf16[2,64,1024]{2,1,0:T(8,128)(2,1)} %refs_0_.1), channel_id=1, source_target_pairs={{0,8},{1,3},{2,10},{3,1},{4,12},{5,7},{6,14},{7,5},{8,0},{9,11},{1... | collective-permute-start | bytes 786440 | tf_op jit(solution)/shard_map/ppermute | solution.py:196
  3.0 6.1 %collective-permute-start.1 = (bf16[2,64,1024]{2,1,0:T(8,128)(2,1)}, bf16[2,64,1024]{2,1,0:T(8,128)(2,1)S(1)}, u32[]{:S(2)}, u32[]{:S(2)}) collective-permute-start(bf16[2,64,1024]{2,1,0:T(8,128)(2,1)} %refs_0_.1), channel_id=1, source_target_pairs={{0,3},{1,0},{2,1},{3,2},{4,7},{5,4},{6,5},{7,6},{8,11},{9,8},{10,9... | collective-permute-start | bytes 786440 | tf_op jit(solution)/shard_map/ppermute | solution.py:196
  6.8 2.3 %collective-permute-start.2 = (bf16[688,128]{1,0:T(8,128)(2,1)S(1)}, bf16[688,128]{1,0:T(8,128)(2,1)S(1)}, u32[]{:S(2)}, u32[]{:S(2)}) collective-permute-start(bf16[688,128]{1,0:T(8,128)(2,1)S(1)} %get-tuple-element.10), channel_id=1, source_target_pairs={{0,1},{1,0},{2,3},{3,2},{4,5},{5,4},{6,7},{7,6},{8,9},{9,8},{10,11... | collective-permute-start | bytes 528392 | tf_op jit(solution)/shard_map/ppermute | solution.py:189
  7.3 1.8 %collective-permute-start.3 = (bf16[688,128]{1,0:T(8,128)(2,1)S(1)}, bf16[688,128]{1,0:T(8,128)(2,1)S(1)}, u32[]{:S(2)}, u32[]{:S(2)}) collective-permute-start(bf16[688,128]{1,0:T(8,128)(2,1)S(1)} %get-tuple-element.11), channel_id=1, source_target_pairs={{0,1},{1,0},{2,3},{3,2},{4,5},{5,4},{6,7},{7,6},{8,9},{9,8},{10,11... | collective-permute-start | bytes 528392 | tf_op jit(solution)/shard_map/ppermute | solution.py:189
  7.4 1.7 %collective-permute-start.4 = (bf16[672,128]{1,0:T(8,128)(2,1)S(1)}, bf16[672,128]{1,0:T(8,128)(2,1)S(1)}, u32[]{:S(2)}, u32[]{:S(2)}) collective-permute-start(bf16[672,128]{1,0:T(8,128)(2,1)S(1)} %get-tuple-element.12), channel_id=1, source_target_pairs={{0,1},{1,0},{2,3},{3,2},{4,5},{5,4},{6,7},{7,6},{8,9},{9,8},{10,11... | collective-permute-start | bytes 516104 | tf_op jit(solution)/shard_map/ppermute | solution.py:189
  7.8 1.3 %copy-start = (bf16[2,64,1024]{2,1,0:T(8,128)(2,1)S(1)}, bf16[2,64,1024]{2,1,0:T(8,128)(2,1)}, u32[]{:S(2)}) copy-start(bf16[2,64,1024]{2,1,0:T(8,128)(2,1)} %refs_0_.1) | copy-start | bytes 786436
  19.6 1.2 %collective-permute-start.5 = (f32[1024]{0:T(1024)S(1)}, f32[1024]{0:T(1024)S(1)}, u32[]{:S(2)}, u32[]{:S(2)}) collective-permute-start(f32[1024]{0:T(1024)S(1)} %bitcast.2), channel_id=1, source_target_pairs={{0,1},{1,0},{2,3},{3,2},{4,5},{5,4},{6,7},{7,6},{8,9},{9,8},{10,11... | collective-permute-start | bytes 12296 | tf_op jit(solution)/shard_map/ppermute | solution.py:189

commit v31 on v30

--- a/solution.py
+++ b/solution.py
@@ -138,7 +138,7 @@
 
 
 def close_kernel(targets, *refs):
-    own_ref, cross_ref, cycle_ref, *got_refs, kept_ref, out_ref = refs
+    own_ref, cycle_ref, cross_ref, *got_refs, kept_ref, out_ref = refs
     first_core = lax.axis_index("stem") % 2 == 0
     pieces = segments(kept_ref.shape[0], kept_ref.shape[1], [ref.shape[0] for ref in got_refs])
     part = None
@@ -196,14 +196,14 @@
         return lax.ppermute(stem_tensor, ("cuts", "stem"), pairs)
 
     assert stems == 4
+    cycle = route(lambda cut, side, core: (cut, side, 0) if core else (cut, 1 - side, 1))
     cross = route(lambda cut, side, core: (cut, 1 - side, 1) if core else (cut ^ 2, side, 0))
-    cycle = route(lambda cut, side, core: (cut, side, 0) if core else (cut, 1 - side, 1))
-    pieces = [stem_tensor, cross, cycle]
+    pieces = [stem_tensor, cycle, cross]
     kept, *sent = branch_sums(mid_tensors, right_tensors, stems)
     got = [swap(x, 1) for x in sent]
     groups = [
         [
-            (2 * side + group) * cuts + 2 * plane + column
+            (2 * side + (plane + group) % 2) * cuts + 2 * plane + column
             for side in range(stems // 2 - 1, -1, -1) for plane in range(cuts // 2 - 1, -1, -1) for column in (1, 0)
         ]
         for group in (0, 1)

time: 21.6 us -> 22.5 us (1.042)
  starting transfers between devices: 4.29 us -> 4.7 us
  blocking collectives: 9.97 us -> 10.3 us
    ppermute x2, starting transfers between devices: 3.03 us -> 3.98 us  [route(): return lax.ppermute(stem_tensor, ('cuts', 'stem'), pairs)]
    ppermute x4, starting transfers between devices: 1.26 us -> 0.71 us  [swap(): return lax.ppermute(x, 'stem', [(s, s ^ p) for s in range(stems)])]
    all_to_all x1, blocking collectives: 9.97 us -> 10.3 us  [on_device(): lax.all_to_all(spread, ('stem', 'cuts'), 0, 0, tiled=True, axis_index_gro...]
  transfers between devices with their start and end apart: 6 -> 6, of which waited for: 1 -> 2; matrix products, arithmetic and copies ran while one was open for 0% -> 0% of each run, Pallas kernels for 23% -> 22%
where the time goes in v31:
time: 22.5 us; the launch traced here: 22.4 us
  blocking collectives  10.3 us (46%)
  Pallas kernels  5.42 us (24%)
  starting transfers between devices  4.7 us (21%)
  waiting for transfers between devices  1.24 us (6%)
  other arithmetic  0.61 us (3%)
    all_to_all x1, blocking collectives, on_device(): lax.all_to_all(spread, ('stem', 'cuts'), 0, 0, tiled=True, axis_index_gro...  10.3 us
    ppermute x2, starting transfers between devices, route(): return lax.ppermute(stem_tensor, ('cuts', 'stem'), pairs)  3.98 us
    pallas_call x1, Pallas kernels, branch_sums(): pl.pallas_call(functools.partial(leave_kernel, total // groups), in_specs...  3.72 us
    pallas_call x1, Pallas kernels, branch_sums(): pl.pallas_call(stay_kernel, out_shape=jax.ShapeDtypeStruct((half, depth,...  1.24 us
    ppermute x4, waiting for transfers between devices, swap(): return lax.ppermute(x, 'stem', [(s, s ^ p) for s in range(stems)])  1.23 us
    ppermute x4, starting transfers between devices, swap(): return lax.ppermute(x, 'stem', [(s, s ^ p) for s in range(stems)])  0.71 us
    add x1, other arithmetic, on_device(): return total + swap(total, 1)  0.6 us
    pallas_call x1, Pallas kernels, close(): pl.pallas_call(functools.partial(close_kernel, targets if whole_tiles els...  0.46 us
  transfers between devices with their start and end apart: 6, of which 2 were waited for; matrix products, arithmetic and copies ran while one was open for 0% of the time, Pallas kernels for 22%

profile of v31, /device:TPU:0, one launch (start us, length us, event | category | flops | bytes accessed | tf_op | source)
XLA Modules:
  0.0 22.4 jit_solution(7456000600794926882)
XLA Ops:
  0.0 2.4 %collective-permute-start = (bf16[2,64,1024]{2,1,0:T(8,128)(2,1)}, bf16[2,64,1024]{2,1,0:T(8,128)(2,1)S(1)}, u32[]{:S(2)}, u32[]{:S(2)}) collective-permute-start(bf16[2,64,1024]{2,1,0:T(8,128)(2,1)} %refs_0_.1), channel_id=1, source_target_pairs={{0,3},{1,0},{2,1},{3,2},{4,7},{5,4},{6,5},{7,6},{8,11},{9,8},{10,9... | collective-permute-start | bytes 786440 | tf_op jit(solution)/shard_map/ppermute | solution.py:196
  2.4 1.6 %collective-permute-start.1 = (bf16[2,64,1024]{2,1,0:T(8,128)(2,1)}, bf16[2,64,1024]{2,1,0:T(8,128)(2,1)S(1)}, u32[]{:S(2)}, u32[]{:S(2)}) collective-permute-start(bf16[2,64,1024]{2,1,0:T(8,128)(2,1)} %refs_0_.1), channel_id=1, source_target_pairs={{0,8},{1,3},{2,10},{3,1},{4,12},{5,7},{6,14},{7,5},{8,0},{9,11},{1... | collective-permute-start | bytes 786440 | tf_op jit(solution)/shard_map/ppermute | solution.py:196
  4.0 3.7 %leave.1 = (bf16[16,512,128]{2,1,0:T(8,128)(2,1)S(1)}, bf16[4,16,128,128]{3,2,1,0:T(8,128)(2,1)S(1)}, bf16[688,128]{1,0:T(8,128)(2,1)S(1)}, bf16[688,128]{1,0:T(8,128)(2,1)S(1)}, bf16[672,128]{1,0:T(8,128)(2,1)S(1)}) custom-call(bf16[16,512,128]{2,1,0:T(8,128)(2,1)} %mid_hbm.1, bf16[8,16,64,128]{3,2,1,0:T(8,128)(2,1)} %right_hbm.1), custom_call_target="tpu_custom_call" | custom-call | flops 1073741824 | bytes 4194304 | tf_op jit(solution)/shard_map/leave/pallas_call | solution.py:113
  7.7 0.1 collective-permute-start.2
  7.8 0.5 %collective-permute-start.3 = (bf16[688,128]{1,0:T(8,128)(2,1)S(1)}, bf16[688,128]{1,0:T(8,128)(2,1)S(1)}, u32[]{:S(2)}, u32[]{:S(2)}) collective-permute-start(bf16[688,128]{1,0:T(8,128)(2,1)S(1)} %get-tuple-element.11), channel_id=1, source_target_pairs={{0,1},{1,0},{2,3},{3,2},{4,5},{5,4},{6,7},{7,6},{8,9},{9,8},{10,11... | collective-permute-start | bytes 528392 | tf_op jit(solution)/shard_map/ppermute | solution.py:189
  8.3 0.1 collective-permute-start.4
  8.4 0.0 copy-start
  8.4 1.2 %stay.1.refs_6_ = f32[4,512,128]{2,1,0:T(8,128)S(1)} custom-call(bf16[16,512,128]{2,1,0:T(8,128)(2,1)S(1)} %get-tuple-element.13.mid_ref, bf16[4,16,128,128]{3,2,1,0:T(8,128)(2,1)S(1)} %get-tuple-element.14.wide_ref), custom_call_target="tpu_custom_call" | custom-call | flops 1073741824 | bytes 4194304 | tf_op jit(solution)/shard_map/stay/pallas_call | solution.py:130
  9.6 0.1 collective-permute-done.4.refs_5_
  9.7 0.0 collective-permute-done.2.refs_3_
  9.7 0.0 collective-permute-done.3.refs_4_
  9.7 0.0 collective-permute-done.refs_1_
  9.7 0.0 collective-permute-done.1.refs_2_
  9.7 0.0 copy-done
  9.7 0.5 %close.1 = bf16[16,8,128]{2,1,0:T(8,128)(2,1)S(1)} custom-call(bf16[2,64,1024]{2,1,0:T(8,128)(2,1)S(1)} %copy-done, bf16[2,64,1024]{2,1,0:T(8,128)(2,1)S(1)} %collective-permute-done.refs_1_, bf16[2,64,1024]{2,1,0:T(8,128)(2,1)S(1)} %collective-permute-done.1.refs_2_, bf16[688,128]{1,0:T(8,128)(2,1)S(1)} %collective-permute-done.2.refs_3_, ...), custom_call_target="tpu_custom_call" | custom-call | flops 134217728 | bytes 1048576 | tf_op jit(solution)/shard_map/close/pallas_call | solution.py:174
  10.2 10.3 %all_to_all.5 = bf16[16,8,128]{2,1,0:T(8,128)(2,1)S(1)} all-to-all(bf16[16,8,128]{2,1,0:T(8,128)(2,1)S(1)} %close.1), channel_id=1, replica_groups={{31,27,22,18,15,11,6,2,29,25,20,16,13,9,4,0},{30,26,23,19,14,10,7,3,28,..., dimensions={0} | all-to-all | bytes 65536 | tf_op jit(solution)/shard_map/all_to_all | solution.py:213
  20.5 0.1 collective-permute-start.5
  20.6 1.2 %collective-permute-done.5 = f32[1024]{0:T(1024)S(1)} collective-permute-done((f32[1024]{0:T(1024)S(1)}, f32[1024]{0:T(1024)S(1)}, u32[]{:S(2)}, u32[]{:S(2)}) %collective-permute-start.5) | collective-permute-done | bytes 4128 | tf_op jit(solution)/shard_map/ppermute | solution.py:189
  21.8 0.6 %bitcast_add_fusion = f32[1024]{0:T(1024)} fusion(f32[1024]{0:T(1024)S(1)} %collective-permute-done.5, f32[8,128]{1,0:T(8,128)S(1)} %convert_reduce_fusion), kind=kLoop, calls=%fused_computation.1 | loop fusion | flops 1024 | bytes 12288 | tf_op jit(solution)/shard_map/add | solution.py:215
  (1 shorter events, 0.0 us)
Async XLA Ops:
  0.0 9.7 %collective-permute-start = (bf16[2,64,1024]{2,1,0:T(8,128)(2,1)}, bf16[2,64,1024]{2,1,0:T(8,128)(2,1)S(1)}, u32[]{:S(2)}, u32[]{:S(2)}) collective-permute-start(bf16[2,64,1024]{2,1,0:T(8,128)(2,1)} %refs_0_.1), channel_id=1, source_target_pairs={{0,3},{1,0},{2,1},{3,2},{4,7},{5,4},{6,5},{7,6},{8,11},{9,8},{10,9... | collective-permute-start | bytes 786440 | tf_op jit(solution)/shard_map/ppermute | solution.py:196
  2.4 7.3 %collective-permute-start.1 = (bf16[2,64,1024]{2,1,0:T(8,128)(2,1)}, bf16[2,64,1024]{2,1,0:T(8,128)(2,1)S(1)}, u32[]{:S(2)}, u32[]{:S(2)}) collective-permute-start(bf16[2,64,1024]{2,1,0:T(8,128)(2,1)} %refs_0_.1), channel_id=1, source_target_pairs={{0,8},{1,3},{2,10},{3,1},{4,12},{5,7},{6,14},{7,5},{8,0},{9,11},{1... | collective-permute-start | bytes 786440 | tf_op jit(solution)/shard_map/ppermute | solution.py:196
  7.7 2.0 %collective-permute-start.2 = (bf16[688,128]{1,0:T(8,128)(2,1)S(1)}, bf16[688,128]{1,0:T(8,128)(2,1)S(1)}, u32[]{:S(2)}, u32[]{:S(2)}) collective-permute-start(bf16[688,128]{1,0:T(8,128)(2,1)S(1)} %get-tuple-element.10), channel_id=1, source_target_pairs={{0,1},{1,0},{2,3},{3,2},{4,5},{5,4},{6,7},{7,6},{8,9},{9,8},{10,11... | collective-permute-start | bytes 528392 | tf_op jit(solution)/shard_map/ppermute | solution.py:189
  7.8 1.9 %collective-permute-start.3 = (bf16[688,128]{1,0:T(8,128)(2,1)S(1)}, bf16[688,128]{1,0:T(8,128)(2,1)S(1)}, u32[]{:S(2)}, u32[]{:S(2)}) collective-permute-start(bf16[688,128]{1,0:T(8,128)(2,1)S(1)} %get-tuple-element.11), channel_id=1, source_target_pairs={{0,1},{1,0},{2,3},{3,2},{4,5},{5,4},{6,7},{7,6},{8,9},{9,8},{10,11... | collective-permute-start | bytes 528392 | tf_op jit(solution)/shard_map/ppermute | solution.py:189
  8.3 1.4 %collective-permute-start.4 = (bf16[672,128]{1,0:T(8,128)(2,1)S(1)}, bf16[672,128]{1,0:T(8,128)(2,1)S(1)}, u32[]{:S(2)}, u32[]{:S(2)}) collective-permute-start(bf16[672,128]{1,0:T(8,128)(2,1)S(1)} %get-tuple-element.12), channel_id=1, source_target_pairs={{0,1},{1,0},{2,3},{3,2},{4,5},{5,4},{6,7},{7,6},{8,9},{9,8},{10,11... | collective-permute-start | bytes 516104 | tf_op jit(solution)/shard_map/ppermute | solution.py:189
  8.4 1.4 %copy-start = (bf16[2,64,1024]{2,1,0:T(8,128)(2,1)S(1)}, bf16[2,64,1024]{2,1,0:T(8,128)(2,1)}, u32[]{:S(2)}) copy-start(bf16[2,64,1024]{2,1,0:T(8,128)(2,1)} %refs_0_.1) | copy-start | bytes 786436
  20.5 1.2 %collective-permute-start.5 = (f32[1024]{0:T(1024)S(1)}, f32[1024]{0:T(1024)S(1)}, u32[]{:S(2)}, u32[]{:S(2)}) collective-permute-start(f32[1024]{0:T(1024)S(1)} %bitcast.2), channel_id=1, source_target_pairs={{0,1},{1,0},{2,3},{3,2},{4,5},{5,4},{6,7},{7,6},{8,9},{9,8},{10,11... | collective-permute-start | bytes 12296 | tf_op jit(solution)/shard_map/ppermute | solution.py:189

commit v32 on v30

--- a/solution.py
+++ b/solution.py
@@ -203,7 +203,7 @@
     got = [swap(x, 1) for x in sent]
     groups = [
         [
-            (2 * side + group) * cuts + 2 * plane + column
+            (2 * side + (plane + group) % 2) * cuts + 2 * plane + column
             for side in range(stems // 2 - 1, -1, -1) for plane in range(cuts // 2 - 1, -1, -1) for column in (1, 0)
         ]
         for group in (0, 1)

time: 21.6 us -> 22 us (1.019)
  blocking collectives: 9.97 us -> 10.3 us
    all_to_all x1, blocking collectives: 9.97 us -> 10.3 us  [on_device(): lax.all_to_all(spread, ('stem', 'cuts'), 0, 0, tiled=True, axis_index_gro...]
where the time goes in v32:
time: 22 us; the launch traced here: 21.8 us
  blocking collectives  10.3 us (47%)
  Pallas kernels  5.43 us (25%)
  starting transfers between devices  4.18 us (19%)
  waiting for transfers between devices  1.17 us (5%)
  other arithmetic  0.61 us (3%)
    all_to_all x1, blocking collectives, on_device(): lax.all_to_all(spread, ('stem', 'cuts'), 0, 0, tiled=True, axis_index_gro...  10.3 us
    pallas_call x1, Pallas kernels, branch_sums(): pl.pallas_call(functools.partial(leave_kernel, total // groups), in_specs...  3.72 us
    ppermute x2, starting transfers between devices, route(): return lax.ppermute(stem_tensor, ('cuts', 'stem'), pairs)  3.03 us
    pallas_call x1, Pallas kernels, branch_sums(): pl.pallas_call(stay_kernel, out_shape=jax.ShapeDtypeStruct((half, depth,...  1.24 us
    ppermute x4, waiting for transfers between devices, swap(): return lax.ppermute(x, 'stem', [(s, s ^ p) for s in range(stems)])  1.16 us
    ppermute x4, starting transfers between devices, swap(): return lax.ppermute(x, 'stem', [(s, s ^ p) for s in range(stems)])  1.15 us
    add x1, other arithmetic, on_device(): return total + swap(total, 1)  0.6 us
    pallas_call x1, Pallas kernels, close(): pl.pallas_call(functools.partial(close_kernel, targets if whole_tiles els...  0.46 us
  transfers between devices with their start and end apart: 6, of which 1 were waited for; matrix products, arithmetic and copies ran while one was open for 0% of the time, Pallas kernels for 23%

profile of v32, /device:TPU:0, one launch (start us, length us, event | category | flops | bytes accessed | tf_op | source)
XLA Modules:
  0.0 21.8 jit_solution(7812198222474006556)
XLA Ops:
  0.0 3.0 %collective-permute-start = (bf16[2,64,1024]{2,1,0:T(8,128)(2,1)}, bf16[2,64,1024]{2,1,0:T(8,128)(2,1)S(1)}, u32[]{:S(2)}, u32[]{:S(2)}) collective-permute-start(bf16[2,64,1024]{2,1,0:T(8,128)(2,1)} %refs_0_.1), channel_id=1, source_target_pairs={{0,8},{1,3},{2,10},{3,1},{4,12},{5,7},{6,14},{7,5},{8,0},{9,11},{1... | collective-permute-start | bytes 786440 | tf_op jit(solution)/shard_map/ppermute | solution.py:196
  3.0 0.0 collective-permute-start.1
  3.0 3.7 %leave.1 = (bf16[16,512,128]{2,1,0:T(8,128)(2,1)S(1)}, bf16[4,16,128,128]{3,2,1,0:T(8,128)(2,1)S(1)}, bf16[688,128]{1,0:T(8,128)(2,1)S(1)}, bf16[688,128]{1,0:T(8,128)(2,1)S(1)}, bf16[672,128]{1,0:T(8,128)(2,1)S(1)}) custom-call(bf16[16,512,128]{2,1,0:T(8,128)(2,1)} %mid_hbm.1, bf16[8,16,64,128]{3,2,1,0:T(8,128)(2,1)} %right_hbm.1), custom_call_target="tpu_custom_call" | custom-call | flops 1073741824 | bytes 4194304 | tf_op jit(solution)/shard_map/leave/pallas_call | solution.py:113
  6.8 0.6 %collective-permute-start.2 = (bf16[688,128]{1,0:T(8,128)(2,1)S(1)}, bf16[688,128]{1,0:T(8,128)(2,1)S(1)}, u32[]{:S(2)}, u32[]{:S(2)}) collective-permute-start(bf16[688,128]{1,0:T(8,128)(2,1)S(1)} %get-tuple-element.10), channel_id=1, source_target_pairs={{0,1},{1,0},{2,3},{3,2},{4,5},{5,4},{6,7},{7,6},{8,9},{9,8},{10,11... | collective-permute-start | bytes 528392 | tf_op jit(solution)/shard_map/ppermute | solution.py:189
  7.3 0.1 collective-permute-start.3
  7.4 0.4 %collective-permute-start.4 = (bf16[672,128]{1,0:T(8,128)(2,1)S(1)}, bf16[672,128]{1,0:T(8,128)(2,1)S(1)}, u32[]{:S(2)}, u32[]{:S(2)}) collective-permute-start(bf16[672,128]{1,0:T(8,128)(2,1)S(1)} %get-tuple-element.12), channel_id=1, source_target_pairs={{0,1},{1,0},{2,3},{3,2},{4,5},{5,4},{6,7},{7,6},{8,9},{9,8},{10,11... | collective-permute-start | bytes 516104 | tf_op jit(solution)/shard_map/ppermute | solution.py:189
  7.8 0.0 copy-start
  7.8 1.2 %stay.1.refs_6_ = f32[4,512,128]{2,1,0:T(8,128)S(1)} custom-call(bf16[16,512,128]{2,1,0:T(8,128)(2,1)S(1)} %get-tuple-element.13.mid_ref, bf16[4,16,128,128]{3,2,1,0:T(8,128)(2,1)S(1)} %get-tuple-element.14.wide_ref), custom_call_target="tpu_custom_call" | custom-call | flops 1073741824 | bytes 4194304 | tf_op jit(solution)/shard_map/stay/pallas_call | solution.py:130
  9.1 0.0 collective-permute-done.4.refs_5_
  9.1 0.0 collective-permute-done.2.refs_3_
  9.1 0.0 collective-permute-done.3.refs_4_
  9.1 0.0 collective-permute-done.refs_1_
  9.1 0.0 collective-permute-done.1.refs_2_
  9.1 0.0 copy-done
  9.2 0.5 %close.1 = bf16[16,8,128]{2,1,0:T(8,128)(2,1)S(1)} custom-call(bf16[2,64,1024]{2,1,0:T(8,128)(2,1)S(1)} %copy-done, bf16[2,64,1024]{2,1,0:T(8,128)(2,1)S(1)} %collective-permute-done.refs_1_, bf16[2,64,1024]{2,1,0:T(8,128)(2,1)S(1)} %collective-permute-done.1.refs_2_, bf16[688,128]{1,0:T(8,128)(2,1)S(1)} %collective-permute-done.2.refs_3_, ...), custom_call_target="tpu_custom_call" | custom-call | flops 134217728 | bytes 1048576 | tf_op jit(solution)/shard_map/close/pallas_call | solution.py:174
  9.6 10.3 %all_to_all.5 = bf16[16,8,128]{2,1,0:T(8,128)(2,1)S(1)} all-to-all(bf16[16,8,128]{2,1,0:T(8,128)(2,1)S(1)} %close.1), channel_id=1, replica_groups={{31,27,22,18,15,11,6,2,29,25,20,16,13,9,4,0},{30,26,23,19,14,10,7,3,28,..., dimensions={0} | all-to-all | bytes 65536 | tf_op jit(solution)/shard_map/all_to_all | solution.py:213
  20.0 0.1 collective-permute-start.5
  20.0 1.2 %collective-permute-done.5 = f32[1024]{0:T(1024)S(1)} collective-permute-done((f32[1024]{0:T(1024)S(1)}, f32[1024]{0:T(1024)S(1)}, u32[]{:S(2)}, u32[]{:S(2)}) %collective-permute-start.5) | collective-permute-done | bytes 4128 | tf_op jit(solution)/shard_map/ppermute | solution.py:189
  21.2 0.6 %bitcast_add_fusion = f32[1024]{0:T(1024)} fusion(f32[1024]{0:T(1024)S(1)} %collective-permute-done.5, f32[8,128]{1,0:T(8,128)S(1)} %convert_reduce_fusion), kind=kLoop, calls=%fused_computation.1 | loop fusion | flops 1024 | bytes 12288 | tf_op jit(solution)/shard_map/add | solution.py:215
  (1 shorter events, 0.0 us)
Async XLA Ops:
  0.0 9.1 %collective-permute-start = (bf16[2,64,1024]{2,1,0:T(8,128)(2,1)}, bf16[2,64,1024]{2,1,0:T(8,128)(2,1)S(1)}, u32[]{:S(2)}, u32[]{:S(2)}) collective-permute-start(bf16[2,64,1024]{2,1,0:T(8,128)(2,1)} %refs_0_.1), channel_id=1, source_target_pairs={{0,8},{1,3},{2,10},{3,1},{4,12},{5,7},{6,14},{7,5},{8,0},{9,11},{1... | collective-permute-start | bytes 786440 | tf_op jit(solution)/shard_map/ppermute | solution.py:196
  3.0 6.1 %collective-permute-start.1 = (bf16[2,64,1024]{2,1,0:T(8,128)(2,1)}, bf16[2,64,1024]{2,1,0:T(8,128)(2,1)S(1)}, u32[]{:S(2)}, u32[]{:S(2)}) collective-permute-start(bf16[2,64,1024]{2,1,0:T(8,128)(2,1)} %refs_0_.1), channel_id=1, source_target_pairs={{0,3},{1,0},{2,1},{3,2},{4,7},{5,4},{6,5},{7,6},{8,11},{9,8},{10,9... | collective-permute-start | bytes 786440 | tf_op jit(solution)/shard_map/ppermute | solution.py:196
  6.8 2.3 %collective-permute-start.2 = (bf16[688,128]{1,0:T(8,128)(2,1)S(1)}, bf16[688,128]{1,0:T(8,128)(2,1)S(1)}, u32[]{:S(2)}, u32[]{:S(2)}) collective-permute-start(bf16[688,128]{1,0:T(8,128)(2,1)S(1)} %get-tuple-element.10), channel_id=1, source_target_pairs={{0,1},{1,0},{2,3},{3,2},{4,5},{5,4},{6,7},{7,6},{8,9},{9,8},{10,11... | collective-permute-start | bytes 528392 | tf_op jit(solution)/shard_map/ppermute | solution.py:189
  7.3 1.8 %collective-permute-start.3 = (bf16[688,128]{1,0:T(8,128)(2,1)S(1)}, bf16[688,128]{1,0:T(8,128)(2,1)S(1)}, u32[]{:S(2)}, u32[]{:S(2)}) collective-permute-start(bf16[688,128]{1,0:T(8,128)(2,1)S(1)} %get-tuple-element.11), channel_id=1, source_target_pairs={{0,1},{1,0},{2,3},{3,2},{4,5},{5,4},{6,7},{7,6},{8,9},{9,8},{10,11... | collective-permute-start | bytes 528392 | tf_op jit(solution)/shard_map/ppermute | solution.py:189
  7.4 1.7 %collective-permute-start.4 = (bf16[672,128]{1,0:T(8,128)(2,1)S(1)}, bf16[672,128]{1,0:T(8,128)(2,1)S(1)}, u32[]{:S(2)}, u32[]{:S(2)}) collective-permute-start(bf16[672,128]{1,0:T(8,128)(2,1)S(1)} %get-tuple-element.12), channel_id=1, source_target_pairs={{0,1},{1,0},{2,3},{3,2},{4,5},{5,4},{6,7},{7,6},{8,9},{9,8},{10,11... | collective-permute-start | bytes 516104 | tf_op jit(solution)/shard_map/ppermute | solution.py:189
  7.8 1.3 %copy-start = (bf16[2,64,1024]{2,1,0:T(8,128)(2,1)S(1)}, bf16[2,64,1024]{2,1,0:T(8,128)(2,1)}, u32[]{:S(2)}) copy-start(bf16[2,64,1024]{2,1,0:T(8,128)(2,1)} %refs_0_.1) | copy-start | bytes 786436
  20.0 1.2 %collective-permute-start.5 = (f32[1024]{0:T(1024)S(1)}, f32[1024]{0:T(1024)S(1)}, u32[]{:S(2)}, u32[]{:S(2)}) collective-permute-start(f32[1024]{0:T(1024)S(1)} %bitcast.2), channel_id=1, source_target_pairs={{0,1},{1,0},{2,3},{3,2},{4,5},{5,4},{6,7},{7,6},{8,9},{9,8},{10,11... | collective-permute-start | bytes 12296 | tf_op jit(solution)/shard_map/ppermute | solution.py:189

commit v33 on v30

--- a/solution.py
+++ b/solution.py
@@ -137,24 +137,54 @@
     return kept, *sent
 
 
+def stacked(block):
+    half = block.shape[-1] // 2
+    return jnp.concatenate([block[:, :half], block[:, half:]], axis=0)
+
+
+def fold_kernel(own_ref, cycle_ref, kept_ref, *refs):
+    *got_refs, part_ref, far_ref = refs
+    blocks, depth, width = kept_ref.shape
+    own = own_ref.shape[0]
+    first_core = lax.axis_index("stem") % 2 == 0
+    pieces = segments(blocks, depth, [ref.shape[0] for ref in got_refs])
+    part = None
+    for b in range(blocks):
+        got = [got_refs[piece][at:at + count] for block, _, piece, at, count in pieces if block == b]
+        sums = kept_ref[b] + jnp.concatenate(got, axis=0).astype(jnp.float32)
+        high = sums.astype(jnp.bfloat16)
+        low = (sums - high.astype(jnp.float32)).astype(jnp.bfloat16)
+        both = jnp.concatenate([high, low], axis=1)
+        if b < own:
+            term = jnp.dot(stacked(jnp.where(first_core, own_ref[b], cycle_ref[b])), both, preferred_element_type=jnp.float32)
+            part = term if part is None else part + term
+        else:
+            far_ref[b - own] = both
+    part_ref[...] = part
+
+
+def fold(own, cycle, kept, got):
+    count, rows, _ = own.shape
+    blocks, depth, width = kept.shape
+    return pl.pallas_call(
+        fold_kernel,
+        out_shape=[
+            jax.ShapeDtypeStruct((2 * rows, 2 * width), jnp.float32),
+            jax.ShapeDtypeStruct((blocks - count, depth, 2 * width), jnp.bfloat16),
+        ],
+        compiler_params=pltpu.CompilerParams(vmem_limit_bytes=24 * MIB),
+        cost_estimate=pl.CostEstimate(flops=8 * rows * kept.size, bytes_accessed=MIB, transcendentals=0),
+        name="fold",
+    )(own, cycle, kept, *got)
+
+
 def close_kernel(targets, *refs):
-    own_ref, cross_ref, cycle_ref, *got_refs, kept_ref, out_ref = refs
+    cycle_ref, cross_ref, part_ref, far_ref, out_ref = refs
     first_core = lax.axis_index("stem") % 2 == 0
-    pieces = segments(kept_ref.shape[0], kept_ref.shape[1], [ref.shape[0] for ref in got_refs])
-    part = None
-    at = 0
-    for when_first, when_second in ((own_ref, cycle_ref), (cycle_ref, cross_ref)):
-        for b in range(own_ref.shape[0]):
-            block = jnp.where(first_core, when_first[b], when_second[b])
-            half = block.shape[-1] // 2
-            rows = jnp.concatenate([block[:, :half], block[:, half:]], axis=0)
-            got = [got_refs[piece][row:row + count] for block_at, _, piece, row, count in pieces if block_at == at]
-            sums = kept_ref[at] + jnp.concatenate(got, axis=0).astype(jnp.float32)
-            high = sums.astype(jnp.bfloat16)
-            low = (sums - high.astype(jnp.float32)).astype(jnp.bfloat16)
-            term = jnp.dot(rows, jnp.concatenate([high, low], axis=1), preferred_element_type=jnp.float32)
-            part = term if part is None else part + term
-            at += 1
+    part = part_ref[...]
+    for b in range(far_ref.shape[0]):
+        block = jnp.where(first_core, cycle_ref[b], cross_ref[b])
+        part += jnp.dot(stacked(block), far_ref[b], preferred_element_type=jnp.float32)
     width = part.shape[1] // 2
     part = part[:, :width] + part[:, width:]
     half = part.shape[0] // 2
@@ -167,17 +197,17 @@
             out_ref[at] = total[c * rows:(c + 1) * rows].astype(out_ref.dtype)
 
 
-def close(stems, kept, got, cuts, targets):
-    rows, width = stems[0].shape[1], kept.shape[2]
+def close(stems, part, far, cuts, targets):
+    rows, width = part.shape[0] // 2, part.shape[1] // 2
     whole_tiles = rows % (8 * cuts) == 0
     shape = (len(targets), rows // cuts, width) if whole_tiles else (rows, width)
     out = pl.pallas_call(
         functools.partial(close_kernel, targets if whole_tiles else None),
         out_shape=jax.ShapeDtypeStruct(shape, jnp.bfloat16 if whole_tiles else jnp.float32),
         compiler_params=pltpu.CompilerParams(vmem_limit_bytes=24 * MIB),
-        cost_estimate=pl.CostEstimate(flops=8 * rows * kept.size, bytes_accessed=MIB, transcendentals=0),
+        cost_estimate=pl.CostEstimate(flops=4 * rows * far.size, bytes_accessed=MIB, transcendentals=0),
         name="close",
-    )(*stems, *got, kept)
+    )(*stems, part, far)
     return out if whole_tiles else out.reshape(cuts, -1)[np.array(targets)]
 
 
@@ -198,7 +228,6 @@
     assert stems == 4
     cross = route(lambda cut, side, core: (cut, 1 - side, 1) if core else (cut ^ 2, side, 0))
     cycle = route(lambda cut, side, core: (cut, side, 0) if core else (cut, 1 - side, 1))
-    pieces = [stem_tensor, cross, cycle]
     kept, *sent = branch_sums(mid_tensors, right_tensors, stems)
     got = [swap(x, 1) for x in sent]
     groups = [
@@ -209,7 +238,8 @@
         for group in (0, 1)
     ]
     targets = [at % cuts for at in groups[0]]
-    spread = close(pieces, kept, got, cuts, targets)
+    part, far = fold(stem_tensor, cycle, kept, got)
+    spread = close([cycle, cross], part, far, cuts, targets)
     parts = lax.all_to_all(spread, ("stem", "cuts"), 0, 0, tiled=True, axis_index_groups=groups)
     total = jnp.sum(parts.astype(jnp.float32), axis=0).reshape(-1)
     return total + swap(total, 1)

time: 21.6 us -> 22.1 us (1.023)
  starting transfers between devices: 4.29 us -> 4.8 us
    ppermute x2, starting transfers between devices: 3.03 us -> 3.98 us  [route(): return lax.ppermute(stem_tensor, ('cuts', 'stem'), pairs)]
    ppermute x4, starting transfers between devices: 1.26 us -> 0.82 us  [swap(): return lax.ppermute(x, 'stem', [(s, s ^ p) for s in range(stems)])]
    pallas_call x0 -> x1, Pallas kernels: none -> 0.32 us  [fold(): pl.pallas_call(fold_kernel, out_shape=[jax.ShapeDtypeStruct((2 * rows, 2...]
    all_to_all x1, blocking collectives: 9.97 us -> 9.75 us  [on_device(): lax.all_to_all(spread, ('stem', 'cuts'), 0, 0, tiled=True, axis_index_gro...]
  transfers between devices with their start and end apart: 6 -> 6, of which waited for: 1 -> 2; matrix products, arithmetic and copies ran while one was open for 0% -> 0% of each run, Pallas kernels for 23% -> 24%
where the time goes in v33:
time: 22.1 us; the launch traced here: 22 us
  blocking collectives  9.75 us (44%)
  Pallas kernels  5.6 us (25%)
  starting transfers between devices  4.8 us (22%)
  waiting for transfers between devices  1.14 us (5%)
  other arithmetic  0.61 us (3%)
    all_to_all x1, blocking collectives, on_device(): lax.all_to_all(spread, ('stem', 'cuts'), 0, 0, tiled=True, axis_index_gro...  9.75 us
    ppermute x2, starting transfers between devices, route(): return lax.ppermute(stem_tensor, ('cuts', 'stem'), pairs)  3.98 us
    pallas_call x1, Pallas kernels, branch_sums(): pl.pallas_call(functools.partial(leave_kernel, total // groups), in_specs...  3.72 us
    pallas_call x1, Pallas kernels, branch_sums(): pl.pallas_call(stay_kernel, out_shape=jax.ShapeDtypeStruct((half, depth,...  1.24 us
    ppermute x4, waiting for transfers between devices, swap(): return lax.ppermute(x, 'stem', [(s, s ^ p) for s in range(stems)])  1.14 us
    ppermute x4, starting transfers between devices, swap(): return lax.ppermute(x, 'stem', [(s, s ^ p) for s in range(stems)])  0.82 us
    add x1, other arithmetic, on_device(): return total + swap(total, 1)  0.6 us
  transfers between devices with their start and end apart: 6, of which 2 were waited for; matrix products, arithmetic and copies ran while one was open for 0% of the time, Pallas kernels for 24%

profile of v33, /device:TPU:0, one launch (start us, length us, event | category | flops | bytes accessed | tf_op | source)
XLA Modules:
  0.0 22.0 jit_solution(5853008863438657420)
XLA Ops:
  0.0 2.4 %collective-permute-start = (bf16[2,64,1024]{2,1,0:T(8,128)(2,1)}, bf16[2,64,1024]{2,1,0:T(8,128)(2,1)S(1)}, u32[]{:S(2)}, u32[]{:S(2)}) collective-permute-start(bf16[2,64,1024]{2,1,0:T(8,128)(2,1)} %own_ref.1), channel_id=1, source_target_pairs={{0,3},{1,0},{2,1},{3,2},{4,7},{5,4},{6,5},{7,6},{8,11},{9,8},{10,9... | collective-permute-start | bytes 786440 | tf_op jit(solution)/shard_map/ppermute | solution.py:226
  2.4 1.6 %collective-permute-start.1 = (bf16[2,64,1024]{2,1,0:T(8,128)(2,1)}, bf16[2,64,1024]{2,1,0:T(8,128)(2,1)S(1)}, u32[]{:S(2)}, u32[]{:S(2)}) collective-permute-start(bf16[2,64,1024]{2,1,0:T(8,128)(2,1)} %own_ref.1), channel_id=1, source_target_pairs={{0,8},{1,3},{2,10},{3,1},{4,12},{5,7},{6,14},{7,5},{8,0},{9,11},{1... | collective-permute-start | bytes 786440 | tf_op jit(solution)/shard_map/ppermute | solution.py:226
  4.0 3.7 %leave.1 = (bf16[16,512,128]{2,1,0:T(8,128)(2,1)S(1)}, bf16[4,16,128,128]{3,2,1,0:T(8,128)(2,1)S(1)}, bf16[688,128]{1,0:T(8,128)(2,1)S(1)}, bf16[688,128]{1,0:T(8,128)(2,1)S(1)}, bf16[672,128]{1,0:T(8,128)(2,1)S(1)}) custom-call(bf16[16,512,128]{2,1,0:T(8,128)(2,1)} %mid_hbm.1, bf16[8,16,64,128]{3,2,1,0:T(8,128)(2,1)} %right_hbm.1), custom_call_target="tpu_custom_call" | custom-call | flops 1073741824 | bytes 4194304 | tf_op jit(solution)/shard_map/leave/pallas_call | solution.py:113
  7.7 0.1 collective-permute-start.2
  7.8 0.5 %collective-permute-start.3 = (bf16[688,128]{1,0:T(8,128)(2,1)S(1)}, bf16[688,128]{1,0:T(8,128)(2,1)S(1)}, u32[]{:S(2)}, u32[]{:S(2)}) collective-permute-start(bf16[688,128]{1,0:T(8,128)(2,1)S(1)} %get-tuple-element.15), channel_id=1, source_target_pairs={{0,1},{1,0},{2,3},{3,2},{4,5},{5,4},{6,7},{7,6},{8,9},{9,8},{10,11... | collective-permute-start | bytes 528392 | tf_op jit(solution)/shard_map/ppermute | solution.py:219
  8.3 0.1 collective-permute-start.4
  8.4 0.0 copy-start
  8.4 1.2 %stay.1.kept_ref = f32[4,512,128]{2,1,0:T(8,128)S(1)} custom-call(bf16[16,512,128]{2,1,0:T(8,128)(2,1)S(1)} %get-tuple-element.12.mid_ref, bf16[4,16,128,128]{3,2,1,0:T(8,128)(2,1)S(1)} %get-tuple-element.13.wide_ref), custom_call_target="tpu_custom_call" | custom-call | flops 1073741824 | bytes 4194304 | tf_op jit(solution)/shard_map/stay/pallas_call | solution.py:130
  9.6 0.1 collective-permute-done.4.refs_2_
  9.7 0.0 collective-permute-done.2.refs_0_
  9.7 0.0 collective-permute-done.3.refs_1_
  9.7 0.0 collective-permute-done.cycle_ref.refs_0_
  9.7 0.0 copy-done
  9.7 0.3 %fold.1 = (f32[128,256]{1,0:T(8,128)S(1)}, bf16[2,512,256]{2,1,0:T(8,128)(2,1)S(1)}) custom-call(bf16[2,64,1024]{2,1,0:T(8,128)(2,1)S(1)} %copy-done, bf16[2,64,1024]{2,1,0:T(8,128)(2,1)S(1)} %collective-permute-done.cycle_ref.refs_0_, f32[4,512,128]{2,1,0:T(8,128)S(1)} %stay.1.kept_ref, bf16[688,128]{1,0:T(8,128)(2,1)S(1)} %collective-permute-done.2.refs_0_, ...), custom_call_target="tpu_custom_call" | custom-call | flops 134217728 | bytes 1048576 | tf_op jit(solution)/shard_map/fold/pallas_call | solution.py:169
  10.1 0.0 collective-permute-done.1.refs_1_
  10.1 0.3 %close.1 = bf16[16,8,128]{2,1,0:T(8,128)(2,1)S(1)} custom-call(bf16[2,64,1024]{2,1,0:T(8,128)(2,1)S(1)} %collective-permute-done.cycle_ref.refs_0_, bf16[2,64,1024]{2,1,0:T(8,128)(2,1)S(1)} %collective-permute-done.1.refs_1_, f32[128,256]{1,0:T(8,128)S(1)} %get-tuple-element.17.refs_2_, bf16[2,512,256]{2,1,0:T(8,128)(2,1)S(1)} %get-tuple-element.18.refs_3_), custom_call_target="tpu_custom_call" | custom-call | flops 67108864 | bytes 1048576 | tf_op jit(solution)/shard_map/close/pallas_call | solution.py:204
  10.4 9.8 %all_to_all.5 = bf16[16,8,128]{2,1,0:T(8,128)(2,1)S(1)} all-to-all(bf16[16,8,128]{2,1,0:T(8,128)(2,1)S(1)} %close.1), channel_id=1, replica_groups={{30,26,22,18,14,10,6,2,28,24,20,16,12,8,4,0},{31,27,23,19,15,11,7,3,29,..., dimensions={0} | all-to-all | bytes 65536 | tf_op jit(solution)/shard_map/all_to_all | solution.py:243
  20.1 0.2 collective-permute-start.5
  20.3 1.1 %collective-permute-done.5 = f32[1024]{0:T(1024)S(1)} collective-permute-done((f32[1024]{0:T(1024)S(1)}, f32[1024]{0:T(1024)S(1)}, u32[]{:S(2)}, u32[]{:S(2)}) %collective-permute-start.5) | collective-permute-done | bytes 4128 | tf_op jit(solution)/shard_map/ppermute | solution.py:219
  21.4 0.6 %bitcast_add_fusion = f32[1024]{0:T(1024)} fusion(f32[1024]{0:T(1024)S(1)} %collective-permute-done.5, f32[8,128]{1,0:T(8,128)S(1)} %convert_reduce_fusion), kind=kLoop, calls=%fused_computation.1 | loop fusion | flops 1024 | bytes 12288 | tf_op jit(solution)/shard_map/add | solution.py:245
  (1 shorter events, 0.0 us)
Async XLA Ops:
  0.0 9.7 %collective-permute-start = (bf16[2,64,1024]{2,1,0:T(8,128)(2,1)}, bf16[2,64,1024]{2,1,0:T(8,128)(2,1)S(1)}, u32[]{:S(2)}, u32[]{:S(2)}) collective-permute-start(bf16[2,64,1024]{2,1,0:T(8,128)(2,1)} %own_ref.1), channel_id=1, source_target_pairs={{0,3},{1,0},{2,1},{3,2},{4,7},{5,4},{6,5},{7,6},{8,11},{9,8},{10,9... | collective-permute-start | bytes 786440 | tf_op jit(solution)/shard_map/ppermute | solution.py:226
  2.4 7.6 %collective-permute-start.1 = (bf16[2,64,1024]{2,1,0:T(8,128)(2,1)}, bf16[2,64,1024]{2,1,0:T(8,128)(2,1)S(1)}, u32[]{:S(2)}, u32[]{:S(2)}) collective-permute-start(bf16[2,64,1024]{2,1,0:T(8,128)(2,1)} %own_ref.1), channel_id=1, source_target_pairs={{0,8},{1,3},{2,10},{3,1},{4,12},{5,7},{6,14},{7,5},{8,0},{9,11},{1... | collective-permute-start | bytes 786440 | tf_op jit(solution)/shard_map/ppermute | solution.py:226
  7.7 2.0 %collective-permute-start.2 = (bf16[688,128]{1,0:T(8,128)(2,1)S(1)}, bf16[688,128]{1,0:T(8,128)(2,1)S(1)}, u32[]{:S(2)}, u32[]{:S(2)}) collective-permute-start(bf16[688,128]{1,0:T(8,128)(2,1)S(1)} %get-tuple-element.14), channel_id=1, source_target_pairs={{0,1},{1,0},{2,3},{3,2},{4,5},{5,4},{6,7},{7,6},{8,9},{9,8},{10,11... | collective-permute-start | bytes 528392 | tf_op jit(solution)/shard_map/ppermute | solution.py:219
  7.8 1.9 %collective-permute-start.3 = (bf16[688,128]{1,0:T(8,128)(2,1)S(1)}, bf16[688,128]{1,0:T(8,128)(2,1)S(1)}, u32[]{:S(2)}, u32[]{:S(2)}) collective-permute-start(bf16[688,128]{1,0:T(8,128)(2,1)S(1)} %get-tuple-element.15), channel_id=1, source_target_pairs={{0,1},{1,0},{2,3},{3,2},{4,5},{5,4},{6,7},{7,6},{8,9},{9,8},{10,11... | collective-permute-start | bytes 528392 | tf_op jit(solution)/shard_map/ppermute | solution.py:219
  8.3 1.4 %collective-permute-start.4 = (bf16[672,128]{1,0:T(8,128)(2,1)S(1)}, bf16[672,128]{1,0:T(8,128)(2,1)S(1)}, u32[]{:S(2)}, u32[]{:S(2)}) collective-permute-start(bf16[672,128]{1,0:T(8,128)(2,1)S(1)} %get-tuple-element.16), channel_id=1, source_target_pairs={{0,1},{1,0},{2,3},{3,2},{4,5},{5,4},{6,7},{7,6},{8,9},{9,8},{10,11... | collective-permute-start | bytes 516104 | tf_op jit(solution)/shard_map/ppermute | solution.py:219
  8.4 1.3 %copy-start = (bf16[2,64,1024]{2,1,0:T(8,128)(2,1)S(1)}, bf16[2,64,1024]{2,1,0:T(8,128)(2,1)}, u32[]{:S(2)}) copy-start(bf16[2,64,1024]{2,1,0:T(8,128)(2,1)} %own_ref.1) | copy-start | bytes 786436
  20.1 1.2 %collective-permute-start.5 = (f32[1024]{0:T(1024)S(1)}, f32[1024]{0:T(1024)S(1)}, u32[]{:S(2)}, u32[]{:S(2)}) collective-permute-start(f32[1024]{0:T(1024)S(1)} %bitcast.2), channel_id=1, source_target_pairs={{0,1},{1,0},{2,3},{3,2},{4,5},{5,4},{6,7},{7,6},{8,9},{9,8},{10,11... | collective-permute-start | bytes 12296 | tf_op jit(solution)/shard_map/ppermute | solution.py:219

commit v34 on v30

--- a/solution.py
+++ b/solution.py
@@ -9,7 +9,7 @@
 from jax.sharding import PartitionSpec as P
 
 MIB = 1024 * 1024
-LEAVE_MIB = 48
+LEAVE_MIB = 49
 
 
 def turn(x):
@@ -40,7 +40,16 @@
     pairs = mid_ref.shape[0]
     left = jnp.concatenate([mid_ref[j] for j in range(pairs)], axis=1)
     blocks, _, rows, width = wide_ref.shape
-    right = [wide_ref[b].reshape(pairs * rows, width) for b in range(blocks)]
+    if rows == width:
+        right = [wide_ref[b].reshape(pairs * rows, width) for b in range(blocks)]
+    else:
+        right = []
+        for b in range(blocks):
+            both = []
+            for j in range(pairs):
+                upper = wide_ref[b, j]
+                both += [upper, turn(upper.astype(jnp.float32)).astype(upper.dtype)]
+            right.append(jnp.concatenate(both, axis=0))
     return jnp.dot(left, jnp.concatenate(right, axis=1), preferred_element_type=jnp.float32)
 
 
@@ -89,7 +98,8 @@
     for b, row, piece, at, count in segments(total // 2, depth, sizes):
         part = sums[row:row + count, b * width:(b + 1) * width]
         sent_refs[piece][at:at + count] = part.astype(jnp.bfloat16)
-    widen(stay_ref, 1)
+    for q in range(half):
+        right_copy(q, stay_ref, 1).wait()
 
 
 def stay_kernel(mid_ref, wide_ref, kept_ref):
@@ -116,7 +126,7 @@
         out_specs=[vmem] * (2 + len(sizes)),
         out_shape=[
             jax.ShapeDtypeStruct(mid.shape, mid.dtype),
-            jax.ShapeDtypeStruct(wide, right.dtype),
+            jax.ShapeDtypeStruct((half, pairs, inner, width), right.dtype),
         ] + [jax.ShapeDtypeStruct((size, width), jnp.bfloat16) for size in sizes],
         scratch_shapes=[
             pltpu.VMEM(wide, right.dtype),

time: 21.6 us -> 21 us (0.972)
  Pallas kernels: 5.43 us -> 5.07 us
  blocking collectives: 9.97 us -> 9.7 us
  starting transfers between devices: 4.29 us -> 4.51 us
    pallas_call x1, Pallas kernels: 3.72 us -> 3.31 us  [branch_sums(): pl.pallas_call(functools.partial(leave_kernel, total // groups), in_specs...]
    all_to_all x1, blocking collectives: 9.97 us -> 9.7 us  [on_device(): lax.all_to_all(spread, ('stem', 'cuts'), 0, 0, tiled=True, axis_index_gro...]
    ppermute x4, waiting for transfers between devices: 1.06 us -> 0.84 us  [swap(): return lax.ppermute(x, 'stem', [(s, s ^ p) for s in range(stems)])]
    ppermute x4, starting transfers between devices: 1.26 us -> 1.48 us  [swap(): return lax.ppermute(x, 'stem', [(s, s ^ p) for s in range(stems)])]
  transfers between devices with their start and end apart: 6 -> 6, of which waited for: 1 -> 1; matrix products, arithmetic and copies ran while one was open for 0% -> 0% of each run, Pallas kernels for 23% -> 22%
where the time goes in v34:
time: 21 us; the launch traced here: 20.8 us
  blocking collectives  9.7 us (46%)
  Pallas kernels  5.07 us (24%)
  starting transfers between devices  4.51 us (21%)
  waiting for transfers between devices  0.89 us (4%)
  other arithmetic  0.61 us (3%)
    all_to_all x1, blocking collectives, on_device(): lax.all_to_all(spread, ('stem', 'cuts'), 0, 0, tiled=True, axis_index_gro...  9.7 us
    pallas_call x1, Pallas kernels, branch_sums(): pl.pallas_call(functools.partial(leave_kernel, total // groups), in_specs...  3.31 us
    ppermute x2, starting transfers between devices, route(): return lax.ppermute(stem_tensor, ('cuts', 'stem'), pairs)  3.03 us
    ppermute x4, starting transfers between devices, swap(): return lax.ppermute(x, 'stem', [(s, s ^ p) for s in range(stems)])  1.48 us
    pallas_call x1, Pallas kernels, branch_sums(): pl.pallas_call(stay_kernel, out_shape=jax.ShapeDtypeStruct((half, depth,...  1.32 us
    ppermute x4, waiting for transfers between devices, swap(): return lax.ppermute(x, 'stem', [(s, s ^ p) for s in range(stems)])  0.84 us
    add x1, other arithmetic, on_device(): return total + swap(total, 1)  0.6 us
    pallas_call x1, Pallas kernels, close(): pl.pallas_call(functools.partial(close_kernel, targets if whole_tiles els...  0.44 us
  transfers between devices with their start and end apart: 6, of which 1 were waited for; matrix products, arithmetic and copies ran while one was open for 0% of the time, Pallas kernels for 22%

profile of v34, /device:TPU:0, one launch (start us, length us, event | category | flops | bytes accessed | tf_op | source)
XLA Modules:
  0.0 20.8 jit_solution(715446860378104816)
XLA Ops:
  0.0 3.0 %collective-permute-start = (bf16[2,64,1024]{2,1,0:T(8,128)(2,1)}, bf16[2,64,1024]{2,1,0:T(8,128)(2,1)S(1)}, u32[]{:S(2)}, u32[]{:S(2)}) collective-permute-start(bf16[2,64,1024]{2,1,0:T(8,128)(2,1)} %refs_0_.1), channel_id=1, source_target_pairs={{0,8},{1,3},{2,10},{3,1},{4,12},{5,7},{6,14},{7,5},{8,0},{9,11},{1... | collective-permute-start | bytes 786440 | tf_op jit(solution)/shard_map/ppermute | solution.py:206
  3.0 0.0 collective-permute-start.1
  3.0 3.3 %leave.1 = (bf16[16,512,128]{2,1,0:T(8,128)(2,1)S(1)}, bf16[4,16,64,128]{3,2,1,0:T(8,128)(2,1)S(1)}, bf16[688,128]{1,0:T(8,128)(2,1)S(1)}, bf16[688,128]{1,0:T(8,128)(2,1)S(1)}, bf16[672,128]{1,0:T(8,128)(2,1)S(1)}) custom-call(bf16[16,512,128]{2,1,0:T(8,128)(2,1)} %mid_hbm.1, bf16[8,16,64,128]{3,2,1,0:T(8,128)(2,1)} %right_hbm.1), custom_call_target="tpu_custom_call" | custom-call | flops 1073741824 | bytes 4194304 | tf_op jit(solution)/shard_map/leave/pallas_call | solution.py:123
  6.3 0.6 %collective-permute-start.2 = (bf16[688,128]{1,0:T(8,128)(2,1)S(1)}, bf16[688,128]{1,0:T(8,128)(2,1)S(1)}, u32[]{:S(2)}, u32[]{:S(2)}) collective-permute-start(bf16[688,128]{1,0:T(8,128)(2,1)S(1)} %get-tuple-element.10), channel_id=1, source_target_pairs={{0,1},{1,0},{2,3},{3,2},{4,5},{5,4},{6,7},{7,6},{8,9},{9,8},{10,11... | collective-permute-start | bytes 528392 | tf_op jit(solution)/shard_map/ppermute | solution.py:199
  6.9 0.1 collective-permute-start.3
  7.0 0.4 %collective-permute-start.4 = (bf16[672,128]{1,0:T(8,128)(2,1)S(1)}, bf16[672,128]{1,0:T(8,128)(2,1)S(1)}, u32[]{:S(2)}, u32[]{:S(2)}) collective-permute-start(bf16[672,128]{1,0:T(8,128)(2,1)S(1)} %get-tuple-element.12), channel_id=1, source_target_pairs={{0,1},{1,0},{2,3},{3,2},{4,5},{5,4},{6,7},{7,6},{8,9},{9,8},{10,11... | collective-permute-start | bytes 516104 | tf_op jit(solution)/shard_map/ppermute | solution.py:199
  7.4 0.0 copy-start
  7.4 1.3 %stay.1.refs_6_ = f32[4,512,128]{2,1,0:T(8,128)S(1)} custom-call(bf16[16,512,128]{2,1,0:T(8,128)(2,1)S(1)} %get-tuple-element.13.mid_ref, bf16[4,16,64,128]{3,2,1,0:T(8,128)(2,1)S(1)} %get-tuple-element.14.wide_ref), custom_call_target="tpu_custom_call" | custom-call | flops 1073741824 | bytes 4194304 | tf_op jit(solution)/shard_map/stay/pallas_call | solution.py:140
  8.8 0.0 collective-permute-done.4.refs_5_
  8.8 0.0 collective-permute-done.2.refs_3_
  8.8 0.0 collective-permute-done.3.refs_4_
  8.8 0.0 collective-permute-done.refs_1_
  8.8 0.0 collective-permute-done.1.refs_2_
  8.8 0.0 copy-done
  8.9 0.4 %close.1 = bf16[16,8,128]{2,1,0:T(8,128)(2,1)S(1)} custom-call(bf16[2,64,1024]{2,1,0:T(8,128)(2,1)S(1)} %copy-done, bf16[2,64,1024]{2,1,0:T(8,128)(2,1)S(1)} %collective-permute-done.refs_1_, bf16[2,64,1024]{2,1,0:T(8,128)(2,1)S(1)} %collective-permute-done.1.refs_2_, bf16[688,128]{1,0:T(8,128)(2,1)S(1)} %collective-permute-done.2.refs_3_, ...), custom_call_target="tpu_custom_call" | custom-call | flops 134217728 | bytes 1048576 | tf_op jit(solution)/shard_map/close/pallas_call | solution.py:184
  9.3 9.7 %all_to_all.5 = bf16[16,8,128]{2,1,0:T(8,128)(2,1)S(1)} all-to-all(bf16[16,8,128]{2,1,0:T(8,128)(2,1)S(1)} %close.1), channel_id=1, replica_groups={{30,26,22,18,14,10,6,2,28,24,20,16,12,8,4,0},{31,27,23,19,15,11,7,3,29,..., dimensions={0} | all-to-all | bytes 65536 | tf_op jit(solution)/shard_map/all_to_all | solution.py:223
  19.0 0.4 %collective-permute-start.5 = (f32[1024]{0:T(1024)S(1)}, f32[1024]{0:T(1024)S(1)}, u32[]{:S(2)}, u32[]{:S(2)}) collective-permute-start(f32[1024]{0:T(1024)S(1)} %bitcast.2), channel_id=1, source_target_pairs={{0,1},{1,0},{2,3},{3,2},{4,5},{5,4},{6,7},{7,6},{8,9},{9,8},{10,11... | collective-permute-start | bytes 12296 | tf_op jit(solution)/shard_map/ppermute | solution.py:199
  19.4 0.8 %collective-permute-done.5 = f32[1024]{0:T(1024)S(1)} collective-permute-done((f32[1024]{0:T(1024)S(1)}, f32[1024]{0:T(1024)S(1)}, u32[]{:S(2)}, u32[]{:S(2)}) %collective-permute-start.5) | collective-permute-done | bytes 4128 | tf_op jit(solution)/shard_map/ppermute | solution.py:199
  20.2 0.6 %bitcast_add_fusion = f32[1024]{0:T(1024)} fusion(f32[1024]{0:T(1024)S(1)} %collective-permute-done.5, f32[8,128]{1,0:T(8,128)S(1)} %convert_reduce_fusion), kind=kLoop, calls=%fused_computation.1 | loop fusion | flops 1024 | bytes 12288 | tf_op jit(solution)/shard_map/add | solution.py:225
  (1 shorter events, 0.0 us)
Async XLA Ops:
  0.0 8.8 %collective-permute-start = (bf16[2,64,1024]{2,1,0:T(8,128)(2,1)}, bf16[2,64,1024]{2,1,0:T(8,128)(2,1)S(1)}, u32[]{:S(2)}, u32[]{:S(2)}) collective-permute-start(bf16[2,64,1024]{2,1,0:T(8,128)(2,1)} %refs_0_.1), channel_id=1, source_target_pairs={{0,8},{1,3},{2,10},{3,1},{4,12},{5,7},{6,14},{7,5},{8,0},{9,11},{1... | collective-permute-start | bytes 786440 | tf_op jit(solution)/shard_map/ppermute | solution.py:206
  3.0 5.8 %collective-permute-start.1 = (bf16[2,64,1024]{2,1,0:T(8,128)(2,1)}, bf16[2,64,1024]{2,1,0:T(8,128)(2,1)S(1)}, u32[]{:S(2)}, u32[]{:S(2)}) collective-permute-start(bf16[2,64,1024]{2,1,0:T(8,128)(2,1)} %refs_0_.1), channel_id=1, source_target_pairs={{0,3},{1,0},{2,1},{3,2},{4,7},{5,4},{6,5},{7,6},{8,11},{9,8},{10,9... | collective-permute-start | bytes 786440 | tf_op jit(solution)/shard_map/ppermute | solution.py:206
  6.3 2.4 %collective-permute-start.2 = (bf16[688,128]{1,0:T(8,128)(2,1)S(1)}, bf16[688,128]{1,0:T(8,128)(2,1)S(1)}, u32[]{:S(2)}, u32[]{:S(2)}) collective-permute-start(bf16[688,128]{1,0:T(8,128)(2,1)S(1)} %get-tuple-element.10), channel_id=1, source_target_pairs={{0,1},{1,0},{2,3},{3,2},{4,5},{5,4},{6,7},{7,6},{8,9},{9,8},{10,11... | collective-permute-start | bytes 528392 | tf_op jit(solution)/shard_map/ppermute | solution.py:199
  6.9 1.9 %collective-permute-start.3 = (bf16[688,128]{1,0:T(8,128)(2,1)S(1)}, bf16[688,128]{1,0:T(8,128)(2,1)S(1)}, u32[]{:S(2)}, u32[]{:S(2)}) collective-permute-start(bf16[688,128]{1,0:T(8,128)(2,1)S(1)} %get-tuple-element.11), channel_id=1, source_target_pairs={{0,1},{1,0},{2,3},{3,2},{4,5},{5,4},{6,7},{7,6},{8,9},{9,8},{10,11... | collective-permute-start | bytes 528392 | tf_op jit(solution)/shard_map/ppermute | solution.py:199
  7.0 1.8 %collective-permute-start.4 = (bf16[672,128]{1,0:T(8,128)(2,1)S(1)}, bf16[672,128]{1,0:T(8,128)(2,1)S(1)}, u32[]{:S(2)}, u32[]{:S(2)}) collective-permute-start(bf16[672,128]{1,0:T(8,128)(2,1)S(1)} %get-tuple-element.12), channel_id=1, source_target_pairs={{0,1},{1,0},{2,3},{3,2},{4,5},{5,4},{6,7},{7,6},{8,9},{9,8},{10,11... | collective-permute-start | bytes 516104 | tf_op jit(solution)/shard_map/ppermute | solution.py:199
  7.4 1.4 %copy-start = (bf16[2,64,1024]{2,1,0:T(8,128)(2,1)S(1)}, bf16[2,64,1024]{2,1,0:T(8,128)(2,1)}, u32[]{:S(2)}) copy-start(bf16[2,64,1024]{2,1,0:T(8,128)(2,1)} %refs_0_.1) | copy-start | bytes 786436
  19.0 1.2 %collective-permute-start.5 = (f32[1024]{0:T(1024)S(1)}, f32[1024]{0:T(1024)S(1)}, u32[]{:S(2)}, u32[]{:S(2)}) collective-permute-start(f32[1024]{0:T(1024)S(1)} %bitcast.2), channel_id=1, source_target_pairs={{0,1},{1,0},{2,3},{3,2},{4,5},{5,4},{6,7},{7,6},{8,9},{9,8},{10,11... | collective-permute-start | bytes 12296 | tf_op jit(solution)/shard_map/ppermute | solution.py:199

commit v35 on v34

--- a/solution.py
+++ b/solution.py
@@ -214,7 +214,7 @@
     groups = [
         [
             (2 * side + group) * cuts + 2 * plane + column
-            for side in range(stems // 2 - 1, -1, -1) for plane in range(cuts // 2 - 1, -1, -1) for column in (1, 0)
+            for side in range(stems // 2 - 1, -1, -1) for column in (1, 0) for plane in range(cuts // 2 - 1, -1, -1)
         ]
         for group in (0, 1)
     ]

time: 21 us -> 21.1 us (level)
  no operation moved by 1% of the time
where the time goes in v35:
time: 21.1 us; the launch traced here: 20.9 us
  blocking collectives  9.8 us (46%)
  Pallas kernels  5.07 us (24%)
  starting transfers between devices  4.51 us (21%)
  waiting for transfers between devices  0.89 us (4%)
  other arithmetic  0.61 us (3%)
    all_to_all x1, blocking collectives, on_device(): lax.all_to_all(spread, ('stem', 'cuts'), 0, 0, tiled=True, axis_index_gro...  9.8 us
    pallas_call x1, Pallas kernels, branch_sums(): pl.pallas_call(functools.partial(leave_kernel, total // groups), in_specs...  3.31 us
    ppermute x2, starting transfers between devices, route(): return lax.ppermute(stem_tensor, ('cuts', 'stem'), pairs)  3.03 us
    ppermute x4, starting transfers between devices, swap(): return lax.ppermute(x, 'stem', [(s, s ^ p) for s in range(stems)])  1.48 us
    pallas_call x1, Pallas kernels, branch_sums(): pl.pallas_call(stay_kernel, out_shape=jax.ShapeDtypeStruct((half, depth,...  1.32 us
    ppermute x4, waiting for transfers between devices, swap(): return lax.ppermute(x, 'stem', [(s, s ^ p) for s in range(stems)])  0.84 us
    add x1, other arithmetic, on_device(): return total + swap(total, 1)  0.6 us
    pallas_call x1, Pallas kernels, close(): pl.pallas_call(functools.partial(close_kernel, targets if whole_tiles els...  0.44 us
  transfers between devices with their start and end apart: 6, of which 1 were waited for; matrix products, arithmetic and copies ran while one was open for 0% of the time, Pallas kernels for 22%

profile of v35, /device:TPU:0, one launch (start us, length us, event | category | flops | bytes accessed | tf_op | source)
XLA Modules:
  0.0 20.9 jit_solution(1364642383090608356)
XLA Ops:
  0.0 3.0 %collective-permute-start = (bf16[2,64,1024]{2,1,0:T(8,128)(2,1)}, bf16[2,64,1024]{2,1,0:T(8,128)(2,1)S(1)}, u32[]{:S(2)}, u32[]{:S(2)}) collective-permute-start(bf16[2,64,1024]{2,1,0:T(8,128)(2,1)} %refs_0_.1), channel_id=1, source_target_pairs={{0,8},{1,3},{2,10},{3,1},{4,12},{5,7},{6,14},{7,5},{8,0},{9,11},{1... | collective-permute-start | bytes 786440 | tf_op jit(solution)/shard_map/ppermute | solution.py:206
  3.0 0.0 collective-permute-start.1
  3.0 3.3 %leave.1 = (bf16[16,512,128]{2,1,0:T(8,128)(2,1)S(1)}, bf16[4,16,64,128]{3,2,1,0:T(8,128)(2,1)S(1)}, bf16[688,128]{1,0:T(8,128)(2,1)S(1)}, bf16[688,128]{1,0:T(8,128)(2,1)S(1)}, bf16[672,128]{1,0:T(8,128)(2,1)S(1)}) custom-call(bf16[16,512,128]{2,1,0:T(8,128)(2,1)} %mid_hbm.1, bf16[8,16,64,128]{3,2,1,0:T(8,128)(2,1)} %right_hbm.1), custom_call_target="tpu_custom_call" | custom-call | flops 1073741824 | bytes 4194304 | tf_op jit(solution)/shard_map/leave/pallas_call | solution.py:123
  6.3 0.6 %collective-permute-start.2 = (bf16[688,128]{1,0:T(8,128)(2,1)S(1)}, bf16[688,128]{1,0:T(8,128)(2,1)S(1)}, u32[]{:S(2)}, u32[]{:S(2)}) collective-permute-start(bf16[688,128]{1,0:T(8,128)(2,1)S(1)} %get-tuple-element.10), channel_id=1, source_target_pairs={{0,1},{1,0},{2,3},{3,2},{4,5},{5,4},{6,7},{7,6},{8,9},{9,8},{10,11... | collective-permute-start | bytes 528392 | tf_op jit(solution)/shard_map/ppermute | solution.py:199
  6.9 0.1 collective-permute-start.3
  7.0 0.4 %collective-permute-start.4 = (bf16[672,128]{1,0:T(8,128)(2,1)S(1)}, bf16[672,128]{1,0:T(8,128)(2,1)S(1)}, u32[]{:S(2)}, u32[]{:S(2)}) collective-permute-start(bf16[672,128]{1,0:T(8,128)(2,1)S(1)} %get-tuple-element.12), channel_id=1, source_target_pairs={{0,1},{1,0},{2,3},{3,2},{4,5},{5,4},{6,7},{7,6},{8,9},{9,8},{10,11... | collective-permute-start | bytes 516104 | tf_op jit(solution)/shard_map/ppermute | solution.py:199
  7.4 0.0 copy-start
  7.4 1.3 %stay.1.refs_6_ = f32[4,512,128]{2,1,0:T(8,128)S(1)} custom-call(bf16[16,512,128]{2,1,0:T(8,128)(2,1)S(1)} %get-tuple-element.13.mid_ref, bf16[4,16,64,128]{3,2,1,0:T(8,128)(2,1)S(1)} %get-tuple-element.14.wide_ref), custom_call_target="tpu_custom_call" | custom-call | flops 1073741824 | bytes 4194304 | tf_op jit(solution)/shard_map/stay/pallas_call | solution.py:140
  8.8 0.0 collective-permute-done.4.refs_5_
  8.8 0.0 collective-permute-done.2.refs_3_
  8.8 0.0 collective-permute-done.3.refs_4_
  8.8 0.0 collective-permute-done.refs_1_
  8.8 0.0 collective-permute-done.1.refs_2_
  8.8 0.0 copy-done
  8.9 0.4 %close.1 = bf16[16,8,128]{2,1,0:T(8,128)(2,1)S(1)} custom-call(bf16[2,64,1024]{2,1,0:T(8,128)(2,1)S(1)} %copy-done, bf16[2,64,1024]{2,1,0:T(8,128)(2,1)S(1)} %collective-permute-done.refs_1_, bf16[2,64,1024]{2,1,0:T(8,128)(2,1)S(1)} %collective-permute-done.1.refs_2_, bf16[688,128]{1,0:T(8,128)(2,1)S(1)} %collective-permute-done.2.refs_3_, ...), custom_call_target="tpu_custom_call" | custom-call | flops 134217728 | bytes 1048576 | tf_op jit(solution)/shard_map/close/pallas_call | solution.py:184
  9.3 9.8 %all_to_all.5 = bf16[16,8,128]{2,1,0:T(8,128)(2,1)S(1)} all-to-all(bf16[16,8,128]{2,1,0:T(8,128)(2,1)S(1)} %close.1), channel_id=1, replica_groups={{30,22,14,6,26,18,10,2,28,20,12,4,24,16,8,0},{31,23,15,7,27,19,11,3,29,..., dimensions={0} | all-to-all | bytes 65536 | tf_op jit(solution)/shard_map/all_to_all | solution.py:223
  19.1 0.4 %collective-permute-start.5 = (f32[1024]{0:T(1024)S(1)}, f32[1024]{0:T(1024)S(1)}, u32[]{:S(2)}, u32[]{:S(2)}) collective-permute-start(f32[1024]{0:T(1024)S(1)} %bitcast.2), channel_id=1, source_target_pairs={{0,1},{1,0},{2,3},{3,2},{4,5},{5,4},{6,7},{7,6},{8,9},{9,8},{10,11... | collective-permute-start | bytes 12296 | tf_op jit(solution)/shard_map/ppermute | solution.py:199
  19.5 0.8 %collective-permute-done.5 = f32[1024]{0:T(1024)S(1)} collective-permute-done((f32[1024]{0:T(1024)S(1)}, f32[1024]{0:T(1024)S(1)}, u32[]{:S(2)}, u32[]{:S(2)}) %collective-permute-start.5) | collective-permute-done | bytes 4128 | tf_op jit(solution)/shard_map/ppermute | solution.py:199
  20.3 0.6 %bitcast_add_fusion = f32[1024]{0:T(1024)} fusion(f32[1024]{0:T(1024)S(1)} %collective-permute-done.5, f32[8,128]{1,0:T(8,128)S(1)} %convert_reduce_fusion), kind=kLoop, calls=%fused_computation.1 | loop fusion | flops 1024 | bytes 12288 | tf_op jit(solution)/shard_map/add | solution.py:225
  (1 shorter events, 0.0 us)
Async XLA Ops:
  0.0 8.8 %collective-permute-start = (bf16[2,64,1024]{2,1,0:T(8,128)(2,1)}, bf16[2,64,1024]{2,1,0:T(8,128)(2,1)S(1)}, u32[]{:S(2)}, u32[]{:S(2)}) collective-permute-start(bf16[2,64,1024]{2,1,0:T(8,128)(2,1)} %refs_0_.1), channel_id=1, source_target_pairs={{0,8},{1,3},{2,10},{3,1},{4,12},{5,7},{6,14},{7,5},{8,0},{9,11},{1... | collective-permute-start | bytes 786440 | tf_op jit(solution)/shard_map/ppermute | solution.py:206
  3.0 5.8 %collective-permute-start.1 = (bf16[2,64,1024]{2,1,0:T(8,128)(2,1)}, bf16[2,64,1024]{2,1,0:T(8,128)(2,1)S(1)}, u32[]{:S(2)}, u32[]{:S(2)}) collective-permute-start(bf16[2,64,1024]{2,1,0:T(8,128)(2,1)} %refs_0_.1), channel_id=1, source_target_pairs={{0,3},{1,0},{2,1},{3,2},{4,7},{5,4},{6,5},{7,6},{8,11},{9,8},{10,9... | collective-permute-start | bytes 786440 | tf_op jit(solution)/shard_map/ppermute | solution.py:206
  6.3 2.4 %collective-permute-start.2 = (bf16[688,128]{1,0:T(8,128)(2,1)S(1)}, bf16[688,128]{1,0:T(8,128)(2,1)S(1)}, u32[]{:S(2)}, u32[]{:S(2)}) collective-permute-start(bf16[688,128]{1,0:T(8,128)(2,1)S(1)} %get-tuple-element.10), channel_id=1, source_target_pairs={{0,1},{1,0},{2,3},{3,2},{4,5},{5,4},{6,7},{7,6},{8,9},{9,8},{10,11... | collective-permute-start | bytes 528392 | tf_op jit(solution)/shard_map/ppermute | solution.py:199
  6.9 1.9 %collective-permute-start.3 = (bf16[688,128]{1,0:T(8,128)(2,1)S(1)}, bf16[688,128]{1,0:T(8,128)(2,1)S(1)}, u32[]{:S(2)}, u32[]{:S(2)}) collective-permute-start(bf16[688,128]{1,0:T(8,128)(2,1)S(1)} %get-tuple-element.11), channel_id=1, source_target_pairs={{0,1},{1,0},{2,3},{3,2},{4,5},{5,4},{6,7},{7,6},{8,9},{9,8},{10,11... | collective-permute-start | bytes 528392 | tf_op jit(solution)/shard_map/ppermute | solution.py:199
  7.0 1.8 %collective-permute-start.4 = (bf16[672,128]{1,0:T(8,128)(2,1)S(1)}, bf16[672,128]{1,0:T(8,128)(2,1)S(1)}, u32[]{:S(2)}, u32[]{:S(2)}) collective-permute-start(bf16[672,128]{1,0:T(8,128)(2,1)S(1)} %get-tuple-element.12), channel_id=1, source_target_pairs={{0,1},{1,0},{2,3},{3,2},{4,5},{5,4},{6,7},{7,6},{8,9},{9,8},{10,11... | collective-permute-start | bytes 516104 | tf_op jit(solution)/shard_map/ppermute | solution.py:199
  7.4 1.4 %copy-start = (bf16[2,64,1024]{2,1,0:T(8,128)(2,1)S(1)}, bf16[2,64,1024]{2,1,0:T(8,128)(2,1)}, u32[]{:S(2)}) copy-start(bf16[2,64,1024]{2,1,0:T(8,128)(2,1)} %refs_0_.1) | copy-start | bytes 786436
  19.1 1.2 %collective-permute-start.5 = (f32[1024]{0:T(1024)S(1)}, f32[1024]{0:T(1024)S(1)}, u32[]{:S(2)}, u32[]{:S(2)}) collective-permute-start(f32[1024]{0:T(1024)S(1)} %bitcast.2), channel_id=1, source_target_pairs={{0,1},{1,0},{2,3},{3,2},{4,5},{5,4},{6,7},{7,6},{8,9},{9,8},{10,11... | collective-permute-start | bytes 12296 | tf_op jit(solution)/shard_map/ppermute | solution.py:199

commit v36 on v34

--- a/solution.py
+++ b/solution.py
@@ -174,7 +174,7 @@
     else:
         rows = out_ref.shape[1]
         for at, c in enumerate(targets):
-            out_ref[at] = total[c * rows:(c + 1) * rows].astype(out_ref.dtype)
+            out_ref[at] = total[c * rows:(c + 1) * rows]
 
 
 def close(stems, kept, got, cuts, targets):
@@ -183,7 +183,7 @@
     shape = (len(targets), rows // cuts, width) if whole_tiles else (rows, width)
     out = pl.pallas_call(
         functools.partial(close_kernel, targets if whole_tiles else None),
-        out_shape=jax.ShapeDtypeStruct(shape, jnp.bfloat16 if whole_tiles else jnp.float32),
+        out_shape=jax.ShapeDtypeStruct(shape, jnp.float32),
         compiler_params=pltpu.CompilerParams(vmem_limit_bytes=24 * MIB),
         cost_estimate=pl.CostEstimate(flops=8 * rows * kept.size, bytes_accessed=MIB, transcendentals=0),
         name="close",
@@ -221,7 +221,7 @@
     targets = [at % cuts for at in groups[0]]
     spread = close(pieces, kept, got, cuts, targets)
     parts = lax.all_to_all(spread, ("stem", "cuts"), 0, 0, tiled=True, axis_index_groups=groups)
-    total = jnp.sum(parts.astype(jnp.float32), axis=0).reshape(-1)
+    total = jnp.sum(parts, axis=0).reshape(-1)
     return total + swap(total, 1)
 
 

time: 21 us -> 21.6 us (1.029)
  blocking collectives: 9.7 us -> 10.3 us
    all_to_all x1, blocking collectives: 9.7 us -> 10.3 us  [on_device(): lax.all_to_all(spread, ('stem', 'cuts'), 0, 0, tiled=True, axis_index_gro...]
where the time goes in v36:
time: 21.6 us; the launch traced here: 21.5 us
  blocking collectives  10.3 us (48%)
  Pallas kernels  5.07 us (23%)
  starting transfers between devices  4.38 us (20%)
  waiting for transfers between devices  1.02 us (5%)
  other arithmetic  0.61 us (3%)
    all_to_all x1, blocking collectives, on_device(): lax.all_to_all(spread, ('stem', 'cuts'), 0, 0, tiled=True, axis_index_gro...  10.3 us
    pallas_call x1, Pallas kernels, branch_sums(): pl.pallas_call(functools.partial(leave_kernel, total // groups), in_specs...  3.31 us
    ppermute x2, starting transfers between devices, route(): return lax.ppermute(stem_tensor, ('cuts', 'stem'), pairs)  3.03 us
    ppermute x4, starting transfers between devices, swap(): return lax.ppermute(x, 'stem', [(s, s ^ p) for s in range(stems)])  1.35 us
    pallas_call x1, Pallas kernels, branch_sums(): pl.pallas_call(stay_kernel, out_shape=jax.ShapeDtypeStruct((half, depth,...  1.32 us
    ppermute x4, waiting for transfers between devices, swap(): return lax.ppermute(x, 'stem', [(s, s ^ p) for s in range(stems)])  0.97 us
    add x1, other arithmetic, on_device(): return total + swap(total, 1)  0.6 us
    pallas_call x1, Pallas kernels, close(): pl.pallas_call(functools.partial(close_kernel, targets if whole_tiles els...  0.44 us
  transfers between devices with their start and end apart: 6, of which 1 were waited for; matrix products, arithmetic and copies ran while one was open for 0% of the time, Pallas kernels for 22%

profile of v36, /device:TPU:0, one launch (start us, length us, event | category | flops | bytes accessed | tf_op | source)
XLA Modules:
  0.0 21.5 jit_solution(7332889587436193678)
XLA Ops:
  0.0 3.0 %collective-permute-start = (bf16[2,64,1024]{2,1,0:T(8,128)(2,1)}, bf16[2,64,1024]{2,1,0:T(8,128)(2,1)S(1)}, u32[]{:S(2)}, u32[]{:S(2)}) collective-permute-start(bf16[2,64,1024]{2,1,0:T(8,128)(2,1)} %refs_0_.1), channel_id=1, source_target_pairs={{0,8},{1,3},{2,10},{3,1},{4,12},{5,7},{6,14},{7,5},{8,0},{9,11},{1... | collective-permute-start | bytes 786440 | tf_op jit(solution)/shard_map/ppermute | solution.py:206
  3.0 0.0 collective-permute-start.1
  3.0 3.3 %leave.1 = (bf16[16,512,128]{2,1,0:T(8,128)(2,1)S(1)}, bf16[4,16,64,128]{3,2,1,0:T(8,128)(2,1)S(1)}, bf16[688,128]{1,0:T(8,128)(2,1)S(1)}, bf16[688,128]{1,0:T(8,128)(2,1)S(1)}, bf16[672,128]{1,0:T(8,128)(2,1)S(1)}) custom-call(bf16[16,512,128]{2,1,0:T(8,128)(2,1)} %mid_hbm.1, bf16[8,16,64,128]{3,2,1,0:T(8,128)(2,1)} %right_hbm.1), custom_call_target="tpu_custom_call" | custom-call | flops 1073741824 | bytes 4194304 | tf_op jit(solution)/shard_map/leave/pallas_call | solution.py:123
  6.3 0.6 %collective-permute-start.2 = (bf16[688,128]{1,0:T(8,128)(2,1)S(1)}, bf16[688,128]{1,0:T(8,128)(2,1)S(1)}, u32[]{:S(2)}, u32[]{:S(2)}) collective-permute-start(bf16[688,128]{1,0:T(8,128)(2,1)S(1)} %get-tuple-element.10), channel_id=1, source_target_pairs={{0,1},{1,0},{2,3},{3,2},{4,5},{5,4},{6,7},{7,6},{8,9},{9,8},{10,11... | collective-permute-start | bytes 528392 | tf_op jit(solution)/shard_map/ppermute | solution.py:199
  6.9 0.1 collective-permute-start.3
  7.0 0.4 %collective-permute-start.4 = (bf16[672,128]{1,0:T(8,128)(2,1)S(1)}, bf16[672,128]{1,0:T(8,128)(2,1)S(1)}, u32[]{:S(2)}, u32[]{:S(2)}) collective-permute-start(bf16[672,128]{1,0:T(8,128)(2,1)S(1)} %get-tuple-element.12), channel_id=1, source_target_pairs={{0,1},{1,0},{2,3},{3,2},{4,5},{5,4},{6,7},{7,6},{8,9},{9,8},{10,11... | collective-permute-start | bytes 516104 | tf_op jit(solution)/shard_map/ppermute | solution.py:199
  7.4 0.0 copy-start
  7.4 1.3 %stay.1.refs_6_ = f32[4,512,128]{2,1,0:T(8,128)S(1)} custom-call(bf16[16,512,128]{2,1,0:T(8,128)(2,1)S(1)} %get-tuple-element.13.mid_ref, bf16[4,16,64,128]{3,2,1,0:T(8,128)(2,1)S(1)} %get-tuple-element.14.wide_ref), custom_call_target="tpu_custom_call" | custom-call | flops 1073741824 | bytes 4194304 | tf_op jit(solution)/shard_map/stay/pallas_call | solution.py:140
  8.8 0.0 collective-permute-done.4.refs_5_
  8.8 0.0 collective-permute-done.2.refs_3_
  8.8 0.0 collective-permute-done.3.refs_4_
  8.8 0.0 collective-permute-done.refs_1_
  8.8 0.0 collective-permute-done.1.refs_2_
  8.8 0.0 copy-done
  8.9 0.4 %close.1 = f32[16,8,128]{2,1,0:T(8,128)S(1)} custom-call(bf16[2,64,1024]{2,1,0:T(8,128)(2,1)S(1)} %copy-done, bf16[2,64,1024]{2,1,0:T(8,128)(2,1)S(1)} %collective-permute-done.refs_1_, bf16[2,64,1024]{2,1,0:T(8,128)(2,1)S(1)} %collective-permute-done.1.refs_2_, bf16[688,128]{1,0:T(8,128)(2,1)S(1)} %collective-permute-done.2.refs_3_, ...), custom_call_target="tpu_custom_call" | custom-call | flops 134217728 | bytes 1048576 | tf_op jit(solution)/shard_map/close/pallas_call | solution.py:184
  9.3 10.3 %all_to_all.5 = f32[16,8,128]{2,1,0:T(8,128)S(1)} all-to-all(f32[16,8,128]{2,1,0:T(8,128)S(1)} %close.1), channel_id=1, replica_groups={{30,26,22,18,14,10,6,2,28,24,20,16,12,8,4,0},{31,27,23,19,15,11,7,3,29,..., dimensions={0} | all-to-all | bytes 131072 | tf_op jit(solution)/shard_map/all_to_all | solution.py:223
  19.6 0.3 %collective-permute-start.5 = (f32[1024]{0:T(1024)S(1)}, f32[1024]{0:T(1024)S(1)}, u32[]{:S(2)}, u32[]{:S(2)}) collective-permute-start(f32[1024]{0:T(1024)S(1)} %bitcast.2), channel_id=1, source_target_pairs={{0,1},{1,0},{2,3},{3,2},{4,5},{5,4},{6,7},{7,6},{8,9},{9,8},{10,11... | collective-permute-start | bytes 12296 | tf_op jit(solution)/shard_map/ppermute | solution.py:199
  19.9 1.0 %collective-permute-done.5 = f32[1024]{0:T(1024)S(1)} collective-permute-done((f32[1024]{0:T(1024)S(1)}, f32[1024]{0:T(1024)S(1)}, u32[]{:S(2)}, u32[]{:S(2)}) %collective-permute-start.5) | collective-permute-done | bytes 4128 | tf_op jit(solution)/shard_map/ppermute | solution.py:199
  20.9 0.6 %bitcast_add_fusion = f32[1024]{0:T(1024)} fusion(f32[1024]{0:T(1024)S(1)} %collective-permute-done.5, f32[8,128]{1,0:T(8,128)S(1)} %reduce_sum.9), kind=kLoop, calls=%fused_computation | loop fusion | flops 1024 | bytes 12288 | tf_op jit(solution)/shard_map/add | solution.py:225
  (1 shorter events, 0.0 us)
Async XLA Ops:
  0.0 8.8 %collective-permute-start = (bf16[2,64,1024]{2,1,0:T(8,128)(2,1)}, bf16[2,64,1024]{2,1,0:T(8,128)(2,1)S(1)}, u32[]{:S(2)}, u32[]{:S(2)}) collective-permute-start(bf16[2,64,1024]{2,1,0:T(8,128)(2,1)} %refs_0_.1), channel_id=1, source_target_pairs={{0,8},{1,3},{2,10},{3,1},{4,12},{5,7},{6,14},{7,5},{8,0},{9,11},{1... | collective-permute-start | bytes 786440 | tf_op jit(solution)/shard_map/ppermute | solution.py:206
  3.0 5.8 %collective-permute-start.1 = (bf16[2,64,1024]{2,1,0:T(8,128)(2,1)}, bf16[2,64,1024]{2,1,0:T(8,128)(2,1)S(1)}, u32[]{:S(2)}, u32[]{:S(2)}) collective-permute-start(bf16[2,64,1024]{2,1,0:T(8,128)(2,1)} %refs_0_.1), channel_id=1, source_target_pairs={{0,3},{1,0},{2,1},{3,2},{4,7},{5,4},{6,5},{7,6},{8,11},{9,8},{10,9... | collective-permute-start | bytes 786440 | tf_op jit(solution)/shard_map/ppermute | solution.py:206
  6.3 2.4 %collective-permute-start.2 = (bf16[688,128]{1,0:T(8,128)(2,1)S(1)}, bf16[688,128]{1,0:T(8,128)(2,1)S(1)}, u32[]{:S(2)}, u32[]{:S(2)}) collective-permute-start(bf16[688,128]{1,0:T(8,128)(2,1)S(1)} %get-tuple-element.10), channel_id=1, source_target_pairs={{0,1},{1,0},{2,3},{3,2},{4,5},{5,4},{6,7},{7,6},{8,9},{9,8},{10,11... | collective-permute-start | bytes 528392 | tf_op jit(solution)/shard_map/ppermute | solution.py:199
  6.9 1.9 %collective-permute-start.3 = (bf16[688,128]{1,0:T(8,128)(2,1)S(1)}, bf16[688,128]{1,0:T(8,128)(2,1)S(1)}, u32[]{:S(2)}, u32[]{:S(2)}) collective-permute-start(bf16[688,128]{1,0:T(8,128)(2,1)S(1)} %get-tuple-element.11), channel_id=1, source_target_pairs={{0,1},{1,0},{2,3},{3,2},{4,5},{5,4},{6,7},{7,6},{8,9},{9,8},{10,11... | collective-permute-start | bytes 528392 | tf_op jit(solution)/shard_map/ppermute | solution.py:199
  7.0 1.8 %collective-permute-start.4 = (bf16[672,128]{1,0:T(8,128)(2,1)S(1)}, bf16[672,128]{1,0:T(8,128)(2,1)S(1)}, u32[]{:S(2)}, u32[]{:S(2)}) collective-permute-start(bf16[672,128]{1,0:T(8,128)(2,1)S(1)} %get-tuple-element.12), channel_id=1, source_target_pairs={{0,1},{1,0},{2,3},{3,2},{4,5},{5,4},{6,7},{7,6},{8,9},{9,8},{10,11... | collective-permute-start | bytes 516104 | tf_op jit(solution)/shard_map/ppermute | solution.py:199
  7.4 1.4 %copy-start = (bf16[2,64,1024]{2,1,0:T(8,128)(2,1)S(1)}, bf16[2,64,1024]{2,1,0:T(8,128)(2,1)}, u32[]{:S(2)}) copy-start(bf16[2,64,1024]{2,1,0:T(8,128)(2,1)} %refs_0_.1) | copy-start | bytes 786436
  19.6 1.2 %collective-permute-start.5 = (f32[1024]{0:T(1024)S(1)}, f32[1024]{0:T(1024)S(1)}, u32[]{:S(2)}, u32[]{:S(2)}) collective-permute-start(f32[1024]{0:T(1024)S(1)} %bitcast.2), channel_id=1, source_target_pairs={{0,1},{1,0},{2,3},{3,2},{4,5},{5,4},{6,7},{7,6},{8,9},{9,8},{10,11... | collective-permute-start | bytes 12296 | tf_op jit(solution)/shard_map/ppermute | solution.py:199
